TPU v7x, 32 devices: a whole 2x2x4 slice. The times are simulated.
32 devices in a mesh: cuts: 16 (over z, y, core), chan: 2 (over x).
Axes of the slice: x: 2, y: 2, z: 4, core: 2. Of those that a mesh axis runs over, the one named last changes fastest.
Arguments:
- data: bfloat16 [128, 384, 1024], P('cuts', None, 'chan'), may hold values from -6 to 6
- order: int32 [128], P('cuts'), may hold values from 0 to 127, as said below
- chan_factor: bfloat16 [1024, 64], P('chan'), may hold values from -0.1875 to 0.1875
- slice_weights: float32 [128, 64], P('cuts'), may hold values from 0.5 to 2
- smooth_aux: float32 [128, 384, 64], P('cuts', 'chan'), may hold values from -6 to 6
- coupled: float32 [128, 384, 64], P('cuts', 'chan'), may hold values from -6 to 6
- smooth_dual: float32 [128, 384, 64], P('cuts', 'chan'), may hold values from -2 to 2
- coupling_dual: float32 [128, 384, 64], P('cuts', 'chan'), may hold values from -2 to 2
- delta: float32 [64, 64], replicated, may hold values from -0.1125 to 1.1125, as said below
Outputs:
- evolving: float32 [128, 384, 64], P('cuts', 'chan')
- coupled_out: float32 [128, 384, 64], P('cuts', 'chan')
- delta_out: float32 [64, 64], replicated
Inputs may be any that keep to these rules, and one draw needn't show every extreme that they name: `order`: within each aligned block of 8 entries (the slices of one index of cuts) the entries are a permutation of that block's own slice indices; entry k names the stored slice of phase bin k. `delta`: A full-rank matrix.
All inputs are finite; a program needn't handle non-finite values.
Results may differ from a plain program's by a relative error of at most 0.0003.
Values sent between devices are 32-bit elements; how exact they have to be, the bound alone decides.
No kernel may reach another device: no remote copies, remote signals or barrier semaphores. Data moves between devices by JAX's collectives and lax.ppermute only.
A program may use at most 64 MiB of HBM per device.

v0:
```python
import functools

import jax
import jax.numpy as jnp
from jax import lax
from jax.experimental import pallas as pl
from jax.experimental.pallas import tpu as pltpu
from jax.sharding import PartitionSpec as P

INNER = 3
SWEEPS = 4
POLAR = 8

smooth_weight = 1.0
eps_trace = 1e-06
f32 = jnp.float32
bf16 = jnp.bfloat16
NN = (((1,), (0,)), ((), ()))
NT = (((1,), (1,)), ((), ()))


def dot(left, right, dims=NN):
    return lax.dot_general(left, right, dims, preferred_element_type=f32)


def split(value):
    high = value.astype(bf16)
    low = (value - high.astype(f32)).astype(bf16)
    return high, low


def left_triple(value):
    high, low = split(value)
    return jnp.concatenate([high, high, low], axis=1)


def right_triple(value):
    high, low = split(value)
    return jnp.concatenate([high, low, high], axis=0)


def block_mask(rank, group):
    wide = rank * group
    rows = lax.div(lax.broadcasted_iota(jnp.int32, (wide, wide), 0), rank)
    cols = lax.div(lax.broadcasted_iota(jnp.int32, (wide, wide), 1), rank)
    return jnp.where(rows == cols, 1.0, 0.0).astype(bf16)


def wide_eye(rank, group):
    rows = lax.broadcasted_iota(jnp.int32, (rank, rank * group), 0)
    cols = lax.broadcasted_iota(jnp.int32, (rank, rank * group), 1)
    return jnp.where(rows == lax.rem(cols, rank), 1.0, 0.0).astype(f32)


def block_diagonal(value, mask, group):
    high, low = split(value)
    return (
        jnp.concatenate([high] * group, axis=0) * mask,
        jnp.concatenate([low] * group, axis=0) * mask,
    )


def times_blocks(values, blocks, dims=NN):
    rank = values[0].shape[0]
    count = len(values)
    pieces = [split(value) for value in values]
    high = jnp.concatenate([piece[0] for piece in pieces], axis=0)
    both = jnp.concatenate([high] + [piece[1] for piece in pieces], axis=0)
    first = dot(both, blocks[0], dims)
    total = first[: count * rank] + first[count * rank :] + dot(high, blocks[1], dims)
    return [total[at * rank : (at + 1) * rank] for at in range(count)]


def diagonal_blocks(value, rank, group):
    at = lax.div(lax.broadcasted_iota(jnp.int32, (rank, rank * group), 1), rank)
    total = value[:rank]
    for block in range(1, group):
        total = jnp.where(at == block, value[block * rank : (block + 1) * rank], total)
    return total


def group_size(count, rank):
    group = max(1, 256 // rank)
    while count % group:
        group -= 1
    return group


def project_kernel(first, order_ref, me_ref, data_ref, factor_ref, *refs):
    (gram_ref, *outs), held, arrived = refs[:-2], refs[-2], refs[-1]
    parts = len(outs)
    pairs = outs[0].shape[0]
    rows = outs[0].shape[2] // 2
    count = data_ref.shape[0]
    copies = []
    for at in range(2 * pairs):
        stored = lax.rem(order_ref[2 * first + at], count)
        copy = pltpu.make_async_copy(data_ref.at[stored], held.at[at], arrived.at[at])
        copy.start()
        copies.append(copy)
    factor = factor_ref[...]
    gram_ref[...] = dot(factor, factor, NT)
    for pair in range(pairs):
        copies[2 * pair].wait()
        copies[2 * pair + 1].wait()
        for part in reversed(range(parts)):
            start = pl.multiple_of(lax.rem(me_ref[0] + part, parts) * rows, 16)
            both = jnp.concatenate(
                [held[2 * pair, pl.ds(start, rows), :], held[2 * pair + 1, pl.ds(start, rows), :]],
                axis=0,
            )
            outs[part][pair] = dot(both, factor, NT).T


def setup_kernel(grams, chunks, group, *refs):
    gram_refs, refs = refs[:grams], refs[grams:]
    projected_refs, refs = refs[:chunks], refs[chunks:]
    (own_ref, weights_ref, aux_ref, coupled_ref, dual_s_ref, dual_c_ref) = refs[:6]
    (inverse_ref, rho_ref, head_ref, tail_ref, base_ref) = refs[6:]
    count, rank = own_ref.shape
    rows = aux_ref.shape[2]
    pairs = projected_refs[0].shape[0]
    gram = gram_refs[0][...]
    for ref in gram_refs[1:]:
        gram = gram + ref[...]
    eye = wide_eye(rank, 1)
    diagonal = jnp.sum(gram * eye, axis=0, keepdims=True)
    weights = own_ref[...]
    rho = jnp.sum(weights * weights * diagonal, axis=1, keepdims=True) / rank
    rho_lanes = jnp.broadcast_to(rho, rho_ref.shape)
    rho_ref[...] = rho_lanes
    head_ref[...] = rho_lanes[:SWEEPS]
    tail_ref[...] = rho_lanes[count - SWEEPS :]

    edge = 34.0 / 32.0
    lead = 4.0 * edge**3 / (4.0 * edge**3 - 3.0 * edge)
    mask = block_mask(rank, group)
    wide = wide_eye(rank, group)
    starts = range(0, count, group)
    systems = []
    for first in starts:
        scaled = []
        for k in range(first, first + group):
            unit = 1.0 / (34.0 * rho[k : k + 1, :])
            column = weights_ref[:, k : k + 1]
            scaled.append(column * gram * own_ref[k : k + 1, :] * unit + (2.0 / 34.0) * eye)
        systems.append(jnp.concatenate(scaled, axis=1))
    inverses, rests = [], []
    for system in systems:
        rest = wide - system
        blocks = block_diagonal(rest, mask, group)
        (square,) = times_blocks([rest], blocks)
        (cube,) = times_blocks([square], blocks)
        inverses.append(wide + lead * (rest + square))
        rests.append(lead * cube - (lead - 1.0) * rest)
    for step in range(4):
        for at in range(len(systems)):
            blocks = block_diagonal(rests[at], mask, group)
            more, rests[at] = times_blocks([inverses[at], rests[at]], blocks)
            inverses[at] = inverses[at] + more
    for step in range(2):
        for at in range(len(systems)):
            (product,) = times_blocks([inverses[at]], block_diagonal(systems[at], mask, group))
            blocks = block_diagonal(wide - product, mask, group)
            (more,) = times_blocks([inverses[at]], blocks)
            inverses[at] = inverses[at] + more
    for k in range(count):
        unit = 1.0 / (34.0 * rho[k : k + 1, :])
        place = (k % group) * rank
        inverse_ref[k] = left_triple(inverses[k // group][:, place : place + rank] * unit)
    for k in range(count):
        half = (k % 2) * rows
        chunk, pair = divmod(k // 2, pairs)
        own = projected_refs[chunk][pair, :, half : half + rows]
        base_ref[k] = weights_ref[:, k : k + 1] * own + rho[k : k + 1, :] * (
            aux_ref[k] - dual_s_ref[k] + coupled_ref[k] - dual_c_ref[k]
        )


def cross_blocks(lefts, rights, rank):
    group = len(lefts)
    wide = group * rank
    left = [split(value) for value in lefts]
    high = jnp.concatenate([piece[0] for piece in left], axis=0)
    both = jnp.concatenate([high] + [piece[1] for piece in left], axis=0)
    right = left if rights is lefts else [split(value) for value in rights]
    first = dot(both, jnp.concatenate([piece[0] for piece in right], axis=0), NT)
    second = dot(high, jnp.concatenate([piece[1] for piece in right], axis=0), NT)
    return diagonal_blocks(first[:wide] + first[wide:] + second, rank, group)


def summed(refs, chunks, k, rows):
    half = (k % 2) * rows
    chunk, pair = divmod(k // 2, refs[0].shape[0])
    total = None
    for ref in refs[chunk::chunks]:
        piece = ref[pair, :, half : half + rows]
        total = piece if total is None else total + piece
    return total


def first_kernel(chunks, group, *refs):
    base_ref, weights_ref, inverse_ref, dual_s_ref, dual_c_ref = refs[:5]
    recv_refs = refs[5:-3]
    tall_ref, target_ref, gram_ref = refs[-3:]
    count, rank, rows = base_ref.shape
    for first in range(0, count, group):
        talls = []
        for k in range(first, first + group):
            right = base_ref[k]
            if recv_refs:
                right = right + weights_ref[:, k : k + 1] * summed(recv_refs, chunks, k, rows)
            evolving = dot(inverse_ref[k], right_triple(right))
            target_ref[k] = evolving + dual_s_ref[k]
            tall = evolving + dual_c_ref[k]
            tall_ref[k] = tall
            talls.append(tall)
        gram_ref[first // group] = cross_blocks(talls, talls, rank)


def smooth(odd, now, targets, rho, inside_ref, near_ref, far_ref):
    count = len(targets)
    width = SWEEPS
    share = {j: 2.0 * smooth_weight / (rho[j] + 4.0 * smooth_weight) for j in rho}
    pull = {j: (rho[j] / (rho[j] + 4.0 * smooth_weight)) * targets[j] for j in range(count)}
    now = {j: now[j] for j in range(count)}
    for sweep in range(width):
        later = {}
        for j in range(-sweep - 1, count + sweep + 1):
            beside = [now[i] for i in (j - 1, j + 1) if i in now]
            total = beside[0] if len(beside) == 1 else beside[0] + beside[1]
            total = share[j] * total
            later[j] = total + pull[j] if j in pull else total
        now = later
    for j in range(count):
        inside_ref[j] = now[j]
    for j in range(width):
        near_ref[j] = jnp.where(odd == 1, now[j - width], now[count + j])
        far_ref[j] = jnp.where(odd == 1, now[count + j], now[j - width])


def all_rho(before_ref, rho_ref, after_ref):
    count = rho_ref.shape[0]
    rho = {j: rho_ref[j : j + 1, 0:1] for j in range(count)}
    for j in range(SWEEPS):
        rho[j - SWEEPS] = before_ref[j : j + 1, 0:1]
        rho[count + j] = after_ref[j : j + 1, 0:1]
    return rho


def smooth_kernel(
    chunks, odd_ref, aux_ref, target_ref, before_ref, rho_ref, after_ref, weights_ref, *refs
):
    *projected_refs, side_ref, inside_ref, near_ref, far_ref = refs
    count, rank, rows = aux_ref.shape
    for k in range(count):
        side_ref[k] = weights_ref[:, k : k + 1] * summed(projected_refs, chunks, k, rows)
    rho = all_rho(before_ref, rho_ref, after_ref)
    slices = range(count)
    smooth(
        odd_ref[0], [aux_ref[k] for k in slices], [target_ref[k] for k in slices], rho,
        inside_ref, near_ref, far_ref,
    )


def polar(grams, delta):
    rank, wide = grams[0].shape
    group = wide // rank
    mask = block_mask(rank, group)
    eye = wide_eye(rank, group)
    delta_left = left_triple(delta)
    delta_blocks = block_diagonal(jnp.concatenate([delta] * group, axis=1), mask, group)
    currents, roots, scales = [], [], []
    for gram in grams:
        left = dot(delta_left, right_triple(gram))
        (normal,) = times_blocks([left], delta_blocks, NT)
        line = jnp.broadcast_to(jnp.sum(normal * eye, axis=0, keepdims=True), (16, wide))
        high, low = split(line)
        rest = (line - high.astype(f32) - low.astype(f32)).astype(bf16)
        line = dot(high, mask) + dot(low, mask) + dot(rest, mask)
        trace = line[0:1] + eps_trace
        currents.append(normal / trace)
        scales.append(1.0 / jnp.sqrt(trace))
    for step in range(POLAR):
        for at in range(len(grams)):
            product = currents[at]
            blocks = block_diagonal(product, mask, group)
            if step == 0:
                roots.append(1.5 * eye - 0.5 * product)
                (square,) = times_blocks([product], blocks)
            elif step < POLAR - 1:
                square, more = times_blocks([product, roots[at]], blocks)
                roots[at] = 1.5 * roots[at] - 0.5 * more
            else:
                (more,) = times_blocks([roots[at]], blocks)
                roots[at] = 1.5 * roots[at] - 0.5 * more
            if step < POLAR - 1:
                half = 1.5 * product - 0.5 * square
                (more,) = times_blocks([half], blocks)
                currents[at] = 1.5 * half - 0.5 * more
    return roots, scales


def mix(roots, scales, grams, delta, mixed_ref, partial_ref):
    rank, wide = roots[0].shape
    group = wide // rank
    mask = block_mask(rank, group)
    delta_blocks = block_diagonal(jnp.concatenate([delta] * group, axis=1), mask, group)
    left, right = [], []
    for at in range(len(roots)):
        (mixed,) = times_blocks([roots[at]], delta_blocks)
        mixed = mixed * scales[at]
        mixed_ref[at] = mixed
        high, low = split(mixed)
        left += [high, high, low]
        high, low = split(grams[at])
        right += [high, low, high]
    partial = dot(jnp.concatenate(left, axis=1), jnp.concatenate(right, axis=1), NT)
    half = rank // 2
    partial_ref[...] = jnp.concatenate([partial[:half], partial[half:]], axis=1)


def first_polar_kernel(after_ref, delta_ref, *refs):
    *gram_refs, root_ref, scale_ref, gram_ref = refs
    grams = []
    for at in range(gram_ref.shape[0]):
        gram = gram_refs[0][at]
        for ref in gram_refs[1:]:
            gram = gram + ref[at]
        gram_ref[at] = gram
        grams.append(gram)
    roots, scales = polar(grams, delta_ref[...])
    for at in range(len(grams)):
        root_ref[at] = roots[at]
        scale_ref[at] = jnp.broadcast_to(scales[at], scale_ref.shape[1:])


def later_polar_kernel(last, after_ref, delta_ref, change_ref, old_ref, *refs):
    if last:
        *cross_refs, mixed_ref, partial_ref = refs
    else:
        *cross_refs, root_ref, scale_ref, gram_ref = refs
    groups, rank, wide = old_ref.shape
    group = wide // rank
    mask = block_mask(rank, group)
    grams = []
    for at in range(groups):
        cross = cross_refs[0][at]
        for ref in cross_refs[1:]:
            cross = cross + ref[at]
        change = change_ref[at]
        (onward,) = times_blocks([change], block_diagonal(old_ref[at], mask, group))
        onward = cross[:, :wide] + 0.5 * onward
        (one,) = times_blocks([onward], block_diagonal(change, mask, group), NT)
        (other,) = times_blocks([change], block_diagonal(onward, mask, group), NT)
        grams.append(cross[:, wide:] + one + other)
    delta = delta_ref[...]
    roots, scales = polar(grams, delta)
    if last:
        mix(roots, scales, grams, delta, mixed_ref, partial_ref)
    else:
        for at in range(groups):
            gram_ref[at] = grams[at]
            root_ref[at] = roots[at]
            scale_ref[at] = jnp.broadcast_to(scales[at], scale_ref.shape[1:])


def mix_kernel(near_ref, far_ref, delta_ref, root_ref, scale_ref, gram_ref, mixed_ref, partial_ref):
    groups = range(root_ref.shape[0])
    mix(
        [root_ref[at] for at in groups],
        [scale_ref[at, 0:1] for at in groups],
        [gram_ref[at] for at in groups],
        delta_ref[...], mixed_ref, partial_ref,
    )


def ahead_kernel(
    group, odd_ref, after_ref, inside_ref, near_ref, far_ref, target_ref, tall_ref, side_ref, rho_ref,
    inverse_ref, aux_ref, dual_ref, known_ref, cross_ref,
):
    count, rank, _ = inside_ref.shape
    width = SWEEPS
    knowns, talls = [], []
    for k in range(count):
        aux = inside_ref[k]
        if k < width:
            aux = aux + jnp.where(odd_ref[0] == 1, near_ref[k], far_ref[k])
        if k >= count - width:
            at = k - count + width
            aux = aux + jnp.where(odd_ref[0] == 1, far_ref[at], near_ref[at])
        target, tall = target_ref[k], tall_ref[k]
        aux_ref[k] = aux
        dual_ref[k] = target - aux
        known = dot(
            inverse_ref[k],
            right_triple(side_ref[k] + rho_ref[k : k + 1, 0:1] * (2.0 * aux - target - tall)),
        )
        known_ref[k] = known
        talls.append(tall)
        knowns.append(known + tall)
        if len(talls) == group:
            cross_ref[k // group] = jnp.concatenate(
                [cross_blocks(knowns, talls, rank), cross_blocks(knowns, knowns, rank)], axis=1
            )
            knowns, talls = [], []


def new_delta(sum_refs, total, rank):
    packed = sum_refs[0][...]
    for ref in sum_refs[1:]:
        packed = packed + ref[...]
    packed = packed / total
    return jnp.concatenate([packed[:, :rank], packed[:, rank:]], axis=0)


def mixer_kernel(total, mixed_ref, inverse_ref, rho_ref, *refs):
    *sum_refs, delta_ref, change_ref, forward_ref = refs
    groups, rank, wide = mixed_ref.shape
    group = wide // rank
    delta = new_delta(sum_refs, total, rank)
    delta_ref[...] = delta
    delta_left = left_triple(delta.T)
    place = lax.div(lax.broadcasted_iota(jnp.int32, (1, wide), 1), rank)
    for at in range(groups):
        mixer = dot(delta_left, right_triple(mixed_ref[at]))
        slices = range(at * group, (at + 1) * group)
        inverses = jnp.concatenate([inverse_ref[k] for k in slices], axis=0)
        onward = diagonal_blocks(dot(inverses, right_triple(mixer)), rank, group)
        rho = rho_ref[at * group : at * group + 1, 0:1]
        for k in slices[1:]:
            rho = jnp.where(place == k - at * group, rho_ref[k : k + 1, 0:1], rho)
        forward = 2.0 * rho * onward
        forward_ref[at] = forward
        change_ref[at] = forward - mixer


def rows_kernel(odd_ref, aux_ref, before_ref, rho_ref, after_ref, *refs):
    (change_ref, forward_ref, tall_ref, known_ref, dual_ref) = refs[:5]
    (next_ref, target_ref, inside_ref, near_ref, far_ref) = refs[5:]
    targets = new_rows(change_ref, forward_ref, tall_ref, known_ref, next_ref)
    count = len(targets)
    for k in range(count):
        targets[k] = targets[k] + dual_ref[k]
        target_ref[k] = targets[k]
    rho = all_rho(before_ref, rho_ref, after_ref)
    smooth(
        odd_ref[0], [aux_ref[k] for k in range(count)], targets, rho,
        inside_ref, near_ref, far_ref,
    )


def last_rows_kernel(
    after_ref, change_ref, forward_ref, tall_ref, known_ref, next_ref, evolving_ref
):
    evolvings = new_rows(change_ref, forward_ref, tall_ref, known_ref, next_ref)
    for k in range(len(evolvings)):
        evolving_ref[k] = evolvings[k]


def new_rows(change_ref, forward_ref, tall_ref, known_ref, next_ref):
    groups, rank, wide = change_ref.shape
    group = wide // rank
    evolvings = []
    for k in range(groups * group):
        lanes = slice((k % group) * rank, (k % group + 1) * rank)
        change, forward = change_ref[k // group][:, lanes], forward_ref[k // group][:, lanes]
        left = jnp.concatenate([left_triple(change), left_triple(forward)], axis=0)
        tall, known = tall_ref[k], known_ref[k]
        both = dot(left, right_triple(tall))
        next_ref[k] = known + tall + both[:rank]
        evolvings.append(known + both[rank:])
    return evolvings


def last_kernel(total, mixed_ref, tall_ref, *refs):
    *sum_refs, coupled_ref, delta_ref = refs
    groups, rank, wide = mixed_ref.shape
    group = wide // rank
    delta = new_delta(sum_refs, total, rank)
    delta_ref[...] = delta
    delta_left = left_triple(delta.T)
    for at in range(groups):
        mixer = dot(delta_left, right_triple(mixed_ref[at]))
        for k in range(at * group, (at + 1) * group):
            place = (k - at * group) * rank
            coupled_ref[k] = dot(
                left_triple(mixer[:, place : place + rank]), right_triple(tall_ref[k])
            )


per_microsecond = 1_100_000_000


def call(kernel, name, outs, *args, scalars=0, unread=0, microseconds=1, scratch=()):
    flops = int(microseconds * per_microsecond)
    specs = [pl.BlockSpec(memory_space=pltpu.SMEM)] * scalars
    specs += [pl.BlockSpec(memory_space=pl.ANY)] * unread
    specs += [pl.BlockSpec(memory_space=pltpu.VMEM)] * (len(args) - len(specs))
    shapes = [jax.ShapeDtypeStruct(shape, dtype) for shape, dtype in outs]
    moved = sum(arg.size * arg.dtype.itemsize for arg in args)
    moved += sum(shape.size * shape.dtype.itemsize for shape in shapes)
    return pl.pallas_call(
        kernel,
        out_shape=shapes,
        in_specs=specs,
        out_specs=[pl.BlockSpec(memory_space=pltpu.VMEM)] * len(shapes),
        scratch_shapes=list(scratch),
        compiler_params=pltpu.CompilerParams(vmem_limit_bytes=16 * 1024 * 1024),
        cost_estimate=pl.CostEstimate(flops=flops, bytes_accessed=moved, transcendentals=0),
        name=name,
    )(*args)


def rotated(value, axis, shift):
    count = lax.axis_size(axis)
    return lax.ppermute(value, axis, [(i, (i + shift) % count) for i in range(count)])


def swapped(value, axis, first):
    count = lax.axis_size(axis)
    pairs = [((i + first) % count, (i + first + 1) % count) for i in range(0, count, 2)]
    return lax.ppermute(value, axis, pairs + [(b, a) for a, b in pairs])


def from_others(value, axis):
    return [rotated(value, axis, shift) for shift in range(1, lax.axis_size(axis))]


def stage_sizes(count):
    sizes = []
    while count > 1:
        choices = (2, 3, 5, 7, count) if len(sizes) < 2 else (4, 2, 3, 5, 7, count)
        sizes.append(next(size for size in choices if count % size == 0))
        count //= sizes[-1]
    return sizes


def in_stages(value, axis, beside=None):
    count = lax.axis_size(axis)
    stride = 1
    terms = [value]
    for size in stage_sizes(count):
        value = terms[0]
        for term in terms[1:]:
            value = value + term
        if stride > 1 and beside is not None:
            value, beside = lax.optimization_barrier((value, beside))
        terms = [value]
        for shift in range(1, size):
            moves = []
            for i in range(count):
                digit = (i // stride) % size
                other = digit ^ shift if size in (2, 4) else (digit + shift) % size
                moves.append((i, i + (other - digit) * stride))
            terms.append(lax.ppermute(value, axis, moves))
        stride *= size
    return terms if beside is None else (terms, beside)


def body(
    data, order, chan_factor, slice_weights, smooth_aux, coupled, smooth_dual, coupling_dual, delta
):
    count, all_rows, channels = data.shape
    rank = chan_factor.shape[1]
    rows = smooth_aux.shape[1]
    parts = lax.axis_size("chan")
    total = count * lax.axis_size("cuts")
    group = group_size(count, rank)
    groups = count // group
    wide = group * rank
    flip = lambda value: jnp.swapaxes(value, 1, 2)
    aux, coup, dual_s, dual_c = map(flip, (smooth_aux, coupled, smooth_dual, coupling_dual))
    factor = chan_factor.T
    state = ((count, rank, rows), f32)
    quads = ((groups, rank, wide), f32)
    square = ((rank, rank), f32)
    halo = ((SWEEPS, rank, rows), f32)
    lanes = lambda height: ((height, 128), f32)
    scale = ((groups, 8, wide), f32)

    me = lax.axis_index("chan").astype(jnp.int32).reshape(1)
    odd = lax.rem(lax.axis_index("cuts"), 2).astype(jnp.int32).reshape(1)
    weights = slice_weights.T
    chunks = 2 if count % 4 == 0 else 1
    pairs = count // 2 // chunks
    own, arrived, grams = [], [], []
    for chunk in range(chunks):
        gram_part, *projected = call(
            functools.partial(project_kernel, chunk * pairs),
            "project",
            [square] + [((pairs, rank, 2 * rows), f32)] * parts,
            order, me, data, factor,
            scalars=2, unread=1, microseconds=2,
            scratch=[
                pltpu.VMEM((2 * pairs, all_rows, channels), data.dtype),
                pltpu.SemaphoreType.DMA((2 * pairs,)),
            ],
        )
        if chunk == 0:
            grams = [gram_part] + from_others(gram_part, "chan")
        own.append(projected[0])
        arrived.append([rotated(projected[shift], "chan", shift) for shift in range(1, parts)])
    received = [arrived[chunk][at] for at in range(parts - 1) for chunk in range(chunks)]

    inverse, rho, head, tail, base = call(
        functools.partial(setup_kernel, len(grams), chunks, group),
        "setup",
        [((count, rank, 3 * rank), bf16), lanes(count), lanes(SWEEPS), lanes(SWEEPS), state],
        *grams, *own, slice_weights, weights, aux, coup, dual_s, dual_c,
        microseconds=4,
    )
    before = rotated(tail, "cuts", 1)
    after = rotated(head, "cuts", -1)
    tall, target, gram = call(
        functools.partial(first_kernel, chunks, group),
        "first",
        [state, state, quads],
        base, weights, inverse, dual_s, dual_c, *received,
    )
    side, inside, to_near, to_far = call(
        functools.partial(smooth_kernel, chunks),
        "smooth",
        [state, state, halo, halo],
        odd, aux, target, before, rho, after, weights, *own, *received,
        scalars=1,
    )
    for inner in range(INNER):
        last = inner == INNER - 1
        polar_outs = [quads, scale, quads]
        if inner == 0:
            root, scales, gram = call(
                first_polar_kernel,
                "polar",
                polar_outs,
                inside, delta, gram, *from_others(gram, "chan"),
                unread=1, microseconds=5,
            )
        else:
            outs = call(
                functools.partial(later_polar_kernel, last),
                "polar",
                [quads, ((rank // 2, 2 * rank), f32)] if last else polar_outs,
                odd if last else inside, delta, change, gram, cross, *crosses,
                unread=1, microseconds=6,
            )
            if last:
                mixed, partial = outs
            else:
                root, scales, gram = outs
        if last:
            tall, evolving = call(
                last_rows_kernel,
                "rows",
                [state, state],
                mixed, change, forward, tall, known,
                unread=1,
            )
            coup, delta = call(
                functools.partial(last_kernel, total),
                "last",
                [state, square],
                mixed, tall, *in_stages(partial, "cuts"),
            )
            continue
        near = swapped(to_near, "cuts", 0)
        far = swapped(to_far, "cuts", 1)
        mixed, partial = call(
            mix_kernel,
            "mix",
            [quads, ((rank // 2, 2 * rank), f32)],
            near, far, delta, root, scales, gram,
            unread=2,
        )
        aux, dual, known, cross = call(
            functools.partial(ahead_kernel, group),
            "ahead",
            [state, state, state, ((groups, rank, 2 * wide), f32)],
            odd, partial, inside, near, far, target, tall, side, rho, inverse,
            scalars=1, unread=1,
        )
        sums, cross = in_stages(partial, "cuts", beside=cross)
        crosses = from_others(cross, "chan")
        delta, change, forward = call(
            functools.partial(mixer_kernel, total),
            "mixer",
            [square, quads, quads],
            mixed, inverse, rho, *sums,
            microseconds=0.3,
        )
        if inner < INNER - 2:
            tall, target, inside, to_near, to_far = call(
                rows_kernel,
                "rows",
                [state, state, state, halo, halo],
                odd, aux, before, rho, after, change, forward, tall, known, dual,
                scalars=1, microseconds=0.3,
            )
    return (flip(evolving), flip(coup), delta)


def solution(mesh):
    return jax.shard_map(
        body,
        mesh=mesh,
        in_specs=(
            P("cuts", None, "chan"),
            P("cuts"),
            P("chan", None),
            P("cuts", None),
            P("cuts", "chan", None),
            P("cuts", "chan", None),
            P("cuts", "chan", None),
            P("cuts", "chan", None),
            P(),
        ),
        out_specs=(P("cuts", "chan", None), P("cuts", "chan", None), P()),
        check_vma=False,
    )
```

profile of v0, /device:TPU:0, one launch (start us, length us, event | category | flops | bytes accessed | tf_op | source)
XLA Modules:
  0.0 99.0 jit_solution(8101322462886294700)
XLA Ops:
  0.6 1.9 %copy-done.1 = bf16[8,384,512]{2,1,0:T(8,128)(2,1)S(1)} copy-done((bf16[8,384,512]{2,1,0:T(8,128)(2,1)S(1)}, bf16[8,384,512]{2,1,0:T(8,128)(2,1)}, u32[]{:S(2)}) %copy-start.1) | copy-done | bytes 3145752
  4.0 2.4 %project.2 = (f32[64,64]{1,0:T(8,128)S(1)}, f32[2,64,384]{2,1,0:T(8,128)S(1)}, f32[2,64,384]{2,1,0:T(8,128)S(1)}) custom-call(s32[8]{0:T(128)S(1)} %copy-done.8, s32[1]{0:T(128)} %bitcast.2.me_ref, bf16[8,384,512]{2,1,0:T(8,128)(2,1)S(1)} %copy-done.1, bf16[64,512]{1,0:T(8,128)(2,1)S(1)} %bitcast.20), custom_call_target="tpu_custom_call" | custom-call | flops 2200000000 | bytes 3620900 | tf_op jit(solution)/shard_map/project/pallas_call | solution.py:503
  7.1 2.9 %collective-permute-start = (f32[64,64]{1,0:T(8,128)S(1)}, f32[64,64]{1,0:T(8,128)S(1)}, u32[]{:S(2)}, u32[]{:S(2)}) collective-permute-start(f32[64,64]{1,0:T(8,128)S(1)} %get-tuple-element.61.refs_0_), channel_id=1, source_target_pairs={{0,1},{1,0},{2,3},{3,2},{4,5},{5,4},{6,7},{7,6},{8,9},{9,8},{10,11... | collective-permute-start | bytes 49160 | tf_op jit(solution)/shard_map/ppermute | solution.py:517
  10.1 2.6 %project.3 = (f32[64,64]{1,0:T(8,128)}, f32[2,64,384]{2,1,0:T(8,128)S(1)}, f32[2,64,384]{2,1,0:T(8,128)S(1)}) custom-call(s32[8]{0:T(128)S(1)} %copy-done.8, s32[1]{0:T(128)} %bitcast.2.me_ref, bf16[8,384,512]{2,1,0:T(8,128)(2,1)S(1)} %copy-done.1, bf16[64,512]{1,0:T(8,128)(2,1)S(1)} %bitcast.21), custom_call_target="tpu_custom_call" | custom-call | flops 2200000000 | bytes 3620900 | tf_op jit(solution)/shard_map/project/pallas_call | solution.py:503
  13.4 2.0 %collective-permute-start.2 = (f32[2,64,384]{2,1,0:T(8,128)S(1)}, f32[2,64,384]{2,1,0:T(8,128)S(1)}, u32[]{:S(2)}, u32[]{:S(2)}) collective-permute-start(f32[2,64,384]{2,1,0:T(8,128)S(1)} %get-tuple-element.67), channel_id=1, source_target_pairs={{0,1},{1,0},{2,3},{3,2},{4,5},{5,4},{6,7},{7,6},{8,9},{9,8},{10,11... | collective-permute-start | bytes 589832 | tf_op jit(solution)/shard_map/ppermute | solution.py:517
  17.4 2.4 %setup.1 = (bf16[8,64,192]{2,1,0:T(8,128)(2,1)S(1)}, f32[8,128]{1,0:T(8,128)S(1)}, f32[4,128]{1,0:T(4,128)S(1)}, f32[4,128]{1,0:T(4,128)S(1)}, f32[8,64,192]{2,1,0:T(8,128)S(1)}) custom-call(f32[64,64]{1,0:T(8,128)S(1)} %get-tuple-element.61.refs_0_, f32[64,64]{1,0:T(8,128)S(1)} %collective-permute-done.refs_1_, f32[2,64,384]{2,1,0:T(8,128)S(1)} %copy-done.13, ...), custom_call_target="tpu_custom_call" | custom-call | flops 4400000000 | bytes 2600960 | tf_op jit(solution)/shard_map/setup/pallas_call | solution.py:503
  23.2 4.4 %collective-permute-start.4 = (f32[4,128]{1,0:T(4,128)S(1)}, f32[4,128]{1,0:T(4,128)S(1)}, u32[]{:S(2)}, u32[]{:S(2)}) collective-permute-start(f32[4,128]{1,0:T(4,128)S(1)} %get-tuple-element.71), channel_id=1, source_target_pairs={{0,30},{2,0},{4,2},{6,4},{8,6},{10,8},{12,10},{14,12},{16,14},{18,... | collective-permute-start | bytes 6152 | tf_op jit(solution)/shard_map/ppermute | solution.py:517
  27.6 1.3 %collective-permute-done.3.before_ref = f32[4,128]{1,0:T(4,128)S(1)} collective-permute-done((f32[4,128]{1,0:T(4,128)S(1)}, f32[4,128]{1,0:T(4,128)S(1)}, u32[]{:S(2)}, u32[]{:S(2)}) %collective-permute-start.3) | collective-permute-done | bytes 2080 | tf_op jit(solution)/shard_map/ppermute | solution.py:517
  32.5 4.5 %collective-permute-start.6 = (f32[4,64,192]{2,1,0:T(8,128)S(1)}, f32[4,64,192]{2,1,0:T(8,128)S(1)}, u32[]{:S(2)}, u32[]{:S(2)}) collective-permute-start(f32[4,64,192]{2,1,0:T(8,128)S(1)} %get-tuple-element.73), channel_id=1, source_target_pairs={{2,4},{6,8},{10,12},{14,16},{18,20},{22,24},{26,28},{30,0},{4,2},{... | collective-permute-start | bytes 589832 | tf_op jit(solution)/shard_map/ppermute | solution.py:523
  37.0 4.7 %polar.3 = (f32[2,64,256]{2,1,0:T(8,128)S(1)}, f32[2,8,256]{2,1,0:T(8,128)S(1)}, f32[2,64,256]{2,1,0:T(8,128)S(1)}) custom-call(f32[8,64,192]{2,1,0:T(8,128)S(1)} %get-tuple-element.74.after_ref.inside_ref, f32[64,64]{1,0:T(8,128)S(1)} %copy-done.7, f32[2,64,256]{2,1,0:T(8,128)S(1)} %get-tuple-element.75.refs_0_, ...), custom_call_target="tpu_custom_call" | custom-call | flops 5500000256 | bytes 950272 | tf_op jit(solution)/shard_map/polar/pallas_call | solution.py:503
  44.2 3.5 %collective-permute-done.9 = f32[32,128]{1,0:T(8,128)S(1)} collective-permute-done((f32[32,128]{1,0:T(8,128)S(1)}, f32[32,128]{1,0:T(8,128)S(1)}, u32[]{:S(2)}, u32[]{:S(2)}) %collective-permute-start.9) | collective-permute-done | bytes 16416 | tf_op jit(solution)/shard_map/ppermute | solution.py:556
  48.8 2.3 %collective-permute-start.12 = (f32[32,128]{1,0:T(8,128)S(1)}, f32[32,128]{1,0:T(8,128)S(1)}, u32[]{:S(2)}, u32[]{:S(2)}) collective-permute-start(f32[32,128]{1,0:T(8,128)S(1)} %add.19.refs_0_), channel_id=1, source_target_pairs={{0,24},{2,26},{4,28},{6,30},{8,16},{10,18},{12,20},{14,22},{16,8},... | collective-permute-start | bytes 49160 | tf_op jit(solution)/shard_map/ppermute | solution.py:556
  51.1 2.1 %collective-permute-start.10 = (f32[32,128]{1,0:T(8,128)S(1)}, f32[32,128]{1,0:T(8,128)S(1)}, u32[]{:S(2)}, u32[]{:S(2)}) collective-permute-start(f32[32,128]{1,0:T(8,128)S(1)} %add.19.refs_0_), channel_id=1, source_target_pairs={{0,8},{2,10},{4,12},{6,14},{8,0},{10,2},{12,4},{14,6},{16,24},{18,... | collective-permute-start | bytes 49160 | tf_op jit(solution)/shard_map/ppermute | solution.py:556
  53.2 1.2 %collective-permute-done.12.refs_3_ = f32[32,128]{1,0:T(8,128)S(1)} collective-permute-done((f32[32,128]{1,0:T(8,128)S(1)}, f32[32,128]{1,0:T(8,128)S(1)}, u32[]{:S(2)}, u32[]{:S(2)}) %collective-permute-start.12) | collective-permute-done | bytes 16416 | tf_op jit(solution)/shard_map/ppermute | solution.py:556
  54.4 1.4 %collective-permute-done.11.refs_2_ = f32[32,128]{1,0:T(8,128)S(1)} collective-permute-done((f32[32,128]{1,0:T(8,128)S(1)}, f32[32,128]{1,0:T(8,128)S(1)}, u32[]{:S(2)}, u32[]{:S(2)}) %collective-permute-start.11) | collective-permute-done | bytes 16416 | tf_op jit(solution)/shard_map/ppermute | solution.py:556
  57.1 2.9 %collective-permute-start.14 = (f32[4,64,192]{2,1,0:T(8,128)S(1)}, f32[4,64,192]{2,1,0:T(8,128)S(1)}, u32[]{:S(2)}, u32[]{:S(2)}) collective-permute-start(f32[4,64,192]{2,1,0:T(8,128)S(1)} %get-tuple-element.93), channel_id=1, source_target_pairs={{2,4},{6,8},{10,12},{14,16},{18,20},{22,24},{26,28},{30,0},{4,2},{... | collective-permute-start | bytes 589832 | tf_op jit(solution)/shard_map/ppermute | solution.py:523
  60.1 5.1 %polar.4 = (f32[2,64,256]{2,1,0:T(8,128)S(1)}, f32[2,8,256]{2,1,0:T(8,128)S(1)}, f32[2,64,256]{2,1,0:T(8,128)S(1)}) custom-call(f32[8,64,192]{2,1,0:T(8,128)S(1)} %get-tuple-element.95.after_ref.inside_ref, f32[64,64]{1,0:T(8,128)S(1)} %get-tuple-element.94.delta_ref, f32[2,64,256]{2,1,0:T(8,128)S(1)} %get-tuple-element.88.refs_0_.change_ref, ...), custom_call_target="tpu_custom_call" | custom-call | flops 6600000000 | bytes 1474560 | tf_op jit(solution)/shard_map/polar/pallas_call | solution.py:503
  66.8 1.5 %ahead.3 = (f32[8,64,192]{2,1,0:T(8,128)}, f32[8,64,192]{2,1,0:T(8,128)}, f32[8,64,192]{2,1,0:T(8,128)S(1)}, f32[2,64,512]{2,1,0:T(8,128)S(1)}) custom-call(s32[1]{0:T(128)} %bitcast.odd_ref.after_ref, f32[32,128]{1,0:T(8,128)S(1)} %get-tuple-element.101.after_ref, f32[8,64,192]{2,1,0:T(8,128)S(1)} %get-tuple-element.95.after_ref.inside_ref, ...), custom_call_target="tpu_custom_call" | custom-call | flops 1100000000 | bytes 3624964 | tf_op jit(solution)/shard_map/ahead/pallas_call | solution.py:503
  68.3 1.6 %collective-permute-start.17 = (f32[32,128]{1,0:T(8,128)S(1)}, f32[32,128]{1,0:T(8,128)S(1)}, u32[]{:S(2)}, u32[]{:S(2)}) collective-permute-start(f32[32,128]{1,0:T(8,128)S(1)} %add.20), channel_id=1, source_target_pairs={{0,4},{2,6},{4,0},{6,2},{8,12},{10,14},{12,8},{14,10},{16,20},{18,... | collective-permute-start | bytes 49160 | tf_op jit(solution)/shard_map/ppermute | solution.py:556
  69.9 2.2 %collective-permute-done.17 = f32[32,128]{1,0:T(8,128)S(1)} collective-permute-done((f32[32,128]{1,0:T(8,128)S(1)}, f32[32,128]{1,0:T(8,128)S(1)}, u32[]{:S(2)}, u32[]{:S(2)}) %collective-permute-start.17) | collective-permute-done | bytes 16416 | tf_op jit(solution)/shard_map/ppermute | solution.py:556
  72.9 1.6 %collective-permute-start.20 = (f32[32,128]{1,0:T(8,128)S(1)}, f32[32,128]{1,0:T(8,128)S(1)}, u32[]{:S(2)}, u32[]{:S(2)}) collective-permute-start(f32[32,128]{1,0:T(8,128)S(1)} %add.21.refs_0_), channel_id=1, source_target_pairs={{0,24},{2,26},{4,28},{6,30},{8,16},{10,18},{12,20},{14,22},{16,8},... | collective-permute-start | bytes 49160 | tf_op jit(solution)/shard_map/ppermute | solution.py:556
  75.6 1.7 %collective-permute-start.18 = (f32[32,128]{1,0:T(8,128)S(1)}, f32[32,128]{1,0:T(8,128)S(1)}, u32[]{:S(2)}, u32[]{:S(2)}) collective-permute-start(f32[32,128]{1,0:T(8,128)S(1)} %add.21.refs_0_), channel_id=1, source_target_pairs={{0,8},{2,10},{4,12},{6,14},{8,0},{10,2},{12,4},{14,6},{16,24},{18,... | collective-permute-start | bytes 49160 | tf_op jit(solution)/shard_map/ppermute | solution.py:556
  77.3 1.1 %collective-permute-done.20.refs_3_ = f32[32,128]{1,0:T(8,128)S(1)} collective-permute-done((f32[32,128]{1,0:T(8,128)S(1)}, f32[32,128]{1,0:T(8,128)S(1)}, u32[]{:S(2)}, u32[]{:S(2)}) %collective-permute-start.20) | collective-permute-done | bytes 16416 | tf_op jit(solution)/shard_map/ppermute | solution.py:556
  79.9 5.5 %polar.5 = (f32[2,64,256]{2,1,0:T(8,128)S(1)}, f32[32,128]{1,0:T(8,128)S(1)}) custom-call(s32[1]{0:T(128)} %bitcast.odd_ref.after_ref, f32[64,64]{1,0:T(8,128)S(1)} %get-tuple-element.108.delta_ref, f32[2,64,256]{2,1,0:T(8,128)S(1)} %get-tuple-element.109.change_ref, f32[2,64,256]{2,1,0:T(8,128)S(1)} %get-tuple-element.99.gram_ref.old_ref, ...), custom_call_target="tpu_custom_call" | custom-call | flops 6600000000 | bytes 950276 | tf_op jit(solution)/shard_map/polar/pallas_call | solution.py:503
  85.4 1.2 %collective-permute-done.22 = f32[32,128]{1,0:T(8,128)S(1)} collective-permute-done((f32[32,128]{1,0:T(8,128)S(1)}, f32[32,128]{1,0:T(8,128)S(1)}, u32[]{:S(2)}, u32[]{:S(2)}) %collective-permute-start.22) | collective-permute-done | bytes 16416 | tf_op jit(solution)/shard_map/ppermute | solution.py:556
  86.6 1.5 %collective-permute-start.23 = (f32[32,128]{1,0:T(8,128)S(1)}, f32[32,128]{1,0:T(8,128)S(1)}, u32[]{:S(2)}, u32[]{:S(2)}) collective-permute-start(f32[32,128]{1,0:T(8,128)S(1)} %add.22), channel_id=1, source_target_pairs={{0,4},{2,6},{4,0},{6,2},{8,12},{10,14},{12,8},{14,10},{16,20},{18,... | collective-permute-start | bytes 49160 | tf_op jit(solution)/shard_map/ppermute | solution.py:556
  88.2 2.2 %collective-permute-done.23 = f32[32,128]{1,0:T(8,128)S(1)} collective-permute-done((f32[32,128]{1,0:T(8,128)S(1)}, f32[32,128]{1,0:T(8,128)S(1)}, u32[]{:S(2)}, u32[]{:S(2)}) %collective-permute-start.23) | collective-permute-done | bytes 16416 | tf_op jit(solution)/shard_map/ppermute | solution.py:556
  90.4 2.2 %collective-permute-start.26 = (f32[32,128]{1,0:T(8,128)S(1)}, f32[32,128]{1,0:T(8,128)S(1)}, u32[]{:S(2)}, u32[]{:S(2)}) collective-permute-start(f32[32,128]{1,0:T(8,128)S(1)} %add.23.refs_0_), channel_id=1, source_target_pairs={{0,24},{2,26},{4,28},{6,30},{8,16},{10,18},{12,20},{14,22},{16,8},... | collective-permute-start | bytes 49160 | tf_op jit(solution)/shard_map/ppermute | solution.py:556
  93.5 1.3 %collective-permute-start.24 = (f32[32,128]{1,0:T(8,128)S(1)}, f32[32,128]{1,0:T(8,128)S(1)}, u32[]{:S(2)}, u32[]{:S(2)}) collective-permute-start(f32[32,128]{1,0:T(8,128)S(1)} %add.23.refs_0_), channel_id=1, source_target_pairs={{0,8},{2,10},{4,12},{6,14},{8,0},{10,2},{12,4},{14,6},{16,24},{18,... | collective-permute-start | bytes 49160 | tf_op jit(solution)/shard_map/ppermute | solution.py:556
  94.8 1.1 %rows.3 = (f32[8,64,192]{2,1,0:T(8,128)S(1)}, f32[8,64,192]{2,1,0:T(8,128)}) custom-call(f32[2,64,256]{2,1,0:T(8,128)S(1)} %get-tuple-element.111.after_ref.mixed_ref, f32[2,64,256]{2,1,0:T(8,128)S(1)} %get-tuple-element.109.change_ref, f32[2,64,256]{2,1,0:T(8,128)S(1)} %get-tuple-element.112.forward_ref, f32[8,64,192]{2,1,0:T(8,128)S(1)} %get-tuple-element.103.tall_ref, ...), custom_call_target="tpu_custom_call" | custom-call | flops 1100000000 | bytes 1966080 | tf_op jit(solution)/shard_map/rows/pallas_call | solution.py:503
  95.9 1.4 %collective-permute-done.25.refs_2_ = f32[32,128]{1,0:T(8,128)S(1)} collective-permute-done((f32[32,128]{1,0:T(8,128)S(1)}, f32[32,128]{1,0:T(8,128)S(1)}, u32[]{:S(2)}, u32[]{:S(2)}) %collective-permute-start.25) | collective-permute-done | bytes 16416 | tf_op jit(solution)/shard_map/ppermute | solution.py:556
  97.4 1.6 %last.1 = (f32[8,64,192]{2,1,0:T(8,128)}, f32[64,64]{1,0:T(8,128)}) custom-call(f32[2,64,256]{2,1,0:T(8,128)S(1)} %get-tuple-element.111.after_ref.mixed_ref, f32[8,64,192]{2,1,0:T(8,128)S(1)} %get-tuple-element.115.tall_ref, f32[32,128]{1,0:T(8,128)S(1)} %add.23.refs_0_, f32[32,128]{1,0:T(8,128)S(1)} %collective-permute-done.24.refs_1_, ...), custom_call_target="tpu_custom_call" | custom-call | flops 1100000000 | bytes 999424 | tf_op jit(solution)/shard_map/last/pallas_call | solution.py:503
  (82 shorter events, 22.7 us)
Async XLA Ops:
  7.1 8.4 %collective-permute-start = (f32[64,64]{1,0:T(8,128)S(1)}, f32[64,64]{1,0:T(8,128)S(1)}, u32[]{:S(2)}, u32[]{:S(2)}) collective-permute-start(f32[64,64]{1,0:T(8,128)S(1)} %get-tuple-element.61.refs_0_), channel_id=1, source_target_pairs={{0,1},{1,0},{2,3},{3,2},{4,5},{5,4},{6,7},{7,6},{8,9},{9,8},{10,11... | collective-permute-start | bytes 49160 | tf_op jit(solution)/shard_map/ppermute | solution.py:517
  10.0 5.5 %copy-start.2 = (f32[8,192,64]{1,2,0:T(8,128)S(1)}, f32[8,192,64]{1,2,0:T(8,128)}, u32[]{:S(2)}) copy-start(f32[8,192,64]{1,2,0:T(8,128)} %param.14) | copy-start | bytes 1179652
  10.0 5.5 %copy-start.3 = (f32[8,192,64]{1,2,0:T(8,128)S(1)}, f32[8,192,64]{1,2,0:T(8,128)}, u32[]{:S(2)}) copy-start(f32[8,192,64]{1,2,0:T(8,128)} %param.15) | copy-start | bytes 1179652
  10.0 5.5 %copy-start.4 = (f32[8,192,64]{1,2,0:T(8,128)S(1)}, f32[8,192,64]{1,2,0:T(8,128)}, u32[]{:S(2)}) copy-start(f32[8,192,64]{1,2,0:T(8,128)} %param.16) | copy-start | bytes 1179652
  10.0 5.5 %copy-start.5 = (f32[8,192,64]{1,2,0:T(8,128)S(1)}, f32[8,192,64]{1,2,0:T(8,128)}, u32[]{:S(2)}) copy-start(f32[8,192,64]{1,2,0:T(8,128)} %param.13) | copy-start | bytes 1179652
  10.0 9.8 %collective-permute-start.1 = (f32[2,64,384]{2,1,0:T(8,128)S(1)}, f32[2,64,384]{2,1,0:T(8,128)S(1)}, u32[]{:S(2)}, u32[]{:S(2)}) collective-permute-start(f32[2,64,384]{2,1,0:T(8,128)S(1)} %get-tuple-element.66), channel_id=1, source_target_pairs={{0,1},{1,0},{2,3},{3,2},{4,5},{5,4},{6,7},{7,6},{8,9},{9,8},{10,11... | collective-permute-start | bytes 589832 | tf_op jit(solution)/shard_map/ppermute | solution.py:517
  13.4 7.3 %collective-permute-start.2 = (f32[2,64,384]{2,1,0:T(8,128)S(1)}, f32[2,64,384]{2,1,0:T(8,128)S(1)}, u32[]{:S(2)}, u32[]{:S(2)}) collective-permute-start(f32[2,64,384]{2,1,0:T(8,128)S(1)} %get-tuple-element.67), channel_id=1, source_target_pairs={{0,1},{1,0},{2,3},{3,2},{4,5},{5,4},{6,7},{7,6},{8,9},{9,8},{10,11... | collective-permute-start | bytes 589832 | tf_op jit(solution)/shard_map/ppermute | solution.py:517
  20.7 16.3 %copy-start.7 = (f32[64,64]{1,0:T(8,128)S(1)}, f32[64,64]{1,0:T(8,128)}, u32[]{:S(2)}) copy-start(f32[64,64]{1,0:T(8,128)} %delta_ref.3) | copy-start | bytes 49156
  22.3 14.7 %collective-permute-start.7 = (f32[2,64,256]{2,1,0:T(8,128)S(1)}, f32[2,64,256]{2,1,0:T(8,128)S(1)}, u32[]{:S(2)}, u32[]{:S(2)}) collective-permute-start(f32[2,64,256]{2,1,0:T(8,128)S(1)} %get-tuple-element.75.refs_0_), channel_id=1, source_target_pairs={{0,1},{1,0},{2,3},{3,2},{4,5},{5,4},{6,7},{7,6},{8,9},{9,8},{10,11... | collective-permute-start | bytes 393224 | tf_op jit(solution)/shard_map/ppermute | solution.py:517
  23.2 5.7 %collective-permute-start.3 = (f32[4,128]{1,0:T(4,128)S(1)}, f32[4,128]{1,0:T(4,128)S(1)}, u32[]{:S(2)}, u32[]{:S(2)}) collective-permute-start(f32[4,128]{1,0:T(4,128)S(1)} %get-tuple-element.69), channel_id=1, source_target_pairs={{0,2},{2,4},{4,6},{6,8},{8,10},{10,12},{12,14},{14,16},{16,18},{18... | collective-permute-start | bytes 6152 | tf_op jit(solution)/shard_map/ppermute | solution.py:517
  23.2 5.8 %collective-permute-start.4 = (f32[4,128]{1,0:T(4,128)S(1)}, f32[4,128]{1,0:T(4,128)S(1)}, u32[]{:S(2)}, u32[]{:S(2)}) collective-permute-start(f32[4,128]{1,0:T(4,128)S(1)} %get-tuple-element.71), channel_id=1, source_target_pairs={{0,30},{2,0},{4,2},{6,4},{8,6},{10,8},{12,10},{14,12},{16,14},{18,... | collective-permute-start | bytes 6152 | tf_op jit(solution)/shard_map/ppermute | solution.py:517
  32.5 9.3 %collective-permute-start.5 = (f32[4,64,192]{2,1,0:T(8,128)S(1)}, f32[4,64,192]{2,1,0:T(8,128)S(1)}, u32[]{:S(2)}, u32[]{:S(2)}) collective-permute-start(f32[4,64,192]{2,1,0:T(8,128)S(1)} %get-tuple-element.72), channel_id=1, source_target_pairs={{0,2},{4,6},{8,10},{12,14},{16,18},{20,22},{24,26},{28,30},{2,0},{... | collective-permute-start | bytes 589832 | tf_op jit(solution)/shard_map/ppermute | solution.py:523
  32.5 9.2 %collective-permute-start.6 = (f32[4,64,192]{2,1,0:T(8,128)S(1)}, f32[4,64,192]{2,1,0:T(8,128)S(1)}, u32[]{:S(2)}, u32[]{:S(2)}) collective-permute-start(f32[4,64,192]{2,1,0:T(8,128)S(1)} %get-tuple-element.73), channel_id=1, source_target_pairs={{2,4},{6,8},{10,12},{14,16},{18,20},{22,24},{26,28},{30,0},{4,2},{... | collective-permute-start | bytes 589832 | tf_op jit(solution)/shard_map/ppermute | solution.py:523
  42.2 1.6 %collective-permute-start.8 = (f32[32,128]{1,0:T(8,128)S(1)}, f32[32,128]{1,0:T(8,128)S(1)}, u32[]{:S(2)}, u32[]{:S(2)}) collective-permute-start(f32[32,128]{1,0:T(8,128)S(1)} %get-tuple-element.79.after_ref), channel_id=1, source_target_pairs={{0,2},{2,0},{4,6},{6,4},{8,10},{10,8},{12,14},{14,12},{16,18},{18,... | collective-permute-start | bytes 49160 | tf_op jit(solution)/shard_map/ppermute | solution.py:556
  43.8 3.8 %collective-permute-start.9 = (f32[32,128]{1,0:T(8,128)S(1)}, f32[32,128]{1,0:T(8,128)S(1)}, u32[]{:S(2)}, u32[]{:S(2)}) collective-permute-start(f32[32,128]{1,0:T(8,128)S(1)} %add.18), channel_id=1, source_target_pairs={{0,4},{2,6},{4,0},{6,2},{8,12},{10,14},{12,8},{14,10},{16,20},{18,... | collective-permute-start | bytes 49160 | tf_op jit(solution)/shard_map/ppermute | solution.py:556
  47.7 12.4 %collective-permute-start.15 = (f32[2,64,512]{2,1,0:T(8,128)S(1)}, f32[2,64,512]{2,1,0:T(8,128)S(1)}, u32[]{:S(2)}, u32[]{:S(2)}) collective-permute-start(f32[2,64,512]{2,1,0:T(8,128)S(1)} %get-tuple-element.96.refs_0_), channel_id=1, source_target_pairs={{0,1},{1,0},{2,3},{3,2},{4,5},{5,4},{6,7},{7,6},{8,9},{9,8},{10,11... | collective-permute-start | bytes 786440 | tf_op jit(solution)/shard_map/ppermute | solution.py:517
  48.8 5.6 %collective-permute-start.12 = (f32[32,128]{1,0:T(8,128)S(1)}, f32[32,128]{1,0:T(8,128)S(1)}, u32[]{:S(2)}, u32[]{:S(2)}) collective-permute-start(f32[32,128]{1,0:T(8,128)S(1)} %add.19.refs_0_), channel_id=1, source_target_pairs={{0,24},{2,26},{4,28},{6,30},{8,16},{10,18},{12,20},{14,22},{16,8},... | collective-permute-start | bytes 49160 | tf_op jit(solution)/shard_map/ppermute | solution.py:556
  51.1 4.6 %collective-permute-start.11 = (f32[32,128]{1,0:T(8,128)S(1)}, f32[32,128]{1,0:T(8,128)S(1)}, u32[]{:S(2)}, u32[]{:S(2)}) collective-permute-start(f32[32,128]{1,0:T(8,128)S(1)} %add.19.refs_0_), channel_id=1, source_target_pairs={{0,16},{2,18},{4,20},{6,22},{8,24},{10,26},{12,28},{14,30},{16,0},... | collective-permute-start | bytes 49160 | tf_op jit(solution)/shard_map/ppermute | solution.py:556
  51.1 4.6 %collective-permute-start.10 = (f32[32,128]{1,0:T(8,128)S(1)}, f32[32,128]{1,0:T(8,128)S(1)}, u32[]{:S(2)}, u32[]{:S(2)}) collective-permute-start(f32[32,128]{1,0:T(8,128)S(1)} %add.19.refs_0_), channel_id=1, source_target_pairs={{0,8},{2,10},{4,12},{6,14},{8,0},{10,2},{12,4},{14,6},{16,24},{18,... | collective-permute-start | bytes 49160 | tf_op jit(solution)/shard_map/ppermute | solution.py:556
  57.1 8.1 %collective-permute-start.13 = (f32[4,64,192]{2,1,0:T(8,128)S(1)}, f32[4,64,192]{2,1,0:T(8,128)S(1)}, u32[]{:S(2)}, u32[]{:S(2)}) collective-permute-start(f32[4,64,192]{2,1,0:T(8,128)S(1)} %get-tuple-element.92), channel_id=1, source_target_pairs={{0,2},{4,6},{8,10},{12,14},{16,18},{20,22},{24,26},{28,30},{2,0},{... | collective-permute-start | bytes 589832 | tf_op jit(solution)/shard_map/ppermute | solution.py:523
  57.1 8.7 %collective-permute-start.14 = (f32[4,64,192]{2,1,0:T(8,128)S(1)}, f32[4,64,192]{2,1,0:T(8,128)S(1)}, u32[]{:S(2)}, u32[]{:S(2)}) collective-permute-start(f32[4,64,192]{2,1,0:T(8,128)S(1)} %get-tuple-element.93), channel_id=1, source_target_pairs={{2,4},{6,8},{10,12},{14,16},{18,20},{22,24},{26,28},{30,0},{4,2},{... | collective-permute-start | bytes 589832 | tf_op jit(solution)/shard_map/ppermute | solution.py:523
  66.3 2.0 %collective-permute-start.16 = (f32[32,128]{1,0:T(8,128)S(1)}, f32[32,128]{1,0:T(8,128)S(1)}, u32[]{:S(2)}, u32[]{:S(2)}) collective-permute-start(f32[32,128]{1,0:T(8,128)S(1)} %get-tuple-element.101.after_ref), channel_id=1, source_target_pairs={{0,2},{2,0},{4,6},{6,4},{8,10},{10,8},{12,14},{14,12},{16,18},{18,... | collective-permute-start | bytes 49160 | tf_op jit(solution)/shard_map/ppermute | solution.py:556
  68.3 3.8 %collective-permute-start.17 = (f32[32,128]{1,0:T(8,128)S(1)}, f32[32,128]{1,0:T(8,128)S(1)}, u32[]{:S(2)}, u32[]{:S(2)}) collective-permute-start(f32[32,128]{1,0:T(8,128)S(1)} %add.20), channel_id=1, source_target_pairs={{0,4},{2,6},{4,0},{6,2},{8,12},{10,14},{12,8},{14,10},{16,20},{18,... | collective-permute-start | bytes 49160 | tf_op jit(solution)/shard_map/ppermute | solution.py:556
  72.1 7.8 %collective-permute-start.21 = (f32[2,64,512]{2,1,0:T(8,128)S(1)}, f32[2,64,512]{2,1,0:T(8,128)S(1)}, u32[]{:S(2)}, u32[]{:S(2)}) collective-permute-start(f32[2,64,512]{2,1,0:T(8,128)S(1)} %get-tuple-element.110.refs_0_), channel_id=1, source_target_pairs={{0,1},{1,0},{2,3},{3,2},{4,5},{5,4},{6,7},{7,6},{8,9},{9,8},{10,11... | collective-permute-start | bytes 786440 | tf_op jit(solution)/shard_map/ppermute | solution.py:517
  72.9 5.5 %collective-permute-start.20 = (f32[32,128]{1,0:T(8,128)S(1)}, f32[32,128]{1,0:T(8,128)S(1)}, u32[]{:S(2)}, u32[]{:S(2)}) collective-permute-start(f32[32,128]{1,0:T(8,128)S(1)} %add.21.refs_0_), channel_id=1, source_target_pairs={{0,24},{2,26},{4,28},{6,30},{8,16},{10,18},{12,20},{14,22},{16,8},... | collective-permute-start | bytes 49160 | tf_op jit(solution)/shard_map/ppermute | solution.py:556
  74.5 4.6 %collective-permute-start.19 = (f32[32,128]{1,0:T(8,128)S(1)}, f32[32,128]{1,0:T(8,128)S(1)}, u32[]{:S(2)}, u32[]{:S(2)}) collective-permute-start(f32[32,128]{1,0:T(8,128)S(1)} %add.21.refs_0_), channel_id=1, source_target_pairs={{0,16},{2,18},{4,20},{6,22},{8,24},{10,26},{12,28},{14,30},{16,0},... | collective-permute-start | bytes 49160 | tf_op jit(solution)/shard_map/ppermute | solution.py:556
  75.6 3.7 %collective-permute-start.18 = (f32[32,128]{1,0:T(8,128)S(1)}, f32[32,128]{1,0:T(8,128)S(1)}, u32[]{:S(2)}, u32[]{:S(2)}) collective-permute-start(f32[32,128]{1,0:T(8,128)S(1)} %add.21.refs_0_), channel_id=1, source_target_pairs={{0,8},{2,10},{4,12},{6,14},{8,0},{10,2},{12,4},{14,6},{16,24},{18,... | collective-permute-start | bytes 49160 | tf_op jit(solution)/shard_map/ppermute | solution.py:556
  85.4 1.2 %collective-permute-start.22 = (f32[32,128]{1,0:T(8,128)S(1)}, f32[32,128]{1,0:T(8,128)S(1)}, u32[]{:S(2)}, u32[]{:S(2)}) collective-permute-start(f32[32,128]{1,0:T(8,128)S(1)} %get-tuple-element.116), channel_id=1, source_target_pairs={{0,2},{2,0},{4,6},{6,4},{8,10},{10,8},{12,14},{14,12},{16,18},{18,... | collective-permute-start | bytes 49160 | tf_op jit(solution)/shard_map/ppermute | solution.py:556
  86.6 3.7 %collective-permute-start.23 = (f32[32,128]{1,0:T(8,128)S(1)}, f32[32,128]{1,0:T(8,128)S(1)}, u32[]{:S(2)}, u32[]{:S(2)}) collective-permute-start(f32[32,128]{1,0:T(8,128)S(1)} %add.22), channel_id=1, source_target_pairs={{0,4},{2,6},{4,0},{6,2},{8,12},{10,14},{12,8},{14,10},{16,20},{18,... | collective-permute-start | bytes 49160 | tf_op jit(solution)/shard_map/ppermute | solution.py:556
  90.4 5.5 %collective-permute-start.26 = (f32[32,128]{1,0:T(8,128)S(1)}, f32[32,128]{1,0:T(8,128)S(1)}, u32[]{:S(2)}, u32[]{:S(2)}) collective-permute-start(f32[32,128]{1,0:T(8,128)S(1)} %add.23.refs_0_), channel_id=1, source_target_pairs={{0,24},{2,26},{4,28},{6,30},{8,16},{10,18},{12,20},{14,22},{16,8},... | collective-permute-start | bytes 49160 | tf_op jit(solution)/shard_map/ppermute | solution.py:556
  92.6 4.7 %collective-permute-start.25 = (f32[32,128]{1,0:T(8,128)S(1)}, f32[32,128]{1,0:T(8,128)S(1)}, u32[]{:S(2)}, u32[]{:S(2)}) collective-permute-start(f32[32,128]{1,0:T(8,128)S(1)} %add.23.refs_0_), channel_id=1, source_target_pairs={{0,16},{2,18},{4,20},{6,22},{8,24},{10,26},{12,28},{14,30},{16,0},... | collective-permute-start | bytes 49160 | tf_op jit(solution)/shard_map/ppermute | solution.py:556
  93.5 3.9 %collective-permute-start.24 = (f32[32,128]{1,0:T(8,128)S(1)}, f32[32,128]{1,0:T(8,128)S(1)}, u32[]{:S(2)}, u32[]{:S(2)}) collective-permute-start(f32[32,128]{1,0:T(8,128)S(1)} %add.23.refs_0_), channel_id=1, source_target_pairs={{0,8},{2,10},{4,12},{6,14},{8,0},{10,2},{12,4},{14,6},{16,24},{18,... | collective-permute-start | bytes 49160 | tf_op jit(solution)/shard_map/ppermute | solution.py:556
  (13 other events, 16.7 us)
where the time goes:
time: 99.4 us; the launch traced here: 99 us
  starting transfers between devices  37 us (37%)
  Pallas kernels  32.3 us (32%)
  waiting for transfers between devices  18 us (18%)
  local copies, waits for them, and re-layouts  10.8 us (11%)
    pallas_call x17, Pallas kernels, call(): pl.pallas_call(kernel, out_shape=shapes, in_specs=specs, out_specs=[pl.Bl...  32.3 us
    ppermute x15, starting transfers between devices, in_stages(): terms.append(lax.ppermute(value, axis, moves))  17.2 us
    ppermute x15, waiting for transfers between devices, in_stages(): terms.append(lax.ppermute(value, axis, moves))  15.2 us
    ppermute x8, starting transfers between devices, rotated(): lax.ppermute(value, axis, [(i, (i + shift) % count) for i in range(count)])  12.3 us
    unnamed x37, local copies, waits for them, and re-layouts  10.8 us
    ppermute x4, starting transfers between devices, swapped(): return lax.ppermute(value, axis, pairs + [(b, a) for a, b in pairs])  7.53 us
    ppermute x8, waiting for transfers between devices, rotated(): lax.ppermute(value, axis, [(i, (i + shift) % count) for i in range(count)])  2.14 us
  transfers between devices with their start and end apart: 27, of which 14 were waited for; matrix products, arithmetic and copies ran while one was open for 0% of the time, Pallas kernels for 21%

commit v1 on v0

--- a/solution.py
+++ b/solution.py
@@ -86,51 +86,47 @@
     return group
 
 
-def project_kernel(first, order_ref, me_ref, data_ref, factor_ref, *refs):
-    (gram_ref, *outs), held, arrived = refs[:-2], refs[-2], refs[-1]
-    parts = len(outs)
-    pairs = outs[0].shape[0]
-    rows = outs[0].shape[2] // 2
-    count = data_ref.shape[0]
-    copies = []
-    for at in range(2 * pairs):
-        stored = lax.rem(order_ref[2 * first + at], count)
-        copy = pltpu.make_async_copy(data_ref.at[stored], held.at[at], arrived.at[at])
-        copy.start()
-        copies.append(copy)
+def factor_kernel(factor_ref, gram_ref):
     factor = factor_ref[...]
     gram_ref[...] = dot(factor, factor, NT)
+
+
+def project_kernel(first, order_ref, me_ref, after_ref, data_ref, factor_ref, *outs):
+    parts = len(outs)
+    pairs, rows, _ = outs[0].shape
+    count = data_ref.shape[0]
+    factor = factor_ref[...]
+    empty = jnp.zeros_like(factor)
+    sides = [
+        jnp.concatenate([factor, empty], axis=0),
+        jnp.concatenate([empty, factor], axis=0),
+    ]
     for pair in range(pairs):
-        copies[2 * pair].wait()
-        copies[2 * pair + 1].wait()
+        stored = [lax.rem(order_ref[2 * (first + pair) + at], count) for at in range(2)]
         for part in reversed(range(parts)):
             start = pl.multiple_of(lax.rem(me_ref[0] + part, parts) * rows, 16)
-            both = jnp.concatenate(
-                [held[2 * pair, pl.ds(start, rows), :], held[2 * pair + 1, pl.ds(start, rows), :]],
-                axis=0,
-            )
-            outs[part][pair] = dot(both, factor, NT).T
-
-
-def setup_kernel(grams, chunks, group, *refs):
+            place = pl.ds(start, rows)
+            outs[part][pair] = dot(data_ref[stored[0], place, :], sides[0], NT) + dot(
+                data_ref[stored[1], place, :], sides[1], NT
+            )
+
+
+def setup_kernel(grams, group, *refs):
     gram_refs, refs = refs[:grams], refs[grams:]
-    projected_refs, refs = refs[:chunks], refs[chunks:]
-    (own_ref, weights_ref, aux_ref, coupled_ref, dual_s_ref, dual_c_ref) = refs[:6]
-    (inverse_ref, rho_ref, head_ref, tail_ref, base_ref) = refs[6:]
+    (own_ref, aux_ref, coupled_ref, dual_s_ref, dual_c_ref) = refs[:5]
+    (inverse_ref, mover_ref, rho_ref, diagonal_ref, columns_ref, base_ref) = refs[5:]
     count, rank = own_ref.shape
-    rows = aux_ref.shape[2]
-    pairs = projected_refs[0].shape[0]
     gram = gram_refs[0][...]
     for ref in gram_refs[1:]:
         gram = gram + ref[...]
     eye = wide_eye(rank, 1)
     diagonal = jnp.sum(gram * eye, axis=0, keepdims=True)
+    diagonal_ref[...] = jnp.broadcast_to(diagonal, diagonal_ref.shape)
     weights = own_ref[...]
+    columns = weights.T
+    columns_ref[...] = columns
     rho = jnp.sum(weights * weights * diagonal, axis=1, keepdims=True) / rank
-    rho_lanes = jnp.broadcast_to(rho, rho_ref.shape)
-    rho_ref[...] = rho_lanes
-    head_ref[...] = rho_lanes[:SWEEPS]
-    tail_ref[...] = rho_lanes[count - SWEEPS :]
+    rho_ref[...] = jnp.broadcast_to(rho, rho_ref.shape)
 
     edge = 34.0 / 32.0
     lead = 4.0 * edge**3 / (4.0 * edge**3 - 3.0 * edge)
@@ -142,8 +138,8 @@
         scaled = []
         for k in range(first, first + group):
             unit = 1.0 / (34.0 * rho[k : k + 1, :])
-            column = weights_ref[:, k : k + 1]
-            scaled.append(column * gram * own_ref[k : k + 1, :] * unit + (2.0 / 34.0) * eye)
+            column = columns[:, k : k + 1]
+            scaled.append(column * gram * weights[k : k + 1, :] * unit + (2.0 / 34.0) * eye)
         systems.append(jnp.concatenate(scaled, axis=1))
     inverses, rests = [], []
     for system in systems:
@@ -164,17 +160,24 @@
             blocks = block_diagonal(wide - product, mask, group)
             (more,) = times_blocks([inverses[at]], blocks)
             inverses[at] = inverses[at] + more
-    for k in range(count):
-        unit = 1.0 / (34.0 * rho[k : k + 1, :])
-        place = (k % group) * rank
-        inverse_ref[k] = left_triple(inverses[k // group][:, place : place + rank] * unit)
-    for k in range(count):
-        half = (k % 2) * rows
-        chunk, pair = divmod(k // 2, pairs)
-        own = projected_refs[chunk][pair, :, half : half + rows]
-        base_ref[k] = weights_ref[:, k : k + 1] * own + rho[k : k + 1, :] * (
-            aux_ref[k] - dual_s_ref[k] + coupled_ref[k] - dual_c_ref[k]
-        )
+    pair_mask = block_mask(rank, 2)
+    for k in range(0, count, 2):
+        both = []
+        for j in (k, k + 1):
+            place = (j % group) * rank
+            unit = 1.0 / (34.0 * rho[j : j + 1, :])
+            both.append(inverses[j // group][:, place : place + rank] * unit)
+            inverse = left_triple(both[-1])
+            inverse_ref[j] = inverse
+            base_ref[j] = dot(
+                inverse,
+                right_triple(
+                    rho[j : j + 1, :] * (aux_ref[j] - dual_s_ref[j] + coupled_ref[j] - dual_c_ref[j])
+                ),
+            )
+        line = jnp.concatenate([weights[k : k + 1, :], weights[k + 1 : k + 2, :]], axis=1)
+        high, low = block_diagonal(jnp.concatenate(both, axis=1) * line, pair_mask, 2)
+        mover_ref[k // 2] = jnp.concatenate([high, high, low], axis=1)
 
 
 def cross_blocks(lefts, rights, rank):
@@ -189,33 +192,31 @@
     return diagonal_blocks(first[:wide] + first[wide:] + second, rank, group)
 
 
-def summed(refs, chunks, k, rows):
-    half = (k % 2) * rows
-    chunk, pair = divmod(k // 2, refs[0].shape[0])
+def summed(refs, chunks, pair):
+    chunk, at = divmod(pair, refs[0].shape[0])
     total = None
     for ref in refs[chunk::chunks]:
-        piece = ref[pair, :, half : half + rows]
-        total = piece if total is None else total + piece
+        total = ref[at] if total is None else total + ref[at]
     return total
 
 
 def first_kernel(chunks, group, *refs):
-    base_ref, weights_ref, inverse_ref, dual_s_ref, dual_c_ref = refs[:5]
-    recv_refs = refs[5:-3]
-    tall_ref, target_ref, gram_ref = refs[-3:]
+    base_ref, mover_ref, dual_s_ref, dual_c_ref = refs[2:6]
+    *projected_refs, tall_ref, target_ref, gram_ref = refs[6:]
     count, rank, rows = base_ref.shape
+    talls = []
+    for k in range(0, count, 2):
+        high, low = split(summed(projected_refs, chunks, k // 2))
+        both = dot(mover_ref[k // 2], jnp.concatenate([high, low, high], axis=1), NT)
+        for j in (k, k + 1):
+            evolving = base_ref[j] + both[(j - k) * rank : (j - k + 1) * rank]
+            target_ref[j] = evolving + dual_s_ref[j]
+            tall = evolving + dual_c_ref[j]
+            tall_ref[j] = tall
+            talls.append(tall)
     for first in range(0, count, group):
-        talls = []
-        for k in range(first, first + group):
-            right = base_ref[k]
-            if recv_refs:
-                right = right + weights_ref[:, k : k + 1] * summed(recv_refs, chunks, k, rows)
-            evolving = dot(inverse_ref[k], right_triple(right))
-            target_ref[k] = evolving + dual_s_ref[k]
-            tall = evolving + dual_c_ref[k]
-            tall_ref[k] = tall
-            talls.append(tall)
-        gram_ref[first // group] = cross_blocks(talls, talls, rank)
+        some = talls[first : first + group]
+        gram_ref[first // group] = cross_blocks(some, some, rank)
 
 
 def smooth(odd, now, targets, rho, inside_ref, near_ref, far_ref):
@@ -243,24 +244,31 @@
     count = rho_ref.shape[0]
     rho = {j: rho_ref[j : j + 1, 0:1] for j in range(count)}
     for j in range(SWEEPS):
-        rho[j - SWEEPS] = before_ref[j : j + 1, 0:1]
+        rho[j - SWEEPS] = before_ref[count - SWEEPS + j : count - SWEEPS + j + 1, 0:1]
         rho[count + j] = after_ref[j : j + 1, 0:1]
     return rho
 
 
 def smooth_kernel(
-    chunks, odd_ref, aux_ref, target_ref, before_ref, rho_ref, after_ref, weights_ref, *refs
+    chunks, odd_ref, aux_ref, target_ref, before_ref, rho_ref, after_ref, diagonal_ref,
+    columns_ref, *refs
 ):
-    *projected_refs, side_ref, inside_ref, near_ref, far_ref = refs
+    *projected_refs, side_ref, past_ref, next_ref, inside_ref, near_ref, far_ref = refs
     count, rank, rows = aux_ref.shape
-    for k in range(count):
-        side_ref[k] = weights_ref[:, k : k + 1] * summed(projected_refs, chunks, k, rows)
-    rho = all_rho(before_ref, rho_ref, after_ref)
+    for source, place in ((before_ref, past_ref), (after_ref, next_ref)):
+        weights = source[...]
+        rho = jnp.sum(weights * weights * diagonal_ref[...], axis=1, keepdims=True) / rank
+        place[...] = jnp.broadcast_to(rho, place.shape)
+    rho = all_rho(past_ref, rho_ref, next_ref)
     slices = range(count)
     smooth(
         odd_ref[0], [aux_ref[k] for k in slices], [target_ref[k] for k in slices], rho,
         inside_ref, near_ref, far_ref,
     )
+    for k in range(0, count, 2):
+        both = summed(projected_refs, chunks, k // 2).T
+        side_ref[k] = columns_ref[:, k : k + 1] * both[:rank]
+        side_ref[k + 1] = columns_ref[:, k + 1 : k + 2] * both[rank:]
 
 
 def polar(grams, delta):
@@ -406,6 +414,14 @@
             knowns, talls = [], []
 
 
+def add_kernel(*refs):
+    *term_refs, total_ref = refs
+    total = term_refs[0][...]
+    for ref in term_refs[1:]:
+        total = total + ref[...]
+    total_ref[...] = total
+
+
 def new_delta(sum_refs, total, rank):
     packed = sum_refs[0][...]
     for ref in sum_refs[1:]:
@@ -492,7 +508,9 @@
 per_microsecond = 1_100_000_000
 
 
-def call(kernel, name, outs, *args, scalars=0, unread=0, microseconds=1, scratch=()):
+def call(
+    kernel, name, outs, *args, scalars=0, unread=0, microseconds=0.3
+):
     flops = int(microseconds * per_microsecond)
     specs = [pl.BlockSpec(memory_space=pltpu.SMEM)] * scalars
     specs += [pl.BlockSpec(memory_space=pl.ANY)] * unread
@@ -505,7 +523,6 @@
         out_shape=shapes,
         in_specs=specs,
         out_specs=[pl.BlockSpec(memory_space=pltpu.VMEM)] * len(shapes),
-        scratch_shapes=list(scratch),
         compiler_params=pltpu.CompilerParams(vmem_limit_bytes=16 * 1024 * 1024),
         cost_estimate=pl.CostEstimate(flops=flops, bytes_accessed=moved, transcendentals=0),
         name=name,
@@ -530,7 +547,7 @@
 def stage_sizes(count):
     sizes = []
     while count > 1:
-        choices = (2, 3, 5, 7, count) if len(sizes) < 2 else (4, 2, 3, 5, 7, count)
+        choices = (8, 4, 2, 3, 5, 7, count) if sizes else (2, 3, 5, 7, count)
         sizes.append(next(size for size in choices if count % size == 0))
         count //= sizes[-1]
     return sizes
@@ -542,8 +559,8 @@
     terms = [value]
     for size in stage_sizes(count):
         value = terms[0]
-        for term in terms[1:]:
-            value = value + term
+        if len(terms) > 1:
+            (value,) = call(add_kernel, "add", [(value.shape, f32)], *terms, microseconds=0.1)
         if stride > 1 and beside is not None:
             value, beside = lax.optimization_barrier((value, beside))
         terms = [value]
@@ -551,7 +568,7 @@
             moves = []
             for i in range(count):
                 digit = (i // stride) % size
-                other = digit ^ shift if size in (2, 4) else (digit + shift) % size
+                other = digit ^ shift if size in (2, 4, 8) else (digit + shift) % size
                 moves.append((i, i + (other - digit) * stride))
             terms.append(lax.ppermute(value, axis, moves))
         stride *= size
@@ -581,48 +598,51 @@
 
     me = lax.axis_index("chan").astype(jnp.int32).reshape(1)
     odd = lax.rem(lax.axis_index("cuts"), 2).astype(jnp.int32).reshape(1)
-    weights = slice_weights.T
     chunks = 2 if count % 4 == 0 else 1
     pairs = count // 2 // chunks
-    own, arrived, grams = [], [], []
+    (gram_part,) = call(factor_kernel, "factor", [square], factor)
+    grams = [gram_part] + from_others(gram_part, "chan")
+    own, arrived = [], []
     for chunk in range(chunks):
-        gram_part, *projected = call(
+        projected = call(
             functools.partial(project_kernel, chunk * pairs),
             "project",
-            [square] + [((pairs, rank, 2 * rows), f32)] * parts,
-            order, me, data, factor,
-            scalars=2, unread=1, microseconds=2,
-            scratch=[
-                pltpu.VMEM((2 * pairs, all_rows, channels), data.dtype),
-                pltpu.SemaphoreType.DMA((2 * pairs,)),
-            ],
+            [((pairs, rows, 2 * rank), f32)] * parts,
+            order, me, gram_part, data, factor,
+            scalars=2, unread=1,
         )
-        if chunk == 0:
-            grams = [gram_part] + from_others(gram_part, "chan")
         own.append(projected[0])
         arrived.append([rotated(projected[shift], "chan", shift) for shift in range(1, parts)])
     received = [arrived[chunk][at] for at in range(parts - 1) for chunk in range(chunks)]
 
-    inverse, rho, head, tail, base = call(
-        functools.partial(setup_kernel, len(grams), chunks, group),
+    late_weights, _ = lax.optimization_barrier((slice_weights, own[-1]))
+    before = rotated(late_weights, "cuts", 1)
+    after = rotated(late_weights, "cuts", -1)
+    inverse, mover, rho, diagonal, columns, base = call(
+        functools.partial(setup_kernel, len(grams), group),
         "setup",
-        [((count, rank, 3 * rank), bf16), lanes(count), lanes(SWEEPS), lanes(SWEEPS), state],
-        *grams, *own, slice_weights, weights, aux, coup, dual_s, dual_c,
-        microseconds=4,
+        [
+            ((count, rank, 3 * rank), bf16),
+            ((count // 2, 2 * rank, 6 * rank), bf16),
+            lanes(count),
+            ((count, rank), f32),
+            ((rank, count), f32),
+            state,
+        ],
+        *grams, slice_weights, aux, coup, dual_s, dual_c,
     )
-    before = rotated(tail, "cuts", 1)
-    after = rotated(head, "cuts", -1)
     tall, target, gram = call(
         functools.partial(first_kernel, chunks, group),
         "first",
         [state, state, quads],
-        base, weights, inverse, dual_s, dual_c, *received,
+        before, after, base, mover, dual_s, dual_c, *own, *received,
+        unread=2,
     )
-    side, inside, to_near, to_far = call(
+    side, before, after, inside, to_near, to_far = call(
         functools.partial(smooth_kernel, chunks),
         "smooth",
-        [state, state, halo, halo],
-        odd, aux, target, before, rho, after, weights, *own, *received,
+        [state, lanes(count), lanes(count), state, halo, halo],
+        odd, aux, target, before, rho, after, diagonal, columns, *own, *received,
         scalars=1,
     )
     for inner in range(INNER):
@@ -634,7 +654,7 @@
                 "polar",
                 polar_outs,
                 inside, delta, gram, *from_others(gram, "chan"),
-                unread=1, microseconds=5,
+                unread=1, microseconds=3,
             )
         else:
             outs = call(
@@ -642,7 +662,7 @@
                 "polar",
                 [quads, ((rank // 2, 2 * rank), f32)] if last else polar_outs,
                 odd if last else inside, delta, change, gram, cross, *crosses,
-                unread=1, microseconds=6,
+                unread=1, microseconds=3,
             )
             if last:
                 mixed, partial = outs
@@ -686,7 +706,6 @@
             "mixer",
             [square, quads, quads],
             mixed, inverse, rho, *sums,
-            microseconds=0.3,
         )
         if inner < INNER - 2:
             tall, target, inside, to_near, to_far = call(
@@ -694,7 +713,7 @@
                 "rows",
                 [state, state, state, halo, halo],
                 odd, aux, before, rho, after, change, forward, tall, known, dual,
-                scalars=1, microseconds=0.3,
+                scalars=1,
             )
     return (flip(evolving), flip(coup), delta)
 

time: 99.4 us -> 101 us (1.016)
  starting transfers between devices: 37 us -> 54 us
  local copies, waits for them, and re-layouts: 10.8 us -> 3.4 us
  waiting for transfers between devices: 18 us -> 12.1 us
  Pallas kernels: 32.3 us -> 29.9 us
    ppermute x15 -> x24, starting transfers between devices: 17.2 us -> 33.1 us  [in_stages(): terms.append(lax.ppermute(value, axis, moves))]
    unnamed x37 -> x18, local copies, waits for them, and re-layouts: 10.8 us -> 3.4 us
    ppermute x15 -> x24, waiting for transfers between devices: 15.2 us -> 8.64 us  [in_stages(): terms.append(lax.ppermute(value, axis, moves))]
    pallas_call x17 -> x21, Pallas kernels: 32.3 us -> 29.9 us  [call(): pl.pallas_call(kernel, out_shape=shapes, in_specs=specs, out_specs=[pl.Bl...]
    ppermute x8, waiting for transfers between devices: 2.14 us -> 3.47 us  [rotated(): lax.ppermute(value, axis, [(i, (i + shift) % count) for i in range(count)])]
    ppermute x4, starting transfers between devices: 7.53 us -> 8.76 us  [swapped(): return lax.ppermute(value, axis, pairs + [(b, a) for a, b in pairs])]
  transfers between devices with their start and end apart: 27 -> 36, of which waited for: 14 -> 13; matrix products, arithmetic and copies ran while one was open for 0% -> 0% of each run, Pallas kernels for 21% -> 20%
where the time goes in v1:
time: 101 us; the launch traced here: 100 us
  starting transfers between devices  54 us (53%)
  Pallas kernels  29.9 us (30%)
  waiting for transfers between devices  12.1 us (12%)
  local copies, waits for them, and re-layouts  3.4 us (3%)
    ppermute x24, starting transfers between devices, in_stages(): terms.append(lax.ppermute(value, axis, moves))  33.1 us
    pallas_call x21, Pallas kernels, call(): pl.pallas_call(kernel, out_shape=shapes, in_specs=specs, out_specs=[pl.Bl...  29.9 us
    ppermute x8, starting transfers between devices, rotated(): lax.ppermute(value, axis, [(i, (i + shift) % count) for i in range(count)])  12.2 us
    ppermute x4, starting transfers between devices, swapped(): return lax.ppermute(value, axis, pairs + [(b, a) for a, b in pairs])  8.76 us
    ppermute x24, waiting for transfers between devices, in_stages(): terms.append(lax.ppermute(value, axis, moves))  8.64 us
    ppermute x8, waiting for transfers between devices, rotated(): lax.ppermute(value, axis, [(i, (i + shift) % count) for i in range(count)])  3.47 us
    unnamed x18, local copies, waits for them, and re-layouts  3.4 us
  transfers between devices with their start and end apart: 36, of which 13 were waited for; matrix products, arithmetic and copies ran while one was open for 0% of the time, Pallas kernels for 20%

profile of v1, /device:TPU:0, one launch (start us, length us, event | category | flops | bytes accessed | tf_op | source)
XLA Modules:
  0.0 100.4 jit_solution(447851390391016594)
XLA Ops:
  1.6 1.9 %copy-done = bf16[8,384,512]{2,1,0:T(8,128)(2,1)S(1)} copy-done((bf16[8,384,512]{2,1,0:T(8,128)(2,1)S(1)}, bf16[8,384,512]{2,1,0:T(8,128)(2,1)}, u32[]{:S(2)}) %copy-start) | copy-done | bytes 3145752
  5.3 3.0 %collective-permute-start.3 = (f32[2,192,128]{2,1,0:T(8,128)S(1)}, f32[2,192,128]{2,1,0:T(8,128)S(1)}, u32[]{:S(2)}, u32[]{:S(2)}) collective-permute-start(f32[2,192,128]{2,1,0:T(8,128)S(1)} %get-tuple-element.65), channel_id=1, source_target_pairs={{0,1},{1,0},{2,3},{3,2},{4,5},{5,4},{6,7},{7,6},{8,9},{9,8},{10,11... | collective-permute-start | bytes 589832 | tf_op jit(solution)/shard_map/ppermute | solution.py:534
  9.5 2.0 %collective-permute-start.2 = (f32[64,64]{1,0:T(8,128)S(1)}, f32[64,64]{1,0:T(8,128)S(1)}, u32[]{:S(2)}, u32[]{:S(2)}) collective-permute-start(f32[64,64]{1,0:T(8,128)S(1)} %factor.1.after_ref.refs_0_), channel_id=1, source_target_pairs={{0,1},{1,0},{2,3},{3,2},{4,5},{5,4},{6,7},{7,6},{8,9},{9,8},{10,11... | collective-permute-start | bytes 49160 | tf_op jit(solution)/shard_map/ppermute | solution.py:534
  11.5 3.2 %collective-permute-start.1 = (f32[8,64]{1,0:T(8,128)S(1)}, f32[8,64]{1,0:T(8,128)S(1)}, u32[]{:S(2)}, u32[]{:S(2)}) collective-permute-start(f32[8,64]{1,0:T(8,128)S(1)} %copy-done.6), channel_id=1, source_target_pairs={{0,30},{2,0},{4,2},{6,4},{8,6},{10,8},{12,10},{14,12},{16,14},{18,... | collective-permute-start | bytes 6152 | tf_op jit(solution)/shard_map/ppermute | solution.py:534
  14.7 3.5 %collective-permute-done.2.refs_1_ = f32[64,64]{1,0:T(8,128)S(1)} collective-permute-done((f32[64,64]{1,0:T(8,128)S(1)}, f32[64,64]{1,0:T(8,128)S(1)}, u32[]{:S(2)}, u32[]{:S(2)}) %collective-permute-start.2) | collective-permute-done | bytes 16416 | tf_op jit(solution)/shard_map/ppermute | solution.py:534
  18.1 2.7 %setup.1 = (bf16[8,64,192]{2,1,0:T(8,128)(2,1)S(1)}, bf16[4,128,384]{2,1,0:T(8,128)(2,1)S(1)}, f32[8,128]{1,0:T(8,128)S(1)}, f32[8,64]{1,0:T(8,128)S(1)}, f32[64...) custom-call(f32[64,64]{1,0:T(8,128)S(1)} %factor.1.after_ref.refs_0_, f32[64,64]{1,0:T(8,128)S(1)} %collective-permute-done.2.refs_1_, ...), custom_call_target="tpu_custom_call" | custom-call | flops 330000000 | bytes 2598912 | tf_op jit(solution)/shard_map/setup/pallas_call | solution.py:521
  21.7 1.8 %collective-permute-start.7 = (f32[2,64,256]{2,1,0:T(8,128)S(1)}, f32[2,64,256]{2,1,0:T(8,128)S(1)}, u32[]{:S(2)}, u32[]{:S(2)}) collective-permute-start(f32[2,64,256]{2,1,0:T(8,128)S(1)} %get-tuple-element.74.refs_0_), channel_id=1, source_target_pairs={{0,1},{1,0},{2,3},{3,2},{4,5},{5,4},{6,7},{7,6},{8,9},{9,8},{10,11... | collective-permute-start | bytes 393224 | tf_op jit(solution)/shard_map/ppermute | solution.py:534
  24.3 4.7 %collective-permute-start.6 = (f32[4,64,192]{2,1,0:T(8,128)S(1)}, f32[4,64,192]{2,1,0:T(8,128)S(1)}, u32[]{:S(2)}, u32[]{:S(2)}) collective-permute-start(f32[4,64,192]{2,1,0:T(8,128)S(1)} %get-tuple-element.72), channel_id=1, source_target_pairs={{2,4},{6,8},{10,12},{14,16},{18,20},{22,24},{26,28},{30,0},{4,2},{... | collective-permute-start | bytes 589832 | tf_op jit(solution)/shard_map/ppermute | solution.py:540
  28.9 4.7 %polar.3 = (f32[2,64,256]{2,1,0:T(8,128)S(1)}, f32[2,8,256]{2,1,0:T(8,128)S(1)}, f32[2,64,256]{2,1,0:T(8,128)S(1)}) custom-call(f32[8,64,192]{2,1,0:T(8,128)S(1)} %get-tuple-element.73.after_ref.inside_ref, f32[64,64]{1,0:T(8,128)S(1)} %copy-done.8, f32[2,64,256]{2,1,0:T(8,128)S(1)} %get-tuple-element.74.refs_0_, ...), custom_call_target="tpu_custom_call" | custom-call | flops 3300000000 | bytes 950272 | tf_op jit(solution)/shard_map/polar/pallas_call | solution.py:521
  35.9 4.1 %collective-permute-start.15 = (f32[32,128]{1,0:T(8,128)S(1)}, f32[32,128]{1,0:T(8,128)S(1)}, u32[]{:S(2)}, u32[]{:S(2)}) collective-permute-start(f32[32,128]{1,0:T(8,128)S(1)} %add.3.refs_0_), channel_id=1, source_target_pairs={{0,28},{2,30},{4,24},{6,26},{8,20},{10,22},{12,16},{14,18},{16,12}... | collective-permute-start | bytes 49160 | tf_op jit(solution)/shard_map/ppermute | solution.py:573
  41.1 2.5 %collective-permute-start.12 = (f32[32,128]{1,0:T(8,128)S(1)}, f32[32,128]{1,0:T(8,128)S(1)}, u32[]{:S(2)}, u32[]{:S(2)}) collective-permute-start(f32[32,128]{1,0:T(8,128)S(1)} %add.3.refs_0_), channel_id=1, source_target_pairs={{0,16},{2,18},{4,20},{6,22},{8,24},{10,26},{12,28},{14,30},{16,0},... | collective-permute-start | bytes 49160 | tf_op jit(solution)/shard_map/ppermute | solution.py:573
  43.6 1.8 %collective-permute-start.11 = (f32[32,128]{1,0:T(8,128)S(1)}, f32[32,128]{1,0:T(8,128)S(1)}, u32[]{:S(2)}, u32[]{:S(2)}) collective-permute-start(f32[32,128]{1,0:T(8,128)S(1)} %add.3.refs_0_), channel_id=1, source_target_pairs={{0,12},{2,14},{4,8},{6,10},{8,4},{10,6},{12,0},{14,2},{16,28},{18,... | collective-permute-start | bytes 49160 | tf_op jit(solution)/shard_map/ppermute | solution.py:573
  45.9 1.1 %collective-permute-start.9 = (f32[32,128]{1,0:T(8,128)S(1)}, f32[32,128]{1,0:T(8,128)S(1)}, u32[]{:S(2)}, u32[]{:S(2)}) collective-permute-start(f32[32,128]{1,0:T(8,128)S(1)} %add.3.refs_0_), channel_id=1, source_target_pairs={{0,4},{2,6},{4,0},{6,2},{8,12},{10,14},{12,8},{14,10},{16,20},{18,... | collective-permute-start | bytes 49160 | tf_op jit(solution)/shard_map/ppermute | solution.py:573
  47.1 1.1 %collective-permute-done.11.refs_3_ = f32[32,128]{1,0:T(8,128)S(1)} collective-permute-done((f32[32,128]{1,0:T(8,128)S(1)}, f32[32,128]{1,0:T(8,128)S(1)}, u32[]{:S(2)}, u32[]{:S(2)}) %collective-permute-start.11) | collective-permute-done | bytes 16416 | tf_op jit(solution)/shard_map/ppermute | solution.py:573
  51.1 4.0 %collective-permute-start.17 = (f32[4,64,192]{2,1,0:T(8,128)S(1)}, f32[4,64,192]{2,1,0:T(8,128)S(1)}, u32[]{:S(2)}, u32[]{:S(2)}) collective-permute-start(f32[4,64,192]{2,1,0:T(8,128)S(1)} %get-tuple-element.93), channel_id=1, source_target_pairs={{2,4},{6,8},{10,12},{14,16},{18,20},{22,24},{26,28},{30,0},{4,2},{... | collective-permute-start | bytes 589832 | tf_op jit(solution)/shard_map/ppermute | solution.py:540
  55.0 5.1 %polar.4 = (f32[2,64,256]{2,1,0:T(8,128)S(1)}, f32[2,8,256]{2,1,0:T(8,128)S(1)}, f32[2,64,256]{2,1,0:T(8,128)S(1)}) custom-call(f32[8,64,192]{2,1,0:T(8,128)S(1)} %get-tuple-element.95.after_ref.inside_ref, f32[64,64]{1,0:T(8,128)S(1)} %get-tuple-element.94.delta_ref, f32[2,64,256]{2,1,0:T(8,128)S(1)} %get-tuple-element.88.refs_0_.change_ref, ...), custom_call_target="tpu_custom_call" | custom-call | flops 3300000000 | bytes 1474560 | tf_op jit(solution)/shard_map/polar/pallas_call | solution.py:521
  60.7 1.5 %ahead.3 = (f32[8,64,192]{2,1,0:T(8,128)}, f32[8,64,192]{2,1,0:T(8,128)}, f32[8,64,192]{2,1,0:T(8,128)S(1)}, f32[2,64,512]{2,1,0:T(8,128)S(1)}) custom-call(s32[1]{0:T(128)} %bitcast.odd_ref.after_ref, f32[32,128]{1,0:T(8,128)S(1)} %get-tuple-element.101.refs_0_.after_ref, f32[8,64,192]{2,1,0:T(8,128)S(1)} %get-tuple-element.95.after_ref.inside_ref, ...), custom_call_target="tpu_custom_call" | custom-call | flops 330000000 | bytes 3624964 | tf_op jit(solution)/shard_map/ahead/pallas_call | solution.py:521
  62.2 1.5 %collective-permute-start.27 = (f32[2,64,512]{2,1,0:T(8,128)S(1)}, f32[2,64,512]{2,1,0:T(8,128)S(1)}, u32[]{:S(2)}, u32[]{:S(2)}) collective-permute-start(f32[2,64,512]{2,1,0:T(8,128)S(1)} %get-tuple-element.108.refs_0_), channel_id=1, source_target_pairs={{0,1},{1,0},{2,3},{3,2},{4,5},{5,4},{6,7},{7,6},{8,9},{9,8},{10,11... | collective-permute-start | bytes 786440 | tf_op jit(solution)/shard_map/ppermute | solution.py:534
  63.8 3.7 %collective-permute-start.26 = (f32[32,128]{1,0:T(8,128)S(1)}, f32[32,128]{1,0:T(8,128)S(1)}, u32[]{:S(2)}, u32[]{:S(2)}) collective-permute-start(f32[32,128]{1,0:T(8,128)S(1)} %add.4.refs_0_), channel_id=1, source_target_pairs={{0,28},{2,30},{4,24},{6,26},{8,20},{10,22},{12,16},{14,18},{16,12}... | collective-permute-start | bytes 49160 | tf_op jit(solution)/shard_map/ppermute | solution.py:573
  67.7 1.3 %collective-permute-start.24 = (f32[32,128]{1,0:T(8,128)S(1)}, f32[32,128]{1,0:T(8,128)S(1)}, u32[]{:S(2)}, u32[]{:S(2)}) collective-permute-start(f32[32,128]{1,0:T(8,128)S(1)} %add.4.refs_0_), channel_id=1, source_target_pairs={{0,20},{2,22},{4,16},{6,18},{8,28},{10,30},{12,24},{14,26},{16,4},... | collective-permute-start | bytes 49160 | tf_op jit(solution)/shard_map/ppermute | solution.py:573
  69.1 2.3 %collective-permute-start.23 = (f32[32,128]{1,0:T(8,128)S(1)}, f32[32,128]{1,0:T(8,128)S(1)}, u32[]{:S(2)}, u32[]{:S(2)}) collective-permute-start(f32[32,128]{1,0:T(8,128)S(1)} %add.4.refs_0_), channel_id=1, source_target_pairs={{0,16},{2,18},{4,20},{6,22},{8,24},{10,26},{12,28},{14,30},{16,0},... | collective-permute-start | bytes 49160 | tf_op jit(solution)/shard_map/ppermute | solution.py:573
  71.4 1.4 %collective-permute-start.22 = (f32[32,128]{1,0:T(8,128)S(1)}, f32[32,128]{1,0:T(8,128)S(1)}, u32[]{:S(2)}, u32[]{:S(2)}) collective-permute-start(f32[32,128]{1,0:T(8,128)S(1)} %add.4.refs_0_), channel_id=1, source_target_pairs={{0,12},{2,14},{4,8},{6,10},{8,4},{10,6},{12,0},{14,2},{16,28},{18,... | collective-permute-start | bytes 49160 | tf_op jit(solution)/shard_map/ppermute | solution.py:573
  73.6 1.3 %collective-permute-start.20 = (f32[32,128]{1,0:T(8,128)S(1)}, f32[32,128]{1,0:T(8,128)S(1)}, u32[]{:S(2)}, u32[]{:S(2)}) collective-permute-start(f32[32,128]{1,0:T(8,128)S(1)} %add.4.refs_0_), channel_id=1, source_target_pairs={{0,4},{2,6},{4,0},{6,2},{8,12},{10,14},{12,8},{14,10},{16,20},{18,... | collective-permute-start | bytes 49160 | tf_op jit(solution)/shard_map/ppermute | solution.py:573
  74.9 1.1 %collective-permute-done.22.refs_3_ = f32[32,128]{1,0:T(8,128)S(1)} collective-permute-done((f32[32,128]{1,0:T(8,128)S(1)}, f32[32,128]{1,0:T(8,128)S(1)}, u32[]{:S(2)}, u32[]{:S(2)}) %collective-permute-start.22) | collective-permute-done | bytes 16416 | tf_op jit(solution)/shard_map/ppermute | solution.py:573
  77.9 5.5 %polar.5 = (f32[2,64,256]{2,1,0:T(8,128)S(1)}, f32[32,128]{1,0:T(8,128)S(1)}) custom-call(s32[1]{0:T(128)} %bitcast.odd_ref.after_ref, f32[64,64]{1,0:T(8,128)S(1)} %get-tuple-element.106.delta_ref, f32[2,64,256]{2,1,0:T(8,128)S(1)} %get-tuple-element.107.change_ref, f32[2,64,256]{2,1,0:T(8,128)S(1)} %get-tuple-element.99.gram_ref.old_ref, ...), custom_call_target="tpu_custom_call" | custom-call | flops 3300000000 | bytes 950276 | tf_op jit(solution)/shard_map/polar/pallas_call | solution.py:521
  83.4 1.2 %collective-permute-done.28.refs_1_ = f32[32,128]{1,0:T(8,128)S(1)} collective-permute-done((f32[32,128]{1,0:T(8,128)S(1)}, f32[32,128]{1,0:T(8,128)S(1)}, u32[]{:S(2)}, u32[]{:S(2)}) %collective-permute-start.28) | collective-permute-done | bytes 16416 | tf_op jit(solution)/shard_map/ppermute | solution.py:573
  84.6 4.5 %collective-permute-start.35 = (f32[32,128]{1,0:T(8,128)S(1)}, f32[32,128]{1,0:T(8,128)S(1)}, u32[]{:S(2)}, u32[]{:S(2)}) collective-permute-start(f32[32,128]{1,0:T(8,128)S(1)} %add.5.refs_0_), channel_id=1, source_target_pairs={{0,28},{2,30},{4,24},{6,26},{8,20},{10,22},{12,16},{14,18},{16,12}... | collective-permute-start | bytes 49160 | tf_op jit(solution)/shard_map/ppermute | solution.py:573
  89.8 2.5 %collective-permute-start.32 = (f32[32,128]{1,0:T(8,128)S(1)}, f32[32,128]{1,0:T(8,128)S(1)}, u32[]{:S(2)}, u32[]{:S(2)}) collective-permute-start(f32[32,128]{1,0:T(8,128)S(1)} %add.5.refs_0_), channel_id=1, source_target_pairs={{0,16},{2,18},{4,20},{6,22},{8,24},{10,26},{12,28},{14,30},{16,0},... | collective-permute-start | bytes 49160 | tf_op jit(solution)/shard_map/ppermute | solution.py:573
  92.3 2.2 %collective-permute-start.31 = (f32[32,128]{1,0:T(8,128)S(1)}, f32[32,128]{1,0:T(8,128)S(1)}, u32[]{:S(2)}, u32[]{:S(2)}) collective-permute-start(f32[32,128]{1,0:T(8,128)S(1)} %add.5.refs_0_), channel_id=1, source_target_pairs={{0,12},{2,14},{4,8},{6,10},{8,4},{10,6},{12,0},{14,2},{16,28},{18,... | collective-permute-start | bytes 49160 | tf_op jit(solution)/shard_map/ppermute | solution.py:573
  95.8 1.2 %rows.3 = (f32[8,64,192]{2,1,0:T(8,128)S(1)}, f32[8,64,192]{2,1,0:T(8,128)}) custom-call(f32[2,64,256]{2,1,0:T(8,128)S(1)} %get-tuple-element.109.after_ref.mixed_ref, f32[2,64,256]{2,1,0:T(8,128)S(1)} %get-tuple-element.107.change_ref, f32[2,64,256]{2,1,0:T(8,128)S(1)} %get-tuple-element.110.forward_ref, f32[8,64,192]{2,1,0:T(8,128)S(1)} %get-tuple-element.103.tall_ref, ...), custom_call_target="tpu_custom_call" | custom-call | flops 330000000 | bytes 1966080 | tf_op jit(solution)/shard_map/rows/pallas_call | solution.py:521
  96.9 1.3 %collective-permute-done.30.refs_2_ = f32[32,128]{1,0:T(8,128)S(1)} collective-permute-done((f32[32,128]{1,0:T(8,128)S(1)}, f32[32,128]{1,0:T(8,128)S(1)}, u32[]{:S(2)}, u32[]{:S(2)}) %collective-permute-start.30) | collective-permute-done | bytes 16416 | tf_op jit(solution)/shard_map/ppermute | solution.py:573
  98.8 1.6 %last.1 = (f32[8,64,192]{2,1,0:T(8,128)}, f32[64,64]{1,0:T(8,128)}) custom-call(f32[2,64,256]{2,1,0:T(8,128)S(1)} %get-tuple-element.109.after_ref.mixed_ref, f32[8,64,192]{2,1,0:T(8,128)S(1)} %get-tuple-element.113.tall_ref, f32[32,128]{1,0:T(8,128)S(1)} %add.5.refs_0_, f32[32,128]{1,0:T(8,128)S(1)} %collective-permute-done.29.refs_1_, ...), custom_call_target="tpu_custom_call" | custom-call | flops 330000000 | bytes 1064960 | tf_op jit(solution)/shard_map/last/pallas_call | solution.py:521
  (79 shorter events, 18.3 us)
Async XLA Ops:
  5.3 15.5 %collective-permute-start.3 = (f32[2,192,128]{2,1,0:T(8,128)S(1)}, f32[2,192,128]{2,1,0:T(8,128)S(1)}, u32[]{:S(2)}, u32[]{:S(2)}) collective-permute-start(f32[2,192,128]{2,1,0:T(8,128)S(1)} %get-tuple-element.65), channel_id=1, source_target_pairs={{0,1},{1,0},{2,3},{3,2},{4,5},{5,4},{6,7},{7,6},{8,9},{9,8},{10,11... | collective-permute-start | bytes 589832 | tf_op jit(solution)/shard_map/ppermute | solution.py:534
  9.4 11.4 %collective-permute-start.4 = (f32[2,192,128]{2,1,0:T(8,128)S(1)}, f32[2,192,128]{2,1,0:T(8,128)S(1)}, u32[]{:S(2)}, u32[]{:S(2)}) collective-permute-start(f32[2,192,128]{2,1,0:T(8,128)S(1)} %get-tuple-element.66), channel_id=1, source_target_pairs={{0,1},{1,0},{2,3},{3,2},{4,5},{5,4},{6,7},{7,6},{8,9},{9,8},{10,11... | collective-permute-start | bytes 589832 | tf_op jit(solution)/shard_map/ppermute | solution.py:534
  9.5 8.6 %collective-permute-start.2 = (f32[64,64]{1,0:T(8,128)S(1)}, f32[64,64]{1,0:T(8,128)S(1)}, u32[]{:S(2)}, u32[]{:S(2)}) collective-permute-start(f32[64,64]{1,0:T(8,128)S(1)} %factor.1.after_ref.refs_0_), channel_id=1, source_target_pairs={{0,1},{1,0},{2,3},{3,2},{4,5},{5,4},{6,7},{7,6},{8,9},{9,8},{10,11... | collective-permute-start | bytes 49160 | tf_op jit(solution)/shard_map/ppermute | solution.py:534
  11.5 9.3 %collective-permute-start.1 = (f32[8,64]{1,0:T(8,128)S(1)}, f32[8,64]{1,0:T(8,128)S(1)}, u32[]{:S(2)}, u32[]{:S(2)}) collective-permute-start(f32[8,64]{1,0:T(8,128)S(1)} %copy-done.6), channel_id=1, source_target_pairs={{0,30},{2,0},{4,2},{6,4},{8,6},{10,8},{12,10},{14,12},{16,14},{18,... | collective-permute-start | bytes 6152 | tf_op jit(solution)/shard_map/ppermute | solution.py:534
  14.7 6.2 %collective-permute-start = (f32[8,64]{1,0:T(8,128)S(1)}, f32[8,64]{1,0:T(8,128)S(1)}, u32[]{:S(2)}, u32[]{:S(2)}) collective-permute-start(f32[8,64]{1,0:T(8,128)S(1)} %copy-done.6), channel_id=1, source_target_pairs={{0,2},{2,4},{4,6},{6,8},{8,10},{10,12},{12,14},{14,16},{16,18},{18... | collective-permute-start | bytes 6152 | tf_op jit(solution)/shard_map/ppermute | solution.py:534
  21.7 7.3 %collective-permute-start.7 = (f32[2,64,256]{2,1,0:T(8,128)S(1)}, f32[2,64,256]{2,1,0:T(8,128)S(1)}, u32[]{:S(2)}, u32[]{:S(2)}) collective-permute-start(f32[2,64,256]{2,1,0:T(8,128)S(1)} %get-tuple-element.74.refs_0_), channel_id=1, source_target_pairs={{0,1},{1,0},{2,3},{3,2},{4,5},{5,4},{6,7},{7,6},{8,9},{9,8},{10,11... | collective-permute-start | bytes 393224 | tf_op jit(solution)/shard_map/ppermute | solution.py:534
  24.2 9.4 %collective-permute-start.5 = (f32[4,64,192]{2,1,0:T(8,128)S(1)}, f32[4,64,192]{2,1,0:T(8,128)S(1)}, u32[]{:S(2)}, u32[]{:S(2)}) collective-permute-start(f32[4,64,192]{2,1,0:T(8,128)S(1)} %get-tuple-element.71), channel_id=1, source_target_pairs={{0,2},{4,6},{8,10},{12,14},{16,18},{20,22},{24,26},{28,30},{2,0},{... | collective-permute-start | bytes 589832 | tf_op jit(solution)/shard_map/ppermute | solution.py:540
  24.3 9.4 %collective-permute-start.6 = (f32[4,64,192]{2,1,0:T(8,128)S(1)}, f32[4,64,192]{2,1,0:T(8,128)S(1)}, u32[]{:S(2)}, u32[]{:S(2)}) collective-permute-start(f32[4,64,192]{2,1,0:T(8,128)S(1)} %get-tuple-element.72), channel_id=1, source_target_pairs={{2,4},{6,8},{10,12},{14,16},{18,20},{22,24},{26,28},{30,0},{4,2},{... | collective-permute-start | bytes 589832 | tf_op jit(solution)/shard_map/ppermute | solution.py:540
  35.4 19.6 %collective-permute-start.18 = (f32[2,64,512]{2,1,0:T(8,128)S(1)}, f32[2,64,512]{2,1,0:T(8,128)S(1)}, u32[]{:S(2)}, u32[]{:S(2)}) collective-permute-start(f32[2,64,512]{2,1,0:T(8,128)S(1)} %get-tuple-element.96.refs_0_), channel_id=1, source_target_pairs={{0,1},{1,0},{2,3},{3,2},{4,5},{5,4},{6,7},{7,6},{8,9},{9,8},{10,11... | collective-permute-start | bytes 786440 | tf_op jit(solution)/shard_map/ppermute | solution.py:534
  35.9 7.7 %collective-permute-start.15 = (f32[32,128]{1,0:T(8,128)S(1)}, f32[32,128]{1,0:T(8,128)S(1)}, u32[]{:S(2)}, u32[]{:S(2)}) collective-permute-start(f32[32,128]{1,0:T(8,128)S(1)} %add.3.refs_0_), channel_id=1, source_target_pairs={{0,28},{2,30},{4,24},{6,26},{8,20},{10,22},{12,16},{14,18},{16,12}... | collective-permute-start | bytes 49160 | tf_op jit(solution)/shard_map/ppermute | solution.py:573
  40.0 5.5 %collective-permute-start.14 = (f32[32,128]{1,0:T(8,128)S(1)}, f32[32,128]{1,0:T(8,128)S(1)}, u32[]{:S(2)}, u32[]{:S(2)}) collective-permute-start(f32[32,128]{1,0:T(8,128)S(1)} %add.3.refs_0_), channel_id=1, source_target_pairs={{0,24},{2,26},{4,28},{6,30},{8,16},{10,18},{12,20},{14,22},{16,8},... | collective-permute-start | bytes 49160 | tf_op jit(solution)/shard_map/ppermute | solution.py:573
  40.0 5.9 %collective-permute-start.13 = (f32[32,128]{1,0:T(8,128)S(1)}, f32[32,128]{1,0:T(8,128)S(1)}, u32[]{:S(2)}, u32[]{:S(2)}) collective-permute-start(f32[32,128]{1,0:T(8,128)S(1)} %add.3.refs_0_), channel_id=1, source_target_pairs={{0,20},{2,22},{4,16},{6,18},{8,28},{10,30},{12,24},{14,26},{16,4},... | collective-permute-start | bytes 49160 | tf_op jit(solution)/shard_map/ppermute | solution.py:573
  41.1 6.0 %collective-permute-start.12 = (f32[32,128]{1,0:T(8,128)S(1)}, f32[32,128]{1,0:T(8,128)S(1)}, u32[]{:S(2)}, u32[]{:S(2)}) collective-permute-start(f32[32,128]{1,0:T(8,128)S(1)} %add.3.refs_0_), channel_id=1, source_target_pairs={{0,16},{2,18},{4,20},{6,22},{8,24},{10,26},{12,28},{14,30},{16,0},... | collective-permute-start | bytes 49160 | tf_op jit(solution)/shard_map/ppermute | solution.py:573
  43.6 4.6 %collective-permute-start.11 = (f32[32,128]{1,0:T(8,128)S(1)}, f32[32,128]{1,0:T(8,128)S(1)}, u32[]{:S(2)}, u32[]{:S(2)}) collective-permute-start(f32[32,128]{1,0:T(8,128)S(1)} %add.3.refs_0_), channel_id=1, source_target_pairs={{0,12},{2,14},{4,8},{6,10},{8,4},{10,6},{12,0},{14,2},{16,28},{18,... | collective-permute-start | bytes 49160 | tf_op jit(solution)/shard_map/ppermute | solution.py:573
  45.6 3.7 %collective-permute-start.10 = (f32[32,128]{1,0:T(8,128)S(1)}, f32[32,128]{1,0:T(8,128)S(1)}, u32[]{:S(2)}, u32[]{:S(2)}) collective-permute-start(f32[32,128]{1,0:T(8,128)S(1)} %add.3.refs_0_), channel_id=1, source_target_pairs={{0,8},{2,10},{4,12},{6,14},{8,0},{10,2},{12,4},{14,6},{16,24},{18,... | collective-permute-start | bytes 49160 | tf_op jit(solution)/shard_map/ppermute | solution.py:573
  51.0 9.2 %collective-permute-start.16 = (f32[4,64,192]{2,1,0:T(8,128)S(1)}, f32[4,64,192]{2,1,0:T(8,128)S(1)}, u32[]{:S(2)}, u32[]{:S(2)}) collective-permute-start(f32[4,64,192]{2,1,0:T(8,128)S(1)} %get-tuple-element.92), channel_id=1, source_target_pairs={{0,2},{4,6},{8,10},{12,14},{16,18},{20,22},{24,26},{28,30},{2,0},{... | collective-permute-start | bytes 589832 | tf_op jit(solution)/shard_map/ppermute | solution.py:540
  51.1 9.1 %collective-permute-start.17 = (f32[4,64,192]{2,1,0:T(8,128)S(1)}, f32[4,64,192]{2,1,0:T(8,128)S(1)}, u32[]{:S(2)}, u32[]{:S(2)}) collective-permute-start(f32[4,64,192]{2,1,0:T(8,128)S(1)} %get-tuple-element.93), channel_id=1, source_target_pairs={{2,4},{6,8},{10,12},{14,16},{18,20},{22,24},{26,28},{30,0},{4,2},{... | collective-permute-start | bytes 589832 | tf_op jit(solution)/shard_map/ppermute | solution.py:540
  62.2 15.7 %collective-permute-start.27 = (f32[2,64,512]{2,1,0:T(8,128)S(1)}, f32[2,64,512]{2,1,0:T(8,128)S(1)}, u32[]{:S(2)}, u32[]{:S(2)}) collective-permute-start(f32[2,64,512]{2,1,0:T(8,128)S(1)} %get-tuple-element.108.refs_0_), channel_id=1, source_target_pairs={{0,1},{1,0},{2,3},{3,2},{4,5},{5,4},{6,7},{7,6},{8,9},{9,8},{10,11... | collective-permute-start | bytes 786440 | tf_op jit(solution)/shard_map/ppermute | solution.py:534
  63.8 7.7 %collective-permute-start.26 = (f32[32,128]{1,0:T(8,128)S(1)}, f32[32,128]{1,0:T(8,128)S(1)}, u32[]{:S(2)}, u32[]{:S(2)}) collective-permute-start(f32[32,128]{1,0:T(8,128)S(1)} %add.4.refs_0_), channel_id=1, source_target_pairs={{0,28},{2,30},{4,24},{6,26},{8,20},{10,22},{12,16},{14,18},{16,12}... | collective-permute-start | bytes 49160 | tf_op jit(solution)/shard_map/ppermute | solution.py:573
  67.5 5.5 %collective-permute-start.25 = (f32[32,128]{1,0:T(8,128)S(1)}, f32[32,128]{1,0:T(8,128)S(1)}, u32[]{:S(2)}, u32[]{:S(2)}) collective-permute-start(f32[32,128]{1,0:T(8,128)S(1)} %add.4.refs_0_), channel_id=1, source_target_pairs={{0,24},{2,26},{4,28},{6,30},{8,16},{10,18},{12,20},{14,22},{16,8},... | collective-permute-start | bytes 49160 | tf_op jit(solution)/shard_map/ppermute | solution.py:573
  67.7 5.9 %collective-permute-start.24 = (f32[32,128]{1,0:T(8,128)S(1)}, f32[32,128]{1,0:T(8,128)S(1)}, u32[]{:S(2)}, u32[]{:S(2)}) collective-permute-start(f32[32,128]{1,0:T(8,128)S(1)} %add.4.refs_0_), channel_id=1, source_target_pairs={{0,20},{2,22},{4,16},{6,18},{8,28},{10,30},{12,24},{14,26},{16,4},... | collective-permute-start | bytes 49160 | tf_op jit(solution)/shard_map/ppermute | solution.py:573
  69.1 5.8 %collective-permute-start.23 = (f32[32,128]{1,0:T(8,128)S(1)}, f32[32,128]{1,0:T(8,128)S(1)}, u32[]{:S(2)}, u32[]{:S(2)}) collective-permute-start(f32[32,128]{1,0:T(8,128)S(1)} %add.4.refs_0_), channel_id=1, source_target_pairs={{0,16},{2,18},{4,20},{6,22},{8,24},{10,26},{12,28},{14,30},{16,0},... | collective-permute-start | bytes 49160 | tf_op jit(solution)/shard_map/ppermute | solution.py:573
  71.4 4.6 %collective-permute-start.22 = (f32[32,128]{1,0:T(8,128)S(1)}, f32[32,128]{1,0:T(8,128)S(1)}, u32[]{:S(2)}, u32[]{:S(2)}) collective-permute-start(f32[32,128]{1,0:T(8,128)S(1)} %add.4.refs_0_), channel_id=1, source_target_pairs={{0,12},{2,14},{4,8},{6,10},{8,4},{10,6},{12,0},{14,2},{16,28},{18,... | collective-permute-start | bytes 49160 | tf_op jit(solution)/shard_map/ppermute | solution.py:573
  73.0 3.7 %collective-permute-start.21 = (f32[32,128]{1,0:T(8,128)S(1)}, f32[32,128]{1,0:T(8,128)S(1)}, u32[]{:S(2)}, u32[]{:S(2)}) collective-permute-start(f32[32,128]{1,0:T(8,128)S(1)} %add.4.refs_0_), channel_id=1, source_target_pairs={{0,8},{2,10},{4,12},{6,14},{8,0},{10,2},{12,4},{14,6},{16,24},{18,... | collective-permute-start | bytes 49160 | tf_op jit(solution)/shard_map/ppermute | solution.py:573
  73.6 3.7 %collective-permute-start.20 = (f32[32,128]{1,0:T(8,128)S(1)}, f32[32,128]{1,0:T(8,128)S(1)}, u32[]{:S(2)}, u32[]{:S(2)}) collective-permute-start(f32[32,128]{1,0:T(8,128)S(1)} %add.4.refs_0_), channel_id=1, source_target_pairs={{0,4},{2,6},{4,0},{6,2},{8,12},{10,14},{12,8},{14,10},{16,20},{18,... | collective-permute-start | bytes 49160 | tf_op jit(solution)/shard_map/ppermute | solution.py:573
  84.6 9.8 %collective-permute-start.35 = (f32[32,128]{1,0:T(8,128)S(1)}, f32[32,128]{1,0:T(8,128)S(1)}, u32[]{:S(2)}, u32[]{:S(2)}) collective-permute-start(f32[32,128]{1,0:T(8,128)S(1)} %add.5.refs_0_), channel_id=1, source_target_pairs={{0,28},{2,30},{4,24},{6,26},{8,20},{10,22},{12,16},{14,18},{16,12}... | collective-permute-start | bytes 49160 | tf_op jit(solution)/shard_map/ppermute | solution.py:573
  89.1 5.9 %collective-permute-start.34 = (f32[32,128]{1,0:T(8,128)S(1)}, f32[32,128]{1,0:T(8,128)S(1)}, u32[]{:S(2)}, u32[]{:S(2)}) collective-permute-start(f32[32,128]{1,0:T(8,128)S(1)} %add.5.refs_0_), channel_id=1, source_target_pairs={{0,24},{2,26},{4,28},{6,30},{8,16},{10,18},{12,20},{14,22},{16,8},... | collective-permute-start | bytes 49160 | tf_op jit(solution)/shard_map/ppermute | solution.py:573
  89.2 7.7 %collective-permute-start.33 = (f32[32,128]{1,0:T(8,128)S(1)}, f32[32,128]{1,0:T(8,128)S(1)}, u32[]{:S(2)}, u32[]{:S(2)}) collective-permute-start(f32[32,128]{1,0:T(8,128)S(1)} %add.5.refs_0_), channel_id=1, source_target_pairs={{0,20},{2,22},{4,16},{6,18},{8,28},{10,30},{12,24},{14,26},{16,4},... | collective-permute-start | bytes 49160 | tf_op jit(solution)/shard_map/ppermute | solution.py:573
  89.8 7.1 %collective-permute-start.32 = (f32[32,128]{1,0:T(8,128)S(1)}, f32[32,128]{1,0:T(8,128)S(1)}, u32[]{:S(2)}, u32[]{:S(2)}) collective-permute-start(f32[32,128]{1,0:T(8,128)S(1)} %add.5.refs_0_), channel_id=1, source_target_pairs={{0,16},{2,18},{4,20},{6,22},{8,24},{10,26},{12,28},{14,30},{16,0},... | collective-permute-start | bytes 49160 | tf_op jit(solution)/shard_map/ppermute | solution.py:573
  92.3 4.7 %collective-permute-start.31 = (f32[32,128]{1,0:T(8,128)S(1)}, f32[32,128]{1,0:T(8,128)S(1)}, u32[]{:S(2)}, u32[]{:S(2)}) collective-permute-start(f32[32,128]{1,0:T(8,128)S(1)} %add.5.refs_0_), channel_id=1, source_target_pairs={{0,12},{2,14},{4,8},{6,10},{8,4},{10,6},{12,0},{14,2},{16,28},{18,... | collective-permute-start | bytes 49160 | tf_op jit(solution)/shard_map/ppermute | solution.py:573
  94.4 3.7 %collective-permute-start.30 = (f32[32,128]{1,0:T(8,128)S(1)}, f32[32,128]{1,0:T(8,128)S(1)}, u32[]{:S(2)}, u32[]{:S(2)}) collective-permute-start(f32[32,128]{1,0:T(8,128)S(1)} %add.5.refs_0_), channel_id=1, source_target_pairs={{0,8},{2,10},{4,12},{6,14},{8,0},{10,2},{12,4},{14,6},{16,24},{18,... | collective-permute-start | bytes 49160 | tf_op jit(solution)/shard_map/ppermute | solution.py:573
  95.1 3.7 %collective-permute-start.29 = (f32[32,128]{1,0:T(8,128)S(1)}, f32[32,128]{1,0:T(8,128)S(1)}, u32[]{:S(2)}, u32[]{:S(2)}) collective-permute-start(f32[32,128]{1,0:T(8,128)S(1)} %add.5.refs_0_), channel_id=1, source_target_pairs={{0,4},{2,6},{4,0},{6,2},{8,12},{10,14},{12,8},{14,10},{16,20},{18,... | collective-permute-start | bytes 49160 | tf_op jit(solution)/shard_map/ppermute | solution.py:573
  (13 other events, 85.0 us)

commit v2 on v1

--- a/solution.py
+++ b/solution.py
@@ -91,24 +91,50 @@
     gram_ref[...] = dot(factor, factor, NT)
 
 
-def project_kernel(first, order_ref, me_ref, after_ref, data_ref, factor_ref, *outs):
+def project_kernel(order_ref, me_ref, first_ref, second_ref, factor_ref, after_ref, *outs):
     parts = len(outs)
-    pairs, rows, _ = outs[0].shape
-    count = data_ref.shape[0]
+    rows = outs[0].shape[1]
     factor = factor_ref[...]
     empty = jnp.zeros_like(factor)
     sides = [
         jnp.concatenate([factor, empty], axis=0),
         jnp.concatenate([empty, factor], axis=0),
     ]
-    for pair in range(pairs):
-        stored = [lax.rem(order_ref[2 * (first + pair) + at], count) for at in range(2)]
-        for part in reversed(range(parts)):
-            start = pl.multiple_of(lax.rem(me_ref[0] + part, parts) * rows, 16)
-            place = pl.ds(start, rows)
-            outs[part][pair] = dot(data_ref[stored[0], place, :], sides[0], NT) + dot(
-                data_ref[stored[1], place, :], sides[1], NT
-            )
+    for part in reversed(range(parts)):
+        start = pl.multiple_of(lax.rem(me_ref[0] + part, parts) * rows, 16)
+        place = pl.ds(start, rows)
+        outs[part][0] = dot(first_ref[0, place, :], sides[0], NT) + dot(
+            second_ref[0, place, :], sides[1], NT
+        )
+
+
+def project(first, pairs, parts, rows, order, me, data, factor, after):
+    count, all_rows, channels = data.shape
+    rank = factor.shape[0]
+    spec = lambda odd: pl.BlockSpec(
+        (1, all_rows, channels),
+        lambda i, order, me: (lax.rem(order[2 * (first + i) + odd], count), 0, 0),
+    )
+    return pl.pallas_call(
+        project_kernel,
+        out_shape=[jax.ShapeDtypeStruct((pairs, rows, 2 * rank), f32)] * parts,
+        grid_spec=pltpu.PrefetchScalarGridSpec(
+            num_scalar_prefetch=2,
+            grid=(pairs,),
+            in_specs=[
+                spec(0),
+                spec(1),
+                pl.BlockSpec((rank, channels), lambda i, order, me: (0, 0)),
+                pl.BlockSpec(memory_space=pl.ANY),
+            ],
+            out_specs=[pl.BlockSpec((1, rows, 2 * rank), lambda i, order, me: (i, 0, 0))] * parts,
+        ),
+        compiler_params=pltpu.CompilerParams(vmem_limit_bytes=16 * 1024 * 1024),
+        cost_estimate=pl.CostEstimate(
+            flops=2 * per_microsecond, bytes_accessed=data.size, transcendentals=0
+        ),
+        name="project",
+    )(order, me, data, data, factor, after)
 
 
 def setup_kernel(grams, group, *refs):
@@ -490,26 +516,29 @@
 
 
 def last_kernel(total, mixed_ref, tall_ref, *refs):
-    *sum_refs, coupled_ref, delta_ref = refs
+    *sum_refs, coupled_ref, delta_ref, made, sent = refs
     groups, rank, wide = mixed_ref.shape
     group = wide // rank
     delta = new_delta(sum_refs, total, rank)
     delta_ref[...] = delta
     delta_left = left_triple(delta.T)
+    copies = []
     for at in range(groups):
         mixer = dot(delta_left, right_triple(mixed_ref[at]))
         for k in range(at * group, (at + 1) * group):
             place = (k - at * group) * rank
-            coupled_ref[k] = dot(
-                left_triple(mixer[:, place : place + rank]), right_triple(tall_ref[k])
-            )
+            made[k] = dot(left_triple(mixer[:, place : place + rank]), right_triple(tall_ref[k]))
+            copies.append(pltpu.make_async_copy(made.at[k], coupled_ref.at[k], sent.at[k]))
+            copies[-1].start()
+    for copy in copies:
+        copy.wait()
 
 
 per_microsecond = 1_100_000_000
 
 
 def call(
-    kernel, name, outs, *args, scalars=0, unread=0, microseconds=0.3
+    kernel, name, outs, *args, scalars=0, unread=0, far_outs=0, microseconds=0.3, scratch=()
 ):
     flops = int(microseconds * per_microsecond)
     specs = [pl.BlockSpec(memory_space=pltpu.SMEM)] * scalars
@@ -522,7 +551,9 @@
         kernel,
         out_shape=shapes,
         in_specs=specs,
-        out_specs=[pl.BlockSpec(memory_space=pltpu.VMEM)] * len(shapes),
+        out_specs=[pl.BlockSpec(memory_space=pl.ANY)] * far_outs
+        + [pl.BlockSpec(memory_space=pltpu.VMEM)] * (len(shapes) - far_outs),
+        scratch_shapes=list(scratch),
         compiler_params=pltpu.CompilerParams(vmem_limit_bytes=16 * 1024 * 1024),
         cost_estimate=pl.CostEstimate(flops=flops, bytes_accessed=moved, transcendentals=0),
         name=name,
@@ -547,8 +578,7 @@
 def stage_sizes(count):
     sizes = []
     while count > 1:
-        choices = (8, 4, 2, 3, 5, 7, count) if sizes else (2, 3, 5, 7, count)
-        sizes.append(next(size for size in choices if count % size == 0))
+        sizes.append(next(size for size in (4, 2, 3, 5, 7, count) if count % size == 0))
         count //= sizes[-1]
     return sizes
 
@@ -568,7 +598,7 @@
             moves = []
             for i in range(count):
                 digit = (i // stride) % size
-                other = digit ^ shift if size in (2, 4, 8) else (digit + shift) % size
+                other = digit ^ shift if size in (2, 4) else (digit + shift) % size
                 moves.append((i, i + (other - digit) * stride))
             terms.append(lax.ppermute(value, axis, moves))
         stride *= size
@@ -604,13 +634,11 @@
     grams = [gram_part] + from_others(gram_part, "chan")
     own, arrived = [], []
     for chunk in range(chunks):
-        projected = call(
-            functools.partial(project_kernel, chunk * pairs),
-            "project",
-            [((pairs, rows, 2 * rank), f32)] * parts,
-            order, me, gram_part, data, factor,
-            scalars=2, unread=1,
+        projected = project(
+            chunk * pairs, pairs, parts, rows, order, me, data, factor, gram_part
         )
+        if chunk == 0:
+            projected, grams = lax.optimization_barrier((projected, grams))
         own.append(projected[0])
         arrived.append([rotated(projected[shift], "chan", shift) for shift in range(1, parts)])
     received = [arrived[chunk][at] for at in range(parts - 1) for chunk in range(chunks)]
@@ -681,6 +709,11 @@
                 "last",
                 [state, square],
                 mixed, tall, *in_stages(partial, "cuts"),
+                far_outs=1,
+                scratch=[
+                    pltpu.VMEM((count, rank, rows), f32),
+                    pltpu.SemaphoreType.DMA((count,)),
+                ],
             )
             continue
         near = swapped(to_near, "cuts", 0)

time: 101 us -> 87.6 us (0.87)
  starting transfers between devices: 54 us -> 35.6 us
  waiting for transfers between devices: 12.1 us -> 15.6 us
    ppermute x24 -> x18, starting transfers between devices: 33.1 us -> 19.3 us  [in_stages(): terms.append(lax.ppermute(value, axis, moves))]
    ppermute x4, starting transfers between devices: 8.76 us -> 5.18 us  [swapped(): return lax.ppermute(value, axis, pairs + [(b, a) for a, b in pairs])]
    pallas_call x0 -> x2, Pallas kernels: none -> 2.56 us  [project(): pl.pallas_call(project_kernel, out_shape=[jax.ShapeDtypeStruct((pairs, ro...]
    ppermute x4, waiting for transfers between devices: 0.01 us -> 1.74 us  [swapped(): return lax.ppermute(value, axis, pairs + [(b, a) for a, b in pairs])]
    pallas_call x21 -> x19, Pallas kernels: 29.9 us -> 28.3 us  [call(): pl.pallas_call(kernel, out_shape=shapes, in_specs=specs, out_specs=[pl.Bl...]
    ppermute x24 -> x18, waiting for transfers between devices: 8.64 us -> 9.84 us  [in_stages(): terms.append(lax.ppermute(value, axis, moves))]
    ppermute x8, starting transfers between devices: 12.2 us -> 11.1 us  [rotated(): lax.ppermute(value, axis, [(i, (i + shift) % count) for i in range(count)])]
    unnamed x18 -> x20, local copies, waits for them, and re-layouts: 3.4 us -> 4.26 us
  transfers between devices with their start and end apart: 36 -> 30, of which waited for: 13 -> 16; matrix products, arithmetic and copies ran while one was open for 0% -> 0% of each run, Pallas kernels for 20% -> 24%
where the time goes in v2:
time: 87.6 us; the launch traced here: 87.4 us
  starting transfers between devices  35.6 us (41%)
  Pallas kernels  30.8 us (35%)
  waiting for transfers between devices  15.6 us (18%)
  local copies, waits for them, and re-layouts  4.26 us (5%)
  between operations  1.07 us (1%)
    pallas_call x19, Pallas kernels, call(): pl.pallas_call(kernel, out_shape=shapes, in_specs=specs, out_specs=[pl.Bl...  28.3 us
    ppermute x18, starting transfers between devices, in_stages(): terms.append(lax.ppermute(value, axis, moves))  19.3 us
    ppermute x8, starting transfers between devices, rotated(): lax.ppermute(value, axis, [(i, (i + shift) % count) for i in range(count)])  11.1 us
    ppermute x18, waiting for transfers between devices, in_stages(): terms.append(lax.ppermute(value, axis, moves))  9.84 us
    ppermute x4, starting transfers between devices, swapped(): return lax.ppermute(value, axis, pairs + [(b, a) for a, b in pairs])  5.18 us
    unnamed x20, local copies, waits for them, and re-layouts  4.26 us
    ppermute x8, waiting for transfers between devices, rotated(): lax.ppermute(value, axis, [(i, (i + shift) % count) for i in range(count)])  4.04 us
    pallas_call x2, Pallas kernels, project(): pl.pallas_call(project_kernel, out_shape=[jax.ShapeDtypeStruct((pairs, ro...  2.56 us
  transfers between devices with their start and end apart: 30, of which 16 were waited for; matrix products, arithmetic and copies ran while one was open for 0% of the time, Pallas kernels for 24%

profile of v2, /device:TPU:0, one launch (start us, length us, event | category | flops | bytes accessed | tf_op | source)
XLA Modules:
  0.0 87.4 jit_solution(18067238455305729514)
XLA Ops:
  1.6 3.0 %collective-permute-start.2 = (f32[64,64]{1,0:T(8,128)S(1)}, f32[64,64]{1,0:T(8,128)S(1)}, u32[]{:S(2)}, u32[]{:S(2)}) collective-permute-start(f32[64,64]{1,0:T(8,128)S(1)} %factor.1.after_ref.refs_0_), channel_id=1, source_target_pairs={{0,1},{1,0},{2,3},{3,2},{4,5},{5,4},{6,7},{7,6},{8,9},{9,8},{10,11... | collective-permute-start | bytes 49160 | tf_op jit(solution)/shard_map/ppermute | solution.py:565
  4.6 1.9 %copy-done.5 = bf16[8,384,512]{2,1,0:T(8,128)(2,1)S(1)} copy-done((bf16[8,384,512]{2,1,0:T(8,128)(2,1)S(1)}, bf16[8,384,512]{2,1,0:T(8,128)(2,1)}, u32[]{:S(2)}) %copy-start.5) | copy-done | bytes 3145752
  8.0 1.3 %project.2 = (f32[2,192,128]{2,1,0:T(8,128)S(1)}, f32[2,192,128]{2,1,0:T(8,128)S(1)}) custom-call(s32[8]{0:T(128)S(1)} %copy-done.9, s32[1]{0:T(128)} %bitcast.2.me_ref, bf16[8,384,512]{2,1,0:T(8,128)(2,1)S(1)} %copy-done.5, bf16[8,384,512]{2,1,0:T(8,128)(2,1)S(1)} %copy-done.5, bf16[64,512]{1,0:T(8,128)(2,1)S(1)} %bitcast.17, ...), custom_call_target="tpu_custom_call" | custom-call | flops 2200000000 | bytes 1572864 | tf_op jit(solution)/shard_map/project/pallas_call | solution.py:118
  9.4 1.3 %project.3 = (f32[2,192,128]{2,1,0:T(8,128)S(1)}, f32[2,192,128]{2,1,0:T(8,128)S(1)}) custom-call(s32[8]{0:T(128)S(1)} %copy-done.9, s32[1]{0:T(128)} %bitcast.2.me_ref, bf16[8,384,512]{2,1,0:T(8,128)(2,1)S(1)} %copy-done.5, bf16[8,384,512]{2,1,0:T(8,128)(2,1)S(1)} %copy-done.5, bf16[64,512]{1,0:T(8,128)(2,1)S(1)} %bitcast.18, ...), custom_call_target="tpu_custom_call" | custom-call | flops 2200000000 | bytes 1572864 | tf_op jit(solution)/shard_map/project/pallas_call | solution.py:118
  10.7 2.1 %collective-permute-start.3 = (f32[2,192,128]{2,1,0:T(8,128)S(1)}, f32[2,192,128]{2,1,0:T(8,128)S(1)}, u32[]{:S(2)}, u32[]{:S(2)}) collective-permute-start(f32[2,192,128]{2,1,0:T(8,128)S(1)} %get-tuple-element.73), channel_id=1, source_target_pairs={{0,1},{1,0},{2,3},{3,2},{4,5},{5,4},{6,7},{7,6},{8,9},{9,8},{10,11... | collective-permute-start | bytes 589832 | tf_op jit(solution)/shard_map/ppermute | solution.py:565
  12.8 3.2 %collective-permute-start.1 = (f32[8,64]{1,0:T(8,128)S(1)}, f32[8,64]{1,0:T(8,128)S(1)}, u32[]{:S(2)}, u32[]{:S(2)}) collective-permute-start(f32[8,64]{1,0:T(8,128)S(1)} %copy-done.4), channel_id=1, source_target_pairs={{0,30},{2,0},{4,2},{6,4},{8,6},{10,8},{12,10},{14,12},{16,14},{18,... | collective-permute-start | bytes 6152 | tf_op jit(solution)/shard_map/ppermute | solution.py:565
  16.0 2.7 %setup.1 = (bf16[8,64,192]{2,1,0:T(8,128)(2,1)S(1)}, bf16[4,128,384]{2,1,0:T(8,128)(2,1)S(1)}, f32[8,128]{1,0:T(8,128)S(1)}, f32[8,64]{1,0:T(8,128)S(1)}, f32[64...) custom-call(f32[64,64]{1,0:T(8,128)S(1)} %factor.1.after_ref.refs_0_, f32[64,64]{1,0:T(8,128)S(1)} %collective-permute-done.2.refs_1_, ...), custom_call_target="tpu_custom_call" | custom-call | flops 330000000 | bytes 2598912 | tf_op jit(solution)/shard_map/setup/pallas_call | solution.py:550
  18.7 3.0 %collective-permute-done.refs_0_.before_ref = f32[8,64]{1,0:T(8,128)S(1)} collective-permute-done((f32[8,64]{1,0:T(8,128)S(1)}, f32[8,64]{1,0:T(8,128)S(1)}, u32[]{:S(2)}, u32[]{:S(2)}) %collective-permute-start) | collective-permute-done | bytes 2080 | tf_op jit(solution)/shard_map/ppermute | solution.py:565
  23.9 2.9 %collective-permute-start.6 = (f32[4,64,192]{2,1,0:T(8,128)S(1)}, f32[4,64,192]{2,1,0:T(8,128)S(1)}, u32[]{:S(2)}, u32[]{:S(2)}) collective-permute-start(f32[4,64,192]{2,1,0:T(8,128)S(1)} %get-tuple-element.80), channel_id=1, source_target_pairs={{2,4},{6,8},{10,12},{14,16},{18,20},{22,24},{26,28},{30,0},{4,2},{... | collective-permute-start | bytes 589832 | tf_op jit(solution)/shard_map/ppermute | solution.py:571
  27.6 4.7 %polar.3 = (f32[2,64,256]{2,1,0:T(8,128)S(1)}, f32[2,8,256]{2,1,0:T(8,128)S(1)}, f32[2,64,256]{2,1,0:T(8,128)S(1)}) custom-call(f32[8,64,192]{2,1,0:T(8,128)S(1)} %get-tuple-element.81.after_ref.inside_ref, f32[64,64]{1,0:T(8,128)S(1)} %copy-done.8, f32[2,64,256]{2,1,0:T(8,128)S(1)} %get-tuple-element.82.refs_0_, ...), custom_call_target="tpu_custom_call" | custom-call | flops 3300000000 | bytes 950272 | tf_op jit(solution)/shard_map/polar/pallas_call | solution.py:550
  33.1 2.1 %collective-permute-start.9 = (f32[32,128]{1,0:T(8,128)S(1)}, f32[32,128]{1,0:T(8,128)S(1)}, u32[]{:S(2)}, u32[]{:S(2)}) collective-permute-start(f32[32,128]{1,0:T(8,128)S(1)} %get-tuple-element.86.after_ref.refs_0_), channel_id=1, source_target_pairs={{0,4},{2,6},{4,0},{6,2},{8,12},{10,14},{12,8},{14,10},{16,20},{18,... | collective-permute-start | bytes 49160 | tf_op jit(solution)/shard_map/ppermute | solution.py:603
  35.2 1.0 %ahead.2 = (f32[8,64,192]{2,1,0:T(8,128)S(1)}, f32[8,64,192]{2,1,0:T(8,128)S(1)}, f32[8,64,192]{2,1,0:T(8,128)S(1)}, f32[2,64,512]{2,1,0:T(8,128)S(1)}) custom-call(s32[1]{0:T(128)} %bitcast.odd_ref.after_ref, f32[32,128]{1,0:T(8,128)S(1)} %get-tuple-element.86.after_ref.refs_0_, f32[8,64,192]{2,1,0:T(8,128)S(1)} %get-tuple-element.81.after_ref.inside_ref, ...), custom_call_target="tpu_custom_call" | custom-call | flops 330000000 | bytes 3624964 | tf_op jit(solution)/shard_map/ahead/pallas_call | solution.py:550
  37.1 1.6 %collective-permute-start.16 = (f32[2,64,512]{2,1,0:T(8,128)S(1)}, f32[2,64,512]{2,1,0:T(8,128)S(1)}, u32[]{:S(2)}, u32[]{:S(2)}) collective-permute-start(f32[2,64,512]{2,1,0:T(8,128)S(1)} %get-tuple-element.104.refs_0_), channel_id=1, source_target_pairs={{0,1},{1,0},{2,3},{3,2},{4,5},{5,4},{6,7},{7,6},{8,9},{9,8},{10,11... | collective-permute-start | bytes 786440 | tf_op jit(solution)/shard_map/ppermute | solution.py:565
  38.6 3.1 %collective-permute-start.13 = (f32[32,128]{1,0:T(8,128)S(1)}, f32[32,128]{1,0:T(8,128)S(1)}, u32[]{:S(2)}, u32[]{:S(2)}) collective-permute-start(f32[32,128]{1,0:T(8,128)S(1)} %add.3.refs_0_), channel_id=1, source_target_pairs={{0,24},{2,26},{4,28},{6,30},{8,16},{10,18},{12,20},{14,22},{16,8},... | collective-permute-start | bytes 49160 | tf_op jit(solution)/shard_map/ppermute | solution.py:603
  41.8 1.3 %collective-permute-start.11 = (f32[32,128]{1,0:T(8,128)S(1)}, f32[32,128]{1,0:T(8,128)S(1)}, u32[]{:S(2)}, u32[]{:S(2)}) collective-permute-start(f32[32,128]{1,0:T(8,128)S(1)} %add.3.refs_0_), channel_id=1, source_target_pairs={{0,8},{2,10},{4,12},{6,14},{8,0},{10,2},{12,4},{14,6},{16,24},{18,... | collective-permute-start | bytes 49160 | tf_op jit(solution)/shard_map/ppermute | solution.py:603
  43.0 1.1 %collective-permute-done.13.refs_3_ = f32[32,128]{1,0:T(8,128)S(1)} collective-permute-done((f32[32,128]{1,0:T(8,128)S(1)}, f32[32,128]{1,0:T(8,128)S(1)}, u32[]{:S(2)}, u32[]{:S(2)}) %collective-permute-start.13) | collective-permute-done | bytes 16416 | tf_op jit(solution)/shard_map/ppermute | solution.py:603
  44.2 2.2 %collective-permute-done.12.refs_2_ = f32[32,128]{1,0:T(8,128)S(1)} collective-permute-done((f32[32,128]{1,0:T(8,128)S(1)}, f32[32,128]{1,0:T(8,128)S(1)}, u32[]{:S(2)}, u32[]{:S(2)}) %collective-permute-start.12) | collective-permute-done | bytes 16416 | tf_op jit(solution)/shard_map/ppermute | solution.py:603
  47.8 2.1 %collective-permute-start.15 = (f32[4,64,192]{2,1,0:T(8,128)S(1)}, f32[4,64,192]{2,1,0:T(8,128)S(1)}, u32[]{:S(2)}, u32[]{:S(2)}) collective-permute-start(f32[4,64,192]{2,1,0:T(8,128)S(1)} %get-tuple-element.101), channel_id=1, source_target_pairs={{2,4},{6,8},{10,12},{14,16},{18,20},{22,24},{26,28},{30,0},{4,2},{... | collective-permute-start | bytes 589832 | tf_op jit(solution)/shard_map/ppermute | solution.py:571
  49.9 5.1 %polar.4 = (f32[2,64,256]{2,1,0:T(8,128)S(1)}, f32[2,8,256]{2,1,0:T(8,128)S(1)}, f32[2,64,256]{2,1,0:T(8,128)S(1)}) custom-call(f32[8,64,192]{2,1,0:T(8,128)S(1)} %get-tuple-element.103.after_ref.inside_ref, f32[64,64]{1,0:T(8,128)S(1)} %get-tuple-element.102.delta_ref, f32[2,64,256]{2,1,0:T(8,128)S(1)} %get-tuple-element.96.refs_0_.change_ref, ...), custom_call_target="tpu_custom_call" | custom-call | flops 3300000000 | bytes 1474560 | tf_op jit(solution)/shard_map/polar/pallas_call | solution.py:550
  55.0 1.4 %collective-permute-done.15.far_ref = f32[4,64,192]{2,1,0:T(8,128)S(1)} collective-permute-done((f32[4,64,192]{2,1,0:T(8,128)S(1)}, f32[4,64,192]{2,1,0:T(8,128)S(1)}, u32[]{:S(2)}, u32[]{:S(2)}) %collective-permute-start.15) | collective-permute-done | bytes 196640 | tf_op jit(solution)/shard_map/ppermute | solution.py:571
  57.0 2.1 %collective-permute-start.18 = (f32[32,128]{1,0:T(8,128)S(1)}, f32[32,128]{1,0:T(8,128)S(1)}, u32[]{:S(2)}, u32[]{:S(2)}) collective-permute-start(f32[32,128]{1,0:T(8,128)S(1)} %get-tuple-element.109.refs_0_.after_ref), channel_id=1, source_target_pairs={{0,4},{2,6},{4,0},{6,2},{8,12},{10,14},{12,8},{14,10},{16,20},{18,... | collective-permute-start | bytes 49160 | tf_op jit(solution)/shard_map/ppermute | solution.py:603
  59.1 1.5 %ahead.3 = (f32[8,64,192]{2,1,0:T(8,128)}, f32[8,64,192]{2,1,0:T(8,128)}, f32[8,64,192]{2,1,0:T(8,128)S(1)}, f32[2,64,512]{2,1,0:T(8,128)S(1)}) custom-call(s32[1]{0:T(128)} %bitcast.odd_ref.after_ref, f32[32,128]{1,0:T(8,128)S(1)} %get-tuple-element.109.refs_0_.after_ref, f32[8,64,192]{2,1,0:T(8,128)S(1)} %get-tuple-element.103.after_ref.inside_ref, ...), custom_call_target="tpu_custom_call" | custom-call | flops 330000000 | bytes 3624964 | tf_op jit(solution)/shard_map/ahead/pallas_call | solution.py:550
  61.6 2.3 %collective-permute-start.22 = (f32[32,128]{1,0:T(8,128)S(1)}, f32[32,128]{1,0:T(8,128)S(1)}, u32[]{:S(2)}, u32[]{:S(2)}) collective-permute-start(f32[32,128]{1,0:T(8,128)S(1)} %add.4.refs_0_), channel_id=1, source_target_pairs={{0,24},{2,26},{4,28},{6,30},{8,16},{10,18},{12,20},{14,22},{16,8},... | collective-permute-start | bytes 49160 | tf_op jit(solution)/shard_map/ppermute | solution.py:603
  63.9 2.1 %collective-permute-start.20 = (f32[32,128]{1,0:T(8,128)S(1)}, f32[32,128]{1,0:T(8,128)S(1)}, u32[]{:S(2)}, u32[]{:S(2)}) collective-permute-start(f32[32,128]{1,0:T(8,128)S(1)} %add.4.refs_0_), channel_id=1, source_target_pairs={{0,8},{2,10},{4,12},{6,14},{8,0},{10,2},{12,4},{14,6},{16,24},{18,... | collective-permute-start | bytes 49160 | tf_op jit(solution)/shard_map/ppermute | solution.py:603
  66.0 1.1 %collective-permute-done.22.refs_3_ = f32[32,128]{1,0:T(8,128)S(1)} collective-permute-done((f32[32,128]{1,0:T(8,128)S(1)}, f32[32,128]{1,0:T(8,128)S(1)}, u32[]{:S(2)}, u32[]{:S(2)}) %collective-permute-start.22) | collective-permute-done | bytes 16416 | tf_op jit(solution)/shard_map/ppermute | solution.py:603
  67.1 1.4 %collective-permute-done.21.refs_2_ = f32[32,128]{1,0:T(8,128)S(1)} collective-permute-done((f32[32,128]{1,0:T(8,128)S(1)}, f32[32,128]{1,0:T(8,128)S(1)}, u32[]{:S(2)}, u32[]{:S(2)}) %collective-permute-start.21) | collective-permute-done | bytes 16416 | tf_op jit(solution)/shard_map/ppermute | solution.py:603
  69.4 5.5 %polar.5 = (f32[2,64,256]{2,1,0:T(8,128)S(1)}, f32[32,128]{1,0:T(8,128)S(1)}) custom-call(s32[1]{0:T(128)} %bitcast.odd_ref.after_ref, f32[64,64]{1,0:T(8,128)S(1)} %get-tuple-element.114.delta_ref, f32[2,64,256]{2,1,0:T(8,128)S(1)} %get-tuple-element.115.change_ref, f32[2,64,256]{2,1,0:T(8,128)S(1)} %get-tuple-element.107.gram_ref.old_ref, ...), custom_call_target="tpu_custom_call" | custom-call | flops 3300000000 | bytes 950276 | tf_op jit(solution)/shard_map/polar/pallas_call | solution.py:550
  76.7 1.3 %collective-permute-done.26.refs_3_ = f32[32,128]{1,0:T(8,128)S(1)} collective-permute-done((f32[32,128]{1,0:T(8,128)S(1)}, f32[32,128]{1,0:T(8,128)S(1)}, u32[]{:S(2)}, u32[]{:S(2)}) %collective-permute-start.26) | collective-permute-done | bytes 16416 | tf_op jit(solution)/shard_map/ppermute | solution.py:603
  78.9 1.4 %collective-permute-start.29 = (f32[32,128]{1,0:T(8,128)S(1)}, f32[32,128]{1,0:T(8,128)S(1)}, u32[]{:S(2)}, u32[]{:S(2)}) collective-permute-start(f32[32,128]{1,0:T(8,128)S(1)} %add.5.refs_0_), channel_id=1, source_target_pairs={{0,24},{2,26},{4,28},{6,30},{8,16},{10,18},{12,20},{14,22},{16,8},... | collective-permute-start | bytes 49160 | tf_op jit(solution)/shard_map/ppermute | solution.py:603
  81.1 2.2 %collective-permute-start.27 = (f32[32,128]{1,0:T(8,128)S(1)}, f32[32,128]{1,0:T(8,128)S(1)}, u32[]{:S(2)}, u32[]{:S(2)}) collective-permute-start(f32[32,128]{1,0:T(8,128)S(1)} %add.5.refs_0_), channel_id=1, source_target_pairs={{0,8},{2,10},{4,12},{6,14},{8,0},{10,2},{12,4},{14,6},{16,24},{18,... | collective-permute-start | bytes 49160 | tf_op jit(solution)/shard_map/ppermute | solution.py:603
  83.3 1.1 %rows.3 = (f32[8,64,192]{2,1,0:T(8,128)S(1)}, f32[8,64,192]{2,1,0:T(8,128)}) custom-call(f32[2,64,256]{2,1,0:T(8,128)S(1)} %get-tuple-element.117.after_ref.mixed_ref, f32[2,64,256]{2,1,0:T(8,128)S(1)} %get-tuple-element.115.change_ref, f32[2,64,256]{2,1,0:T(8,128)S(1)} %get-tuple-element.118.forward_ref, f32[8,64,192]{2,1,0:T(8,128)S(1)} %get-tuple-element.111.tall_ref, ...), custom_call_target="tpu_custom_call" | custom-call | flops 330000000 | bytes 1966080 | tf_op jit(solution)/shard_map/rows/pallas_call | solution.py:550
  85.1 2.1 %last.1 = (f32[8,64,192]{2,1,0:T(8,128)}, f32[64,64]{1,0:T(8,128)}) custom-call(f32[2,64,256]{2,1,0:T(8,128)S(1)} %get-tuple-element.117.after_ref.mixed_ref, f32[8,64,192]{2,1,0:T(8,128)S(1)} %get-tuple-element.121.tall_ref, f32[32,128]{1,0:T(8,128)S(1)} %add.5.refs_0_, f32[32,128]{1,0:T(8,128)S(1)} %collective-permute-done.27.refs_1_, ...), custom_call_target="tpu_custom_call" | custom-call | flops 330000000 | bytes 999424 | tf_op jit(solution)/shard_map/last/pallas_call | solution.py:550
  (69 shorter events, 15.2 us)
Async XLA Ops:
  1.6 9.1 %collective-permute-start.2 = (f32[64,64]{1,0:T(8,128)S(1)}, f32[64,64]{1,0:T(8,128)S(1)}, u32[]{:S(2)}, u32[]{:S(2)}) collective-permute-start(f32[64,64]{1,0:T(8,128)S(1)} %factor.1.after_ref.refs_0_), channel_id=1, source_target_pairs={{0,1},{1,0},{2,3},{3,2},{4,5},{5,4},{6,7},{7,6},{8,9},{9,8},{10,11... | collective-permute-start | bytes 49160 | tf_op jit(solution)/shard_map/ppermute | solution.py:565
  9.3 6.7 %copy-start = (f32[8,192,64]{1,2,0:T(8,128)S(1)}, f32[8,192,64]{1,2,0:T(8,128)}, u32[]{:S(2)}) copy-start(f32[8,192,64]{1,2,0:T(8,128)} %param.15) | copy-start | bytes 1179652
  9.4 12.3 %collective-permute-start.4 = (f32[2,192,128]{2,1,0:T(8,128)S(1)}, f32[2,192,128]{2,1,0:T(8,128)S(1)}, u32[]{:S(2)}, u32[]{:S(2)}) collective-permute-start(f32[2,192,128]{2,1,0:T(8,128)S(1)} %get-tuple-element.74), channel_id=1, source_target_pairs={{0,1},{1,0},{2,3},{3,2},{4,5},{5,4},{6,7},{7,6},{8,9},{9,8},{10,11... | collective-permute-start | bytes 589832 | tf_op jit(solution)/shard_map/ppermute | solution.py:565
  10.7 11.0 %collective-permute-start.3 = (f32[2,192,128]{2,1,0:T(8,128)S(1)}, f32[2,192,128]{2,1,0:T(8,128)S(1)}, u32[]{:S(2)}, u32[]{:S(2)}) collective-permute-start(f32[2,192,128]{2,1,0:T(8,128)S(1)} %get-tuple-element.73), channel_id=1, source_target_pairs={{0,1},{1,0},{2,3},{3,2},{4,5},{5,4},{6,7},{7,6},{8,9},{9,8},{10,11... | collective-permute-start | bytes 589832 | tf_op jit(solution)/shard_map/ppermute | solution.py:565
  12.8 5.9 %collective-permute-start.1 = (f32[8,64]{1,0:T(8,128)S(1)}, f32[8,64]{1,0:T(8,128)S(1)}, u32[]{:S(2)}, u32[]{:S(2)}) collective-permute-start(f32[8,64]{1,0:T(8,128)S(1)} %copy-done.4), channel_id=1, source_target_pairs={{0,30},{2,0},{4,2},{6,4},{8,6},{10,8},{12,10},{14,12},{16,14},{18,... | collective-permute-start | bytes 6152 | tf_op jit(solution)/shard_map/ppermute | solution.py:565
  16.0 5.7 %collective-permute-start = (f32[8,64]{1,0:T(8,128)S(1)}, f32[8,64]{1,0:T(8,128)S(1)}, u32[]{:S(2)}, u32[]{:S(2)}) collective-permute-start(f32[8,64]{1,0:T(8,128)S(1)} %copy-done.4), channel_id=1, source_target_pairs={{0,2},{2,4},{4,6},{6,8},{8,10},{10,12},{12,14},{14,16},{16,18},{18... | collective-permute-start | bytes 6152 | tf_op jit(solution)/shard_map/ppermute | solution.py:565
  16.0 11.6 %copy-start.8 = (f32[64,64]{1,0:T(8,128)S(1)}, f32[64,64]{1,0:T(8,128)}, u32[]{:S(2)}) copy-start(f32[64,64]{1,0:T(8,128)} %delta_ref.3) | copy-start | bytes 49156
  22.5 5.0 %collective-permute-start.7 = (f32[2,64,256]{2,1,0:T(8,128)S(1)}, f32[2,64,256]{2,1,0:T(8,128)S(1)}, u32[]{:S(2)}, u32[]{:S(2)}) collective-permute-start(f32[2,64,256]{2,1,0:T(8,128)S(1)} %get-tuple-element.82.refs_0_), channel_id=1, source_target_pairs={{0,1},{1,0},{2,3},{3,2},{4,5},{5,4},{6,7},{7,6},{8,9},{9,8},{10,11... | collective-permute-start | bytes 393224 | tf_op jit(solution)/shard_map/ppermute | solution.py:565
  23.8 8.4 %collective-permute-start.5 = (f32[4,64,192]{2,1,0:T(8,128)S(1)}, f32[4,64,192]{2,1,0:T(8,128)S(1)}, u32[]{:S(2)}, u32[]{:S(2)}) collective-permute-start(f32[4,64,192]{2,1,0:T(8,128)S(1)} %get-tuple-element.79), channel_id=1, source_target_pairs={{0,2},{4,6},{8,10},{12,14},{16,18},{20,22},{24,26},{28,30},{2,0},{... | collective-permute-start | bytes 589832 | tf_op jit(solution)/shard_map/ppermute | solution.py:571
  23.9 8.7 %collective-permute-start.6 = (f32[4,64,192]{2,1,0:T(8,128)S(1)}, f32[4,64,192]{2,1,0:T(8,128)S(1)}, u32[]{:S(2)}, u32[]{:S(2)}) collective-permute-start(f32[4,64,192]{2,1,0:T(8,128)S(1)} %get-tuple-element.80), channel_id=1, source_target_pairs={{2,4},{6,8},{10,12},{14,16},{18,20},{22,24},{26,28},{30,0},{4,2},{... | collective-permute-start | bytes 589832 | tf_op jit(solution)/shard_map/ppermute | solution.py:571
  33.1 3.2 %collective-permute-start.10 = (f32[32,128]{1,0:T(8,128)S(1)}, f32[32,128]{1,0:T(8,128)S(1)}, u32[]{:S(2)}, u32[]{:S(2)}) collective-permute-start(f32[32,128]{1,0:T(8,128)S(1)} %get-tuple-element.86.after_ref.refs_0_), channel_id=1, source_target_pairs={{0,6},{2,4},{4,2},{6,0},{8,14},{10,12},{12,10},{14,8},{16,22},{18,... | collective-permute-start | bytes 49160 | tf_op jit(solution)/shard_map/ppermute | solution.py:603
  33.1 3.9 %collective-permute-start.9 = (f32[32,128]{1,0:T(8,128)S(1)}, f32[32,128]{1,0:T(8,128)S(1)}, u32[]{:S(2)}, u32[]{:S(2)}) collective-permute-start(f32[32,128]{1,0:T(8,128)S(1)} %get-tuple-element.86.after_ref.refs_0_), channel_id=1, source_target_pairs={{0,4},{2,6},{4,0},{6,2},{8,12},{10,14},{12,8},{14,10},{16,20},{18,... | collective-permute-start | bytes 49160 | tf_op jit(solution)/shard_map/ppermute | solution.py:603
  35.2 1.9 %collective-permute-start.8 = (f32[32,128]{1,0:T(8,128)S(1)}, f32[32,128]{1,0:T(8,128)S(1)}, u32[]{:S(2)}, u32[]{:S(2)}) collective-permute-start(f32[32,128]{1,0:T(8,128)S(1)} %get-tuple-element.86.after_ref.refs_0_), channel_id=1, source_target_pairs={{0,2},{2,0},{4,6},{6,4},{8,10},{10,8},{12,14},{14,12},{16,18},{18,... | collective-permute-start | bytes 49160 | tf_op jit(solution)/shard_map/ppermute | solution.py:603
  37.1 12.8 %collective-permute-start.16 = (f32[2,64,512]{2,1,0:T(8,128)S(1)}, f32[2,64,512]{2,1,0:T(8,128)S(1)}, u32[]{:S(2)}, u32[]{:S(2)}) collective-permute-start(f32[2,64,512]{2,1,0:T(8,128)S(1)} %get-tuple-element.104.refs_0_), channel_id=1, source_target_pairs={{0,1},{1,0},{2,3},{3,2},{4,5},{5,4},{6,7},{7,6},{8,9},{9,8},{10,11... | collective-permute-start | bytes 786440 | tf_op jit(solution)/shard_map/ppermute | solution.py:565
  38.6 5.5 %collective-permute-start.13 = (f32[32,128]{1,0:T(8,128)S(1)}, f32[32,128]{1,0:T(8,128)S(1)}, u32[]{:S(2)}, u32[]{:S(2)}) collective-permute-start(f32[32,128]{1,0:T(8,128)S(1)} %add.3.refs_0_), channel_id=1, source_target_pairs={{0,24},{2,26},{4,28},{6,30},{8,16},{10,18},{12,20},{14,22},{16,8},... | collective-permute-start | bytes 49160 | tf_op jit(solution)/shard_map/ppermute | solution.py:603
  41.8 4.6 %collective-permute-start.12 = (f32[32,128]{1,0:T(8,128)S(1)}, f32[32,128]{1,0:T(8,128)S(1)}, u32[]{:S(2)}, u32[]{:S(2)}) collective-permute-start(f32[32,128]{1,0:T(8,128)S(1)} %add.3.refs_0_), channel_id=1, source_target_pairs={{0,16},{2,18},{4,20},{6,22},{8,24},{10,26},{12,28},{14,30},{16,0},... | collective-permute-start | bytes 49160 | tf_op jit(solution)/shard_map/ppermute | solution.py:603
  41.8 4.6 %collective-permute-start.11 = (f32[32,128]{1,0:T(8,128)S(1)}, f32[32,128]{1,0:T(8,128)S(1)}, u32[]{:S(2)}, u32[]{:S(2)}) collective-permute-start(f32[32,128]{1,0:T(8,128)S(1)} %add.3.refs_0_), channel_id=1, source_target_pairs={{0,8},{2,10},{4,12},{6,14},{8,0},{10,2},{12,4},{14,6},{16,24},{18,... | collective-permute-start | bytes 49160 | tf_op jit(solution)/shard_map/ppermute | solution.py:603
  47.7 7.3 %collective-permute-start.14 = (f32[4,64,192]{2,1,0:T(8,128)S(1)}, f32[4,64,192]{2,1,0:T(8,128)S(1)}, u32[]{:S(2)}, u32[]{:S(2)}) collective-permute-start(f32[4,64,192]{2,1,0:T(8,128)S(1)} %get-tuple-element.100), channel_id=1, source_target_pairs={{0,2},{4,6},{8,10},{12,14},{16,18},{20,22},{24,26},{28,30},{2,0},{... | collective-permute-start | bytes 589832 | tf_op jit(solution)/shard_map/ppermute | solution.py:571
  47.8 8.7 %collective-permute-start.15 = (f32[4,64,192]{2,1,0:T(8,128)S(1)}, f32[4,64,192]{2,1,0:T(8,128)S(1)}, u32[]{:S(2)}, u32[]{:S(2)}) collective-permute-start(f32[4,64,192]{2,1,0:T(8,128)S(1)} %get-tuple-element.101), channel_id=1, source_target_pairs={{2,4},{6,8},{10,12},{14,16},{18,20},{22,24},{26,28},{30,0},{4,2},{... | collective-permute-start | bytes 589832 | tf_op jit(solution)/shard_map/ppermute | solution.py:571
  57.0 3.6 %collective-permute-start.19 = (f32[32,128]{1,0:T(8,128)S(1)}, f32[32,128]{1,0:T(8,128)S(1)}, u32[]{:S(2)}, u32[]{:S(2)}) collective-permute-start(f32[32,128]{1,0:T(8,128)S(1)} %get-tuple-element.109.refs_0_.after_ref), channel_id=1, source_target_pairs={{0,6},{2,4},{4,2},{6,0},{8,14},{10,12},{12,10},{14,8},{16,22},{18,... | collective-permute-start | bytes 49160 | tf_op jit(solution)/shard_map/ppermute | solution.py:603
  57.0 3.9 %collective-permute-start.18 = (f32[32,128]{1,0:T(8,128)S(1)}, f32[32,128]{1,0:T(8,128)S(1)}, u32[]{:S(2)}, u32[]{:S(2)}) collective-permute-start(f32[32,128]{1,0:T(8,128)S(1)} %get-tuple-element.109.refs_0_.after_ref), channel_id=1, source_target_pairs={{0,4},{2,6},{4,0},{6,2},{8,12},{10,14},{12,8},{14,10},{16,20},{18,... | collective-permute-start | bytes 49160 | tf_op jit(solution)/shard_map/ppermute | solution.py:603
  59.1 1.9 %collective-permute-start.17 = (f32[32,128]{1,0:T(8,128)S(1)}, f32[32,128]{1,0:T(8,128)S(1)}, u32[]{:S(2)}, u32[]{:S(2)}) collective-permute-start(f32[32,128]{1,0:T(8,128)S(1)} %get-tuple-element.109.refs_0_.after_ref), channel_id=1, source_target_pairs={{0,2},{2,0},{4,6},{6,4},{8,10},{10,8},{12,14},{14,12},{16,18},{18,... | collective-permute-start | bytes 49160 | tf_op jit(solution)/shard_map/ppermute | solution.py:603
  61.0 8.4 %collective-permute-start.23 = (f32[2,64,512]{2,1,0:T(8,128)S(1)}, f32[2,64,512]{2,1,0:T(8,128)S(1)}, u32[]{:S(2)}, u32[]{:S(2)}) collective-permute-start(f32[2,64,512]{2,1,0:T(8,128)S(1)} %get-tuple-element.116.refs_0_), channel_id=1, source_target_pairs={{0,1},{1,0},{2,3},{3,2},{4,5},{5,4},{6,7},{7,6},{8,9},{9,8},{10,11... | collective-permute-start | bytes 786440 | tf_op jit(solution)/shard_map/ppermute | solution.py:565
  61.6 5.5 %collective-permute-start.22 = (f32[32,128]{1,0:T(8,128)S(1)}, f32[32,128]{1,0:T(8,128)S(1)}, u32[]{:S(2)}, u32[]{:S(2)}) collective-permute-start(f32[32,128]{1,0:T(8,128)S(1)} %add.4.refs_0_), channel_id=1, source_target_pairs={{0,24},{2,26},{4,28},{6,30},{8,16},{10,18},{12,20},{14,22},{16,8},... | collective-permute-start | bytes 49160 | tf_op jit(solution)/shard_map/ppermute | solution.py:603
  63.9 4.6 %collective-permute-start.21 = (f32[32,128]{1,0:T(8,128)S(1)}, f32[32,128]{1,0:T(8,128)S(1)}, u32[]{:S(2)}, u32[]{:S(2)}) collective-permute-start(f32[32,128]{1,0:T(8,128)S(1)} %add.4.refs_0_), channel_id=1, source_target_pairs={{0,16},{2,18},{4,20},{6,22},{8,24},{10,26},{12,28},{14,30},{16,0},... | collective-permute-start | bytes 49160 | tf_op jit(solution)/shard_map/ppermute | solution.py:603
  63.9 4.6 %collective-permute-start.20 = (f32[32,128]{1,0:T(8,128)S(1)}, f32[32,128]{1,0:T(8,128)S(1)}, u32[]{:S(2)}, u32[]{:S(2)}) collective-permute-start(f32[32,128]{1,0:T(8,128)S(1)} %add.4.refs_0_), channel_id=1, source_target_pairs={{0,8},{2,10},{4,12},{6,14},{8,0},{10,2},{12,4},{14,6},{16,24},{18,... | collective-permute-start | bytes 49160 | tf_op jit(solution)/shard_map/ppermute | solution.py:603
  74.8 3.2 %collective-permute-start.26 = (f32[32,128]{1,0:T(8,128)S(1)}, f32[32,128]{1,0:T(8,128)S(1)}, u32[]{:S(2)}, u32[]{:S(2)}) collective-permute-start(f32[32,128]{1,0:T(8,128)S(1)} %get-tuple-element.122.refs_0_), channel_id=1, source_target_pairs={{0,6},{2,4},{4,2},{6,0},{8,14},{10,12},{12,10},{14,8},{16,22},{18,... | collective-permute-start | bytes 49160 | tf_op jit(solution)/shard_map/ppermute | solution.py:603
  74.9 4.0 %collective-permute-start.25 = (f32[32,128]{1,0:T(8,128)S(1)}, f32[32,128]{1,0:T(8,128)S(1)}, u32[]{:S(2)}, u32[]{:S(2)}) collective-permute-start(f32[32,128]{1,0:T(8,128)S(1)} %get-tuple-element.122.refs_0_), channel_id=1, source_target_pairs={{0,4},{2,6},{4,0},{6,2},{8,12},{10,14},{12,8},{14,10},{16,20},{18,... | collective-permute-start | bytes 49160 | tf_op jit(solution)/shard_map/ppermute | solution.py:603
  75.9 3.0 %collective-permute-start.24 = (f32[32,128]{1,0:T(8,128)S(1)}, f32[32,128]{1,0:T(8,128)S(1)}, u32[]{:S(2)}, u32[]{:S(2)}) collective-permute-start(f32[32,128]{1,0:T(8,128)S(1)} %get-tuple-element.122.refs_0_), channel_id=1, source_target_pairs={{0,2},{2,0},{4,6},{6,4},{8,10},{10,8},{12,14},{14,12},{16,18},{18,... | collective-permute-start | bytes 49160 | tf_op jit(solution)/shard_map/ppermute | solution.py:603
  78.9 5.7 %collective-permute-start.29 = (f32[32,128]{1,0:T(8,128)S(1)}, f32[32,128]{1,0:T(8,128)S(1)}, u32[]{:S(2)}, u32[]{:S(2)}) collective-permute-start(f32[32,128]{1,0:T(8,128)S(1)} %add.5.refs_0_), channel_id=1, source_target_pairs={{0,24},{2,26},{4,28},{6,30},{8,16},{10,18},{12,20},{14,22},{16,8},... | collective-permute-start | bytes 49160 | tf_op jit(solution)/shard_map/ppermute | solution.py:603
  80.2 4.6 %collective-permute-start.28 = (f32[32,128]{1,0:T(8,128)S(1)}, f32[32,128]{1,0:T(8,128)S(1)}, u32[]{:S(2)}, u32[]{:S(2)}) collective-permute-start(f32[32,128]{1,0:T(8,128)S(1)} %add.5.refs_0_), channel_id=1, source_target_pairs={{0,16},{2,18},{4,20},{6,22},{8,24},{10,26},{12,28},{14,30},{16,0},... | collective-permute-start | bytes 49160 | tf_op jit(solution)/shard_map/ppermute | solution.py:603
  81.1 3.9 %collective-permute-start.27 = (f32[32,128]{1,0:T(8,128)S(1)}, f32[32,128]{1,0:T(8,128)S(1)}, u32[]{:S(2)}, u32[]{:S(2)}) collective-permute-start(f32[32,128]{1,0:T(8,128)S(1)} %add.5.refs_0_), channel_id=1, source_target_pairs={{0,8},{2,10},{4,12},{6,14},{8,0},{10,2},{12,4},{14,6},{16,24},{18,... | collective-permute-start | bytes 49160 | tf_op jit(solution)/shard_map/ppermute | solution.py:603
  (8 other events, 27.7 us)

commit v3 on v2

--- a/solution.py
+++ b/solution.py
@@ -52,23 +52,23 @@
     return jnp.where(rows == lax.rem(cols, rank), 1.0, 0.0).astype(f32)
 
 
-def block_diagonal(value, mask, group):
+def block_diagonal(value, mask, group, dims=NN):
     high, low = split(value)
-    return (
-        jnp.concatenate([high] * group, axis=0) * mask,
-        jnp.concatenate([low] * group, axis=0) * mask,
+    high = jnp.concatenate([high] * group, axis=0) * mask
+    low = jnp.concatenate([low] * group, axis=0) * mask
+    empty = jnp.zeros_like(high)
+    one, other = ([high, low], [high, empty]) if dims == NN else ([high, high], [low, empty])
+    return jnp.concatenate(
+        [jnp.concatenate(one, axis=1), jnp.concatenate(other, axis=1)], axis=0
     )
 
 
 def times_blocks(values, blocks, dims=NN):
-    rank = values[0].shape[0]
-    count = len(values)
-    pieces = [split(value) for value in values]
-    high = jnp.concatenate([piece[0] for piece in pieces], axis=0)
-    both = jnp.concatenate([high] + [piece[1] for piece in pieces], axis=0)
-    first = dot(both, blocks[0], dims)
-    total = first[: count * rank] + first[count * rank :] + dot(high, blocks[1], dims)
-    return [total[at * rank : (at + 1) * rank] for at in range(count)]
+    rank, wide = values[0].shape
+    left = [jnp.concatenate(split(value), axis=1) for value in values]
+    total = dot(jnp.concatenate(left, axis=0), blocks, dims)
+    total = total[:, :wide] + total[:, wide:]
+    return [total[at * rank : (at + 1) * rank] for at in range(len(values))]
 
 
 def diagonal_blocks(value, rank, group):
@@ -80,7 +80,7 @@
 
 
 def group_size(count, rank):
-    group = max(1, 256 // rank)
+    group = max(1, 128 // rank)
     while count % group:
         group -= 1
     return group
@@ -129,7 +129,6 @@
             ],
             out_specs=[pl.BlockSpec((1, rows, 2 * rank), lambda i, order, me: (i, 0, 0))] * parts,
         ),
-        compiler_params=pltpu.CompilerParams(vmem_limit_bytes=16 * 1024 * 1024),
         cost_estimate=pl.CostEstimate(
             flops=2 * per_microsecond, bytes_accessed=data.size, transcendentals=0
         ),
@@ -202,20 +201,22 @@
                 ),
             )
         line = jnp.concatenate([weights[k : k + 1, :], weights[k + 1 : k + 2, :]], axis=1)
-        high, low = block_diagonal(jnp.concatenate(both, axis=1) * line, pair_mask, 2)
+        high, low = split(jnp.concatenate(both, axis=1) * line)
+        high = jnp.concatenate([high, high], axis=0) * pair_mask
+        low = jnp.concatenate([low, low], axis=0) * pair_mask
         mover_ref[k // 2] = jnp.concatenate([high, high, low], axis=1)
 
 
 def cross_blocks(lefts, rights, rank):
     group = len(lefts)
     wide = group * rank
-    left = [split(value) for value in lefts]
-    high = jnp.concatenate([piece[0] for piece in left], axis=0)
-    both = jnp.concatenate([high] + [piece[1] for piece in left], axis=0)
-    right = left if rights is lefts else [split(value) for value in rights]
-    first = dot(both, jnp.concatenate([piece[0] for piece in right], axis=0), NT)
-    second = dot(high, jnp.concatenate([piece[1] for piece in right], axis=0), NT)
-    return diagonal_blocks(first[:wide] + first[wide:] + second, rank, group)
+    left = jnp.concatenate(split(jnp.concatenate(lefts, axis=0)), axis=0)
+    right = left
+    if rights is not lefts:
+        right = jnp.concatenate(split(jnp.concatenate(rights, axis=0)), axis=0)
+    total = dot(left, right, NT)
+    total = total[:wide, :wide] + total[:wide, wide:] + total[wide:, :wide]
+    return diagonal_blocks(total, rank, group)
 
 
 def summed(refs, chunks, pair):
@@ -303,7 +304,7 @@
     mask = block_mask(rank, group)
     eye = wide_eye(rank, group)
     delta_left = left_triple(delta)
-    delta_blocks = block_diagonal(jnp.concatenate([delta] * group, axis=1), mask, group)
+    delta_blocks = block_diagonal(jnp.concatenate([delta] * group, axis=1), mask, group, NT)
     currents, roots, scales = [], [], []
     for gram in grams:
         left = dot(delta_left, right_triple(gram))
@@ -385,8 +386,8 @@
         change = change_ref[at]
         (onward,) = times_blocks([change], block_diagonal(old_ref[at], mask, group))
         onward = cross[:, :wide] + 0.5 * onward
-        (one,) = times_blocks([onward], block_diagonal(change, mask, group), NT)
-        (other,) = times_blocks([change], block_diagonal(onward, mask, group), NT)
+        (one,) = times_blocks([onward], block_diagonal(change, mask, group, NT), NT)
+        (other,) = times_blocks([change], block_diagonal(onward, mask, group, NT), NT)
         grams.append(cross[:, wide:] + one + other)
     delta = delta_ref[...]
     roots, scales = polar(grams, delta)
@@ -516,29 +517,26 @@
 
 
 def last_kernel(total, mixed_ref, tall_ref, *refs):
-    *sum_refs, coupled_ref, delta_ref, made, sent = refs
+    *sum_refs, coupled_ref, delta_ref = refs
     groups, rank, wide = mixed_ref.shape
     group = wide // rank
     delta = new_delta(sum_refs, total, rank)
     delta_ref[...] = delta
     delta_left = left_triple(delta.T)
-    copies = []
     for at in range(groups):
         mixer = dot(delta_left, right_triple(mixed_ref[at]))
         for k in range(at * group, (at + 1) * group):
             place = (k - at * group) * rank
-            made[k] = dot(left_triple(mixer[:, place : place + rank]), right_triple(tall_ref[k]))
-            copies.append(pltpu.make_async_copy(made.at[k], coupled_ref.at[k], sent.at[k]))
-            copies[-1].start()
-    for copy in copies:
-        copy.wait()
+            coupled_ref[k] = dot(
+                left_triple(mixer[:, place : place + rank]), right_triple(tall_ref[k])
+            )
 
 
 per_microsecond = 1_100_000_000
 
 
 def call(
-    kernel, name, outs, *args, scalars=0, unread=0, far_outs=0, microseconds=0.3, scratch=()
+    kernel, name, outs, *args, scalars=0, unread=0, microseconds=0.3
 ):
     flops = int(microseconds * per_microsecond)
     specs = [pl.BlockSpec(memory_space=pltpu.SMEM)] * scalars
@@ -551,9 +549,7 @@
         kernel,
         out_shape=shapes,
         in_specs=specs,
-        out_specs=[pl.BlockSpec(memory_space=pl.ANY)] * far_outs
-        + [pl.BlockSpec(memory_space=pltpu.VMEM)] * (len(shapes) - far_outs),
-        scratch_shapes=list(scratch),
+        out_specs=[pl.BlockSpec(memory_space=pltpu.VMEM)] * len(shapes),
         compiler_params=pltpu.CompilerParams(vmem_limit_bytes=16 * 1024 * 1024),
         cost_estimate=pl.CostEstimate(flops=flops, bytes_accessed=moved, transcendentals=0),
         name=name,
@@ -709,11 +705,6 @@
                 "last",
                 [state, square],
                 mixed, tall, *in_stages(partial, "cuts"),
-                far_outs=1,
-                scratch=[
-                    pltpu.VMEM((count, rank, rows), f32),
-                    pltpu.SemaphoreType.DMA((count,)),
-                ],
             )
             continue
         near = swapped(to_near, "cuts", 0)
@@ -733,6 +724,8 @@
             scalars=1, unread=1,
         )
         sums, cross = in_stages(partial, "cuts", beside=cross)
+        if inner < INNER - 2:
+            sums, cross = lax.optimization_barrier((sums, cross))
         crosses = from_others(cross, "chan")
         delta, change, forward = call(
             functools.partial(mixer_kernel, total),

time: 87.6 us -> 90.7 us (1.035)
  Pallas kernels: 30.8 us -> 35 us
  local copies, waits for them, and re-layouts: 4.26 us -> 2.8 us
    pallas_call x2, Pallas kernels: 2.56 us -> 6.64 us  [project(): pl.pallas_call(project_kernel, out_shape=[jax.ShapeDtypeStruct((pairs, ro...]
    unnamed x20 -> x24, local copies, waits for them, and re-layouts: 4.26 us -> 2.8 us
  transfers between devices with their start and end apart: 30 -> 30, of which waited for: 16 -> 14; matrix products, arithmetic and copies ran while one was open for 0% -> 0% of each run, Pallas kernels for 24% -> 28%
where the time goes in v3:
time: 90.7 us; the launch traced here: 90.4 us
  starting transfers between devices  35.4 us (39%)
  Pallas kernels  35 us (39%)
  waiting for transfers between devices  16.2 us (18%)
  local copies, waits for them, and re-layouts  2.8 us (3%)
  between operations  0.91 us (1%)
    pallas_call x19, Pallas kernels, call(): pl.pallas_call(kernel, out_shape=shapes, in_specs=specs, out_specs=[pl.Bl...  28.4 us
    ppermute x18, starting transfers between devices, in_stages(): terms.append(lax.ppermute(value, axis, moves))  19.4 us
    ppermute x8, starting transfers between devices, rotated(): lax.ppermute(value, axis, [(i, (i + shift) % count) for i in range(count)])  10.9 us
    ppermute x18, waiting for transfers between devices, in_stages(): terms.append(lax.ppermute(value, axis, moves))  9.79 us
    pallas_call x2, Pallas kernels, project(): pl.pallas_call(project_kernel, out_shape=[jax.ShapeDtypeStruct((pairs, ro...  6.64 us
    ppermute x4, starting transfers between devices, swapped(): return lax.ppermute(value, axis, pairs + [(b, a) for a, b in pairs])  5.18 us
    ppermute x8, waiting for transfers between devices, rotated(): lax.ppermute(value, axis, [(i, (i + shift) % count) for i in range(count)])  4.22 us
    unnamed x24, local copies, waits for them, and re-layouts  2.8 us
  transfers between devices with their start and end apart: 30, of which 14 were waited for; matrix products, arithmetic and copies ran while one was open for 0% of the time, Pallas kernels for 28%

profile of v3, /device:TPU:0, one launch (start us, length us, event | category | flops | bytes accessed | tf_op | source)
XLA Modules:
  0.0 90.4 jit_solution(6039381097662439098)
XLA Ops:
  2.2 2.9 %collective-permute-start.2 = (f32[64,64]{1,0:T(8,128)}, f32[64,64]{1,0:T(8,128)S(1)}, u32[]{:S(2)}, u32[]{:S(2)}) collective-permute-start(f32[64,64]{1,0:T(8,128)} %factor.1.after_ref.refs_0_), channel_id=1, source_target_pairs={{0,1},{1,0},{2,3},{3,2},{4,5},{5,4},{6,7},{7,6},{8,9},{9,8},{10,11... | collective-permute-start | bytes 49160 | tf_op jit(solution)/shard_map/ppermute | solution.py:561
  5.2 3.2 %project.2 = (f32[2,192,128]{2,1,0:T(8,128)}, f32[2,192,128]{2,1,0:T(8,128)}) custom-call(s32[8]{0:T(128)} %order_ref.3, s32[1]{0:T(128)} %bitcast.2.me_ref, bf16[8,384,512]{2,1,0:T(8,128)(2,1)} %second_ref.3, bf16[8,384,512]{2,1,0:T(8,128)(2,1)} %second_ref.3, bf16[64,512]{1,0:T(8,128)(2,1)} %bitcast.16, f32[64,64]{1,0:T(8,128)} %factor.1.after_ref.refs_0_), custom_call_target="tpu_custom_call" | custom-call | flops 2200000000 | bytes 1572864 | tf_op jit(solution)/shard_map/project/pallas_call | solution.py:118
  8.6 3.4 %project.3 = (f32[2,192,128]{2,1,0:T(8,128)}, f32[2,192,128]{2,1,0:T(8,128)}) custom-call(s32[8]{0:T(128)} %order_ref.3, s32[1]{0:T(128)} %bitcast.2.me_ref, bf16[8,384,512]{2,1,0:T(8,128)(2,1)} %second_ref.3, bf16[8,384,512]{2,1,0:T(8,128)(2,1)} %second_ref.3, bf16[64,512]{1,0:T(8,128)(2,1)} %bitcast.17, f32[64,64]{1,0:T(8,128)} %factor.1.after_ref.refs_0_), custom_call_target="tpu_custom_call" | custom-call | flops 2200000000 | bytes 1572864 | tf_op jit(solution)/shard_map/project/pallas_call | solution.py:118
  12.0 1.9 %collective-permute-start.3 = (f32[2,192,128]{2,1,0:T(8,128)}, f32[2,192,128]{2,1,0:T(8,128)S(1)}, u32[]{:S(2)}, u32[]{:S(2)}) collective-permute-start(f32[2,192,128]{2,1,0:T(8,128)} %get-tuple-element.78), channel_id=1, source_target_pairs={{0,1},{1,0},{2,3},{3,2},{4,5},{5,4},{6,7},{7,6},{8,9},{9,8},{10,11... | collective-permute-start | bytes 589832 | tf_op jit(solution)/shard_map/ppermute | solution.py:561
  13.9 3.2 %collective-permute-start.1 = (f32[8,64]{1,0:T(8,128)S(1)}, f32[8,64]{1,0:T(8,128)S(1)}, u32[]{:S(2)}, u32[]{:S(2)}) collective-permute-start(f32[8,64]{1,0:T(8,128)S(1)} %copy-done.9), channel_id=1, source_target_pairs={{0,30},{2,0},{4,2},{6,4},{8,6},{10,8},{12,10},{14,12},{16,14},{18,... | collective-permute-start | bytes 6152 | tf_op jit(solution)/shard_map/ppermute | solution.py:561
  17.1 3.0 %setup.1 = (bf16[8,64,192]{2,1,0:T(8,128)(2,1)S(1)}, bf16[4,128,384]{2,1,0:T(8,128)(2,1)S(1)}, f32[8,128]{1,0:T(8,128)S(1)}, f32[8,64]{1,0:T(8,128)S(1)}, f32[64...) custom-call(f32[64,64]{1,0:T(8,128)} %factor.1.after_ref.refs_0_, f32[64,64]{1,0:T(8,128)S(1)} %collective-permute-done.2.refs_1_, ...), custom_call_target="tpu_custom_call" | custom-call | flops 330000000 | bytes 2598912 | tf_op jit(solution)/shard_map/setup/pallas_call | solution.py:548
  20.1 2.7 %collective-permute-done.refs_0_.before_ref = f32[8,64]{1,0:T(8,128)S(1)} collective-permute-done((f32[8,64]{1,0:T(8,128)S(1)}, f32[8,64]{1,0:T(8,128)S(1)}, u32[]{:S(2)}, u32[]{:S(2)}) %collective-permute-start) | collective-permute-done | bytes 2080 | tf_op jit(solution)/shard_map/ppermute | solution.py:561
  23.8 1.4 %first.1 = (f32[8,64,192]{2,1,0:T(8,128)S(1)}, f32[8,64,192]{2,1,0:T(8,128)S(1)}, f32[4,64,128]{2,1,0:T(8,128)}) custom-call(f32[8,64]{1,0:T(8,128)S(1)} %collective-permute-done.refs_0_.before_ref, f32[8,64]{1,0:T(8,128)S(1)} %collective-permute-done.1.refs_1_.after_ref, f32[8,64,192]{2,1,0:T(8,128)S(1)} %get-tuple-element.75.refs_2_, ...), custom_call_target="tpu_custom_call" | custom-call | flops 330000000 | bytes 3280896 | tf_op jit(solution)/shard_map/first/pallas_call | solution.py:548
  27.6 1.6 %collective-permute-start.6 = (f32[4,64,192]{2,1,0:T(8,128)S(1)}, f32[4,64,192]{2,1,0:T(8,128)S(1)}, u32[]{:S(2)}, u32[]{:S(2)}) collective-permute-start(f32[4,64,192]{2,1,0:T(8,128)S(1)} %get-tuple-element.85), channel_id=1, source_target_pairs={{2,4},{6,8},{10,12},{14,16},{18,20},{22,24},{26,28},{30,0},{4,2},{... | collective-permute-start | bytes 589832 | tf_op jit(solution)/shard_map/ppermute | solution.py:567
  29.1 1.3 %collective-permute-done.7.refs_1_ = f32[4,64,128]{2,1,0:T(8,128)S(1)} collective-permute-done((f32[4,64,128]{2,1,0:T(8,128)}, f32[4,64,128]{2,1,0:T(8,128)S(1)}, u32[]{:S(2)}, u32[]{:S(2)}) %collective-permute-start.7) | collective-permute-done | bytes 131104 | tf_op jit(solution)/shard_map/ppermute | solution.py:561
  30.4 4.4 %polar.3 = (f32[4,64,128]{2,1,0:T(8,128)S(1)}, f32[4,8,128]{2,1,0:T(8,128)S(1)}, f32[4,64,128]{2,1,0:T(8,128)S(1)}) custom-call(f32[8,64,192]{2,1,0:T(8,128)S(1)} %get-tuple-element.86.after_ref.inside_ref, f32[64,64]{1,0:T(8,128)S(1)} %copy-done.11, f32[4,64,128]{2,1,0:T(8,128)} %get-tuple-element.87.refs_0_, f32[4,64,128]{2,1,0:T(8,128)S(1)} %collective-permute-done.7.refs_1_), custom_call_target="tpu_custom_call" | custom-call | flops 3300000000 | bytes 950272 | tf_op jit(solution)/shard_map/polar/pallas_call | solution.py:548
  34.8 1.4 %collective-permute-done.6.far_ref = f32[4,64,192]{2,1,0:T(8,128)S(1)} collective-permute-done((f32[4,64,192]{2,1,0:T(8,128)S(1)}, f32[4,64,192]{2,1,0:T(8,128)S(1)}, u32[]{:S(2)}, u32[]{:S(2)}) %collective-permute-start.6) | collective-permute-done | bytes 196640 | tf_op jit(solution)/shard_map/ppermute | solution.py:567
  36.8 2.1 %collective-permute-start.9 = (f32[32,128]{1,0:T(8,128)S(1)}, f32[32,128]{1,0:T(8,128)S(1)}, u32[]{:S(2)}, u32[]{:S(2)}) collective-permute-start(f32[32,128]{1,0:T(8,128)S(1)} %get-tuple-element.91.after_ref.refs_0_), channel_id=1, source_target_pairs={{0,4},{2,6},{4,0},{6,2},{8,12},{10,14},{12,8},{14,10},{16,20},{18,... | collective-permute-start | bytes 49160 | tf_op jit(solution)/shard_map/ppermute | solution.py:599
  38.9 1.2 %ahead.2 = (f32[8,64,192]{2,1,0:T(8,128)S(1)}, f32[8,64,192]{2,1,0:T(8,128)S(1)}, f32[8,64,192]{2,1,0:T(8,128)S(1)}, f32[4,64,256]{2,1,0:T(8,128)S(1)}) custom-call(s32[1]{0:T(128)} %bitcast.odd_ref.after_ref, f32[32,128]{1,0:T(8,128)S(1)} %get-tuple-element.91.after_ref.refs_0_, f32[8,64,192]{2,1,0:T(8,128)S(1)} %get-tuple-element.86.after_ref.inside_ref, ...), custom_call_target="tpu_custom_call" | custom-call | flops 330000000 | bytes 3624964 | tf_op jit(solution)/shard_map/ahead/pallas_call | solution.py:548
  40.8 1.8 %collective-permute-start.13 = (f32[32,128]{1,0:T(8,128)S(1)}, f32[32,128]{1,0:T(8,128)S(1)}, u32[]{:S(2)}, u32[]{:S(2)}) collective-permute-start(f32[32,128]{1,0:T(8,128)S(1)} %add.3.refs_0_), channel_id=1, source_target_pairs={{0,24},{2,26},{4,28},{6,30},{8,16},{10,18},{12,20},{14,22},{16,8},... | collective-permute-start | bytes 49160 | tf_op jit(solution)/shard_map/ppermute | solution.py:599
  42.6 2.7 %collective-permute-start.11 = (f32[32,128]{1,0:T(8,128)S(1)}, f32[32,128]{1,0:T(8,128)S(1)}, u32[]{:S(2)}, u32[]{:S(2)}) collective-permute-start(f32[32,128]{1,0:T(8,128)S(1)} %add.3.refs_0_), channel_id=1, source_target_pairs={{0,8},{2,10},{4,12},{6,14},{8,0},{10,2},{12,4},{14,6},{16,24},{18,... | collective-permute-start | bytes 49160 | tf_op jit(solution)/shard_map/ppermute | solution.py:599
  45.2 1.1 %collective-permute-done.13.refs_3_ = f32[32,128]{1,0:T(8,128)S(1)} collective-permute-done((f32[32,128]{1,0:T(8,128)S(1)}, f32[32,128]{1,0:T(8,128)S(1)}, u32[]{:S(2)}, u32[]{:S(2)}) %collective-permute-start.13) | collective-permute-done | bytes 16416 | tf_op jit(solution)/shard_map/ppermute | solution.py:599
  47.2 1.4 %collective-permute-start.16 = (f32[4,64,256]{2,1,0:T(8,128)S(1)}, f32[4,64,256]{2,1,0:T(8,128)S(1)}, u32[]{:S(2)}, u32[]{:S(2)}) collective-permute-start(f32[4,64,256]{2,1,0:T(8,128)S(1)} %get-tuple-element.114.refs_0_), channel_id=1, source_target_pairs={{0,1},{1,0},{2,3},{3,2},{4,5},{5,4},{6,7},{7,6},{8,9},{9,8},{10,11... | collective-permute-start | bytes 786440 | tf_op jit(solution)/shard_map/ppermute | solution.py:561
  50.2 3.5 %collective-permute-start.15 = (f32[4,64,192]{2,1,0:T(8,128)S(1)}, f32[4,64,192]{2,1,0:T(8,128)S(1)}, u32[]{:S(2)}, u32[]{:S(2)}) collective-permute-start(f32[4,64,192]{2,1,0:T(8,128)S(1)} %get-tuple-element.111), channel_id=1, source_target_pairs={{2,4},{6,8},{10,12},{14,16},{18,20},{22,24},{26,28},{30,0},{4,2},{... | collective-permute-start | bytes 589832 | tf_op jit(solution)/shard_map/ppermute | solution.py:567
  53.9 4.1 %polar.4 = (f32[4,64,128]{2,1,0:T(8,128)S(1)}, f32[4,8,128]{2,1,0:T(8,128)S(1)}, f32[4,64,128]{2,1,0:T(8,128)S(1)}) custom-call(f32[8,64,192]{2,1,0:T(8,128)S(1)} %get-tuple-element.113.after_ref.inside_ref, f32[64,64]{1,0:T(8,128)S(1)} %get-tuple-element.112.delta_ref, f32[4,64,128]{2,1,0:T(8,128)S(1)} %get-tuple-element.106.refs_0_.change_ref, ...), custom_call_target="tpu_custom_call" | custom-call | flops 3300000000 | bytes 1474560 | tf_op jit(solution)/shard_map/polar/pallas_call | solution.py:548
  59.4 2.1 %collective-permute-start.18 = (f32[32,128]{1,0:T(8,128)S(1)}, f32[32,128]{1,0:T(8,128)S(1)}, u32[]{:S(2)}, u32[]{:S(2)}) collective-permute-start(f32[32,128]{1,0:T(8,128)S(1)} %get-tuple-element.119.refs_0_.after_ref), channel_id=1, source_target_pairs={{0,4},{2,6},{4,0},{6,2},{8,12},{10,14},{12,8},{14,10},{16,20},{18,... | collective-permute-start | bytes 49160 | tf_op jit(solution)/shard_map/ppermute | solution.py:599
  61.4 1.9 %ahead.3 = (f32[8,64,192]{2,1,0:T(8,128)}, f32[8,64,192]{2,1,0:T(8,128)}, f32[8,64,192]{2,1,0:T(8,128)S(1)}, f32[4,64,256]{2,1,0:T(8,128)S(1)}) custom-call(s32[1]{0:T(128)} %bitcast.odd_ref.after_ref, f32[32,128]{1,0:T(8,128)S(1)} %get-tuple-element.119.refs_0_.after_ref, f32[8,64,192]{2,1,0:T(8,128)S(1)} %get-tuple-element.113.after_ref.inside_ref, ...), custom_call_target="tpu_custom_call" | custom-call | flops 330000000 | bytes 3624964 | tf_op jit(solution)/shard_map/ahead/pallas_call | solution.py:548
  64.1 3.6 %collective-permute-start.22 = (f32[32,128]{1,0:T(8,128)S(1)}, f32[32,128]{1,0:T(8,128)S(1)}, u32[]{:S(2)}, u32[]{:S(2)}) collective-permute-start(f32[32,128]{1,0:T(8,128)S(1)} %add.4.refs_0_), channel_id=1, source_target_pairs={{0,24},{2,26},{4,28},{6,30},{8,16},{10,18},{12,20},{14,22},{16,8},... | collective-permute-start | bytes 49160 | tf_op jit(solution)/shard_map/ppermute | solution.py:599
  68.5 1.3 %collective-permute-done.22.refs_3_ = f32[32,128]{1,0:T(8,128)S(1)} collective-permute-done((f32[32,128]{1,0:T(8,128)S(1)}, f32[32,128]{1,0:T(8,128)S(1)}, u32[]{:S(2)}, u32[]{:S(2)}) %collective-permute-start.22) | collective-permute-done | bytes 16416 | tf_op jit(solution)/shard_map/ppermute | solution.py:599
  69.8 2.5 %collective-permute-done.21.refs_2_ = f32[32,128]{1,0:T(8,128)S(1)} collective-permute-done((f32[32,128]{1,0:T(8,128)S(1)}, f32[32,128]{1,0:T(8,128)S(1)}, u32[]{:S(2)}, u32[]{:S(2)}) %collective-permute-start.21) | collective-permute-done | bytes 16416 | tf_op jit(solution)/shard_map/ppermute | solution.py:599
  73.1 4.4 %polar.5 = (f32[4,64,128]{2,1,0:T(8,128)S(1)}, f32[32,128]{1,0:T(8,128)S(1)}) custom-call(s32[1]{0:T(128)} %bitcast.odd_ref.after_ref, f32[64,64]{1,0:T(8,128)S(1)} %get-tuple-element.124.delta_ref, f32[4,64,128]{2,1,0:T(8,128)S(1)} %get-tuple-element.125.change_ref, f32[4,64,128]{2,1,0:T(8,128)S(1)} %get-tuple-element.117.gram_ref.old_ref, ...), custom_call_target="tpu_custom_call" | custom-call | flops 3300000000 | bytes 950276 | tf_op jit(solution)/shard_map/polar/pallas_call | solution.py:548
  78.3 1.2 %collective-permute-start.24 = (f32[32,128]{1,0:T(8,128)S(1)}, f32[32,128]{1,0:T(8,128)S(1)}, u32[]{:S(2)}, u32[]{:S(2)}) collective-permute-start(f32[32,128]{1,0:T(8,128)S(1)} %get-tuple-element.132.refs_0_), channel_id=1, source_target_pairs={{0,2},{2,0},{4,6},{6,4},{8,10},{10,8},{12,14},{14,12},{16,18},{18,... | collective-permute-start | bytes 49160 | tf_op jit(solution)/shard_map/ppermute | solution.py:599
  79.5 1.3 %collective-permute-done.26.refs_3_ = f32[32,128]{1,0:T(8,128)S(1)} collective-permute-done((f32[32,128]{1,0:T(8,128)S(1)}, f32[32,128]{1,0:T(8,128)S(1)}, u32[]{:S(2)}, u32[]{:S(2)}) %collective-permute-start.26) | collective-permute-done | bytes 16416 | tf_op jit(solution)/shard_map/ppermute | solution.py:599
  81.5 2.2 %collective-permute-start.29 = (f32[32,128]{1,0:T(8,128)S(1)}, f32[32,128]{1,0:T(8,128)S(1)}, u32[]{:S(2)}, u32[]{:S(2)}) collective-permute-start(f32[32,128]{1,0:T(8,128)S(1)} %add.5.refs_0_), channel_id=1, source_target_pairs={{0,24},{2,26},{4,28},{6,30},{8,16},{10,18},{12,20},{14,22},{16,8},... | collective-permute-start | bytes 49160 | tf_op jit(solution)/shard_map/ppermute | solution.py:599
  83.9 2.0 %collective-permute-start.27 = (f32[32,128]{1,0:T(8,128)S(1)}, f32[32,128]{1,0:T(8,128)S(1)}, u32[]{:S(2)}, u32[]{:S(2)}) collective-permute-start(f32[32,128]{1,0:T(8,128)S(1)} %add.5.refs_0_), channel_id=1, source_target_pairs={{0,8},{2,10},{4,12},{6,14},{8,0},{10,2},{12,4},{14,6},{16,24},{18,... | collective-permute-start | bytes 49160 | tf_op jit(solution)/shard_map/ppermute | solution.py:599
  87.2 1.2 %collective-permute-done.28.refs_2_ = f32[32,128]{1,0:T(8,128)S(1)} collective-permute-done((f32[32,128]{1,0:T(8,128)S(1)}, f32[32,128]{1,0:T(8,128)S(1)}, u32[]{:S(2)}, u32[]{:S(2)}) %collective-permute-start.28) | collective-permute-done | bytes 16416 | tf_op jit(solution)/shard_map/ppermute | solution.py:599
  88.4 2.0 %last.1 = (f32[8,64,192]{2,1,0:T(8,128)}, f32[64,64]{1,0:T(8,128)}) custom-call(f32[4,64,128]{2,1,0:T(8,128)S(1)} %get-tuple-element.127.after_ref.mixed_ref, f32[8,64,192]{2,1,0:T(8,128)S(1)} %get-tuple-element.131.tall_ref, f32[32,128]{1,0:T(8,128)S(1)} %add.5.refs_0_, f32[32,128]{1,0:T(8,128)S(1)} %collective-permute-done.27.refs_1_, ...), custom_call_target="tpu_custom_call" | custom-call | flops 330000000 | bytes 999424 | tf_op jit(solution)/shard_map/last/pallas_call | solution.py:548
  (73 shorter events, 15.4 us)
Async XLA Ops:
  2.2 9.7 %collective-permute-start.2 = (f32[64,64]{1,0:T(8,128)}, f32[64,64]{1,0:T(8,128)S(1)}, u32[]{:S(2)}, u32[]{:S(2)}) collective-permute-start(f32[64,64]{1,0:T(8,128)} %factor.1.after_ref.refs_0_), channel_id=1, source_target_pairs={{0,1},{1,0},{2,3},{3,2},{4,5},{5,4},{6,7},{7,6},{8,9},{9,8},{10,11... | collective-permute-start | bytes 49160 | tf_op jit(solution)/shard_map/ppermute | solution.py:561
  8.5 14.4 %copy-start.3 = (f32[2,192,128]{2,1,0:T(8,128)S(1)}, f32[2,192,128]{2,1,0:T(8,128)}, u32[]{:S(2)}) copy-start(f32[2,192,128]{2,1,0:T(8,128)} %get-tuple-element.69.refs_7_.refs_1_) | copy-start | bytes 589828
  8.5 14.3 %collective-permute-start.4 = (f32[2,192,128]{2,1,0:T(8,128)}, f32[2,192,128]{2,1,0:T(8,128)S(1)}, u32[]{:S(2)}, u32[]{:S(2)}) collective-permute-start(f32[2,192,128]{2,1,0:T(8,128)} %get-tuple-element.79), channel_id=1, source_target_pairs={{0,1},{1,0},{2,3},{3,2},{4,5},{5,4},{6,7},{7,6},{8,9},{9,8},{10,11... | collective-permute-start | bytes 589832 | tf_op jit(solution)/shard_map/ppermute | solution.py:561
  12.0 13.9 %copy-start.5 = (f32[2,192,128]{2,1,0:T(8,128)S(1)}, f32[2,192,128]{2,1,0:T(8,128)}, u32[]{:S(2)}) copy-start(f32[2,192,128]{2,1,0:T(8,128)} %get-tuple-element.77.refs_6_.refs_0_) | copy-start | bytes 589828
  12.0 10.9 %collective-permute-start.3 = (f32[2,192,128]{2,1,0:T(8,128)}, f32[2,192,128]{2,1,0:T(8,128)S(1)}, u32[]{:S(2)}, u32[]{:S(2)}) collective-permute-start(f32[2,192,128]{2,1,0:T(8,128)} %get-tuple-element.78), channel_id=1, source_target_pairs={{0,1},{1,0},{2,3},{3,2},{4,5},{5,4},{6,7},{7,6},{8,9},{9,8},{10,11... | collective-permute-start | bytes 589832 | tf_op jit(solution)/shard_map/ppermute | solution.py:561
  13.9 6.2 %collective-permute-start.1 = (f32[8,64]{1,0:T(8,128)S(1)}, f32[8,64]{1,0:T(8,128)S(1)}, u32[]{:S(2)}, u32[]{:S(2)}) collective-permute-start(f32[8,64]{1,0:T(8,128)S(1)} %copy-done.9), channel_id=1, source_target_pairs={{0,30},{2,0},{4,2},{6,4},{8,6},{10,8},{12,10},{14,12},{16,14},{18,... | collective-permute-start | bytes 6152 | tf_op jit(solution)/shard_map/ppermute | solution.py:561
  17.1 5.7 %collective-permute-start = (f32[8,64]{1,0:T(8,128)S(1)}, f32[8,64]{1,0:T(8,128)S(1)}, u32[]{:S(2)}, u32[]{:S(2)}) collective-permute-start(f32[8,64]{1,0:T(8,128)S(1)} %copy-done.9), channel_id=1, source_target_pairs={{0,2},{2,4},{4,6},{6,8},{8,10},{10,12},{12,14},{14,16},{16,18},{18... | collective-permute-start | bytes 6152 | tf_op jit(solution)/shard_map/ppermute | solution.py:561
  25.2 5.2 %collective-permute-start.7 = (f32[4,64,128]{2,1,0:T(8,128)}, f32[4,64,128]{2,1,0:T(8,128)S(1)}, u32[]{:S(2)}, u32[]{:S(2)}) collective-permute-start(f32[4,64,128]{2,1,0:T(8,128)} %get-tuple-element.87.refs_0_), channel_id=1, source_target_pairs={{0,1},{1,0},{2,3},{3,2},{4,5},{5,4},{6,7},{7,6},{8,9},{9,8},{10,11... | collective-permute-start | bytes 393224 | tf_op jit(solution)/shard_map/ppermute | solution.py:561
  27.5 7.3 %collective-permute-start.5 = (f32[4,64,192]{2,1,0:T(8,128)S(1)}, f32[4,64,192]{2,1,0:T(8,128)S(1)}, u32[]{:S(2)}, u32[]{:S(2)}) collective-permute-start(f32[4,64,192]{2,1,0:T(8,128)S(1)} %get-tuple-element.84), channel_id=1, source_target_pairs={{0,2},{4,6},{8,10},{12,14},{16,18},{20,22},{24,26},{28,30},{2,0},{... | collective-permute-start | bytes 589832 | tf_op jit(solution)/shard_map/ppermute | solution.py:567
  27.6 8.7 %collective-permute-start.6 = (f32[4,64,192]{2,1,0:T(8,128)S(1)}, f32[4,64,192]{2,1,0:T(8,128)S(1)}, u32[]{:S(2)}, u32[]{:S(2)}) collective-permute-start(f32[4,64,192]{2,1,0:T(8,128)S(1)} %get-tuple-element.85), channel_id=1, source_target_pairs={{2,4},{6,8},{10,12},{14,16},{18,20},{22,24},{26,28},{30,0},{4,2},{... | collective-permute-start | bytes 589832 | tf_op jit(solution)/shard_map/ppermute | solution.py:567
  36.8 3.3 %collective-permute-start.10 = (f32[32,128]{1,0:T(8,128)S(1)}, f32[32,128]{1,0:T(8,128)S(1)}, u32[]{:S(2)}, u32[]{:S(2)}) collective-permute-start(f32[32,128]{1,0:T(8,128)S(1)} %get-tuple-element.91.after_ref.refs_0_), channel_id=1, source_target_pairs={{0,6},{2,4},{4,2},{6,0},{8,14},{10,12},{12,10},{14,8},{16,22},{18,... | collective-permute-start | bytes 49160 | tf_op jit(solution)/shard_map/ppermute | solution.py:599
  36.8 3.9 %collective-permute-start.9 = (f32[32,128]{1,0:T(8,128)S(1)}, f32[32,128]{1,0:T(8,128)S(1)}, u32[]{:S(2)}, u32[]{:S(2)}) collective-permute-start(f32[32,128]{1,0:T(8,128)S(1)} %get-tuple-element.91.after_ref.refs_0_), channel_id=1, source_target_pairs={{0,4},{2,6},{4,0},{6,2},{8,12},{10,14},{12,8},{14,10},{16,20},{18,... | collective-permute-start | bytes 49160 | tf_op jit(solution)/shard_map/ppermute | solution.py:599
  38.9 1.9 %collective-permute-start.8 = (f32[32,128]{1,0:T(8,128)S(1)}, f32[32,128]{1,0:T(8,128)S(1)}, u32[]{:S(2)}, u32[]{:S(2)}) collective-permute-start(f32[32,128]{1,0:T(8,128)S(1)} %get-tuple-element.91.after_ref.refs_0_), channel_id=1, source_target_pairs={{0,2},{2,0},{4,6},{6,4},{8,10},{10,8},{12,14},{14,12},{16,18},{18,... | collective-permute-start | bytes 49160 | tf_op jit(solution)/shard_map/ppermute | solution.py:599
  40.8 5.6 %collective-permute-start.13 = (f32[32,128]{1,0:T(8,128)S(1)}, f32[32,128]{1,0:T(8,128)S(1)}, u32[]{:S(2)}, u32[]{:S(2)}) collective-permute-start(f32[32,128]{1,0:T(8,128)S(1)} %add.3.refs_0_), channel_id=1, source_target_pairs={{0,24},{2,26},{4,28},{6,30},{8,16},{10,18},{12,20},{14,22},{16,8},... | collective-permute-start | bytes 49160 | tf_op jit(solution)/shard_map/ppermute | solution.py:599
  42.6 4.6 %collective-permute-start.12 = (f32[32,128]{1,0:T(8,128)S(1)}, f32[32,128]{1,0:T(8,128)S(1)}, u32[]{:S(2)}, u32[]{:S(2)}) collective-permute-start(f32[32,128]{1,0:T(8,128)S(1)} %add.3.refs_0_), channel_id=1, source_target_pairs={{0,16},{2,18},{4,20},{6,22},{8,24},{10,26},{12,28},{14,30},{16,0},... | collective-permute-start | bytes 49160 | tf_op jit(solution)/shard_map/ppermute | solution.py:599
  42.6 4.6 %collective-permute-start.11 = (f32[32,128]{1,0:T(8,128)S(1)}, f32[32,128]{1,0:T(8,128)S(1)}, u32[]{:S(2)}, u32[]{:S(2)}) collective-permute-start(f32[32,128]{1,0:T(8,128)S(1)} %add.3.refs_0_), channel_id=1, source_target_pairs={{0,8},{2,10},{4,12},{6,14},{8,0},{10,2},{12,4},{14,6},{16,24},{18,... | collective-permute-start | bytes 49160 | tf_op jit(solution)/shard_map/ppermute | solution.py:599
  47.2 6.7 %collective-permute-start.16 = (f32[4,64,256]{2,1,0:T(8,128)S(1)}, f32[4,64,256]{2,1,0:T(8,128)S(1)}, u32[]{:S(2)}, u32[]{:S(2)}) collective-permute-start(f32[4,64,256]{2,1,0:T(8,128)S(1)} %get-tuple-element.114.refs_0_), channel_id=1, source_target_pairs={{0,1},{1,0},{2,3},{3,2},{4,5},{5,4},{6,7},{7,6},{8,9},{9,8},{10,11... | collective-permute-start | bytes 786440 | tf_op jit(solution)/shard_map/ppermute | solution.py:561
  50.1 8.0 %collective-permute-start.14 = (f32[4,64,192]{2,1,0:T(8,128)S(1)}, f32[4,64,192]{2,1,0:T(8,128)S(1)}, u32[]{:S(2)}, u32[]{:S(2)}) collective-permute-start(f32[4,64,192]{2,1,0:T(8,128)S(1)} %get-tuple-element.110), channel_id=1, source_target_pairs={{0,2},{4,6},{8,10},{12,14},{16,18},{20,22},{24,26},{28,30},{2,0},{... | collective-permute-start | bytes 589832 | tf_op jit(solution)/shard_map/ppermute | solution.py:567
  50.2 8.7 %collective-permute-start.15 = (f32[4,64,192]{2,1,0:T(8,128)S(1)}, f32[4,64,192]{2,1,0:T(8,128)S(1)}, u32[]{:S(2)}, u32[]{:S(2)}) collective-permute-start(f32[4,64,192]{2,1,0:T(8,128)S(1)} %get-tuple-element.111), channel_id=1, source_target_pairs={{2,4},{6,8},{10,12},{14,16},{18,20},{22,24},{26,28},{30,0},{4,2},{... | collective-permute-start | bytes 589832 | tf_op jit(solution)/shard_map/ppermute | solution.py:567
  59.4 4.0 %collective-permute-start.19 = (f32[32,128]{1,0:T(8,128)S(1)}, f32[32,128]{1,0:T(8,128)S(1)}, u32[]{:S(2)}, u32[]{:S(2)}) collective-permute-start(f32[32,128]{1,0:T(8,128)S(1)} %get-tuple-element.119.refs_0_.after_ref), channel_id=1, source_target_pairs={{0,6},{2,4},{4,2},{6,0},{8,14},{10,12},{12,10},{14,8},{16,22},{18,... | collective-permute-start | bytes 49160 | tf_op jit(solution)/shard_map/ppermute | solution.py:599
  59.4 4.0 %collective-permute-start.18 = (f32[32,128]{1,0:T(8,128)S(1)}, f32[32,128]{1,0:T(8,128)S(1)}, u32[]{:S(2)}, u32[]{:S(2)}) collective-permute-start(f32[32,128]{1,0:T(8,128)S(1)} %get-tuple-element.119.refs_0_.after_ref), channel_id=1, source_target_pairs={{0,4},{2,6},{4,0},{6,2},{8,12},{10,14},{12,8},{14,10},{16,20},{18,... | collective-permute-start | bytes 49160 | tf_op jit(solution)/shard_map/ppermute | solution.py:599
  61.4 1.9 %collective-permute-start.17 = (f32[32,128]{1,0:T(8,128)S(1)}, f32[32,128]{1,0:T(8,128)S(1)}, u32[]{:S(2)}, u32[]{:S(2)}) collective-permute-start(f32[32,128]{1,0:T(8,128)S(1)} %get-tuple-element.119.refs_0_.after_ref), channel_id=1, source_target_pairs={{0,2},{2,0},{4,6},{6,4},{8,10},{10,8},{12,14},{14,12},{16,18},{18,... | collective-permute-start | bytes 49160 | tf_op jit(solution)/shard_map/ppermute | solution.py:599
  63.4 9.7 %collective-permute-start.23 = (f32[4,64,256]{2,1,0:T(8,128)S(1)}, f32[4,64,256]{2,1,0:T(8,128)S(1)}, u32[]{:S(2)}, u32[]{:S(2)}) collective-permute-start(f32[4,64,256]{2,1,0:T(8,128)S(1)} %get-tuple-element.126.refs_0_), channel_id=1, source_target_pairs={{0,1},{1,0},{2,3},{3,2},{4,5},{5,4},{6,7},{7,6},{8,9},{9,8},{10,11... | collective-permute-start | bytes 786440 | tf_op jit(solution)/shard_map/ppermute | solution.py:561
  64.1 5.7 %collective-permute-start.22 = (f32[32,128]{1,0:T(8,128)S(1)}, f32[32,128]{1,0:T(8,128)S(1)}, u32[]{:S(2)}, u32[]{:S(2)}) collective-permute-start(f32[32,128]{1,0:T(8,128)S(1)} %add.4.refs_0_), channel_id=1, source_target_pairs={{0,24},{2,26},{4,28},{6,30},{8,16},{10,18},{12,20},{14,22},{16,8},... | collective-permute-start | bytes 49160 | tf_op jit(solution)/shard_map/ppermute | solution.py:599
  67.7 4.6 %collective-permute-start.21 = (f32[32,128]{1,0:T(8,128)S(1)}, f32[32,128]{1,0:T(8,128)S(1)}, u32[]{:S(2)}, u32[]{:S(2)}) collective-permute-start(f32[32,128]{1,0:T(8,128)S(1)} %add.4.refs_0_), channel_id=1, source_target_pairs={{0,16},{2,18},{4,20},{6,22},{8,24},{10,26},{12,28},{14,30},{16,0},... | collective-permute-start | bytes 49160 | tf_op jit(solution)/shard_map/ppermute | solution.py:599
  67.7 4.6 %collective-permute-start.20 = (f32[32,128]{1,0:T(8,128)S(1)}, f32[32,128]{1,0:T(8,128)S(1)}, u32[]{:S(2)}, u32[]{:S(2)}) collective-permute-start(f32[32,128]{1,0:T(8,128)S(1)} %add.4.refs_0_), channel_id=1, source_target_pairs={{0,8},{2,10},{4,12},{6,14},{8,0},{10,2},{12,4},{14,6},{16,24},{18,... | collective-permute-start | bytes 49160 | tf_op jit(solution)/shard_map/ppermute | solution.py:599
  77.6 3.2 %collective-permute-start.26 = (f32[32,128]{1,0:T(8,128)S(1)}, f32[32,128]{1,0:T(8,128)S(1)}, u32[]{:S(2)}, u32[]{:S(2)}) collective-permute-start(f32[32,128]{1,0:T(8,128)S(1)} %get-tuple-element.132.refs_0_), channel_id=1, source_target_pairs={{0,6},{2,4},{4,2},{6,0},{8,14},{10,12},{12,10},{14,8},{16,22},{18,... | collective-permute-start | bytes 49160 | tf_op jit(solution)/shard_map/ppermute | solution.py:599
  77.6 3.8 %collective-permute-start.25 = (f32[32,128]{1,0:T(8,128)S(1)}, f32[32,128]{1,0:T(8,128)S(1)}, u32[]{:S(2)}, u32[]{:S(2)}) collective-permute-start(f32[32,128]{1,0:T(8,128)S(1)} %get-tuple-element.132.refs_0_), channel_id=1, source_target_pairs={{0,4},{2,6},{4,0},{6,2},{8,12},{10,14},{12,8},{14,10},{16,20},{18,... | collective-permute-start | bytes 49160 | tf_op jit(solution)/shard_map/ppermute | solution.py:599
  78.3 3.2 %collective-permute-start.24 = (f32[32,128]{1,0:T(8,128)S(1)}, f32[32,128]{1,0:T(8,128)S(1)}, u32[]{:S(2)}, u32[]{:S(2)}) collective-permute-start(f32[32,128]{1,0:T(8,128)S(1)} %get-tuple-element.132.refs_0_), channel_id=1, source_target_pairs={{0,2},{2,0},{4,6},{6,4},{8,10},{10,8},{12,14},{14,12},{16,18},{18,... | collective-permute-start | bytes 49160 | tf_op jit(solution)/shard_map/ppermute | solution.py:599
  81.5 5.7 %collective-permute-start.29 = (f32[32,128]{1,0:T(8,128)S(1)}, f32[32,128]{1,0:T(8,128)S(1)}, u32[]{:S(2)}, u32[]{:S(2)}) collective-permute-start(f32[32,128]{1,0:T(8,128)S(1)} %add.5.refs_0_), channel_id=1, source_target_pairs={{0,24},{2,26},{4,28},{6,30},{8,16},{10,18},{12,20},{14,22},{16,8},... | collective-permute-start | bytes 49160 | tf_op jit(solution)/shard_map/ppermute | solution.py:599
  83.7 4.7 %collective-permute-start.28 = (f32[32,128]{1,0:T(8,128)S(1)}, f32[32,128]{1,0:T(8,128)S(1)}, u32[]{:S(2)}, u32[]{:S(2)}) collective-permute-start(f32[32,128]{1,0:T(8,128)S(1)} %add.5.refs_0_), channel_id=1, source_target_pairs={{0,16},{2,18},{4,20},{6,22},{8,24},{10,26},{12,28},{14,30},{16,0},... | collective-permute-start | bytes 49160 | tf_op jit(solution)/shard_map/ppermute | solution.py:599
  83.9 4.5 %collective-permute-start.27 = (f32[32,128]{1,0:T(8,128)S(1)}, f32[32,128]{1,0:T(8,128)S(1)}, u32[]{:S(2)}, u32[]{:S(2)}) collective-permute-start(f32[32,128]{1,0:T(8,128)S(1)} %add.5.refs_0_), channel_id=1, source_target_pairs={{0,8},{2,10},{4,12},{6,14},{8,0},{10,2},{12,4},{14,6},{16,24},{18,... | collective-permute-start | bytes 49160 | tf_op jit(solution)/shard_map/ppermute | solution.py:599
  (10 other events, 58.6 us)

commit v4 on v3

--- a/solution.py
+++ b/solution.py
@@ -79,6 +79,12 @@
     return total
 
 
+def from_left(left, values):
+    wide = values[0].shape[1]
+    total = dot(left_triple(left), right_triple(jnp.concatenate(values, axis=1)))
+    return [total[:, at * wide : (at + 1) * wide] for at in range(len(values))]
+
+
 def group_size(count, rank):
     group = max(1, 128 // rank)
     while count % group:
@@ -86,57 +92,46 @@
     return group
 
 
-def factor_kernel(factor_ref, gram_ref):
+def factor_kernel(factor_ref, gram_ref, again_ref):
     factor = factor_ref[...]
     gram_ref[...] = dot(factor, factor, NT)
-
-
-def project_kernel(order_ref, me_ref, first_ref, second_ref, factor_ref, after_ref, *outs):
+    again_ref[...] = factor
+
+
+def project_kernel(me_ref, data_ref, factor_ref, *refs):
+    *outs, held, arrived = refs
     parts = len(outs)
-    rows = outs[0].shape[1]
+    pairs, rows, _ = outs[0].shape
+    count, all_rows, _ = data_ref.shape
+    half = all_rows // 2
+    copies = []
+    for k in range(count):
+        for at in range(2):
+            place = pl.ds(at * half, half)
+            copies.append(
+                pltpu.make_async_copy(
+                    data_ref.at[k, place, :], held.at[k, place, :], arrived.at[2 * k + at]
+                )
+            )
+            copies[-1].start()
     factor = factor_ref[...]
     empty = jnp.zeros_like(factor)
     sides = [
         jnp.concatenate([factor, empty], axis=0),
         jnp.concatenate([empty, factor], axis=0),
     ]
-    for part in reversed(range(parts)):
-        start = pl.multiple_of(lax.rem(me_ref[0] + part, parts) * rows, 16)
-        place = pl.ds(start, rows)
-        outs[part][0] = dot(first_ref[0, place, :], sides[0], NT) + dot(
-            second_ref[0, place, :], sides[1], NT
-        )
-
-
-def project(first, pairs, parts, rows, order, me, data, factor, after):
-    count, all_rows, channels = data.shape
-    rank = factor.shape[0]
-    spec = lambda odd: pl.BlockSpec(
-        (1, all_rows, channels),
-        lambda i, order, me: (lax.rem(order[2 * (first + i) + odd], count), 0, 0),
-    )
-    return pl.pallas_call(
-        project_kernel,
-        out_shape=[jax.ShapeDtypeStruct((pairs, rows, 2 * rank), f32)] * parts,
-        grid_spec=pltpu.PrefetchScalarGridSpec(
-            num_scalar_prefetch=2,
-            grid=(pairs,),
-            in_specs=[
-                spec(0),
-                spec(1),
-                pl.BlockSpec((rank, channels), lambda i, order, me: (0, 0)),
-                pl.BlockSpec(memory_space=pl.ANY),
-            ],
-            out_specs=[pl.BlockSpec((1, rows, 2 * rank), lambda i, order, me: (i, 0, 0))] * parts,
-        ),
-        cost_estimate=pl.CostEstimate(
-            flops=2 * per_microsecond, bytes_accessed=data.size, transcendentals=0
-        ),
-        name="project",
-    )(order, me, data, data, factor, after)
-
-
-def setup_kernel(grams, group, *refs):
+    for pair in range(pairs):
+        for copy in copies[4 * pair : 4 * pair + 4]:
+            copy.wait()
+        for part in reversed(range(parts)):
+            start = pl.multiple_of(lax.rem(me_ref[0] + part, parts) * rows, 16)
+            place = pl.ds(start, rows)
+            outs[part][pair] = dot(held[2 * pair, place, :], sides[0], NT) + dot(
+                held[2 * pair + 1, place, :], sides[1], NT
+            )
+
+
+def setup_kernel(grams, group, order_ref, *refs):
     gram_refs, refs = refs[:grams], refs[grams:]
     (own_ref, aux_ref, coupled_ref, dual_s_ref, dual_c_ref) = refs[:5]
     (inverse_ref, mover_ref, rho_ref, diagonal_ref, columns_ref, base_ref) = refs[5:]
@@ -185,26 +180,22 @@
             blocks = block_diagonal(wide - product, mask, group)
             (more,) = times_blocks([inverses[at]], blocks)
             inverses[at] = inverses[at] + more
-    pair_mask = block_mask(rank, 2)
-    for k in range(0, count, 2):
-        both = []
-        for j in (k, k + 1):
-            place = (j % group) * rank
-            unit = 1.0 / (34.0 * rho[j : j + 1, :])
-            both.append(inverses[j // group][:, place : place + rank] * unit)
-            inverse = left_triple(both[-1])
-            inverse_ref[j] = inverse
-            base_ref[j] = dot(
-                inverse,
-                right_triple(
-                    rho[j : j + 1, :] * (aux_ref[j] - dual_s_ref[j] + coupled_ref[j] - dual_c_ref[j])
-                ),
-            )
-        line = jnp.concatenate([weights[k : k + 1, :], weights[k + 1 : k + 2, :]], axis=1)
-        high, low = split(jnp.concatenate(both, axis=1) * line)
-        high = jnp.concatenate([high, high], axis=0) * pair_mask
-        low = jnp.concatenate([low, low], axis=0) * pair_mask
-        mover_ref[k // 2] = jnp.concatenate([high, high, low], axis=1)
+    for k in range(count):
+        place = (k % group) * rank
+        unit = 1.0 / (34.0 * rho[k : k + 1, :])
+        inverse = inverses[k // group][:, place : place + rank] * unit
+        inverse_ref[k] = left_triple(inverse)
+        base_ref[k] = dot(
+            inverse_ref[k],
+            right_triple(
+                rho[k : k + 1, :] * (aux_ref[k] - dual_s_ref[k] + coupled_ref[k] - dual_c_ref[k])
+            ),
+        )
+        both = jnp.concatenate([inverse * weights[k : k + 1, :]] * 2, axis=1)
+        side = lax.div(lax.broadcasted_iota(jnp.int32, both.shape, 1), rank)
+        both = jnp.where(side == lax.rem(order_ref[k], 2), both, 0.0)
+        high, low = split(both)
+        mover_ref[k] = jnp.concatenate([high, high, low], axis=1)
 
 
 def cross_blocks(lefts, rights, rank):
@@ -219,31 +210,33 @@
     return diagonal_blocks(total, rank, group)
 
 
-def summed(refs, chunks, pair):
-    chunk, at = divmod(pair, refs[0].shape[0])
-    total = None
-    for ref in refs[chunk::chunks]:
-        total = ref[at] if total is None else total + ref[at]
+def summed(refs, at):
+    total = refs[0][at]
+    for ref in refs[1:]:
+        total = total + ref[at]
     return total
 
 
-def first_kernel(chunks, group, *refs):
+def stored_pair(order_ref, refs, k, count):
+    return summed(refs, lax.div(lax.rem(order_ref[k], count), 2))
+
+
+def first_kernel(group, order_ref, *refs):
     base_ref, mover_ref, dual_s_ref, dual_c_ref = refs[2:6]
     *projected_refs, tall_ref, target_ref, gram_ref = refs[6:]
     count, rank, rows = base_ref.shape
     talls = []
-    for k in range(0, count, 2):
-        high, low = split(summed(projected_refs, chunks, k // 2))
-        both = dot(mover_ref[k // 2], jnp.concatenate([high, low, high], axis=1), NT)
-        for j in (k, k + 1):
-            evolving = base_ref[j] + both[(j - k) * rank : (j - k + 1) * rank]
-            target_ref[j] = evolving + dual_s_ref[j]
-            tall = evolving + dual_c_ref[j]
-            tall_ref[j] = tall
-            talls.append(tall)
-    for first in range(0, count, group):
-        some = talls[first : first + group]
-        gram_ref[first // group] = cross_blocks(some, some, rank)
+    for k in range(count):
+        high, low = split(stored_pair(order_ref, projected_refs, k, count))
+        moved = dot(mover_ref[k], jnp.concatenate([high, low, high], axis=1), NT)
+        evolving = base_ref[k] + moved
+        target_ref[k] = evolving + dual_s_ref[k]
+        tall = evolving + dual_c_ref[k]
+        tall_ref[k] = tall
+        talls.append(tall)
+        if len(talls) == group:
+            gram_ref[k // group] = cross_blocks(talls, talls, rank)
+            talls = []
 
 
 def smooth(odd, now, targets, rho, inside_ref, near_ref, far_ref):
@@ -277,7 +270,7 @@
 
 
 def smooth_kernel(
-    chunks, odd_ref, aux_ref, target_ref, before_ref, rho_ref, after_ref, diagonal_ref,
+    odd_ref, order_ref, aux_ref, target_ref, before_ref, rho_ref, after_ref, diagonal_ref,
     columns_ref, *refs
 ):
     *projected_refs, side_ref, past_ref, next_ref, inside_ref, near_ref, far_ref = refs
@@ -292,10 +285,10 @@
         odd_ref[0], [aux_ref[k] for k in slices], [target_ref[k] for k in slices], rho,
         inside_ref, near_ref, far_ref,
     )
-    for k in range(0, count, 2):
-        both = summed(projected_refs, chunks, k // 2).T
-        side_ref[k] = columns_ref[:, k : k + 1] * both[:rank]
-        side_ref[k + 1] = columns_ref[:, k + 1 : k + 2] * both[rank:]
+    for k in slices:
+        both = stored_pair(order_ref, projected_refs, k, count).T
+        own = jnp.where(lax.rem(order_ref[k], 2) == 1, both[rank:], both[:rank])
+        side_ref[k] = columns_ref[:, k : k + 1] * own
 
 
 def polar(grams, delta):
@@ -303,11 +296,9 @@
     group = wide // rank
     mask = block_mask(rank, group)
     eye = wide_eye(rank, group)
-    delta_left = left_triple(delta)
     delta_blocks = block_diagonal(jnp.concatenate([delta] * group, axis=1), mask, group, NT)
     currents, roots, scales = [], [], []
-    for gram in grams:
-        left = dot(delta_left, right_triple(gram))
+    for left in from_left(delta, grams):
         (normal,) = times_blocks([left], delta_blocks, NT)
         line = jnp.broadcast_to(jnp.sum(normal * eye, axis=0, keepdims=True), (16, wide))
         high, low = split(line)
@@ -356,58 +347,33 @@
 
 
 def first_polar_kernel(after_ref, delta_ref, *refs):
-    *gram_refs, root_ref, scale_ref, gram_ref = refs
-    grams = []
-    for at in range(gram_ref.shape[0]):
-        gram = gram_refs[0][at]
-        for ref in gram_refs[1:]:
-            gram = gram + ref[at]
-        gram_ref[at] = gram
-        grams.append(gram)
-    roots, scales = polar(grams, delta_ref[...])
+    *gram_refs, mixed_ref, partial_ref, gram_ref = refs
+    grams = [summed(gram_refs, at) for at in range(gram_ref.shape[0])]
     for at in range(len(grams)):
-        root_ref[at] = roots[at]
-        scale_ref[at] = jnp.broadcast_to(scales[at], scale_ref.shape[1:])
-
-
-def later_polar_kernel(last, after_ref, delta_ref, change_ref, old_ref, *refs):
-    if last:
-        *cross_refs, mixed_ref, partial_ref = refs
-    else:
-        *cross_refs, root_ref, scale_ref, gram_ref = refs
+        gram_ref[at] = grams[at]
+    delta = delta_ref[...]
+    roots, scales = polar(grams, delta)
+    mix(roots, scales, grams, delta, mixed_ref, partial_ref)
+
+
+def later_polar_kernel(after_ref, delta_ref, change_ref, old_ref, *refs):
+    *cross_refs, mixed_ref, partial_ref, gram_ref = refs
     groups, rank, wide = old_ref.shape
     group = wide // rank
     mask = block_mask(rank, group)
     grams = []
     for at in range(groups):
-        cross = cross_refs[0][at]
-        for ref in cross_refs[1:]:
-            cross = cross + ref[at]
+        cross = summed(cross_refs, at)
         change = change_ref[at]
         (onward,) = times_blocks([change], block_diagonal(old_ref[at], mask, group))
         onward = cross[:, :wide] + 0.5 * onward
         (one,) = times_blocks([onward], block_diagonal(change, mask, group, NT), NT)
         (other,) = times_blocks([change], block_diagonal(onward, mask, group, NT), NT)
         grams.append(cross[:, wide:] + one + other)
+        gram_ref[at] = grams[at]
     delta = delta_ref[...]
     roots, scales = polar(grams, delta)
-    if last:
-        mix(roots, scales, grams, delta, mixed_ref, partial_ref)
-    else:
-        for at in range(groups):
-            gram_ref[at] = grams[at]
-            root_ref[at] = roots[at]
-            scale_ref[at] = jnp.broadcast_to(scales[at], scale_ref.shape[1:])
-
-
-def mix_kernel(near_ref, far_ref, delta_ref, root_ref, scale_ref, gram_ref, mixed_ref, partial_ref):
-    groups = range(root_ref.shape[0])
-    mix(
-        [root_ref[at] for at in groups],
-        [scale_ref[at, 0:1] for at in groups],
-        [gram_ref[at] for at in groups],
-        delta_ref[...], mixed_ref, partial_ref,
-    )
+    mix(roots, scales, grams, delta, mixed_ref, partial_ref)
 
 
 def ahead_kernel(
@@ -441,8 +407,8 @@
             knowns, talls = [], []
 
 
-def add_kernel(*refs):
-    *term_refs, total_ref = refs
+def add_kernel(unread, *refs):
+    *term_refs, total_ref = refs[unread:]
     total = term_refs[0][...]
     for ref in term_refs[1:]:
         total = total + ref[...]
@@ -463,10 +429,10 @@
     group = wide // rank
     delta = new_delta(sum_refs, total, rank)
     delta_ref[...] = delta
-    delta_left = left_triple(delta.T)
+    mixers = from_left(delta.T, [mixed_ref[at] for at in range(groups)])
     place = lax.div(lax.broadcasted_iota(jnp.int32, (1, wide), 1), rank)
     for at in range(groups):
-        mixer = dot(delta_left, right_triple(mixed_ref[at]))
+        mixer = mixers[at]
         slices = range(at * group, (at + 1) * group)
         inverses = jnp.concatenate([inverse_ref[k] for k in slices], axis=0)
         onward = diagonal_blocks(dot(inverses, right_triple(mixer)), rank, group)
@@ -493,12 +459,16 @@
     )
 
 
-def last_rows_kernel(
-    after_ref, change_ref, forward_ref, tall_ref, known_ref, next_ref, evolving_ref
-):
+def last_rows_kernel(mixed_ref, change_ref, forward_ref, tall_ref, known_ref, *outs):
+    mixed_tall_ref, evolving_ref, next_ref = outs
     evolvings = new_rows(change_ref, forward_ref, tall_ref, known_ref, next_ref)
+    groups, rank, wide = mixed_ref.shape
+    group = wide // rank
     for k in range(len(evolvings)):
         evolving_ref[k] = evolvings[k]
+        place = (k % group) * rank
+        mixed = left_triple(mixed_ref[k // group][:, place : place + rank])
+        mixed_tall_ref[k] = right_triple(dot(mixed, right_triple(next_ref[k])))
 
 
 def new_rows(change_ref, forward_ref, tall_ref, known_ref, next_ref):
@@ -516,27 +486,20 @@
     return evolvings
 
 
-def last_kernel(total, mixed_ref, tall_ref, *refs):
+def last_kernel(total, mixed_tall_ref, *refs):
     *sum_refs, coupled_ref, delta_ref = refs
-    groups, rank, wide = mixed_ref.shape
-    group = wide // rank
-    delta = new_delta(sum_refs, total, rank)
+    delta = new_delta(sum_refs, total, delta_ref.shape[0])
     delta_ref[...] = delta
     delta_left = left_triple(delta.T)
-    for at in range(groups):
-        mixer = dot(delta_left, right_triple(mixed_ref[at]))
-        for k in range(at * group, (at + 1) * group):
-            place = (k - at * group) * rank
-            coupled_ref[k] = dot(
-                left_triple(mixer[:, place : place + rank]), right_triple(tall_ref[k])
-            )
+    for k in range(coupled_ref.shape[0]):
+        coupled_ref[k] = dot(delta_left, mixed_tall_ref[k])
 
 
 per_microsecond = 1_100_000_000
 
 
 def call(
-    kernel, name, outs, *args, scalars=0, unread=0, microseconds=0.3
+    kernel, name, outs, *args, scalars=0, unread=0, microseconds=0.3, limit=16, scratch=()
 ):
     flops = int(microseconds * per_microsecond)
     specs = [pl.BlockSpec(memory_space=pltpu.SMEM)] * scalars
@@ -550,7 +513,8 @@
         out_shape=shapes,
         in_specs=specs,
         out_specs=[pl.BlockSpec(memory_space=pltpu.VMEM)] * len(shapes),
-        compiler_params=pltpu.CompilerParams(vmem_limit_bytes=16 * 1024 * 1024),
+        scratch_shapes=list(scratch),
+        compiler_params=pltpu.CompilerParams(vmem_limit_bytes=limit * 1024 * 1024),
         cost_estimate=pl.CostEstimate(flops=flops, bytes_accessed=moved, transcendentals=0),
         name=name,
     )(*args)
@@ -582,13 +546,18 @@
 def in_stages(value, axis, beside=None):
     count = lax.axis_size(axis)
     stride = 1
-    terms = [value]
+    terms, firsts = [value], []
     for size in stage_sizes(count):
         value = terms[0]
         if len(terms) > 1:
-            (value,) = call(add_kernel, "add", [(value.shape, f32)], *terms, microseconds=0.1)
-        if stride > 1 and beside is not None:
-            value, beside = lax.optimization_barrier((value, beside))
+            unread = [] if beside is None else [beside]
+            (value,) = call(
+                functools.partial(add_kernel, len(unread)),
+                "add",
+                [(value.shape, f32)],
+                *unread, *terms,
+                unread=len(unread),
+            )
         terms = [value]
         for shift in range(1, size):
             moves = []
@@ -598,7 +567,8 @@
                 moves.append((i, i + (other - digit) * stride))
             terms.append(lax.ppermute(value, axis, moves))
         stride *= size
-    return terms if beside is None else (terms, beside)
+        firsts = firsts or terms
+    return terms, firsts
 
 
 def body(
@@ -624,22 +594,26 @@
 
     me = lax.axis_index("chan").astype(jnp.int32).reshape(1)
     odd = lax.rem(lax.axis_index("cuts"), 2).astype(jnp.int32).reshape(1)
-    chunks = 2 if count % 4 == 0 else 1
-    pairs = count // 2 // chunks
-    (gram_part,) = call(factor_kernel, "factor", [square], factor)
+    gram_part, factor = call(
+        factor_kernel, "factor", [square, (factor.shape, factor.dtype)], factor
+    )
     grams = [gram_part] + from_others(gram_part, "chan")
-    own, arrived = [], []
-    for chunk in range(chunks):
-        projected = project(
-            chunk * pairs, pairs, parts, rows, order, me, data, factor, gram_part
-        )
-        if chunk == 0:
-            projected, grams = lax.optimization_barrier((projected, grams))
-        own.append(projected[0])
-        arrived.append([rotated(projected[shift], "chan", shift) for shift in range(1, parts)])
-    received = [arrived[chunk][at] for at in range(parts - 1) for chunk in range(chunks)]
-
-    late_weights, _ = lax.optimization_barrier((slice_weights, own[-1]))
+    projected = call(
+        project_kernel,
+        "project",
+        [((count // 2, rows, 2 * rank), f32)] * parts,
+        me, data, factor,
+        scalars=1, unread=1, microseconds=2, limit=52,
+        scratch=[
+            pltpu.VMEM((count, all_rows, channels), data.dtype),
+            pltpu.SemaphoreType.DMA((2 * count,)),
+        ],
+    )
+    projected, grams = lax.optimization_barrier((projected, grams))
+    own = projected[0]
+    received = [rotated(projected[shift], "chan", shift) for shift in range(1, parts)]
+
+    late_weights, _ = lax.optimization_barrier((slice_weights, own))
     before = rotated(late_weights, "cuts", 1)
     after = rotated(late_weights, "cuts", -1)
     inverse, mover, rho, diagonal, columns, base = call(
@@ -647,33 +621,33 @@
         "setup",
         [
             ((count, rank, 3 * rank), bf16),
-            ((count // 2, 2 * rank, 6 * rank), bf16),
+            ((count, rank, 6 * rank), bf16),
             lanes(count),
             ((count, rank), f32),
             ((rank, count), f32),
             state,
         ],
-        *grams, slice_weights, aux, coup, dual_s, dual_c,
+        order, *grams, slice_weights, aux, coup, dual_s, dual_c,
+        scalars=1,
     )
     tall, target, gram = call(
-        functools.partial(first_kernel, chunks, group),
+        functools.partial(first_kernel, group),
         "first",
         [state, state, quads],
-        before, after, base, mover, dual_s, dual_c, *own, *received,
-        unread=2,
+        order, before, after, base, mover, dual_s, dual_c, own, *received,
+        scalars=1, unread=2,
     )
     side, before, after, inside, to_near, to_far = call(
-        functools.partial(smooth_kernel, chunks),
+        smooth_kernel,
         "smooth",
         [state, lanes(count), lanes(count), state, halo, halo],
-        odd, aux, target, before, rho, after, diagonal, columns, *own, *received,
-        scalars=1,
-    )
+        odd, order, aux, target, before, rho, after, diagonal, columns, own, *received,
+        scalars=2,
+    )
+    polar_outs = [quads, ((rank // 2, 2 * rank), f32), quads]
     for inner in range(INNER):
-        last = inner == INNER - 1
-        polar_outs = [quads, scale, quads]
         if inner == 0:
-            root, scales, gram = call(
+            mixed, partial, gram = call(
                 first_polar_kernel,
                 "polar",
                 polar_outs,
@@ -681,41 +655,29 @@
                 unread=1, microseconds=3,
             )
         else:
-            outs = call(
-                functools.partial(later_polar_kernel, last),
+            mixed, partial, gram = call(
+                later_polar_kernel,
                 "polar",
-                [quads, ((rank // 2, 2 * rank), f32)] if last else polar_outs,
-                odd if last else inside, delta, change, gram, cross, *crosses,
-                unread=1, microseconds=3,
-            )
-            if last:
-                mixed, partial = outs
-            else:
-                root, scales, gram = outs
-        if last:
-            tall, evolving = call(
+                polar_outs,
+                inside, delta, change, gram, cross, *crosses,
+                unread=1,
+            )
+        if inner == INNER - 1:
+            mixed_tall, evolving, _ = call(
                 last_rows_kernel,
                 "rows",
-                [state, state],
+                [((count, 3 * rank, rows), bf16), state, state],
                 mixed, change, forward, tall, known,
-                unread=1,
             )
             coup, delta = call(
                 functools.partial(last_kernel, total),
                 "last",
                 [state, square],
-                mixed, tall, *in_stages(partial, "cuts"),
+                mixed_tall, *in_stages(partial, "cuts")[0],
             )
             continue
         near = swapped(to_near, "cuts", 0)
         far = swapped(to_far, "cuts", 1)
-        mixed, partial = call(
-            mix_kernel,
-            "mix",
-            [quads, ((rank // 2, 2 * rank), f32)],
-            near, far, delta, root, scales, gram,
-            unread=2,
-        )
         aux, dual, known, cross = call(
             functools.partial(ahead_kernel, group),
             "ahead",
@@ -723,9 +685,11 @@
             odd, partial, inside, near, far, target, tall, side, rho, inverse,
             scalars=1, unread=1,
         )
-        sums, cross = in_stages(partial, "cuts", beside=cross)
+        sums, firsts = in_stages(partial, "cuts", beside=cross)
         if inner < INNER - 2:
             sums, cross = lax.optimization_barrier((sums, cross))
+        else:
+            _, cross = lax.optimization_barrier((firsts, cross))
         crosses = from_others(cross, "chan")
         delta, change, forward = call(
             functools.partial(mixer_kernel, total),

time: 90.7 us -> 82.5 us (0.910)
  Pallas kernels: 35 us -> 30 us
  local copies, waits for them, and re-layouts: 2.8 us -> 0.87 us
  waiting for transfers between devices: 16.2 us -> 14.5 us
    pallas_call x2 -> x0, Pallas kernels: 6.64 us -> none  [project(): pl.pallas_call(project_kernel, out_shape=[jax.ShapeDtypeStruct((pairs, ro...]
    ppermute x8 -> x7, waiting for transfers between devices: 4.22 us -> 6.44 us  [rotated(): lax.ppermute(value, axis, [(i, (i + shift) % count) for i in range(count)])]
    ppermute x4, waiting for transfers between devices: 2.19 us -> 0.01 us  [swapped(): return lax.ppermute(value, axis, pairs + [(b, a) for a, b in pairs])]
    unnamed x24 -> x16, local copies, waits for them, and re-layouts: 2.8 us -> 0.87 us
    ppermute x4, starting transfers between devices: 5.18 us -> 6.99 us  [swapped(): return lax.ppermute(value, axis, pairs + [(b, a) for a, b in pairs])]
    ppermute x18, waiting for transfers between devices: 9.79 us -> 8.03 us  [in_stages(): terms.append(lax.ppermute(value, axis, moves))]
    pallas_call x19 -> x18, Pallas kernels: 28.4 us -> 30 us  [call(): pl.pallas_call(kernel, out_shape=shapes, in_specs=specs, out_specs=[pl.Bl...]
    ppermute x8 -> x7, starting transfers between devices: 10.9 us -> 10.1 us  [rotated(): lax.ppermute(value, axis, [(i, (i + shift) % count) for i in range(count)])]
  transfers between devices with their start and end apart: 30 -> 29, of which waited for: 14 -> 14; matrix products, arithmetic and copies ran while one was open for 0% -> 0% of each run, Pallas kernels for 28% -> 26%
where the time goes in v4:
time: 82.5 us; the launch traced here: 82.3 us
  starting transfers between devices  36.1 us (44%)
  Pallas kernels  30 us (36%)
  waiting for transfers between devices  14.5 us (18%)
  local copies, waits for them, and re-layouts  0.87 us (1%)
  between operations  0.86 us (1%)
    pallas_call x18, Pallas kernels, call(): pl.pallas_call(kernel, out_shape=shapes, in_specs=specs, out_specs=[pl.Bl...  30 us
    ppermute x18, starting transfers between devices, in_stages(): terms.append(lax.ppermute(value, axis, moves))  19 us
    ppermute x7, starting transfers between devices, rotated(): lax.ppermute(value, axis, [(i, (i + shift) % count) for i in range(count)])  10.1 us
    ppermute x18, waiting for transfers between devices, in_stages(): terms.append(lax.ppermute(value, axis, moves))  8.03 us
    ppermute x4, starting transfers between devices, swapped(): return lax.ppermute(value, axis, pairs + [(b, a) for a, b in pairs])  6.99 us
    ppermute x7, waiting for transfers between devices, rotated(): lax.ppermute(value, axis, [(i, (i + shift) % count) for i in range(count)])  6.44 us
  transfers between devices with their start and end apart: 29, of which 14 were waited for; matrix products, arithmetic and copies ran while one was open for 0% of the time, Pallas kernels for 26%

profile of v4, /device:TPU:0, one launch (start us, length us, event | category | flops | bytes accessed | tf_op | source)
XLA Modules:
  0.0 82.3 jit_solution(11535472507006141742)
XLA Ops:
  1.6 3.0 %collective-permute-start = (f32[64,64]{1,0:T(8,128)S(1)}, f32[64,64]{1,0:T(8,128)S(1)}, u32[]{:S(2)}, u32[]{:S(2)}) collective-permute-start(f32[64,64]{1,0:T(8,128)S(1)} %get-tuple-element.68.refs_0_), channel_id=1, source_target_pairs={{0,1},{1,0},{2,3},{3,2},{4,5},{5,4},{6,7},{7,6},{8,9},{9,8},{10,11... | collective-permute-start | bytes 49160 | tf_op jit(solution)/shard_map/ppermute | solution.py:525
  4.7 3.0 %project.1 = (f32[4,192,128]{2,1,0:T(8,128)S(1)}, f32[4,192,128]{2,1,0:T(8,128)S(1)}) custom-call(s32[1]{0:T(128)} %bitcast.2.me_ref, bf16[8,384,512]{2,1,0:T(8,128)(2,1)} %data_ref.1, bf16[64,512]{1,0:T(8,128)(2,1)S(1)} %get-tuple-element.62.factor_ref), custom_call_target="tpu_custom_call" | custom-call | flops 2200000000 | bytes 3997700 | tf_op jit(solution)/shard_map/project/pallas_call | solution.py:511
  8.5 3.2 %collective-permute-start.2 = (f32[8,64]{1,0:T(8,128)S(1)}, f32[8,64]{1,0:T(8,128)S(1)}, u32[]{:S(2)}, u32[]{:S(2)}) collective-permute-start(f32[8,64]{1,0:T(8,128)S(1)} %copy-done.5), channel_id=1, source_target_pairs={{0,30},{2,0},{4,2},{6,4},{8,6},{10,8},{12,10},{14,12},{16,14},{18,... | collective-permute-start | bytes 6152 | tf_op jit(solution)/shard_map/ppermute | solution.py:525
  11.7 2.8 %setup.1 = (bf16[8,64,192]{2,1,0:T(8,128)(2,1)S(1)}, bf16[8,64,384]{2,1,0:T(8,128)(2,1)S(1)}, f32[8,128]{1,0:T(8,128)S(1)}, f32[8,64]{1,0:T(8,128)S(1)}, f32[64,8]{1,0:T(8,128)S(1)}, /*index=5*/f32[8,64,192]{2,1,0:T(8,128)S(1)}) custom-call(s32[8]{0:T(128)S(1)} %copy-done.4, f32[64,64]{1,0:T(8,128)S(1)} %get-tuple-element.68.refs_0_, ...), custom_call_target="tpu_custom_call" | custom-call | flops 330000000 | bytes 2598944 | tf_op jit(solution)/shard_map/setup/pallas_call | solution.py:511
  14.6 2.8 %collective-permute-done.1.refs_0_.before_ref = f32[8,64]{1,0:T(8,128)S(1)} collective-permute-done((f32[8,64]{1,0:T(8,128)S(1)}, f32[8,64]{1,0:T(8,128)S(1)}, u32[]{:S(2)}, u32[]{:S(2)}) %collective-permute-start.1) | collective-permute-done | bytes 2080 | tf_op jit(solution)/shard_map/ppermute | solution.py:525
  18.3 1.9 %first.1 = (f32[8,64,192]{2,1,0:T(8,128)S(1)}, f32[8,64,192]{2,1,0:T(8,128)S(1)}, f32[4,64,128]{2,1,0:T(8,128)S(1)}) custom-call(s32[8]{0:T(128)S(1)} %copy-done.4, f32[8,64]{1,0:T(8,128)S(1)} %collective-permute-done.1.refs_0_.before_ref, f32[8,64]{1,0:T(8,128)S(1)} %collective-permute-done.2.refs_1_.after_ref, ...), custom_call_target="tpu_custom_call" | custom-call | flops 330000000 | bytes 3280928 | tf_op jit(solution)/shard_map/first/pallas_call | solution.py:511
  20.9 1.4 %smooth.1 = (f32[8,64,192]{2,1,0:T(8,128)S(1)}, f32[8,128]{1,0:T(8,128)S(1)}, f32[8,128]{1,0:T(8,128)S(1)}, f32[8,64,192]{2,1,0:T(8,128)S(1)}, f32[4,64,192]{2,1,0:T(8,128)S(1)}, /*index=5*/f32[4,64,192]{2,1,0:T(8,128)S(1)}) custom-call(s32[1]{0:T(128)} %bitcast.odd_ref, s32[8]{0:T(128)S(1)} %copy-done.4, f32[8,64,192]{2,1,0:T(8,128)S(1)} %bitcast.10, ...), custom_call_target="tpu_custom_call" | custom-call | flops 330000000 | bytes 2773028 | tf_op jit(solution)/shard_map/smooth/pallas_call | solution.py:511
  22.4 4.6 %collective-permute-start.6 = (f32[4,64,192]{2,1,0:T(8,128)S(1)}, f32[4,64,192]{2,1,0:T(8,128)S(1)}, u32[]{:S(2)}, u32[]{:S(2)}) collective-permute-start(f32[4,64,192]{2,1,0:T(8,128)S(1)} %get-tuple-element.81), channel_id=1, source_target_pairs={{2,4},{6,8},{10,12},{14,16},{18,20},{22,24},{26,28},{30,0},{4,2},{... | collective-permute-start | bytes 589832 | tf_op jit(solution)/shard_map/ppermute | solution.py:531
  27.0 3.8 %polar.3 = (f32[4,64,128]{2,1,0:T(8,128)S(1)}, f32[32,128]{1,0:T(8,128)S(1)}, f32[4,64,128]{2,1,0:T(8,128)S(1)}) custom-call(f32[8,64,192]{2,1,0:T(8,128)S(1)} %get-tuple-element.77.after_ref.inside_ref, f32[64,64]{1,0:T(8,128)S(1)} %copy-done.7, f32[4,64,128]{2,1,0:T(8,128)S(1)} %get-tuple-element.78.refs_0_, f32[4,64,128]{2,1,0:T(8,128)S(1)} %collective-permute-done.4.refs_1_), custom_call_target="tpu_custom_call" | custom-call | flops 3300000000 | bytes 950272 | tf_op jit(solution)/shard_map/polar/pallas_call | solution.py:511
  30.9 1.8 %collective-permute-start.7 = (f32[32,128]{1,0:T(8,128)S(1)}, f32[32,128]{1,0:T(8,128)S(1)}, u32[]{:S(2)}, u32[]{:S(2)}) collective-permute-start(f32[32,128]{1,0:T(8,128)S(1)} %get-tuple-element.79.after_ref.refs_1_), channel_id=1, source_target_pairs={{0,2},{2,0},{4,6},{6,4},{8,10},{10,8},{12,14},{14,12},{16,18},{18,... | collective-permute-start | bytes 49160 | tf_op jit(solution)/shard_map/ppermute | solution.py:568
  32.7 1.2 %ahead.2 = (f32[8,64,192]{2,1,0:T(8,128)S(1)}, f32[8,64,192]{2,1,0:T(8,128)S(1)}, f32[8,64,192]{2,1,0:T(8,128)S(1)}, f32[4,64,256]{2,1,0:T(8,128)S(1)}) custom-call(s32[1]{0:T(128)} %bitcast.odd_ref, f32[32,128]{1,0:T(8,128)S(1)} %get-tuple-element.79.after_ref.refs_1_, f32[8,64,192]{2,1,0:T(8,128)S(1)} %get-tuple-element.77.after_ref.inside_ref, ...), custom_call_target="tpu_custom_call" | custom-call | flops 330000000 | bytes 3624964 | tf_op jit(solution)/shard_map/ahead/pallas_call | solution.py:511
  34.7 2.0 %collective-permute-start.12 = (f32[32,128]{1,0:T(8,128)S(1)}, f32[32,128]{1,0:T(8,128)S(1)}, u32[]{:S(2)}, u32[]{:S(2)}) collective-permute-start(f32[32,128]{1,0:T(8,128)S(1)} %add.3.refs_0_), channel_id=1, source_target_pairs={{0,24},{2,26},{4,28},{6,30},{8,16},{10,18},{12,20},{14,22},{16,8},... | collective-permute-start | bytes 49160 | tf_op jit(solution)/shard_map/ppermute | solution.py:568
  36.6 2.5 %collective-permute-start.10 = (f32[32,128]{1,0:T(8,128)S(1)}, f32[32,128]{1,0:T(8,128)S(1)}, u32[]{:S(2)}, u32[]{:S(2)}) collective-permute-start(f32[32,128]{1,0:T(8,128)S(1)} %add.3.refs_0_), channel_id=1, source_target_pairs={{0,8},{2,10},{4,12},{6,14},{8,0},{10,2},{12,4},{14,6},{16,24},{18,... | collective-permute-start | bytes 49160 | tf_op jit(solution)/shard_map/ppermute | solution.py:568
  39.1 1.1 %collective-permute-done.12.refs_3_ = f32[32,128]{1,0:T(8,128)S(1)} collective-permute-done((f32[32,128]{1,0:T(8,128)S(1)}, f32[32,128]{1,0:T(8,128)S(1)}, u32[]{:S(2)}, u32[]{:S(2)}) %collective-permute-start.12) | collective-permute-done | bytes 16416 | tf_op jit(solution)/shard_map/ppermute | solution.py:568
  41.3 1.1 %collective-permute-start.13 = (f32[4,64,256]{2,1,0:T(8,128)S(1)}, f32[4,64,256]{2,1,0:T(8,128)S(1)}, u32[]{:S(2)}, u32[]{:S(2)}) collective-permute-start(f32[4,64,256]{2,1,0:T(8,128)S(1)} %get-tuple-element.101.refs_0_), channel_id=1, source_target_pairs={{0,1},{1,0},{2,3},{3,2},{4,5},{5,4},{6,7},{7,6},{8,9},{9,8},{10,11... | collective-permute-start | bytes 786440 | tf_op jit(solution)/shard_map/ppermute | solution.py:525
  43.7 2.3 %collective-permute-start.15 = (f32[4,64,192]{2,1,0:T(8,128)S(1)}, f32[4,64,192]{2,1,0:T(8,128)S(1)}, u32[]{:S(2)}, u32[]{:S(2)}) collective-permute-start(f32[4,64,192]{2,1,0:T(8,128)S(1)} %get-tuple-element.105), channel_id=1, source_target_pairs={{2,4},{6,8},{10,12},{14,16},{18,20},{22,24},{26,28},{30,0},{4,2},{... | collective-permute-start | bytes 589832 | tf_op jit(solution)/shard_map/ppermute | solution.py:531
  46.0 2.7 %collective-permute-done.13.refs_1_ = f32[4,64,256]{2,1,0:T(8,128)S(1)} collective-permute-done((f32[4,64,256]{2,1,0:T(8,128)S(1)}, f32[4,64,256]{2,1,0:T(8,128)S(1)}, u32[]{:S(2)}, u32[]{:S(2)}) %collective-permute-start.13) | collective-permute-done | bytes 262176 | tf_op jit(solution)/shard_map/ppermute | solution.py:525
  48.7 4.4 %polar.4 = (f32[4,64,128]{2,1,0:T(8,128)S(1)}, f32[32,128]{1,0:T(8,128)S(1)}, f32[4,64,128]{2,1,0:T(8,128)S(1)}) custom-call(f32[8,64,192]{2,1,0:T(8,128)S(1)} %get-tuple-element.98.after_ref.inside_ref, f32[64,64]{1,0:T(8,128)S(1)} %get-tuple-element.99.delta_ref, f32[4,64,128]{2,1,0:T(8,128)S(1)} %get-tuple-element.94.refs_0_.change_ref, ...), custom_call_target="tpu_custom_call" | custom-call | flops 330000000 | bytes 1474560 | tf_op jit(solution)/shard_map/polar/pallas_call | solution.py:511
  53.8 1.2 %collective-permute-start.16 = (f32[32,128]{1,0:T(8,128)S(1)}, f32[32,128]{1,0:T(8,128)S(1)}, u32[]{:S(2)}, u32[]{:S(2)}) collective-permute-start(f32[32,128]{1,0:T(8,128)S(1)} %get-tuple-element.103.after_ref.refs_1_), channel_id=1, source_target_pairs={{0,2},{2,0},{4,6},{6,4},{8,10},{10,8},{12,14},{14,12},{16,18},{18,... | collective-permute-start | bytes 49160 | tf_op jit(solution)/shard_map/ppermute | solution.py:568
  55.0 1.9 %ahead.3 = (f32[8,64,192]{2,1,0:T(8,128)}, f32[8,64,192]{2,1,0:T(8,128)}, f32[8,64,192]{2,1,0:T(8,128)S(1)}, f32[4,64,256]{2,1,0:T(8,128)S(1)}) custom-call(s32[1]{0:T(128)} %bitcast.odd_ref, f32[32,128]{1,0:T(8,128)S(1)} %get-tuple-element.103.after_ref.refs_1_, f32[8,64,192]{2,1,0:T(8,128)S(1)} %get-tuple-element.98.after_ref.inside_ref, ...), custom_call_target="tpu_custom_call" | custom-call | flops 330000000 | bytes 3624964 | tf_op jit(solution)/shard_map/ahead/pallas_call | solution.py:511
  57.0 1.4 %collective-permute-start.22 = (f32[4,64,256]{2,1,0:T(8,128)S(1)}, f32[4,64,256]{2,1,0:T(8,128)S(1)}, u32[]{:S(2)}, u32[]{:S(2)}) collective-permute-start(f32[4,64,256]{2,1,0:T(8,128)S(1)} %get-tuple-element.112.refs_0_), channel_id=1, source_target_pairs={{0,1},{1,0},{2,3},{3,2},{4,5},{5,4},{6,7},{7,6},{8,9},{9,8},{10,11... | collective-permute-start | bytes 786440 | tf_op jit(solution)/shard_map/ppermute | solution.py:525
  58.3 1.5 %collective-permute-start.21 = (f32[32,128]{1,0:T(8,128)S(1)}, f32[32,128]{1,0:T(8,128)S(1)}, u32[]{:S(2)}, u32[]{:S(2)}) collective-permute-start(f32[32,128]{1,0:T(8,128)S(1)} %add.4.refs_0_), channel_id=1, source_target_pairs={{0,24},{2,26},{4,28},{6,30},{8,16},{10,18},{12,20},{14,22},{16,8},... | collective-permute-start | bytes 49160 | tf_op jit(solution)/shard_map/ppermute | solution.py:568
  60.5 2.2 %collective-permute-start.19 = (f32[32,128]{1,0:T(8,128)S(1)}, f32[32,128]{1,0:T(8,128)S(1)}, u32[]{:S(2)}, u32[]{:S(2)}) collective-permute-start(f32[32,128]{1,0:T(8,128)S(1)} %add.4.refs_0_), channel_id=1, source_target_pairs={{0,8},{2,10},{4,12},{6,14},{8,0},{10,2},{12,4},{14,6},{16,24},{18,... | collective-permute-start | bytes 49160 | tf_op jit(solution)/shard_map/ppermute | solution.py:568
  62.7 1.1 %collective-permute-done.21.refs_3_ = f32[32,128]{1,0:T(8,128)S(1)} collective-permute-done((f32[32,128]{1,0:T(8,128)S(1)}, f32[32,128]{1,0:T(8,128)S(1)}, u32[]{:S(2)}, u32[]{:S(2)}) %collective-permute-start.21) | collective-permute-done | bytes 16416 | tf_op jit(solution)/shard_map/ppermute | solution.py:568
  65.2 4.9 %polar.5 = (f32[4,64,128]{2,1,0:T(8,128)S(1)}, f32[32,128]{1,0:T(8,128)S(1)}, f32[4,64,128]{2,1,0:T(8,128)}) custom-call(f32[8,64,192]{2,1,0:T(8,128)S(1)} %get-tuple-element.98.after_ref.inside_ref, f32[64,64]{1,0:T(8,128)S(1)} %get-tuple-element.109.delta_ref, f32[4,64,128]{2,1,0:T(8,128)S(1)} %get-tuple-element.110.change_ref, ...), custom_call_target="tpu_custom_call" | custom-call | flops 330000000 | bytes 1474560 | tf_op jit(solution)/shard_map/polar/pallas_call | solution.py:511
  70.1 1.4 %collective-permute-start.24 = (f32[32,128]{1,0:T(8,128)S(1)}, f32[32,128]{1,0:T(8,128)S(1)}, u32[]{:S(2)}, u32[]{:S(2)}) collective-permute-start(f32[32,128]{1,0:T(8,128)S(1)} %get-tuple-element.118.refs_0_), channel_id=1, source_target_pairs={{0,4},{2,6},{4,0},{6,2},{8,12},{10,14},{12,8},{14,10},{16,20},{18,... | collective-permute-start | bytes 49160 | tf_op jit(solution)/shard_map/ppermute | solution.py:568
  72.0 1.4 %collective-permute-done.25.refs_3_ = f32[32,128]{1,0:T(8,128)S(1)} collective-permute-done((f32[32,128]{1,0:T(8,128)S(1)}, f32[32,128]{1,0:T(8,128)S(1)}, u32[]{:S(2)}, u32[]{:S(2)}) %collective-permute-start.25) | collective-permute-done | bytes 16416 | tf_op jit(solution)/shard_map/ppermute | solution.py:568
  73.9 2.3 %collective-permute-start.28 = (f32[32,128]{1,0:T(8,128)S(1)}, f32[32,128]{1,0:T(8,128)S(1)}, u32[]{:S(2)}, u32[]{:S(2)}) collective-permute-start(f32[32,128]{1,0:T(8,128)S(1)} %add.5.refs_0_), channel_id=1, source_target_pairs={{0,24},{2,26},{4,28},{6,30},{8,16},{10,18},{12,20},{14,22},{16,8},... | collective-permute-start | bytes 49160 | tf_op jit(solution)/shard_map/ppermute | solution.py:568
  76.2 1.1 %collective-permute-start.27 = (f32[32,128]{1,0:T(8,128)S(1)}, f32[32,128]{1,0:T(8,128)S(1)}, u32[]{:S(2)}, u32[]{:S(2)}) collective-permute-start(f32[32,128]{1,0:T(8,128)S(1)} %add.5.refs_0_), channel_id=1, source_target_pairs={{0,16},{2,18},{4,20},{6,22},{8,24},{10,26},{12,28},{14,30},{16,0},... | collective-permute-start | bytes 49160 | tf_op jit(solution)/shard_map/ppermute | solution.py:568
  78.4 1.4 %rows.3 = (bf16[8,192,192]{2,1,0:T(8,128)(2,1)S(1)}, f32[8,64,192]{2,1,0:T(8,128)}, f32[8,64,192]{2,1,0:T(8,128)}) custom-call(f32[4,64,128]{2,1,0:T(8,128)S(1)} %get-tuple-element.113.mixed_ref, f32[4,64,128]{2,1,0:T(8,128)S(1)} %get-tuple-element.110.change_ref, f32[4,64,128]{2,1,0:T(8,128)S(1)} %get-tuple-element.114.forward_ref, ...), custom_call_target="tpu_custom_call" | custom-call | flops 330000000 | bytes 2555904 | tf_op jit(solution)/shard_map/rows/pallas_call | solution.py:511
  79.8 1.1 %collective-permute-done.27.refs_2_ = f32[32,128]{1,0:T(8,128)S(1)} collective-permute-done((f32[32,128]{1,0:T(8,128)S(1)}, f32[32,128]{1,0:T(8,128)S(1)}, u32[]{:S(2)}, u32[]{:S(2)}) %collective-permute-start.27) | collective-permute-done | bytes 16416 | tf_op jit(solution)/shard_map/ppermute | solution.py:568
  81.1 1.2 %last.1 = (f32[8,64,192]{2,1,0:T(8,128)}, f32[64,64]{1,0:T(8,128)}) custom-call(bf16[8,192,192]{2,1,0:T(8,128)(2,1)S(1)} %get-tuple-element.117.mixed_tall_ref, f32[32,128]{1,0:T(8,128)S(1)} %add.5.refs_0_, f32[32,128]{1,0:T(8,128)S(1)} %collective-permute-done.26.refs_1_, f32[32,128]{1,0:T(8,128)S(1)} %collective-permute-done.27.refs_2_, ...), custom_call_target="tpu_custom_call" | custom-call | flops 330000000 | bytes 1064960 | tf_op jit(solution)/shard_map/last/pallas_call | solution.py:511
  (60 shorter events, 11.8 us)
Async XLA Ops:
  1.6 6.0 %collective-permute-start = (f32[64,64]{1,0:T(8,128)S(1)}, f32[64,64]{1,0:T(8,128)S(1)}, u32[]{:S(2)}, u32[]{:S(2)}) collective-permute-start(f32[64,64]{1,0:T(8,128)S(1)} %get-tuple-element.68.refs_0_), channel_id=1, source_target_pairs={{0,1},{1,0},{2,3},{3,2},{4,5},{5,4},{6,7},{7,6},{8,9},{9,8},{10,11... | collective-permute-start | bytes 49160 | tf_op jit(solution)/shard_map/ppermute | solution.py:525
  4.6 7.1 %copy-start.3 = (f32[8,192,64]{1,2,0:T(8,128)S(1)}, f32[8,192,64]{1,2,0:T(8,128)}, u32[]{:S(2)}) copy-start(f32[8,192,64]{1,2,0:T(8,128)} %param.14) | copy-start | bytes 1179652
  4.6 7.1 %copy-start.4 = (s32[8]{0:T(128)S(1)}, s32[8]{0:T(128)}, u32[]{:S(2)}) copy-start(s32[8]{0:T(128)} %order_ref.5) | copy-start | bytes 100
  7.7 10.6 %collective-permute-start.3 = (f32[4,192,128]{2,1,0:T(8,128)S(1)}, f32[4,192,128]{2,1,0:T(8,128)S(1)}, u32[]{:S(2)}, u32[]{:S(2)}) collective-permute-start(f32[4,192,128]{2,1,0:T(8,128)S(1)} %get-tuple-element.72), channel_id=1, source_target_pairs={{0,1},{1,0},{2,3},{3,2},{4,5},{5,4},{6,7},{7,6},{8,9},{9,8},{10,11... | collective-permute-start | bytes 1179656 | tf_op jit(solution)/shard_map/ppermute | solution.py:525
  8.5 6.0 %collective-permute-start.2 = (f32[8,64]{1,0:T(8,128)S(1)}, f32[8,64]{1,0:T(8,128)S(1)}, u32[]{:S(2)}, u32[]{:S(2)}) collective-permute-start(f32[8,64]{1,0:T(8,128)S(1)} %copy-done.5), channel_id=1, source_target_pairs={{0,30},{2,0},{4,2},{6,4},{8,6},{10,8},{12,10},{14,12},{16,14},{18,... | collective-permute-start | bytes 6152 | tf_op jit(solution)/shard_map/ppermute | solution.py:525
  11.7 5.7 %collective-permute-start.1 = (f32[8,64]{1,0:T(8,128)S(1)}, f32[8,64]{1,0:T(8,128)S(1)}, u32[]{:S(2)}, u32[]{:S(2)}) collective-permute-start(f32[8,64]{1,0:T(8,128)S(1)} %copy-done.5), channel_id=1, source_target_pairs={{0,2},{2,4},{4,6},{6,8},{8,10},{10,12},{12,14},{14,16},{16,18},{18... | collective-permute-start | bytes 6152 | tf_op jit(solution)/shard_map/ppermute | solution.py:525
  11.7 15.3 %copy-start.7 = (f32[64,64]{1,0:T(8,128)S(1)}, f32[64,64]{1,0:T(8,128)}, u32[]{:S(2)}) copy-start(f32[64,64]{1,0:T(8,128)} %delta_ref.1) | copy-start | bytes 49156
  20.2 6.8 %collective-permute-start.4 = (f32[4,64,128]{2,1,0:T(8,128)S(1)}, f32[4,64,128]{2,1,0:T(8,128)S(1)}, u32[]{:S(2)}, u32[]{:S(2)}) collective-permute-start(f32[4,64,128]{2,1,0:T(8,128)S(1)} %get-tuple-element.78.refs_0_), channel_id=1, source_target_pairs={{0,1},{1,0},{2,3},{3,2},{4,5},{5,4},{6,7},{7,6},{8,9},{9,8},{10,11... | collective-permute-start | bytes 393224 | tf_op jit(solution)/shard_map/ppermute | solution.py:525
  22.3 10.4 %collective-permute-start.5 = (f32[4,64,192]{2,1,0:T(8,128)S(1)}, f32[4,64,192]{2,1,0:T(8,128)S(1)}, u32[]{:S(2)}, u32[]{:S(2)}) collective-permute-start(f32[4,64,192]{2,1,0:T(8,128)S(1)} %get-tuple-element.80), channel_id=1, source_target_pairs={{0,2},{4,6},{8,10},{12,14},{16,18},{20,22},{24,26},{28,30},{2,0},{... | collective-permute-start | bytes 589832 | tf_op jit(solution)/shard_map/ppermute | solution.py:531
  22.4 10.3 %collective-permute-start.6 = (f32[4,64,192]{2,1,0:T(8,128)S(1)}, f32[4,64,192]{2,1,0:T(8,128)S(1)}, u32[]{:S(2)}, u32[]{:S(2)}) collective-permute-start(f32[4,64,192]{2,1,0:T(8,128)S(1)} %get-tuple-element.81), channel_id=1, source_target_pairs={{2,4},{6,8},{10,12},{14,16},{18,20},{22,24},{26,28},{30,0},{4,2},{... | collective-permute-start | bytes 589832 | tf_op jit(solution)/shard_map/ppermute | solution.py:531
  30.8 3.2 %collective-permute-start.9 = (f32[32,128]{1,0:T(8,128)S(1)}, f32[32,128]{1,0:T(8,128)S(1)}, u32[]{:S(2)}, u32[]{:S(2)}) collective-permute-start(f32[32,128]{1,0:T(8,128)S(1)} %get-tuple-element.79.after_ref.refs_1_), channel_id=1, source_target_pairs={{0,6},{2,4},{4,2},{6,0},{8,14},{10,12},{12,10},{14,8},{16,22},{18,... | collective-permute-start | bytes 49160 | tf_op jit(solution)/shard_map/ppermute | solution.py:568
  30.9 3.8 %collective-permute-start.8 = (f32[32,128]{1,0:T(8,128)S(1)}, f32[32,128]{1,0:T(8,128)S(1)}, u32[]{:S(2)}, u32[]{:S(2)}) collective-permute-start(f32[32,128]{1,0:T(8,128)S(1)} %get-tuple-element.79.after_ref.refs_1_), channel_id=1, source_target_pairs={{0,4},{2,6},{4,0},{6,2},{8,12},{10,14},{12,8},{14,10},{16,20},{18,... | collective-permute-start | bytes 49160 | tf_op jit(solution)/shard_map/ppermute | solution.py:568
  30.9 3.7 %collective-permute-start.7 = (f32[32,128]{1,0:T(8,128)S(1)}, f32[32,128]{1,0:T(8,128)S(1)}, u32[]{:S(2)}, u32[]{:S(2)}) collective-permute-start(f32[32,128]{1,0:T(8,128)S(1)} %get-tuple-element.79.after_ref.refs_1_), channel_id=1, source_target_pairs={{0,2},{2,0},{4,6},{6,4},{8,10},{10,8},{12,14},{14,12},{16,18},{18,... | collective-permute-start | bytes 49160 | tf_op jit(solution)/shard_map/ppermute | solution.py:568
  34.7 5.6 %collective-permute-start.12 = (f32[32,128]{1,0:T(8,128)S(1)}, f32[32,128]{1,0:T(8,128)S(1)}, u32[]{:S(2)}, u32[]{:S(2)}) collective-permute-start(f32[32,128]{1,0:T(8,128)S(1)} %add.3.refs_0_), channel_id=1, source_target_pairs={{0,24},{2,26},{4,28},{6,30},{8,16},{10,18},{12,20},{14,22},{16,8},... | collective-permute-start | bytes 49160 | tf_op jit(solution)/shard_map/ppermute | solution.py:568
  36.6 4.6 %collective-permute-start.11 = (f32[32,128]{1,0:T(8,128)S(1)}, f32[32,128]{1,0:T(8,128)S(1)}, u32[]{:S(2)}, u32[]{:S(2)}) collective-permute-start(f32[32,128]{1,0:T(8,128)S(1)} %add.3.refs_0_), channel_id=1, source_target_pairs={{0,16},{2,18},{4,20},{6,22},{8,24},{10,26},{12,28},{14,30},{16,0},... | collective-permute-start | bytes 49160 | tf_op jit(solution)/shard_map/ppermute | solution.py:568
  36.6 4.6 %collective-permute-start.10 = (f32[32,128]{1,0:T(8,128)S(1)}, f32[32,128]{1,0:T(8,128)S(1)}, u32[]{:S(2)}, u32[]{:S(2)}) collective-permute-start(f32[32,128]{1,0:T(8,128)S(1)} %add.3.refs_0_), channel_id=1, source_target_pairs={{0,8},{2,10},{4,12},{6,14},{8,0},{10,2},{12,4},{14,6},{16,24},{18,... | collective-permute-start | bytes 49160 | tf_op jit(solution)/shard_map/ppermute | solution.py:568
  41.3 7.4 %collective-permute-start.13 = (f32[4,64,256]{2,1,0:T(8,128)S(1)}, f32[4,64,256]{2,1,0:T(8,128)S(1)}, u32[]{:S(2)}, u32[]{:S(2)}) collective-permute-start(f32[4,64,256]{2,1,0:T(8,128)S(1)} %get-tuple-element.101.refs_0_), channel_id=1, source_target_pairs={{0,1},{1,0},{2,3},{3,2},{4,5},{5,4},{6,7},{7,6},{8,9},{9,8},{10,11... | collective-permute-start | bytes 786440 | tf_op jit(solution)/shard_map/ppermute | solution.py:525
  43.6 11.4 %collective-permute-start.14 = (f32[4,64,192]{2,1,0:T(8,128)S(1)}, f32[4,64,192]{2,1,0:T(8,128)S(1)}, u32[]{:S(2)}, u32[]{:S(2)}) collective-permute-start(f32[4,64,192]{2,1,0:T(8,128)S(1)} %get-tuple-element.104), channel_id=1, source_target_pairs={{0,2},{4,6},{8,10},{12,14},{16,18},{20,22},{24,26},{28,30},{2,0},{... | collective-permute-start | bytes 589832 | tf_op jit(solution)/shard_map/ppermute | solution.py:531
  43.7 11.3 %collective-permute-start.15 = (f32[4,64,192]{2,1,0:T(8,128)S(1)}, f32[4,64,192]{2,1,0:T(8,128)S(1)}, u32[]{:S(2)}, u32[]{:S(2)}) collective-permute-start(f32[4,64,192]{2,1,0:T(8,128)S(1)} %get-tuple-element.105), channel_id=1, source_target_pairs={{2,4},{6,8},{10,12},{14,16},{18,20},{22,24},{26,28},{30,0},{4,2},{... | collective-permute-start | bytes 589832 | tf_op jit(solution)/shard_map/ppermute | solution.py:531
  53.1 3.9 %collective-permute-start.18 = (f32[32,128]{1,0:T(8,128)S(1)}, f32[32,128]{1,0:T(8,128)S(1)}, u32[]{:S(2)}, u32[]{:S(2)}) collective-permute-start(f32[32,128]{1,0:T(8,128)S(1)} %get-tuple-element.103.after_ref.refs_1_), channel_id=1, source_target_pairs={{0,6},{2,4},{4,2},{6,0},{8,14},{10,12},{12,10},{14,8},{16,22},{18,... | collective-permute-start | bytes 49160 | tf_op jit(solution)/shard_map/ppermute | solution.py:568
  53.1 3.8 %collective-permute-start.17 = (f32[32,128]{1,0:T(8,128)S(1)}, f32[32,128]{1,0:T(8,128)S(1)}, u32[]{:S(2)}, u32[]{:S(2)}) collective-permute-start(f32[32,128]{1,0:T(8,128)S(1)} %get-tuple-element.103.after_ref.refs_1_), channel_id=1, source_target_pairs={{0,4},{2,6},{4,0},{6,2},{8,12},{10,14},{12,8},{14,10},{16,20},{18,... | collective-permute-start | bytes 49160 | tf_op jit(solution)/shard_map/ppermute | solution.py:568
  53.8 3.2 %collective-permute-start.16 = (f32[32,128]{1,0:T(8,128)S(1)}, f32[32,128]{1,0:T(8,128)S(1)}, u32[]{:S(2)}, u32[]{:S(2)}) collective-permute-start(f32[32,128]{1,0:T(8,128)S(1)} %get-tuple-element.103.after_ref.refs_1_), channel_id=1, source_target_pairs={{0,2},{2,0},{4,6},{6,4},{8,10},{10,8},{12,14},{14,12},{16,18},{18,... | collective-permute-start | bytes 49160 | tf_op jit(solution)/shard_map/ppermute | solution.py:568
  57.0 8.3 %collective-permute-start.22 = (f32[4,64,256]{2,1,0:T(8,128)S(1)}, f32[4,64,256]{2,1,0:T(8,128)S(1)}, u32[]{:S(2)}, u32[]{:S(2)}) collective-permute-start(f32[4,64,256]{2,1,0:T(8,128)S(1)} %get-tuple-element.112.refs_0_), channel_id=1, source_target_pairs={{0,1},{1,0},{2,3},{3,2},{4,5},{5,4},{6,7},{7,6},{8,9},{9,8},{10,11... | collective-permute-start | bytes 786440 | tf_op jit(solution)/shard_map/ppermute | solution.py:525
  58.3 5.5 %collective-permute-start.21 = (f32[32,128]{1,0:T(8,128)S(1)}, f32[32,128]{1,0:T(8,128)S(1)}, u32[]{:S(2)}, u32[]{:S(2)}) collective-permute-start(f32[32,128]{1,0:T(8,128)S(1)} %add.4.refs_0_), channel_id=1, source_target_pairs={{0,24},{2,26},{4,28},{6,30},{8,16},{10,18},{12,20},{14,22},{16,8},... | collective-permute-start | bytes 49160 | tf_op jit(solution)/shard_map/ppermute | solution.py:568
  59.8 4.8 %collective-permute-start.20 = (f32[32,128]{1,0:T(8,128)S(1)}, f32[32,128]{1,0:T(8,128)S(1)}, u32[]{:S(2)}, u32[]{:S(2)}) collective-permute-start(f32[32,128]{1,0:T(8,128)S(1)} %add.4.refs_0_), channel_id=1, source_target_pairs={{0,16},{2,18},{4,20},{6,22},{8,24},{10,26},{12,28},{14,30},{16,0},... | collective-permute-start | bytes 49160 | tf_op jit(solution)/shard_map/ppermute | solution.py:568
  60.5 4.1 %collective-permute-start.19 = (f32[32,128]{1,0:T(8,128)S(1)}, f32[32,128]{1,0:T(8,128)S(1)}, u32[]{:S(2)}, u32[]{:S(2)}) collective-permute-start(f32[32,128]{1,0:T(8,128)S(1)} %add.4.refs_0_), channel_id=1, source_target_pairs={{0,8},{2,10},{4,12},{6,14},{8,0},{10,2},{12,4},{14,6},{16,24},{18,... | collective-permute-start | bytes 49160 | tf_op jit(solution)/shard_map/ppermute | solution.py:568
  70.1 3.3 %collective-permute-start.25 = (f32[32,128]{1,0:T(8,128)S(1)}, f32[32,128]{1,0:T(8,128)S(1)}, u32[]{:S(2)}, u32[]{:S(2)}) collective-permute-start(f32[32,128]{1,0:T(8,128)S(1)} %get-tuple-element.118.refs_0_), channel_id=1, source_target_pairs={{0,6},{2,4},{4,2},{6,0},{8,14},{10,12},{12,10},{14,8},{16,22},{18,... | collective-permute-start | bytes 49160 | tf_op jit(solution)/shard_map/ppermute | solution.py:568
  70.1 3.8 %collective-permute-start.24 = (f32[32,128]{1,0:T(8,128)S(1)}, f32[32,128]{1,0:T(8,128)S(1)}, u32[]{:S(2)}, u32[]{:S(2)}) collective-permute-start(f32[32,128]{1,0:T(8,128)S(1)} %get-tuple-element.118.refs_0_), channel_id=1, source_target_pairs={{0,4},{2,6},{4,0},{6,2},{8,12},{10,14},{12,8},{14,10},{16,20},{18,... | collective-permute-start | bytes 49160 | tf_op jit(solution)/shard_map/ppermute | solution.py:568
  71.6 2.4 %collective-permute-start.23 = (f32[32,128]{1,0:T(8,128)S(1)}, f32[32,128]{1,0:T(8,128)S(1)}, u32[]{:S(2)}, u32[]{:S(2)}) collective-permute-start(f32[32,128]{1,0:T(8,128)S(1)} %get-tuple-element.118.refs_0_), channel_id=1, source_target_pairs={{0,2},{2,0},{4,6},{6,4},{8,10},{10,8},{12,14},{14,12},{16,18},{18,... | collective-permute-start | bytes 49160 | tf_op jit(solution)/shard_map/ppermute | solution.py:568
  73.9 5.8 %collective-permute-start.28 = (f32[32,128]{1,0:T(8,128)S(1)}, f32[32,128]{1,0:T(8,128)S(1)}, u32[]{:S(2)}, u32[]{:S(2)}) collective-permute-start(f32[32,128]{1,0:T(8,128)S(1)} %add.5.refs_0_), channel_id=1, source_target_pairs={{0,24},{2,26},{4,28},{6,30},{8,16},{10,18},{12,20},{14,22},{16,8},... | collective-permute-start | bytes 49160 | tf_op jit(solution)/shard_map/ppermute | solution.py:568
  76.2 4.6 %collective-permute-start.27 = (f32[32,128]{1,0:T(8,128)S(1)}, f32[32,128]{1,0:T(8,128)S(1)}, u32[]{:S(2)}, u32[]{:S(2)}) collective-permute-start(f32[32,128]{1,0:T(8,128)S(1)} %add.5.refs_0_), channel_id=1, source_target_pairs={{0,16},{2,18},{4,20},{6,22},{8,24},{10,26},{12,28},{14,30},{16,0},... | collective-permute-start | bytes 49160 | tf_op jit(solution)/shard_map/ppermute | solution.py:568
  77.4 3.7 %collective-permute-start.26 = (f32[32,128]{1,0:T(8,128)S(1)}, f32[32,128]{1,0:T(8,128)S(1)}, u32[]{:S(2)}, u32[]{:S(2)}) collective-permute-start(f32[32,128]{1,0:T(8,128)S(1)} %add.5.refs_0_), channel_id=1, source_target_pairs={{0,8},{2,10},{4,12},{6,14},{8,0},{10,2},{12,4},{14,6},{16,24},{18,... | collective-permute-start | bytes 49160 | tf_op jit(solution)/shard_map/ppermute | solution.py:568
  (5 other events, 26.0 us)

commit v5 on v4

--- a/solution.py
+++ b/solution.py
@@ -195,7 +195,8 @@
         side = lax.div(lax.broadcasted_iota(jnp.int32, both.shape, 1), rank)
         both = jnp.where(side == lax.rem(order_ref[k], 2), both, 0.0)
         high, low = split(both)
-        mover_ref[k] = jnp.concatenate([high, high, low], axis=1)
+        pair, place = stored_place(order_ref, k, count, rank)
+        mover_ref[pair, place, :] = jnp.concatenate([high, high, low], axis=1)
 
 
 def cross_blocks(lefts, rights, rank):
@@ -217,19 +218,22 @@
     return total
 
 
-def stored_pair(order_ref, refs, k, count):
-    return summed(refs, lax.div(lax.rem(order_ref[k], count), 2))
+def stored_place(order_ref, k, count, rank):
+    stored = lax.rem(order_ref[k], count)
+    return lax.div(stored, 2), pl.ds(pl.multiple_of(lax.rem(stored, 2) * rank, rank), rank)
 
 
 def first_kernel(group, order_ref, *refs):
     base_ref, mover_ref, dual_s_ref, dual_c_ref = refs[2:6]
-    *projected_refs, tall_ref, target_ref, gram_ref = refs[6:]
+    *projected_refs, tall_ref, target_ref, gram_ref, moved = refs[6:]
     count, rank, rows = base_ref.shape
+    for pair in range(count // 2):
+        high, low = split(summed(projected_refs, pair))
+        moved[pair] = dot(mover_ref[pair], jnp.concatenate([high, low, high], axis=1), NT)
     talls = []
     for k in range(count):
-        high, low = split(stored_pair(order_ref, projected_refs, k, count))
-        moved = dot(mover_ref[k], jnp.concatenate([high, low, high], axis=1), NT)
-        evolving = base_ref[k] + moved
+        pair, place = stored_place(order_ref, k, count, rank)
+        evolving = base_ref[k] + moved[pair, place, :]
         target_ref[k] = evolving + dual_s_ref[k]
         tall = evolving + dual_c_ref[k]
         tall_ref[k] = tall
@@ -273,7 +277,7 @@
     odd_ref, order_ref, aux_ref, target_ref, before_ref, rho_ref, after_ref, diagonal_ref,
     columns_ref, *refs
 ):
-    *projected_refs, side_ref, past_ref, next_ref, inside_ref, near_ref, far_ref = refs
+    *projected_refs, side_ref, past_ref, next_ref, inside_ref, near_ref, far_ref, turned = refs
     count, rank, rows = aux_ref.shape
     for source, place in ((before_ref, past_ref), (after_ref, next_ref)):
         weights = source[...]
@@ -285,10 +289,11 @@
         odd_ref[0], [aux_ref[k] for k in slices], [target_ref[k] for k in slices], rho,
         inside_ref, near_ref, far_ref,
     )
+    for pair in range(count // 2):
+        turned[pair] = summed(projected_refs, pair).T
     for k in slices:
-        both = stored_pair(order_ref, projected_refs, k, count).T
-        own = jnp.where(lax.rem(order_ref[k], 2) == 1, both[rank:], both[:rank])
-        side_ref[k] = columns_ref[:, k : k + 1] * own
+        pair, place = stored_place(order_ref, k, count, rank)
+        side_ref[k] = columns_ref[:, k : k + 1] * turned[pair, place, :]
 
 
 def polar(grams, delta):
@@ -356,8 +361,11 @@
     mix(roots, scales, grams, delta, mixed_ref, partial_ref)
 
 
-def later_polar_kernel(after_ref, delta_ref, change_ref, old_ref, *refs):
-    *cross_refs, mixed_ref, partial_ref, gram_ref = refs
+def later_polar_kernel(last, after_ref, delta_ref, change_ref, old_ref, *refs):
+    if last:
+        *cross_refs, mixed_ref, partial_ref = refs
+    else:
+        *cross_refs, mixed_ref, partial_ref, gram_ref = refs
     groups, rank, wide = old_ref.shape
     group = wide // rank
     mask = block_mask(rank, group)
@@ -370,7 +378,8 @@
         (one,) = times_blocks([onward], block_diagonal(change, mask, group, NT), NT)
         (other,) = times_blocks([change], block_diagonal(onward, mask, group, NT), NT)
         grams.append(cross[:, wide:] + one + other)
-        gram_ref[at] = grams[at]
+        if not last:
+            gram_ref[at] = grams[at]
     delta = delta_ref[...]
     roots, scales = polar(grams, delta)
     mix(roots, scales, grams, delta, mixed_ref, partial_ref)
@@ -378,7 +387,7 @@
 
 def ahead_kernel(
     group, odd_ref, after_ref, inside_ref, near_ref, far_ref, target_ref, tall_ref, side_ref, rho_ref,
-    inverse_ref, aux_ref, dual_ref, known_ref, cross_ref,
+    inverse_ref, known_ref, cross_ref, *kept
 ):
     count, rank, _ = inside_ref.shape
     width = SWEEPS
@@ -391,8 +400,10 @@
             at = k - count + width
             aux = aux + jnp.where(odd_ref[0] == 1, far_ref[at], near_ref[at])
         target, tall = target_ref[k], tall_ref[k]
-        aux_ref[k] = aux
-        dual_ref[k] = target - aux
+        if kept:
+            aux_ref, dual_ref = kept
+            aux_ref[k] = aux
+            dual_ref[k] = target - aux
         known = dot(
             inverse_ref[k],
             right_triple(side_ref[k] + rho_ref[k : k + 1, 0:1] * (2.0 * aux - target - tall)),
@@ -621,7 +632,7 @@
         "setup",
         [
             ((count, rank, 3 * rank), bf16),
-            ((count, rank, 6 * rank), bf16),
+            ((count // 2, 2 * rank, 6 * rank), bf16),
             lanes(count),
             ((count, rank), f32),
             ((rank, count), f32),
@@ -636,6 +647,7 @@
         [state, state, quads],
         order, before, after, base, mover, dual_s, dual_c, own, *received,
         scalars=1, unread=2,
+        scratch=[pltpu.VMEM((count // 2, 2 * rank, rows), f32)],
     )
     side, before, after, inside, to_near, to_far = call(
         smooth_kernel,
@@ -643,6 +655,7 @@
         [state, lanes(count), lanes(count), state, halo, halo],
         odd, order, aux, target, before, rho, after, diagonal, columns, own, *received,
         scalars=2,
+        scratch=[pltpu.VMEM((count // 2, 2 * rank, rows), f32)],
     )
     polar_outs = [quads, ((rank // 2, 2 * rank), f32), quads]
     for inner in range(INNER):
@@ -655,19 +668,22 @@
                 unread=1, microseconds=3,
             )
         else:
-            mixed, partial, gram = call(
-                later_polar_kernel,
+            last = inner == INNER - 1
+            mixed, partial, *gram = call(
+                functools.partial(later_polar_kernel, last),
                 "polar",
-                polar_outs,
-                inside, delta, change, gram, cross, *crosses,
+                polar_outs[:2] if last else polar_outs,
+                inside, delta, change, old, cross, *crosses,
                 unread=1,
             )
+            gram = gram[0] if gram else None
         if inner == INNER - 1:
-            mixed_tall, evolving, _ = call(
+            mixed_tall, evolving = call(
                 last_rows_kernel,
                 "rows",
-                [((count, 3 * rank, rows), bf16), state, state],
+                [((count, 3 * rank, rows), bf16), state],
                 mixed, change, forward, tall, known,
+                scratch=[pltpu.VMEM(state[0], f32)],
             )
             coup, delta = call(
                 functools.partial(last_kernel, total),
@@ -678,19 +694,17 @@
             continue
         near = swapped(to_near, "cuts", 0)
         far = swapped(to_far, "cuts", 1)
-        aux, dual, known, cross = call(
+        known, cross, *kept = call(
             functools.partial(ahead_kernel, group),
             "ahead",
-            [state, state, state, ((groups, rank, 2 * wide), f32)],
+            [state, ((groups, rank, 2 * wide), f32)] + [state] * (2 if inner < INNER - 2 else 0),
             odd, partial, inside, near, far, target, tall, side, rho, inverse,
             scalars=1, unread=1,
         )
         sums, firsts = in_stages(partial, "cuts", beside=cross)
-        if inner < INNER - 2:
-            sums, cross = lax.optimization_barrier((sums, cross))
-        else:
-            _, cross = lax.optimization_barrier((firsts, cross))
+        _, cross = lax.optimization_barrier((firsts, cross))
         crosses = from_others(cross, "chan")
+        old = gram
         delta, change, forward = call(
             functools.partial(mixer_kernel, total),
             "mixer",
@@ -702,7 +716,7 @@
                 rows_kernel,
                 "rows",
                 [state, state, state, halo, halo],
-                odd, aux, before, rho, after, change, forward, tall, known, dual,
+                odd, kept[0], before, rho, after, change, forward, tall, known, kept[1],
                 scalars=1,
             )
     return (flip(evolving), flip(coup), delta)

time: 82.5 us -> 79 us (0.958)
  Pallas kernels: 30 us -> 28.1 us
  waiting for transfers between devices: 14.5 us -> 13.3 us
    ppermute x7, waiting for transfers between devices: 6.44 us -> 3.71 us  [rotated(): lax.ppermute(value, axis, [(i, (i + shift) % count) for i in range(count)])]
    pallas_call x18, Pallas kernels: 30 us -> 28.1 us  [call(): pl.pallas_call(kernel, out_shape=shapes, in_specs=specs, out_specs=[pl.Bl...]
    ppermute x18, waiting for transfers between devices: 8.03 us -> 9.44 us  [in_stages(): terms.append(lax.ppermute(value, axis, moves))]
  transfers between devices with their start and end apart: 29 -> 29, of which waited for: 14 -> 15; matrix products, arithmetic and copies ran while one was open for 0% -> 0% of each run, Pallas kernels for 26% -> 27%
where the time goes in v5:
time: 79 us; the launch traced here: 78.8 us
  starting transfers between devices  35.6 us (45%)
  Pallas kernels  28.1 us (36%)
  waiting for transfers between devices  13.3 us (17%)
  between operations  0.89 us (1%)
  local copies, waits for them, and re-layouts  0.87 us (1%)
    pallas_call x18, Pallas kernels, call(): pl.pallas_call(kernel, out_shape=shapes, in_specs=specs, out_specs=[pl.Bl...  28.1 us
    ppermute x18, starting transfers between devices, in_stages(): terms.append(lax.ppermute(value, axis, moves))  19 us
    ppermute x7, starting transfers between devices, rotated(): lax.ppermute(value, axis, [(i, (i + shift) % count) for i in range(count)])  9.75 us
    ppermute x18, waiting for transfers between devices, in_stages(): terms.append(lax.ppermute(value, axis, moves))  9.44 us
    ppermute x4, starting transfers between devices, swapped(): return lax.ppermute(value, axis, pairs + [(b, a) for a, b in pairs])  6.91 us
    ppermute x7, waiting for transfers between devices, rotated(): lax.ppermute(value, axis, [(i, (i + shift) % count) for i in range(count)])  3.71 us
  transfers between devices with their start and end apart: 29, of which 15 were waited for; matrix products, arithmetic and copies ran while one was open for 0% of the time, Pallas kernels for 27%

profile of v5, /device:TPU:0, one launch (start us, length us, event | category | flops | bytes accessed | tf_op | source)
XLA Modules:
  0.0 78.8 jit_solution(6877892968351704675)
XLA Ops:
  1.6 3.0 %collective-permute-start = (f32[64,64]{1,0:T(8,128)S(1)}, f32[64,64]{1,0:T(8,128)S(1)}, u32[]{:S(2)}, u32[]{:S(2)}) collective-permute-start(f32[64,64]{1,0:T(8,128)S(1)} %get-tuple-element.64.refs_0_), channel_id=1, source_target_pairs={{0,1},{1,0},{2,3},{3,2},{4,5},{5,4},{6,7},{7,6},{8,9},{9,8},{10,11... | collective-permute-start | bytes 49160 | tf_op jit(solution)/shard_map/ppermute | solution.py:536
  4.7 3.0 %project.1 = (f32[4,192,128]{2,1,0:T(8,128)S(1)}, f32[4,192,128]{2,1,0:T(8,128)S(1)}) custom-call(s32[1]{0:T(128)} %bitcast.2.me_ref, bf16[8,384,512]{2,1,0:T(8,128)(2,1)} %data_ref.1, bf16[64,512]{1,0:T(8,128)(2,1)S(1)} %get-tuple-element.58.factor_ref), custom_call_target="tpu_custom_call" | custom-call | flops 2200000000 | bytes 3997700 | tf_op jit(solution)/shard_map/project/pallas_call | solution.py:522
  8.5 3.2 %collective-permute-start.2 = (f32[8,64]{1,0:T(8,128)S(1)}, f32[8,64]{1,0:T(8,128)S(1)}, u32[]{:S(2)}, u32[]{:S(2)}) collective-permute-start(f32[8,64]{1,0:T(8,128)S(1)} %copy-done.5), channel_id=1, source_target_pairs={{0,30},{2,0},{4,2},{6,4},{8,6},{10,8},{12,10},{14,12},{16,14},{18,... | collective-permute-start | bytes 6152 | tf_op jit(solution)/shard_map/ppermute | solution.py:536
  11.7 2.8 %setup.1 = (bf16[8,64,192]{2,1,0:T(8,128)(2,1)S(1)}, bf16[4,128,384]{2,1,0:T(8,128)(2,1)S(1)}, f32[8,128]{1,0:T(8,128)S(1)}, f32[8,64]{1,0:T(8,128)S(1)}, f32[64...) custom-call(s32[8]{0:T(128)S(1)} %copy-done.4, f32[64,64]{1,0:T(8,128)S(1)} %get-tuple-element.64.refs_0_, ...), custom_call_target="tpu_custom_call" | custom-call | flops 330000000 | bytes 2598944 | tf_op jit(solution)/shard_map/setup/pallas_call | solution.py:522
  14.6 2.8 %collective-permute-done.1.refs_0_.before_ref = f32[8,64]{1,0:T(8,128)S(1)} collective-permute-done((f32[8,64]{1,0:T(8,128)S(1)}, f32[8,64]{1,0:T(8,128)S(1)}, u32[]{:S(2)}, u32[]{:S(2)}) %collective-permute-start.1) | collective-permute-done | bytes 2080 | tf_op jit(solution)/shard_map/ppermute | solution.py:536
  18.3 1.4 %first.1 = (f32[8,64,192]{2,1,0:T(8,128)S(1)}, f32[8,64,192]{2,1,0:T(8,128)S(1)}, f32[4,64,128]{2,1,0:T(8,128)S(1)}) custom-call(s32[8]{0:T(128)S(1)} %copy-done.4, f32[8,64]{1,0:T(8,128)S(1)} %collective-permute-done.1.refs_0_.before_ref, f32[8,64]{1,0:T(8,128)S(1)} %collective-permute-done.2.refs_1_.after_ref, ...), custom_call_target="tpu_custom_call" | custom-call | flops 330000000 | bytes 3280928 | tf_op jit(solution)/shard_map/first/pallas_call | solution.py:522
  20.3 1.2 %smooth.1 = (f32[8,64,192]{2,1,0:T(8,128)S(1)}, f32[8,128]{1,0:T(8,128)S(1)}, f32[8,128]{1,0:T(8,128)S(1)}, f32[8,64,192]{2,1,0:T(8,128)S(1)}, f32[4,64,192]{2,1,0:T(8,128)S(1)}, /*index=5*/f32[4,64,192]{2,1,0:T(8,128)S(1)}) custom-call(s32[1]{0:T(128)} %bitcast.odd_ref, s32[8]{0:T(128)S(1)} %copy-done.4, f32[8,64,192]{2,1,0:T(8,128)S(1)} %bitcast.10, ...), custom_call_target="tpu_custom_call" | custom-call | flops 330000000 | bytes 2773028 | tf_op jit(solution)/shard_map/smooth/pallas_call | solution.py:522
  21.7 4.6 %collective-permute-start.6 = (f32[4,64,192]{2,1,0:T(8,128)S(1)}, f32[4,64,192]{2,1,0:T(8,128)S(1)}, u32[]{:S(2)}, u32[]{:S(2)}) collective-permute-start(f32[4,64,192]{2,1,0:T(8,128)S(1)} %get-tuple-element.77), channel_id=1, source_target_pairs={{2,4},{6,8},{10,12},{14,16},{18,20},{22,24},{26,28},{30,0},{4,2},{... | collective-permute-start | bytes 589832 | tf_op jit(solution)/shard_map/ppermute | solution.py:542
  26.3 3.8 %polar.3 = (f32[4,64,128]{2,1,0:T(8,128)S(1)}, f32[32,128]{1,0:T(8,128)S(1)}, f32[4,64,128]{2,1,0:T(8,128)S(1)}) custom-call(f32[8,64,192]{2,1,0:T(8,128)S(1)} %get-tuple-element.73.after_ref.inside_ref, f32[64,64]{1,0:T(8,128)S(1)} %copy-done.7, f32[4,64,128]{2,1,0:T(8,128)S(1)} %get-tuple-element.74.refs_0_, f32[4,64,128]{2,1,0:T(8,128)S(1)} %collective-permute-done.4.refs_1_), custom_call_target="tpu_custom_call" | custom-call | flops 3300000000 | bytes 950272 | tf_op jit(solution)/shard_map/polar/pallas_call | solution.py:522
  30.2 1.8 %collective-permute-start.7 = (f32[32,128]{1,0:T(8,128)S(1)}, f32[32,128]{1,0:T(8,128)S(1)}, u32[]{:S(2)}, u32[]{:S(2)}) collective-permute-start(f32[32,128]{1,0:T(8,128)S(1)} %get-tuple-element.75.after_ref.refs_1_), channel_id=1, source_target_pairs={{0,2},{2,0},{4,6},{6,4},{8,10},{10,8},{12,14},{14,12},{16,18},{18,... | collective-permute-start | bytes 49160 | tf_op jit(solution)/shard_map/ppermute | solution.py:579
  32.0 1.2 %ahead.2 = (f32[8,64,192]{2,1,0:T(8,128)S(1)}, f32[4,64,256]{2,1,0:T(8,128)S(1)}, f32[8,64,192]{2,1,0:T(8,128)S(1)}, f32[8,64,192]{2,1,0:T(8,128)S(1)}) custom-call(s32[1]{0:T(128)} %bitcast.odd_ref, f32[32,128]{1,0:T(8,128)S(1)} %get-tuple-element.75.after_ref.refs_1_, f32[8,64,192]{2,1,0:T(8,128)S(1)} %get-tuple-element.73.after_ref.inside_ref, ...), custom_call_target="tpu_custom_call" | custom-call | flops 330000000 | bytes 3624964 | tf_op jit(solution)/shard_map/ahead/pallas_call | solution.py:522
  33.9 1.5 %collective-permute-start.13 = (f32[4,64,256]{2,1,0:T(8,128)S(1)}, f32[4,64,256]{2,1,0:T(8,128)S(1)}, u32[]{:S(2)}, u32[]{:S(2)}) collective-permute-start(f32[4,64,256]{2,1,0:T(8,128)S(1)} %get-tuple-element.93.refs_0_), channel_id=1, source_target_pairs={{0,1},{1,0},{2,3},{3,2},{4,5},{5,4},{6,7},{7,6},{8,9},{9,8},{10,11... | collective-permute-start | bytes 786440 | tf_op jit(solution)/shard_map/ppermute | solution.py:536
  35.4 1.1 %collective-permute-start.12 = (f32[32,128]{1,0:T(8,128)S(1)}, f32[32,128]{1,0:T(8,128)S(1)}, u32[]{:S(2)}, u32[]{:S(2)}) collective-permute-start(f32[32,128]{1,0:T(8,128)S(1)} %add.3.refs_0_), channel_id=1, source_target_pairs={{0,24},{2,26},{4,28},{6,30},{8,16},{10,18},{12,20},{14,22},{16,8},... | collective-permute-start | bytes 49160 | tf_op jit(solution)/shard_map/ppermute | solution.py:579
  36.7 3.1 %collective-permute-start.10 = (f32[32,128]{1,0:T(8,128)S(1)}, f32[32,128]{1,0:T(8,128)S(1)}, u32[]{:S(2)}, u32[]{:S(2)}) collective-permute-start(f32[32,128]{1,0:T(8,128)S(1)} %add.3.refs_0_), channel_id=1, source_target_pairs={{0,8},{2,10},{4,12},{6,14},{8,0},{10,2},{12,4},{14,6},{16,24},{18,... | collective-permute-start | bytes 49160 | tf_op jit(solution)/shard_map/ppermute | solution.py:579
  39.8 1.1 %collective-permute-done.12.refs_3_ = f32[32,128]{1,0:T(8,128)S(1)} collective-permute-done((f32[32,128]{1,0:T(8,128)S(1)}, f32[32,128]{1,0:T(8,128)S(1)}, u32[]{:S(2)}, u32[]{:S(2)}) %collective-permute-start.12) | collective-permute-done | bytes 16416 | tf_op jit(solution)/shard_map/ppermute | solution.py:579
  42.9 2.2 %collective-permute-start.15 = (f32[4,64,192]{2,1,0:T(8,128)S(1)}, f32[4,64,192]{2,1,0:T(8,128)S(1)}, u32[]{:S(2)}, u32[]{:S(2)}) collective-permute-start(f32[4,64,192]{2,1,0:T(8,128)S(1)} %get-tuple-element.97), channel_id=1, source_target_pairs={{2,4},{6,8},{10,12},{14,16},{18,20},{22,24},{26,28},{30,0},{4,2},{... | collective-permute-start | bytes 589832 | tf_op jit(solution)/shard_map/ppermute | solution.py:542
  45.1 4.4 %polar.4 = (f32[4,64,128]{2,1,0:T(8,128)S(1)}, f32[32,128]{1,0:T(8,128)S(1)}, f32[4,64,128]{2,1,0:T(8,128)S(1)}) custom-call(f32[8,64,192]{2,1,0:T(8,128)S(1)} %get-tuple-element.90.after_ref.inside_ref, f32[64,64]{1,0:T(8,128)S(1)} %get-tuple-element.91.delta_ref, f32[4,64,128]{2,1,0:T(8,128)S(1)} %get-tuple-element.86.refs_0_.change_ref, ...), custom_call_target="tpu_custom_call" | custom-call | flops 330000000 | bytes 1474560 | tf_op jit(solution)/shard_map/polar/pallas_call | solution.py:522
  49.5 1.2 %collective-permute-start.18 = (f32[32,128]{1,0:T(8,128)S(1)}, f32[32,128]{1,0:T(8,128)S(1)}, u32[]{:S(2)}, u32[]{:S(2)}) collective-permute-start(f32[32,128]{1,0:T(8,128)S(1)} %get-tuple-element.95.after_ref.refs_1_), channel_id=1, source_target_pairs={{0,6},{2,4},{4,2},{6,0},{8,14},{10,12},{12,10},{14,8},{16,22},{18,... | collective-permute-start | bytes 49160 | tf_op jit(solution)/shard_map/ppermute | solution.py:579
  51.6 1.4 %ahead.3 = (f32[8,64,192]{2,1,0:T(8,128)S(1)}, f32[4,64,256]{2,1,0:T(8,128)S(1)}) custom-call(s32[1]{0:T(128)} %bitcast.odd_ref, f32[32,128]{1,0:T(8,128)S(1)} %get-tuple-element.95.after_ref.refs_1_, f32[8,64,192]{2,1,0:T(8,128)S(1)} %get-tuple-element.90.after_ref.inside_ref, f32[4,64,192]{2,1,0:T(8,128)S(1)} %collective-permute-done.14.near_ref, ...), custom_call_target="tpu_custom_call" | custom-call | flops 330000000 | bytes 2838532 | tf_op jit(solution)/shard_map/ahead/pallas_call | solution.py:522
  53.0 1.4 %collective-permute-done.17.refs_3_ = f32[32,128]{1,0:T(8,128)S(1)} collective-permute-done((f32[32,128]{1,0:T(8,128)S(1)}, f32[32,128]{1,0:T(8,128)S(1)}, u32[]{:S(2)}, u32[]{:S(2)}) %collective-permute-start.17) | collective-permute-done | bytes 16416 | tf_op jit(solution)/shard_map/ppermute | solution.py:579
  55.0 2.4 %collective-permute-start.21 = (f32[32,128]{1,0:T(8,128)S(1)}, f32[32,128]{1,0:T(8,128)S(1)}, u32[]{:S(2)}, u32[]{:S(2)}) collective-permute-start(f32[32,128]{1,0:T(8,128)S(1)} %add.4.refs_0_), channel_id=1, source_target_pairs={{0,24},{2,26},{4,28},{6,30},{8,16},{10,18},{12,20},{14,22},{16,8},... | collective-permute-start | bytes 49160 | tf_op jit(solution)/shard_map/ppermute | solution.py:579
  57.6 1.8 %collective-permute-start.19 = (f32[32,128]{1,0:T(8,128)S(1)}, f32[32,128]{1,0:T(8,128)S(1)}, u32[]{:S(2)}, u32[]{:S(2)}) collective-permute-start(f32[32,128]{1,0:T(8,128)S(1)} %add.4.refs_0_), channel_id=1, source_target_pairs={{0,8},{2,10},{4,12},{6,14},{8,0},{10,2},{12,4},{14,6},{16,24},{18,... | collective-permute-start | bytes 49160 | tf_op jit(solution)/shard_map/ppermute | solution.py:579
  59.3 1.1 %collective-permute-done.21.refs_3_ = f32[32,128]{1,0:T(8,128)S(1)} collective-permute-done((f32[32,128]{1,0:T(8,128)S(1)}, f32[32,128]{1,0:T(8,128)S(1)}, u32[]{:S(2)}, u32[]{:S(2)}) %collective-permute-start.21) | collective-permute-done | bytes 16416 | tf_op jit(solution)/shard_map/ppermute | solution.py:579
  60.5 1.5 %collective-permute-done.20.refs_2_ = f32[32,128]{1,0:T(8,128)S(1)} collective-permute-done((f32[32,128]{1,0:T(8,128)S(1)}, f32[32,128]{1,0:T(8,128)S(1)}, u32[]{:S(2)}, u32[]{:S(2)}) %collective-permute-start.20) | collective-permute-done | bytes 16416 | tf_op jit(solution)/shard_map/ppermute | solution.py:579
  62.6 4.4 %polar.5 = (f32[4,64,128]{2,1,0:T(8,128)S(1)}, f32[32,128]{1,0:T(8,128)S(1)}) custom-call(f32[8,64,192]{2,1,0:T(8,128)S(1)} %get-tuple-element.90.after_ref.inside_ref, f32[64,64]{1,0:T(8,128)S(1)} %get-tuple-element.101.delta_ref, f32[4,64,128]{2,1,0:T(8,128)S(1)} %get-tuple-element.102.change_ref, f32[4,64,128]{2,1,0:T(8,128)S(1)} %get-tuple-element.103.old_ref, ...), custom_call_target="tpu_custom_call" | custom-call | flops 330000000 | bytes 1343488 | tf_op jit(solution)/shard_map/polar/pallas_call | solution.py:522
  67.5 1.4 %collective-permute-start.23 = (f32[32,128]{1,0:T(8,128)S(1)}, f32[32,128]{1,0:T(8,128)S(1)}, u32[]{:S(2)}, u32[]{:S(2)}) collective-permute-start(f32[32,128]{1,0:T(8,128)S(1)} %get-tuple-element.110.refs_0_), channel_id=1, source_target_pairs={{0,2},{2,0},{4,6},{6,4},{8,10},{10,8},{12,14},{14,12},{16,18},{18,... | collective-permute-start | bytes 49160 | tf_op jit(solution)/shard_map/ppermute | solution.py:579
  68.9 1.3 %collective-permute-done.25.refs_3_ = f32[32,128]{1,0:T(8,128)S(1)} collective-permute-done((f32[32,128]{1,0:T(8,128)S(1)}, f32[32,128]{1,0:T(8,128)S(1)}, u32[]{:S(2)}, u32[]{:S(2)}) %collective-permute-start.25) | collective-permute-done | bytes 16416 | tf_op jit(solution)/shard_map/ppermute | solution.py:579
  70.9 1.8 %collective-permute-start.28 = (f32[32,128]{1,0:T(8,128)S(1)}, f32[32,128]{1,0:T(8,128)S(1)}, u32[]{:S(2)}, u32[]{:S(2)}) collective-permute-start(f32[32,128]{1,0:T(8,128)S(1)} %add.5.refs_0_), channel_id=1, source_target_pairs={{0,24},{2,26},{4,28},{6,30},{8,16},{10,18},{12,20},{14,22},{16,8},... | collective-permute-start | bytes 49160 | tf_op jit(solution)/shard_map/ppermute | solution.py:579
  72.7 1.2 %collective-permute-start.27 = (f32[32,128]{1,0:T(8,128)S(1)}, f32[32,128]{1,0:T(8,128)S(1)}, u32[]{:S(2)}, u32[]{:S(2)}) collective-permute-start(f32[32,128]{1,0:T(8,128)S(1)} %add.5.refs_0_), channel_id=1, source_target_pairs={{0,16},{2,18},{4,20},{6,22},{8,24},{10,26},{12,28},{14,30},{16,0},... | collective-permute-start | bytes 49160 | tf_op jit(solution)/shard_map/ppermute | solution.py:579
  73.8 1.5 %collective-permute-start.26 = (f32[32,128]{1,0:T(8,128)S(1)}, f32[32,128]{1,0:T(8,128)S(1)}, u32[]{:S(2)}, u32[]{:S(2)}) collective-permute-start(f32[32,128]{1,0:T(8,128)S(1)} %add.5.refs_0_), channel_id=1, source_target_pairs={{0,8},{2,10},{4,12},{6,14},{8,0},{10,2},{12,4},{14,6},{16,24},{18,... | collective-permute-start | bytes 49160 | tf_op jit(solution)/shard_map/ppermute | solution.py:579
  75.3 1.2 %rows.3 = (bf16[8,192,192]{2,1,0:T(8,128)(2,1)S(1)}, f32[8,64,192]{2,1,0:T(8,128)}) custom-call(f32[4,64,128]{2,1,0:T(8,128)S(1)} %get-tuple-element.105.mixed_ref, f32[4,64,128]{2,1,0:T(8,128)S(1)} %get-tuple-element.102.change_ref, f32[4,64,128]{2,1,0:T(8,128)S(1)} %get-tuple-element.106.forward_ref, f32[8,64,192]{2,1,0:T(8,128)S(1)} %get-tuple-element.99.tall_ref, ...), custom_call_target="tpu_custom_call" | custom-call | flops 330000000 | bytes 2162688 | tf_op jit(solution)/shard_map/rows/pallas_call | solution.py:522
  77.6 1.2 %last.1 = (f32[8,64,192]{2,1,0:T(8,128)}, f32[64,64]{1,0:T(8,128)}) custom-call(bf16[8,192,192]{2,1,0:T(8,128)(2,1)S(1)} %get-tuple-element.109.mixed_tall_ref, f32[32,128]{1,0:T(8,128)S(1)} %add.5.refs_0_, f32[32,128]{1,0:T(8,128)S(1)} %collective-permute-done.26.refs_1_, f32[32,128]{1,0:T(8,128)S(1)} %collective-permute-done.27.refs_2_, ...), custom_call_target="tpu_custom_call" | custom-call | flops 330000000 | bytes 1064960 | tf_op jit(solution)/shard_map/last/pallas_call | solution.py:522
  (60 shorter events, 11.0 us)
Async XLA Ops:
  1.6 6.0 %collective-permute-start = (f32[64,64]{1,0:T(8,128)S(1)}, f32[64,64]{1,0:T(8,128)S(1)}, u32[]{:S(2)}, u32[]{:S(2)}) collective-permute-start(f32[64,64]{1,0:T(8,128)S(1)} %get-tuple-element.64.refs_0_), channel_id=1, source_target_pairs={{0,1},{1,0},{2,3},{3,2},{4,5},{5,4},{6,7},{7,6},{8,9},{9,8},{10,11... | collective-permute-start | bytes 49160 | tf_op jit(solution)/shard_map/ppermute | solution.py:536
  4.6 7.1 %copy-start.3 = (f32[8,192,64]{1,2,0:T(8,128)S(1)}, f32[8,192,64]{1,2,0:T(8,128)}, u32[]{:S(2)}) copy-start(f32[8,192,64]{1,2,0:T(8,128)} %param.14) | copy-start | bytes 1179652
  4.6 7.1 %copy-start.4 = (s32[8]{0:T(128)S(1)}, s32[8]{0:T(128)}, u32[]{:S(2)}) copy-start(s32[8]{0:T(128)} %order_ref.5) | copy-start | bytes 100
  7.7 10.6 %collective-permute-start.3 = (f32[4,192,128]{2,1,0:T(8,128)S(1)}, f32[4,192,128]{2,1,0:T(8,128)S(1)}, u32[]{:S(2)}, u32[]{:S(2)}) collective-permute-start(f32[4,192,128]{2,1,0:T(8,128)S(1)} %get-tuple-element.68), channel_id=1, source_target_pairs={{0,1},{1,0},{2,3},{3,2},{4,5},{5,4},{6,7},{7,6},{8,9},{9,8},{10,11... | collective-permute-start | bytes 1179656 | tf_op jit(solution)/shard_map/ppermute | solution.py:536
  8.5 6.0 %collective-permute-start.2 = (f32[8,64]{1,0:T(8,128)S(1)}, f32[8,64]{1,0:T(8,128)S(1)}, u32[]{:S(2)}, u32[]{:S(2)}) collective-permute-start(f32[8,64]{1,0:T(8,128)S(1)} %copy-done.5), channel_id=1, source_target_pairs={{0,30},{2,0},{4,2},{6,4},{8,6},{10,8},{12,10},{14,12},{16,14},{18,... | collective-permute-start | bytes 6152 | tf_op jit(solution)/shard_map/ppermute | solution.py:536
  11.7 5.7 %collective-permute-start.1 = (f32[8,64]{1,0:T(8,128)S(1)}, f32[8,64]{1,0:T(8,128)S(1)}, u32[]{:S(2)}, u32[]{:S(2)}) collective-permute-start(f32[8,64]{1,0:T(8,128)S(1)} %copy-done.5), channel_id=1, source_target_pairs={{0,2},{2,4},{4,6},{6,8},{8,10},{10,12},{12,14},{14,16},{16,18},{18... | collective-permute-start | bytes 6152 | tf_op jit(solution)/shard_map/ppermute | solution.py:536
  11.7 14.5 %copy-start.7 = (f32[64,64]{1,0:T(8,128)S(1)}, f32[64,64]{1,0:T(8,128)}, u32[]{:S(2)}) copy-start(f32[64,64]{1,0:T(8,128)} %delta_ref.1) | copy-start | bytes 49156
  19.7 6.6 %collective-permute-start.4 = (f32[4,64,128]{2,1,0:T(8,128)S(1)}, f32[4,64,128]{2,1,0:T(8,128)S(1)}, u32[]{:S(2)}, u32[]{:S(2)}) collective-permute-start(f32[4,64,128]{2,1,0:T(8,128)S(1)} %get-tuple-element.74.refs_0_), channel_id=1, source_target_pairs={{0,1},{1,0},{2,3},{3,2},{4,5},{5,4},{6,7},{7,6},{8,9},{9,8},{10,11... | collective-permute-start | bytes 393224 | tf_op jit(solution)/shard_map/ppermute | solution.py:536
  21.6 10.4 %collective-permute-start.5 = (f32[4,64,192]{2,1,0:T(8,128)S(1)}, f32[4,64,192]{2,1,0:T(8,128)S(1)}, u32[]{:S(2)}, u32[]{:S(2)}) collective-permute-start(f32[4,64,192]{2,1,0:T(8,128)S(1)} %get-tuple-element.76), channel_id=1, source_target_pairs={{0,2},{4,6},{8,10},{12,14},{16,18},{20,22},{24,26},{28,30},{2,0},{... | collective-permute-start | bytes 589832 | tf_op jit(solution)/shard_map/ppermute | solution.py:542
  21.7 10.3 %collective-permute-start.6 = (f32[4,64,192]{2,1,0:T(8,128)S(1)}, f32[4,64,192]{2,1,0:T(8,128)S(1)}, u32[]{:S(2)}, u32[]{:S(2)}) collective-permute-start(f32[4,64,192]{2,1,0:T(8,128)S(1)} %get-tuple-element.77), channel_id=1, source_target_pairs={{2,4},{6,8},{10,12},{14,16},{18,20},{22,24},{26,28},{30,0},{4,2},{... | collective-permute-start | bytes 589832 | tf_op jit(solution)/shard_map/ppermute | solution.py:542
  30.1 3.2 %collective-permute-start.9 = (f32[32,128]{1,0:T(8,128)S(1)}, f32[32,128]{1,0:T(8,128)S(1)}, u32[]{:S(2)}, u32[]{:S(2)}) collective-permute-start(f32[32,128]{1,0:T(8,128)S(1)} %get-tuple-element.75.after_ref.refs_1_), channel_id=1, source_target_pairs={{0,6},{2,4},{4,2},{6,0},{8,14},{10,12},{12,10},{14,8},{16,22},{18,... | collective-permute-start | bytes 49160 | tf_op jit(solution)/shard_map/ppermute | solution.py:579
  30.1 3.8 %collective-permute-start.8 = (f32[32,128]{1,0:T(8,128)S(1)}, f32[32,128]{1,0:T(8,128)S(1)}, u32[]{:S(2)}, u32[]{:S(2)}) collective-permute-start(f32[32,128]{1,0:T(8,128)S(1)} %get-tuple-element.75.after_ref.refs_1_), channel_id=1, source_target_pairs={{0,4},{2,6},{4,0},{6,2},{8,12},{10,14},{12,8},{14,10},{16,20},{18,... | collective-permute-start | bytes 49160 | tf_op jit(solution)/shard_map/ppermute | solution.py:579
  30.2 3.7 %collective-permute-start.7 = (f32[32,128]{1,0:T(8,128)S(1)}, f32[32,128]{1,0:T(8,128)S(1)}, u32[]{:S(2)}, u32[]{:S(2)}) collective-permute-start(f32[32,128]{1,0:T(8,128)S(1)} %get-tuple-element.75.after_ref.refs_1_), channel_id=1, source_target_pairs={{0,2},{2,0},{4,6},{6,4},{8,10},{10,8},{12,14},{14,12},{16,18},{18,... | collective-permute-start | bytes 49160 | tf_op jit(solution)/shard_map/ppermute | solution.py:579
  33.9 11.2 %collective-permute-start.13 = (f32[4,64,256]{2,1,0:T(8,128)S(1)}, f32[4,64,256]{2,1,0:T(8,128)S(1)}, u32[]{:S(2)}, u32[]{:S(2)}) collective-permute-start(f32[4,64,256]{2,1,0:T(8,128)S(1)} %get-tuple-element.93.refs_0_), channel_id=1, source_target_pairs={{0,1},{1,0},{2,3},{3,2},{4,5},{5,4},{6,7},{7,6},{8,9},{9,8},{10,11... | collective-permute-start | bytes 786440 | tf_op jit(solution)/shard_map/ppermute | solution.py:536
  35.4 5.5 %collective-permute-start.12 = (f32[32,128]{1,0:T(8,128)S(1)}, f32[32,128]{1,0:T(8,128)S(1)}, u32[]{:S(2)}, u32[]{:S(2)}) collective-permute-start(f32[32,128]{1,0:T(8,128)S(1)} %add.3.refs_0_), channel_id=1, source_target_pairs={{0,24},{2,26},{4,28},{6,30},{8,16},{10,18},{12,20},{14,22},{16,8},... | collective-permute-start | bytes 49160 | tf_op jit(solution)/shard_map/ppermute | solution.py:579
  36.5 4.8 %collective-permute-start.11 = (f32[32,128]{1,0:T(8,128)S(1)}, f32[32,128]{1,0:T(8,128)S(1)}, u32[]{:S(2)}, u32[]{:S(2)}) collective-permute-start(f32[32,128]{1,0:T(8,128)S(1)} %add.3.refs_0_), channel_id=1, source_target_pairs={{0,16},{2,18},{4,20},{6,22},{8,24},{10,26},{12,28},{14,30},{16,0},... | collective-permute-start | bytes 49160 | tf_op jit(solution)/shard_map/ppermute | solution.py:579
  36.7 4.8 %collective-permute-start.10 = (f32[32,128]{1,0:T(8,128)S(1)}, f32[32,128]{1,0:T(8,128)S(1)}, u32[]{:S(2)}, u32[]{:S(2)}) collective-permute-start(f32[32,128]{1,0:T(8,128)S(1)} %add.3.refs_0_), channel_id=1, source_target_pairs={{0,8},{2,10},{4,12},{6,14},{8,0},{10,2},{12,4},{14,6},{16,24},{18,... | collective-permute-start | bytes 49160 | tf_op jit(solution)/shard_map/ppermute | solution.py:579
  42.8 8.6 %collective-permute-start.14 = (f32[4,64,192]{2,1,0:T(8,128)S(1)}, f32[4,64,192]{2,1,0:T(8,128)S(1)}, u32[]{:S(2)}, u32[]{:S(2)}) collective-permute-start(f32[4,64,192]{2,1,0:T(8,128)S(1)} %get-tuple-element.96), channel_id=1, source_target_pairs={{0,2},{4,6},{8,10},{12,14},{16,18},{20,22},{24,26},{28,30},{2,0},{... | collective-permute-start | bytes 589832 | tf_op jit(solution)/shard_map/ppermute | solution.py:542
  42.9 8.7 %collective-permute-start.15 = (f32[4,64,192]{2,1,0:T(8,128)S(1)}, f32[4,64,192]{2,1,0:T(8,128)S(1)}, u32[]{:S(2)}, u32[]{:S(2)}) collective-permute-start(f32[4,64,192]{2,1,0:T(8,128)S(1)} %get-tuple-element.97), channel_id=1, source_target_pairs={{2,4},{6,8},{10,12},{14,16},{18,20},{22,24},{26,28},{30,0},{4,2},{... | collective-permute-start | bytes 589832 | tf_op jit(solution)/shard_map/ppermute | solution.py:542
  49.5 3.5 %collective-permute-start.18 = (f32[32,128]{1,0:T(8,128)S(1)}, f32[32,128]{1,0:T(8,128)S(1)}, u32[]{:S(2)}, u32[]{:S(2)}) collective-permute-start(f32[32,128]{1,0:T(8,128)S(1)} %get-tuple-element.95.after_ref.refs_1_), channel_id=1, source_target_pairs={{0,6},{2,4},{4,2},{6,0},{8,14},{10,12},{12,10},{14,8},{16,22},{18,... | collective-permute-start | bytes 49160 | tf_op jit(solution)/shard_map/ppermute | solution.py:579
  50.6 3.7 %collective-permute-start.17 = (f32[32,128]{1,0:T(8,128)S(1)}, f32[32,128]{1,0:T(8,128)S(1)}, u32[]{:S(2)}, u32[]{:S(2)}) collective-permute-start(f32[32,128]{1,0:T(8,128)S(1)} %get-tuple-element.95.after_ref.refs_1_), channel_id=1, source_target_pairs={{0,4},{2,6},{4,0},{6,2},{8,12},{10,14},{12,8},{14,10},{16,20},{18,... | collective-permute-start | bytes 49160 | tf_op jit(solution)/shard_map/ppermute | solution.py:579
  50.6 3.7 %collective-permute-start.16 = (f32[32,128]{1,0:T(8,128)S(1)}, f32[32,128]{1,0:T(8,128)S(1)}, u32[]{:S(2)}, u32[]{:S(2)}) collective-permute-start(f32[32,128]{1,0:T(8,128)S(1)} %get-tuple-element.95.after_ref.refs_1_), channel_id=1, source_target_pairs={{0,2},{2,0},{4,6},{6,4},{8,10},{10,8},{12,14},{14,12},{16,18},{18,... | collective-permute-start | bytes 49160 | tf_op jit(solution)/shard_map/ppermute | solution.py:579
  54.4 8.2 %collective-permute-start.22 = (f32[4,64,256]{2,1,0:T(8,128)S(1)}, f32[4,64,256]{2,1,0:T(8,128)S(1)}, u32[]{:S(2)}, u32[]{:S(2)}) collective-permute-start(f32[4,64,256]{2,1,0:T(8,128)S(1)} %get-tuple-element.104.refs_0_), channel_id=1, source_target_pairs={{0,1},{1,0},{2,3},{3,2},{4,5},{5,4},{6,7},{7,6},{8,9},{9,8},{10,11... | collective-permute-start | bytes 786440 | tf_op jit(solution)/shard_map/ppermute | solution.py:536
  55.0 5.5 %collective-permute-start.21 = (f32[32,128]{1,0:T(8,128)S(1)}, f32[32,128]{1,0:T(8,128)S(1)}, u32[]{:S(2)}, u32[]{:S(2)}) collective-permute-start(f32[32,128]{1,0:T(8,128)S(1)} %add.4.refs_0_), channel_id=1, source_target_pairs={{0,24},{2,26},{4,28},{6,30},{8,16},{10,18},{12,20},{14,22},{16,8},... | collective-permute-start | bytes 49160 | tf_op jit(solution)/shard_map/ppermute | solution.py:579
  57.4 4.6 %collective-permute-start.20 = (f32[32,128]{1,0:T(8,128)S(1)}, f32[32,128]{1,0:T(8,128)S(1)}, u32[]{:S(2)}, u32[]{:S(2)}) collective-permute-start(f32[32,128]{1,0:T(8,128)S(1)} %add.4.refs_0_), channel_id=1, source_target_pairs={{0,16},{2,18},{4,20},{6,22},{8,24},{10,26},{12,28},{14,30},{16,0},... | collective-permute-start | bytes 49160 | tf_op jit(solution)/shard_map/ppermute | solution.py:579
  57.6 4.4 %collective-permute-start.19 = (f32[32,128]{1,0:T(8,128)S(1)}, f32[32,128]{1,0:T(8,128)S(1)}, u32[]{:S(2)}, u32[]{:S(2)}) collective-permute-start(f32[32,128]{1,0:T(8,128)S(1)} %add.4.refs_0_), channel_id=1, source_target_pairs={{0,8},{2,10},{4,12},{6,14},{8,0},{10,2},{12,4},{14,6},{16,24},{18,... | collective-permute-start | bytes 49160 | tf_op jit(solution)/shard_map/ppermute | solution.py:579
  67.0 3.2 %collective-permute-start.25 = (f32[32,128]{1,0:T(8,128)S(1)}, f32[32,128]{1,0:T(8,128)S(1)}, u32[]{:S(2)}, u32[]{:S(2)}) collective-permute-start(f32[32,128]{1,0:T(8,128)S(1)} %get-tuple-element.110.refs_0_), channel_id=1, source_target_pairs={{0,6},{2,4},{4,2},{6,0},{8,14},{10,12},{12,10},{14,8},{16,22},{18,... | collective-permute-start | bytes 49160 | tf_op jit(solution)/shard_map/ppermute | solution.py:579
  67.0 3.8 %collective-permute-start.24 = (f32[32,128]{1,0:T(8,128)S(1)}, f32[32,128]{1,0:T(8,128)S(1)}, u32[]{:S(2)}, u32[]{:S(2)}) collective-permute-start(f32[32,128]{1,0:T(8,128)S(1)} %get-tuple-element.110.refs_0_), channel_id=1, source_target_pairs={{0,4},{2,6},{4,0},{6,2},{8,12},{10,14},{12,8},{14,10},{16,20},{18,... | collective-permute-start | bytes 49160 | tf_op jit(solution)/shard_map/ppermute | solution.py:579
  67.5 3.4 %collective-permute-start.23 = (f32[32,128]{1,0:T(8,128)S(1)}, f32[32,128]{1,0:T(8,128)S(1)}, u32[]{:S(2)}, u32[]{:S(2)}) collective-permute-start(f32[32,128]{1,0:T(8,128)S(1)} %get-tuple-element.110.refs_0_), channel_id=1, source_target_pairs={{0,2},{2,0},{4,6},{6,4},{8,10},{10,8},{12,14},{14,12},{16,18},{18,... | collective-permute-start | bytes 49160 | tf_op jit(solution)/shard_map/ppermute | solution.py:579
  70.9 5.7 %collective-permute-start.28 = (f32[32,128]{1,0:T(8,128)S(1)}, f32[32,128]{1,0:T(8,128)S(1)}, u32[]{:S(2)}, u32[]{:S(2)}) collective-permute-start(f32[32,128]{1,0:T(8,128)S(1)} %add.5.refs_0_), channel_id=1, source_target_pairs={{0,24},{2,26},{4,28},{6,30},{8,16},{10,18},{12,20},{14,22},{16,8},... | collective-permute-start | bytes 49160 | tf_op jit(solution)/shard_map/ppermute | solution.py:579
  72.7 4.6 %collective-permute-start.27 = (f32[32,128]{1,0:T(8,128)S(1)}, f32[32,128]{1,0:T(8,128)S(1)}, u32[]{:S(2)}, u32[]{:S(2)}) collective-permute-start(f32[32,128]{1,0:T(8,128)S(1)} %add.5.refs_0_), channel_id=1, source_target_pairs={{0,16},{2,18},{4,20},{6,22},{8,24},{10,26},{12,28},{14,30},{16,0},... | collective-permute-start | bytes 49160 | tf_op jit(solution)/shard_map/ppermute | solution.py:579
  73.8 3.7 %collective-permute-start.26 = (f32[32,128]{1,0:T(8,128)S(1)}, f32[32,128]{1,0:T(8,128)S(1)}, u32[]{:S(2)}, u32[]{:S(2)}) collective-permute-start(f32[32,128]{1,0:T(8,128)S(1)} %add.5.refs_0_), channel_id=1, source_target_pairs={{0,8},{2,10},{4,12},{6,14},{8,0},{10,2},{12,4},{14,6},{16,24},{18,... | collective-permute-start | bytes 49160 | tf_op jit(solution)/shard_map/ppermute | solution.py:579
  (5 other events, 26.0 us)

commit v6 on v5

--- a/solution.py
+++ b/solution.py
@@ -92,29 +92,28 @@
     return group
 
 
-def factor_kernel(factor_ref, gram_ref, again_ref):
-    factor = factor_ref[...]
-    gram_ref[...] = dot(factor, factor, NT)
-    again_ref[...] = factor
-
-
-def project_kernel(me_ref, data_ref, factor_ref, *refs):
+def project_kernel(first, pairs, rows, lead, me_ref, data_ref, factor_ref, *refs):
     *outs, held, arrived = refs
-    parts = len(outs)
-    pairs, rows, _ = outs[0].shape
-    count, all_rows, _ = data_ref.shape
-    half = all_rows // 2
+    half = data_ref.shape[1] // 2
     copies = []
-    for k in range(count):
+    for k in range(2 * pairs):
         for at in range(2):
             place = pl.ds(at * half, half)
             copies.append(
                 pltpu.make_async_copy(
-                    data_ref.at[k, place, :], held.at[k, place, :], arrived.at[2 * k + at]
+                    data_ref.at[first + k, place, :], held.at[k, place, :], arrived.at[2 * k + at]
                 )
             )
             copies[-1].start()
     factor = factor_ref[...]
+    rank = factor.shape[0]
+    if lead:
+        *outs, again_ref = outs
+        again_ref[...] = factor
+        gram = dot(factor, factor, NT)
+        for out in outs:
+            out[pairs * rows :, :] = jnp.concatenate([gram[: rank // 2], gram[rank // 2 :]], axis=1)
+    parts = len(outs)
     empty = jnp.zeros_like(factor)
     sides = [
         jnp.concatenate([factor, empty], axis=0),
@@ -126,19 +125,18 @@
         for part in reversed(range(parts)):
             start = pl.multiple_of(lax.rem(me_ref[0] + part, parts) * rows, 16)
             place = pl.ds(start, rows)
-            outs[part][pair] = dot(held[2 * pair, place, :], sides[0], NT) + dot(
-                held[2 * pair + 1, place, :], sides[1], NT
-            )
-
-
-def setup_kernel(grams, group, order_ref, *refs):
-    gram_refs, refs = refs[:grams], refs[grams:]
+            outs[part][pair * rows : (pair + 1) * rows, :] = dot(
+                held[2 * pair, place, :], sides[0], NT
+            ) + dot(held[2 * pair + 1, place, :], sides[1], NT)
+
+
+def setup_kernel(parts, first, group, order_ref, *refs):
+    lead_refs, refs = refs[:parts], refs[parts:]
     (own_ref, aux_ref, coupled_ref, dual_s_ref, dual_c_ref) = refs[:5]
     (inverse_ref, mover_ref, rho_ref, diagonal_ref, columns_ref, base_ref) = refs[5:]
     count, rank = own_ref.shape
-    gram = gram_refs[0][...]
-    for ref in gram_refs[1:]:
-        gram = gram + ref[...]
+    gram = summed(lead_refs, slice(first, None))
+    gram = jnp.concatenate([gram[:, :rank], gram[:, rank:]], axis=0)
     eye = wide_eye(rank, 1)
     diagonal = jnp.sum(gram * eye, axis=0, keepdims=True)
     diagonal_ref[...] = jnp.broadcast_to(diagonal, diagonal_ref.shape)
@@ -223,13 +221,30 @@
     return lax.div(stored, 2), pl.ds(pl.multiple_of(lax.rem(stored, 2) * rank, rank), rank)
 
 
+def move(mover, projected):
+    high, low = split(projected)
+    return dot(mover, jnp.concatenate([high, low, high], axis=1), NT)
+
+
+def move_kernel(mover_ref, *refs):
+    *projected_refs, moved_ref, turned_ref = refs
+    rows = moved_ref.shape[2]
+    for pair in range(moved_ref.shape[0]):
+        projected = summed(projected_refs, slice(pair * rows, (pair + 1) * rows))
+        moved_ref[pair] = move(mover_ref[pair], projected)
+        turned_ref[pair] = projected.T
+
+
 def first_kernel(group, order_ref, *refs):
-    base_ref, mover_ref, dual_s_ref, dual_c_ref = refs[2:6]
-    *projected_refs, tall_ref, target_ref, gram_ref, moved = refs[6:]
+    base_ref, mover_ref, dual_s_ref, dual_c_ref, early_ref = refs[2:7]
+    *projected_refs, tall_ref, target_ref, gram_ref, moved = refs[7:]
     count, rank, rows = base_ref.shape
-    for pair in range(count // 2):
-        high, low = split(summed(projected_refs, pair))
-        moved[pair] = dot(mover_ref[pair], jnp.concatenate([high, low, high], axis=1), NT)
+    early = early_ref.shape[0]
+    for pair in range(early):
+        moved[pair] = early_ref[pair]
+    for pair in range(early, count // 2):
+        place = slice((pair - early) * rows, (pair - early + 1) * rows)
+        moved[pair] = move(mover_ref[pair], summed(projected_refs, place))
     talls = []
     for k in range(count):
         pair, place = stored_place(order_ref, k, count, rank)
@@ -275,7 +290,7 @@
 
 def smooth_kernel(
     odd_ref, order_ref, aux_ref, target_ref, before_ref, rho_ref, after_ref, diagonal_ref,
-    columns_ref, *refs
+    columns_ref, early_ref, *refs
 ):
     *projected_refs, side_ref, past_ref, next_ref, inside_ref, near_ref, far_ref, turned = refs
     count, rank, rows = aux_ref.shape
@@ -289,8 +304,12 @@
         odd_ref[0], [aux_ref[k] for k in slices], [target_ref[k] for k in slices], rho,
         inside_ref, near_ref, far_ref,
     )
-    for pair in range(count // 2):
-        turned[pair] = summed(projected_refs, pair).T
+    early = early_ref.shape[0]
+    for pair in range(early):
+        turned[pair] = early_ref[pair]
+    for pair in range(early, count // 2):
+        place = slice((pair - early) * rows, (pair - early + 1) * rows)
+        turned[pair] = summed(projected_refs, place).T
     for k in slices:
         pair, place = stored_place(order_ref, k, count, rank)
         side_ref[k] = columns_ref[:, k : k + 1] * turned[pair, place, :]
@@ -301,17 +320,21 @@
     group = wide // rank
     mask = block_mask(rank, group)
     eye = wide_eye(rank, group)
-    delta_blocks = block_diagonal(jnp.concatenate([delta] * group, axis=1), mask, group, NT)
-    currents, roots, scales = [], [], []
-    for left in from_left(delta, grams):
-        (normal,) = times_blocks([left], delta_blocks, NT)
-        line = jnp.broadcast_to(jnp.sum(normal * eye, axis=0, keepdims=True), (16, wide))
+    delta_wide = jnp.concatenate([delta] * group, axis=1)
+    delta_blocks = block_diagonal(delta_wide, mask, group, NT)
+    (across,) = from_left(delta.T, [delta_wide])
+    traces = []
+    for gram in grams:
+        line = jnp.broadcast_to(jnp.sum(across * gram, axis=0, keepdims=True), (16, wide))
         high, low = split(line)
         rest = (line - high.astype(f32) - low.astype(f32)).astype(bf16)
         line = dot(high, mask) + dot(low, mask) + dot(rest, mask)
-        trace = line[0:1] + eps_trace
-        currents.append(normal / trace)
-        scales.append(1.0 / jnp.sqrt(trace))
+        traces.append(line[0:1] + eps_trace)
+    rights = [times_blocks([gram], delta_blocks, NT)[0] for gram in grams]
+    normals = from_left(delta, rights)
+    currents = [normal / trace for normal, trace in zip(normals, traces)]
+    scales = [1.0 / jnp.sqrt(trace) for trace in traces]
+    roots = []
     for step in range(POLAR):
         for at in range(len(grams)):
             product = currents[at]
@@ -329,24 +352,24 @@
                 half = 1.5 * product - 0.5 * square
                 (more,) = times_blocks([half], blocks)
                 currents[at] = 1.5 * half - 0.5 * more
-    return roots, scales
-
-
-def mix(roots, scales, grams, delta, mixed_ref, partial_ref):
+    return roots, scales, rights
+
+
+def mix(roots, scales, rights, delta, mixed_ref, partial_ref):
     rank, wide = roots[0].shape
     group = wide // rank
     mask = block_mask(rank, group)
     delta_blocks = block_diagonal(jnp.concatenate([delta] * group, axis=1), mask, group)
     left, right = [], []
     for at in range(len(roots)):
-        (mixed,) = times_blocks([roots[at]], delta_blocks)
-        mixed = mixed * scales[at]
-        mixed_ref[at] = mixed
-        high, low = split(mixed)
+        high, low = split(roots[at] * scales[at])
         left += [high, high, low]
-        high, low = split(grams[at])
+        high, low = split(rights[at])
         right += [high, low, high]
     partial = dot(jnp.concatenate(left, axis=1), jnp.concatenate(right, axis=1), NT)
+    for at in range(len(roots)):
+        (mixed,) = times_blocks([roots[at]], delta_blocks)
+        mixed_ref[at] = mixed * scales[at]
     half = rank // 2
     partial_ref[...] = jnp.concatenate([partial[:half], partial[half:]], axis=1)
 
@@ -357,8 +380,7 @@
     for at in range(len(grams)):
         gram_ref[at] = grams[at]
     delta = delta_ref[...]
-    roots, scales = polar(grams, delta)
-    mix(roots, scales, grams, delta, mixed_ref, partial_ref)
+    mix(*polar(grams, delta), delta, mixed_ref, partial_ref)
 
 
 def later_polar_kernel(last, after_ref, delta_ref, change_ref, old_ref, *refs):
@@ -381,8 +403,7 @@
         if not last:
             gram_ref[at] = grams[at]
     delta = delta_ref[...]
-    roots, scales = polar(grams, delta)
-    mix(roots, scales, grams, delta, mixed_ref, partial_ref)
+    mix(*polar(grams, delta), delta, mixed_ref, partial_ref)
 
 
 def ahead_kernel(
@@ -605,30 +626,31 @@
 
     me = lax.axis_index("chan").astype(jnp.int32).reshape(1)
     odd = lax.rem(lax.axis_index("cuts"), 2).astype(jnp.int32).reshape(1)
-    gram_part, factor = call(
-        factor_kernel, "factor", [square, (factor.shape, factor.dtype)], factor
-    )
-    grams = [gram_part] + from_others(gram_part, "chan")
-    projected = call(
-        project_kernel,
-        "project",
-        [((count // 2, rows, 2 * rank), f32)] * parts,
-        me, data, factor,
-        scalars=1, unread=1, microseconds=2, limit=52,
-        scratch=[
-            pltpu.VMEM((count, all_rows, channels), data.dtype),
-            pltpu.SemaphoreType.DMA((2 * count,)),
-        ],
-    )
-    projected, grams = lax.optimization_barrier((projected, grams))
-    own = projected[0]
-    received = [rotated(projected[shift], "chan", shift) for shift in range(1, parts)]
-
-    late_weights, _ = lax.optimization_barrier((slice_weights, own))
+    early = count // 4
+    own, received = [], []
+    for first, pairs, lead in ((0, early, True), (2 * early, count // 2 - early, False)):
+        height = pairs * rows + (rank // 2 if lead else 0)
+        projected = call(
+            functools.partial(project_kernel, first, pairs, rows, lead),
+            "project",
+            [((height, 2 * rank), f32)] * parts + [(factor.shape, factor.dtype)] * lead,
+            me, data, factor,
+            scalars=1, unread=1, limit=52,
+            scratch=[
+                pltpu.VMEM((2 * pairs, all_rows, channels), data.dtype),
+                pltpu.SemaphoreType.DMA((4 * pairs,)),
+            ],
+        )
+        if lead:
+            *projected, factor = projected
+        own.append(projected[0])
+        received.append([rotated(projected[shift], "chan", shift) for shift in range(1, parts)])
+
+    late_weights, _ = lax.optimization_barrier((slice_weights, own[-1]))
     before = rotated(late_weights, "cuts", 1)
     after = rotated(late_weights, "cuts", -1)
     inverse, mover, rho, diagonal, columns, base = call(
-        functools.partial(setup_kernel, len(grams), group),
+        functools.partial(setup_kernel, parts, early * rows, group),
         "setup",
         [
             ((count, rank, 3 * rank), bf16),
@@ -638,14 +660,18 @@
             ((rank, count), f32),
             state,
         ],
-        order, *grams, slice_weights, aux, coup, dual_s, dual_c,
+        order, own[0], *received[0], slice_weights, aux, coup, dual_s, dual_c,
         scalars=1,
+    )
+    half_state = ((early, 2 * rank, rows), f32)
+    moved, turned = call(
+        move_kernel, "move", [half_state, half_state], mover, own[0], *received[0]
     )
     tall, target, gram = call(
         functools.partial(first_kernel, group),
         "first",
         [state, state, quads],
-        order, before, after, base, mover, dual_s, dual_c, own, *received,
+        order, before, after, base, mover, dual_s, dual_c, moved, own[1], *received[1],
         scalars=1, unread=2,
         scratch=[pltpu.VMEM((count // 2, 2 * rank, rows), f32)],
     )
@@ -653,7 +679,8 @@
         smooth_kernel,
         "smooth",
         [state, lanes(count), lanes(count), state, halo, halo],
-        odd, order, aux, target, before, rho, after, diagonal, columns, own, *received,
+        odd, order, aux, target, before, rho, after, diagonal, columns, turned, own[1],
+        *received[1],
         scalars=2,
         scratch=[pltpu.VMEM((count // 2, 2 * rank, rows), f32)],
     )

time: 79 us -> 76.6 us (0.970)
  waiting for transfers between devices: 13.3 us -> 11.9 us
    ppermute x4, starting transfers between devices: 6.91 us -> 5.43 us  [swapped(): return lax.ppermute(value, axis, pairs + [(b, a) for a, b in pairs])]
    ppermute x7, waiting for transfers between devices: 3.71 us -> 2.5 us  [rotated(): lax.ppermute(value, axis, [(i, (i + shift) % count) for i in range(count)])]
    ppermute x18, waiting for transfers between devices: 9.44 us -> 8.39 us  [in_stages(): terms.append(lax.ppermute(value, axis, moves))]
    ppermute x7, starting transfers between devices: 9.75 us -> 10.6 us  [rotated(): lax.ppermute(value, axis, [(i, (i + shift) % count) for i in range(count)])]
    ppermute x4, waiting for transfers between devices: 0.17 us -> 0.96 us  [swapped(): return lax.ppermute(value, axis, pairs + [(b, a) for a, b in pairs])]
    pallas_call x18 -> x19, Pallas kernels: 28.1 us -> 27.8 us  [call(): pl.pallas_call(kernel, out_shape=shapes, in_specs=specs, out_specs=[pl.Bl...]
  transfers between devices with their start and end apart: 29 -> 29, of which waited for: 15 -> 13; matrix products, arithmetic and copies ran while one was open for 0% -> 0% of each run, Pallas kernels for 27% -> 25%
where the time goes in v6:
time: 76.6 us; the launch traced here: 76.4 us
  starting transfers between devices  35 us (46%)
  Pallas kernels  27.8 us (36%)
  waiting for transfers between devices  11.9 us (16%)
  between operations  0.91 us (1%)
  local copies, waits for them, and re-layouts  0.86 us (1%)
    pallas_call x19, Pallas kernels, call(): pl.pallas_call(kernel, out_shape=shapes, in_specs=specs, out_specs=[pl.Bl...  27.8 us
    ppermute x18, starting transfers between devices, in_stages(): terms.append(lax.ppermute(value, axis, moves))  18.9 us
    ppermute x7, starting transfers between devices, rotated(): lax.ppermute(value, axis, [(i, (i + shift) % count) for i in range(count)])  10.6 us
    ppermute x18, waiting for transfers between devices, in_stages(): terms.append(lax.ppermute(value, axis, moves))  8.39 us
    ppermute x4, starting transfers between devices, swapped(): return lax.ppermute(value, axis, pairs + [(b, a) for a, b in pairs])  5.43 us
    ppermute x7, waiting for transfers between devices, rotated(): lax.ppermute(value, axis, [(i, (i + shift) % count) for i in range(count)])  2.5 us
  transfers between devices with their start and end apart: 29, of which 13 were waited for; matrix products, arithmetic and copies ran while one was open for 0% of the time, Pallas kernels for 25%

profile of v6, /device:TPU:0, one launch (start us, length us, event | category | flops | bytes accessed | tf_op | source)
XLA Modules:
  0.0 76.4 jit_solution(3097453747694575248)
XLA Ops:
  1.5 2.2 %project.2 = (f32[416,128]{1,0:T(8,128)S(1)}, f32[416,128]{1,0:T(8,128)S(1)}, bf16[64,512]{1,0:T(8,128)(2,1)S(1)}) custom-call(s32[1]{0:T(128)} %bitcast.2.me_ref, bf16[8,384,512]{2,1,0:T(8,128)(2,1)} %data_ref.3, bf16[64,512]{1,0:T(8,128)(2,1)S(1)} %bitcast.16), custom_call_target="tpu_custom_call" | custom-call | flops 330000000 | bytes 3702788 | tf_op jit(solution)/shard_map/project/pallas_call | solution.py:543
  3.7 3.0 %collective-permute-start.2 = (f32[416,128]{1,0:T(8,128)S(1)}, f32[416,128]{1,0:T(8,128)S(1)}, u32[]{:S(2)}, u32[]{:S(2)}) collective-permute-start(f32[416,128]{1,0:T(8,128)S(1)} %get-tuple-element.61), channel_id=1, source_target_pairs={{0,1},{1,0},{2,3},{3,2},{4,5},{5,4},{6,7},{7,6},{8,9},{9,8},{10,11... | collective-permute-start | bytes 638984 | tf_op jit(solution)/shard_map/ppermute | solution.py:557
  6.7 2.0 %project.3 = (f32[384,128]{1,0:T(8,128)S(1)}, f32[384,128]{1,0:T(8,128)S(1)}) custom-call(s32[1]{0:T(128)} %bitcast.2.me_ref, bf16[8,384,512]{2,1,0:T(8,128)(2,1)} %data_ref.3, bf16[64,512]{1,0:T(8,128)(2,1)S(1)} %get-tuple-element.57.factor_ref), custom_call_target="tpu_custom_call" | custom-call | flops 330000000 | bytes 3604484 | tf_op jit(solution)/shard_map/project/pallas_call | solution.py:543
  8.8 4.0 %collective-permute-start.1 = (f32[8,64]{1,0:T(8,128)S(1)}, f32[8,64]{1,0:T(8,128)S(1)}, u32[]{:S(2)}, u32[]{:S(2)}) collective-permute-start(f32[8,64]{1,0:T(8,128)S(1)} %copy-done.6), channel_id=1, source_target_pairs={{0,30},{2,0},{4,2},{6,4},{8,6},{10,8},{12,10},{14,12},{16,14},{18,... | collective-permute-start | bytes 6152 | tf_op jit(solution)/shard_map/ppermute | solution.py:557
  12.8 2.9 %setup.1 = (bf16[8,64,192]{2,1,0:T(8,128)(2,1)S(1)}, bf16[4,128,384]{2,1,0:T(8,128)(2,1)S(1)}, f32[8,128]{1,0:T(8,128)S(1)}, f32[8,64]{1,0:T(8,128)S(1)}, f32[64...) custom-call(s32[8]{0:T(128)S(1)} %copy-done.5, f32[416,128]{1,0:T(8,128)S(1)} %get-tuple-element.60.refs_0_, ...), custom_call_target="tpu_custom_call" | custom-call | flops 330000000 | bytes 2992160 | tf_op jit(solution)/shard_map/setup/pallas_call | solution.py:543
  16.0 2.5 %collective-permute-done.refs_0_.before_ref = f32[8,64]{1,0:T(8,128)S(1)} collective-permute-done((f32[8,64]{1,0:T(8,128)S(1)}, f32[8,64]{1,0:T(8,128)S(1)}, u32[]{:S(2)}, u32[]{:S(2)}) %collective-permute-start) | collective-permute-done | bytes 2080 | tf_op jit(solution)/shard_map/ppermute | solution.py:557
  18.5 1.2 %first.1 = (f32[8,64,192]{2,1,0:T(8,128)S(1)}, f32[8,64,192]{2,1,0:T(8,128)S(1)}, f32[4,64,128]{2,1,0:T(8,128)S(1)}) custom-call(s32[8]{0:T(128)S(1)} %copy-done.5, f32[8,64]{1,0:T(8,128)S(1)} %collective-permute-done.refs_0_.before_ref, f32[8,64]{1,0:T(8,128)S(1)} %collective-permute-done.1.refs_1_.after_ref, f32[8,64,192]{2,1,0:T(8,128)S(1)} %get-tuple-element.62.refs_2_, ...), custom_call_target="tpu_custom_call" | custom-call | flops 330000000 | bytes 3084320 | tf_op jit(solution)/shard_map/first/pallas_call | solution.py:543
  19.7 1.5 %collective-permute-start.4 = (f32[4,64,128]{2,1,0:T(8,128)S(1)}, f32[4,64,128]{2,1,0:T(8,128)S(1)}, u32[]{:S(2)}, u32[]{:S(2)}) collective-permute-start(f32[4,64,128]{2,1,0:T(8,128)S(1)} %get-tuple-element.72.refs_0_), channel_id=1, source_target_pairs={{0,1},{1,0},{2,3},{3,2},{4,5},{5,4},{6,7},{7,6},{8,9},{9,8},{10,11... | collective-permute-start | bytes 393224 | tf_op jit(solution)/shard_map/ppermute | solution.py:557
  21.3 1.2 %smooth.1 = (f32[8,64,192]{2,1,0:T(8,128)S(1)}, f32[8,128]{1,0:T(8,128)S(1)}, f32[8,128]{1,0:T(8,128)S(1)}, f32[8,64,192]{2,1,0:T(8,128)S(1)}, f32[4,64,192]{2,1,0:T(8,128)S(1)}, /*index=5*/f32[4,64,192]{2,1,0:T(8,128)S(1)}) custom-call(s32[1]{0:T(128)} %bitcast.odd_ref, s32[8]{0:T(128)S(1)} %copy-done.5, f32[8,64,192]{2,1,0:T(8,128)S(1)} %bitcast.10, ...), custom_call_target="tpu_custom_call" | custom-call | flops 330000000 | bytes 2576420 | tf_op jit(solution)/shard_map/smooth/pallas_call | solution.py:543
  22.5 2.8 %collective-permute-start.6 = (f32[4,64,192]{2,1,0:T(8,128)S(1)}, f32[4,64,192]{2,1,0:T(8,128)S(1)}, u32[]{:S(2)}, u32[]{:S(2)}) collective-permute-start(f32[4,64,192]{2,1,0:T(8,128)S(1)} %get-tuple-element.75), channel_id=1, source_target_pairs={{2,4},{6,8},{10,12},{14,16},{18,20},{22,24},{26,28},{30,0},{4,2},{... | collective-permute-start | bytes 589832 | tf_op jit(solution)/shard_map/ppermute | solution.py:563
  25.3 3.4 %polar.3 = (f32[4,64,128]{2,1,0:T(8,128)S(1)}, f32[32,128]{1,0:T(8,128)S(1)}, f32[4,64,128]{2,1,0:T(8,128)S(1)}) custom-call(f32[8,64,192]{2,1,0:T(8,128)S(1)} %get-tuple-element.71.after_ref.inside_ref, f32[64,64]{1,0:T(8,128)S(1)} %copy-done.7, f32[4,64,128]{2,1,0:T(8,128)S(1)} %get-tuple-element.72.refs_0_, f32[4,64,128]{2,1,0:T(8,128)S(1)} %collective-permute-done.4.refs_1_), custom_call_target="tpu_custom_call" | custom-call | flops 3300000000 | bytes 950272 | tf_op jit(solution)/shard_map/polar/pallas_call | solution.py:543
  28.8 1.8 %collective-permute-start.7 = (f32[32,128]{1,0:T(8,128)S(1)}, f32[32,128]{1,0:T(8,128)S(1)}, u32[]{:S(2)}, u32[]{:S(2)}) collective-permute-start(f32[32,128]{1,0:T(8,128)S(1)} %get-tuple-element.73.after_ref.refs_1_), channel_id=1, source_target_pairs={{0,2},{2,0},{4,6},{6,4},{8,10},{10,8},{12,14},{14,12},{16,18},{18,... | collective-permute-start | bytes 49160 | tf_op jit(solution)/shard_map/ppermute | solution.py:600
  31.2 1.2 %ahead.2 = (f32[8,64,192]{2,1,0:T(8,128)S(1)}, f32[4,64,256]{2,1,0:T(8,128)S(1)}, f32[8,64,192]{2,1,0:T(8,128)S(1)}, f32[8,64,192]{2,1,0:T(8,128)S(1)}) custom-call(s32[1]{0:T(128)} %bitcast.odd_ref, f32[32,128]{1,0:T(8,128)S(1)} %get-tuple-element.73.after_ref.refs_1_, f32[8,64,192]{2,1,0:T(8,128)S(1)} %get-tuple-element.71.after_ref.inside_ref, ...), custom_call_target="tpu_custom_call" | custom-call | flops 330000000 | bytes 3624964 | tf_op jit(solution)/shard_map/ahead/pallas_call | solution.py:543
  33.5 1.8 %collective-permute-start.12 = (f32[32,128]{1,0:T(8,128)S(1)}, f32[32,128]{1,0:T(8,128)S(1)}, u32[]{:S(2)}, u32[]{:S(2)}) collective-permute-start(f32[32,128]{1,0:T(8,128)S(1)} %add.3.refs_0_), channel_id=1, source_target_pairs={{0,24},{2,26},{4,28},{6,30},{8,16},{10,18},{12,20},{14,22},{16,8},... | collective-permute-start | bytes 49160 | tf_op jit(solution)/shard_map/ppermute | solution.py:600
  35.3 2.5 %collective-permute-start.10 = (f32[32,128]{1,0:T(8,128)S(1)}, f32[32,128]{1,0:T(8,128)S(1)}, u32[]{:S(2)}, u32[]{:S(2)}) collective-permute-start(f32[32,128]{1,0:T(8,128)S(1)} %add.3.refs_0_), channel_id=1, source_target_pairs={{0,8},{2,10},{4,12},{6,14},{8,0},{10,2},{12,4},{14,6},{16,24},{18,... | collective-permute-start | bytes 49160 | tf_op jit(solution)/shard_map/ppermute | solution.py:600
  37.9 1.2 %collective-permute-done.12.refs_3_ = f32[32,128]{1,0:T(8,128)S(1)} collective-permute-done((f32[32,128]{1,0:T(8,128)S(1)}, f32[32,128]{1,0:T(8,128)S(1)}, u32[]{:S(2)}, u32[]{:S(2)}) %collective-permute-start.12) | collective-permute-done | bytes 16416 | tf_op jit(solution)/shard_map/ppermute | solution.py:600
  41.3 2.5 %collective-permute-start.15 = (f32[4,64,192]{2,1,0:T(8,128)S(1)}, f32[4,64,192]{2,1,0:T(8,128)S(1)}, u32[]{:S(2)}, u32[]{:S(2)}) collective-permute-start(f32[4,64,192]{2,1,0:T(8,128)S(1)} %get-tuple-element.95), channel_id=1, source_target_pairs={{2,4},{6,8},{10,12},{14,16},{18,20},{22,24},{26,28},{30,0},{4,2},{... | collective-permute-start | bytes 589832 | tf_op jit(solution)/shard_map/ppermute | solution.py:563
  43.9 3.9 %polar.4 = (f32[4,64,128]{2,1,0:T(8,128)S(1)}, f32[32,128]{1,0:T(8,128)S(1)}, f32[4,64,128]{2,1,0:T(8,128)S(1)}) custom-call(f32[8,64,192]{2,1,0:T(8,128)S(1)} %get-tuple-element.88.after_ref.inside_ref, f32[64,64]{1,0:T(8,128)S(1)} %get-tuple-element.89.delta_ref, f32[4,64,128]{2,1,0:T(8,128)S(1)} %get-tuple-element.84.refs_0_.change_ref, ...), custom_call_target="tpu_custom_call" | custom-call | flops 330000000 | bytes 1474560 | tf_op jit(solution)/shard_map/polar/pallas_call | solution.py:543
  50.0 1.4 %ahead.3 = (f32[8,64,192]{2,1,0:T(8,128)S(1)}, f32[4,64,256]{2,1,0:T(8,128)S(1)}) custom-call(s32[1]{0:T(128)} %bitcast.odd_ref, f32[32,128]{1,0:T(8,128)S(1)} %get-tuple-element.93.after_ref.refs_1_, f32[8,64,192]{2,1,0:T(8,128)S(1)} %get-tuple-element.88.after_ref.inside_ref, f32[4,64,192]{2,1,0:T(8,128)S(1)} %collective-permute-done.14.near_ref, ...), custom_call_target="tpu_custom_call" | custom-call | flops 330000000 | bytes 2838532 | tf_op jit(solution)/shard_map/ahead/pallas_call | solution.py:543
  51.9 1.1 %collective-permute-start.22 = (f32[4,64,256]{2,1,0:T(8,128)S(1)}, f32[4,64,256]{2,1,0:T(8,128)S(1)}, u32[]{:S(2)}, u32[]{:S(2)}) collective-permute-start(f32[4,64,256]{2,1,0:T(8,128)S(1)} %get-tuple-element.102.refs_0_), channel_id=1, source_target_pairs={{0,1},{1,0},{2,3},{3,2},{4,5},{5,4},{6,7},{7,6},{8,9},{9,8},{10,11... | collective-permute-start | bytes 786440 | tf_op jit(solution)/shard_map/ppermute | solution.py:557
  53.0 2.6 %collective-permute-start.21 = (f32[32,128]{1,0:T(8,128)S(1)}, f32[32,128]{1,0:T(8,128)S(1)}, u32[]{:S(2)}, u32[]{:S(2)}) collective-permute-start(f32[32,128]{1,0:T(8,128)S(1)} %add.4.refs_0_), channel_id=1, source_target_pairs={{0,24},{2,26},{4,28},{6,30},{8,16},{10,18},{12,20},{14,22},{16,8},... | collective-permute-start | bytes 49160 | tf_op jit(solution)/shard_map/ppermute | solution.py:600
  55.8 1.6 %collective-permute-start.19 = (f32[32,128]{1,0:T(8,128)S(1)}, f32[32,128]{1,0:T(8,128)S(1)}, u32[]{:S(2)}, u32[]{:S(2)}) collective-permute-start(f32[32,128]{1,0:T(8,128)S(1)} %add.4.refs_0_), channel_id=1, source_target_pairs={{0,8},{2,10},{4,12},{6,14},{8,0},{10,2},{12,4},{14,6},{16,24},{18,... | collective-permute-start | bytes 49160 | tf_op jit(solution)/shard_map/ppermute | solution.py:600
  57.4 1.3 %collective-permute-done.21.refs_3_ = f32[32,128]{1,0:T(8,128)S(1)} collective-permute-done((f32[32,128]{1,0:T(8,128)S(1)}, f32[32,128]{1,0:T(8,128)S(1)}, u32[]{:S(2)}, u32[]{:S(2)}) %collective-permute-start.21) | collective-permute-done | bytes 16416 | tf_op jit(solution)/shard_map/ppermute | solution.py:600
  58.7 1.5 %collective-permute-done.20.refs_2_ = f32[32,128]{1,0:T(8,128)S(1)} collective-permute-done((f32[32,128]{1,0:T(8,128)S(1)}, f32[32,128]{1,0:T(8,128)S(1)}, u32[]{:S(2)}, u32[]{:S(2)}) %collective-permute-start.20) | collective-permute-done | bytes 16416 | tf_op jit(solution)/shard_map/ppermute | solution.py:600
  60.8 3.9 %polar.5 = (f32[4,64,128]{2,1,0:T(8,128)S(1)}, f32[32,128]{1,0:T(8,128)S(1)}) custom-call(f32[8,64,192]{2,1,0:T(8,128)S(1)} %get-tuple-element.88.after_ref.inside_ref, f32[64,64]{1,0:T(8,128)S(1)} %get-tuple-element.99.delta_ref, f32[4,64,128]{2,1,0:T(8,128)S(1)} %get-tuple-element.100.change_ref, f32[4,64,128]{2,1,0:T(8,128)S(1)} %get-tuple-element.101.old_ref, ...), custom_call_target="tpu_custom_call" | custom-call | flops 330000000 | bytes 1343488 | tf_op jit(solution)/shard_map/polar/pallas_call | solution.py:543
  65.2 1.4 %collective-permute-start.23 = (f32[32,128]{1,0:T(8,128)S(1)}, f32[32,128]{1,0:T(8,128)S(1)}, u32[]{:S(2)}, u32[]{:S(2)}) collective-permute-start(f32[32,128]{1,0:T(8,128)S(1)} %get-tuple-element.108.refs_0_), channel_id=1, source_target_pairs={{0,2},{2,0},{4,6},{6,4},{8,10},{10,8},{12,14},{14,12},{16,18},{18,... | collective-permute-start | bytes 49160 | tf_op jit(solution)/shard_map/ppermute | solution.py:600
  66.6 1.3 %collective-permute-done.25.refs_3_ = f32[32,128]{1,0:T(8,128)S(1)} collective-permute-done((f32[32,128]{1,0:T(8,128)S(1)}, f32[32,128]{1,0:T(8,128)S(1)}, u32[]{:S(2)}, u32[]{:S(2)}) %collective-permute-start.25) | collective-permute-done | bytes 16416 | tf_op jit(solution)/shard_map/ppermute | solution.py:600
  68.6 1.8 %collective-permute-start.28 = (f32[32,128]{1,0:T(8,128)S(1)}, f32[32,128]{1,0:T(8,128)S(1)}, u32[]{:S(2)}, u32[]{:S(2)}) collective-permute-start(f32[32,128]{1,0:T(8,128)S(1)} %add.5.refs_0_), channel_id=1, source_target_pairs={{0,24},{2,26},{4,28},{6,30},{8,16},{10,18},{12,20},{14,22},{16,8},... | collective-permute-start | bytes 49160 | tf_op jit(solution)/shard_map/ppermute | solution.py:600
  70.4 1.1 %collective-permute-start.27 = (f32[32,128]{1,0:T(8,128)S(1)}, f32[32,128]{1,0:T(8,128)S(1)}, u32[]{:S(2)}, u32[]{:S(2)}) collective-permute-start(f32[32,128]{1,0:T(8,128)S(1)} %add.5.refs_0_), channel_id=1, source_target_pairs={{0,16},{2,18},{4,20},{6,22},{8,24},{10,26},{12,28},{14,30},{16,0},... | collective-permute-start | bytes 49160 | tf_op jit(solution)/shard_map/ppermute | solution.py:600
  71.4 1.6 %collective-permute-start.26 = (f32[32,128]{1,0:T(8,128)S(1)}, f32[32,128]{1,0:T(8,128)S(1)}, u32[]{:S(2)}, u32[]{:S(2)}) collective-permute-start(f32[32,128]{1,0:T(8,128)S(1)} %add.5.refs_0_), channel_id=1, source_target_pairs={{0,8},{2,10},{4,12},{6,14},{8,0},{10,2},{12,4},{14,6},{16,24},{18,... | collective-permute-start | bytes 49160 | tf_op jit(solution)/shard_map/ppermute | solution.py:600
  73.0 1.2 %rows.3 = (bf16[8,192,192]{2,1,0:T(8,128)(2,1)S(1)}, f32[8,64,192]{2,1,0:T(8,128)}) custom-call(f32[4,64,128]{2,1,0:T(8,128)S(1)} %get-tuple-element.103.mixed_ref, f32[4,64,128]{2,1,0:T(8,128)S(1)} %get-tuple-element.100.change_ref, f32[4,64,128]{2,1,0:T(8,128)S(1)} %get-tuple-element.104.forward_ref, f32[8,64,192]{2,1,0:T(8,128)S(1)} %get-tuple-element.97.tall_ref, ...), custom_call_target="tpu_custom_call" | custom-call | flops 330000000 | bytes 2162688 | tf_op jit(solution)/shard_map/rows/pallas_call | solution.py:543
  75.2 1.2 %last.1 = (f32[8,64,192]{2,1,0:T(8,128)}, f32[64,64]{1,0:T(8,128)}) custom-call(bf16[8,192,192]{2,1,0:T(8,128)(2,1)S(1)} %get-tuple-element.107.mixed_tall_ref, f32[32,128]{1,0:T(8,128)S(1)} %add.5.refs_0_, f32[32,128]{1,0:T(8,128)S(1)} %collective-permute-done.26.refs_1_, f32[32,128]{1,0:T(8,128)S(1)} %collective-permute-done.27.refs_2_, ...), custom_call_target="tpu_custom_call" | custom-call | flops 330000000 | bytes 1064960 | tf_op jit(solution)/shard_map/last/pallas_call | solution.py:543
  (61 shorter events, 11.0 us)
Async XLA Ops:
  1.5 11.3 %copy-start.2 = (f32[8,192,64]{1,2,0:T(8,128)S(1)}, f32[8,192,64]{1,2,0:T(8,128)}, u32[]{:S(2)}) copy-start(f32[8,192,64]{1,2,0:T(8,128)} %param.16) | copy-start | bytes 1179652
  1.5 11.3 %copy-start.3 = (f32[8,192,64]{1,2,0:T(8,128)S(1)}, f32[8,192,64]{1,2,0:T(8,128)}, u32[]{:S(2)}) copy-start(f32[8,192,64]{1,2,0:T(8,128)} %param.14) | copy-start | bytes 1179652
  1.5 11.3 %copy-start.5 = (s32[8]{0:T(128)S(1)}, s32[8]{0:T(128)}, u32[]{:S(2)}) copy-start(s32[8]{0:T(128)} %order_ref.5) | copy-start | bytes 100
  3.7 9.1 %collective-permute-start.2 = (f32[416,128]{1,0:T(8,128)S(1)}, f32[416,128]{1,0:T(8,128)S(1)}, u32[]{:S(2)}, u32[]{:S(2)}) collective-permute-start(f32[416,128]{1,0:T(8,128)S(1)} %get-tuple-element.61), channel_id=1, source_target_pairs={{0,1},{1,0},{2,3},{3,2},{4,5},{5,4},{6,7},{7,6},{8,9},{9,8},{10,11... | collective-permute-start | bytes 638984 | tf_op jit(solution)/shard_map/ppermute | solution.py:557
  8.7 9.8 %collective-permute-start.3 = (f32[384,128]{1,0:T(8,128)S(1)}, f32[384,128]{1,0:T(8,128)S(1)}, u32[]{:S(2)}, u32[]{:S(2)}) collective-permute-start(f32[384,128]{1,0:T(8,128)S(1)} %get-tuple-element.65), channel_id=1, source_target_pairs={{0,1},{1,0},{2,3},{3,2},{4,5},{5,4},{6,7},{7,6},{8,9},{9,8},{10,11... | collective-permute-start | bytes 589832 | tf_op jit(solution)/shard_map/ppermute | solution.py:557
  8.8 7.2 %collective-permute-start.1 = (f32[8,64]{1,0:T(8,128)S(1)}, f32[8,64]{1,0:T(8,128)S(1)}, u32[]{:S(2)}, u32[]{:S(2)}) collective-permute-start(f32[8,64]{1,0:T(8,128)S(1)} %copy-done.6), channel_id=1, source_target_pairs={{0,30},{2,0},{4,2},{6,4},{8,6},{10,8},{12,10},{14,12},{16,14},{18,... | collective-permute-start | bytes 6152 | tf_op jit(solution)/shard_map/ppermute | solution.py:557
  12.8 5.7 %collective-permute-start = (f32[8,64]{1,0:T(8,128)S(1)}, f32[8,64]{1,0:T(8,128)S(1)}, u32[]{:S(2)}, u32[]{:S(2)}) collective-permute-start(f32[8,64]{1,0:T(8,128)S(1)} %copy-done.6), channel_id=1, source_target_pairs={{0,2},{2,4},{4,6},{6,8},{8,10},{10,12},{12,14},{14,16},{16,18},{18... | collective-permute-start | bytes 6152 | tf_op jit(solution)/shard_map/ppermute | solution.py:557
  19.7 5.6 %collective-permute-start.4 = (f32[4,64,128]{2,1,0:T(8,128)S(1)}, f32[4,64,128]{2,1,0:T(8,128)S(1)}, u32[]{:S(2)}, u32[]{:S(2)}) collective-permute-start(f32[4,64,128]{2,1,0:T(8,128)S(1)} %get-tuple-element.72.refs_0_), channel_id=1, source_target_pairs={{0,1},{1,0},{2,3},{3,2},{4,5},{5,4},{6,7},{7,6},{8,9},{9,8},{10,11... | collective-permute-start | bytes 393224 | tf_op jit(solution)/shard_map/ppermute | solution.py:557
  22.5 8.1 %collective-permute-start.5 = (f32[4,64,192]{2,1,0:T(8,128)S(1)}, f32[4,64,192]{2,1,0:T(8,128)S(1)}, u32[]{:S(2)}, u32[]{:S(2)}) collective-permute-start(f32[4,64,192]{2,1,0:T(8,128)S(1)} %get-tuple-element.74), channel_id=1, source_target_pairs={{0,2},{4,6},{8,10},{12,14},{16,18},{20,22},{24,26},{28,30},{2,0},{... | collective-permute-start | bytes 589832 | tf_op jit(solution)/shard_map/ppermute | solution.py:563
  22.5 8.7 %collective-permute-start.6 = (f32[4,64,192]{2,1,0:T(8,128)S(1)}, f32[4,64,192]{2,1,0:T(8,128)S(1)}, u32[]{:S(2)}, u32[]{:S(2)}) collective-permute-start(f32[4,64,192]{2,1,0:T(8,128)S(1)} %get-tuple-element.75), channel_id=1, source_target_pairs={{2,4},{6,8},{10,12},{14,16},{18,20},{22,24},{26,28},{30,0},{4,2},{... | collective-permute-start | bytes 589832 | tf_op jit(solution)/shard_map/ppermute | solution.py:563
  28.7 3.8 %collective-permute-start.9 = (f32[32,128]{1,0:T(8,128)S(1)}, f32[32,128]{1,0:T(8,128)S(1)}, u32[]{:S(2)}, u32[]{:S(2)}) collective-permute-start(f32[32,128]{1,0:T(8,128)S(1)} %get-tuple-element.73.after_ref.refs_1_), channel_id=1, source_target_pairs={{0,6},{2,4},{4,2},{6,0},{8,14},{10,12},{12,10},{14,8},{16,22},{18,... | collective-permute-start | bytes 49160 | tf_op jit(solution)/shard_map/ppermute | solution.py:600
  28.7 3.8 %collective-permute-start.8 = (f32[32,128]{1,0:T(8,128)S(1)}, f32[32,128]{1,0:T(8,128)S(1)}, u32[]{:S(2)}, u32[]{:S(2)}) collective-permute-start(f32[32,128]{1,0:T(8,128)S(1)} %get-tuple-element.73.after_ref.refs_1_), channel_id=1, source_target_pairs={{0,4},{2,6},{4,0},{6,2},{8,12},{10,14},{12,8},{14,10},{16,20},{18,... | collective-permute-start | bytes 49160 | tf_op jit(solution)/shard_map/ppermute | solution.py:600
  28.8 3.7 %collective-permute-start.7 = (f32[32,128]{1,0:T(8,128)S(1)}, f32[32,128]{1,0:T(8,128)S(1)}, u32[]{:S(2)}, u32[]{:S(2)}) collective-permute-start(f32[32,128]{1,0:T(8,128)S(1)} %get-tuple-element.73.after_ref.refs_1_), channel_id=1, source_target_pairs={{0,2},{2,0},{4,6},{6,4},{8,10},{10,8},{12,14},{14,12},{16,18},{18,... | collective-permute-start | bytes 49160 | tf_op jit(solution)/shard_map/ppermute | solution.py:600
  32.5 11.3 %collective-permute-start.13 = (f32[4,64,256]{2,1,0:T(8,128)S(1)}, f32[4,64,256]{2,1,0:T(8,128)S(1)}, u32[]{:S(2)}, u32[]{:S(2)}) collective-permute-start(f32[4,64,256]{2,1,0:T(8,128)S(1)} %get-tuple-element.91.refs_0_), channel_id=1, source_target_pairs={{0,1},{1,0},{2,3},{3,2},{4,5},{5,4},{6,7},{7,6},{8,9},{9,8},{10,11... | collective-permute-start | bytes 786440 | tf_op jit(solution)/shard_map/ppermute | solution.py:557
  33.5 5.6 %collective-permute-start.12 = (f32[32,128]{1,0:T(8,128)S(1)}, f32[32,128]{1,0:T(8,128)S(1)}, u32[]{:S(2)}, u32[]{:S(2)}) collective-permute-start(f32[32,128]{1,0:T(8,128)S(1)} %add.3.refs_0_), channel_id=1, source_target_pairs={{0,24},{2,26},{4,28},{6,30},{8,16},{10,18},{12,20},{14,22},{16,8},... | collective-permute-start | bytes 49160 | tf_op jit(solution)/shard_map/ppermute | solution.py:600
  35.3 4.6 %collective-permute-start.11 = (f32[32,128]{1,0:T(8,128)S(1)}, f32[32,128]{1,0:T(8,128)S(1)}, u32[]{:S(2)}, u32[]{:S(2)}) collective-permute-start(f32[32,128]{1,0:T(8,128)S(1)} %add.3.refs_0_), channel_id=1, source_target_pairs={{0,16},{2,18},{4,20},{6,22},{8,24},{10,26},{12,28},{14,30},{16,0},... | collective-permute-start | bytes 49160 | tf_op jit(solution)/shard_map/ppermute | solution.py:600
  35.3 4.6 %collective-permute-start.10 = (f32[32,128]{1,0:T(8,128)S(1)}, f32[32,128]{1,0:T(8,128)S(1)}, u32[]{:S(2)}, u32[]{:S(2)}) collective-permute-start(f32[32,128]{1,0:T(8,128)S(1)} %add.3.refs_0_), channel_id=1, source_target_pairs={{0,8},{2,10},{4,12},{6,14},{8,0},{10,2},{12,4},{14,6},{16,24},{18,... | collective-permute-start | bytes 49160 | tf_op jit(solution)/shard_map/ppermute | solution.py:600
  41.3 8.4 %collective-permute-start.14 = (f32[4,64,192]{2,1,0:T(8,128)S(1)}, f32[4,64,192]{2,1,0:T(8,128)S(1)}, u32[]{:S(2)}, u32[]{:S(2)}) collective-permute-start(f32[4,64,192]{2,1,0:T(8,128)S(1)} %get-tuple-element.94), channel_id=1, source_target_pairs={{0,2},{4,6},{8,10},{12,14},{16,18},{20,22},{24,26},{28,30},{2,0},{... | collective-permute-start | bytes 589832 | tf_op jit(solution)/shard_map/ppermute | solution.py:563
  41.3 8.7 %collective-permute-start.15 = (f32[4,64,192]{2,1,0:T(8,128)S(1)}, f32[4,64,192]{2,1,0:T(8,128)S(1)}, u32[]{:S(2)}, u32[]{:S(2)}) collective-permute-start(f32[4,64,192]{2,1,0:T(8,128)S(1)} %get-tuple-element.95), channel_id=1, source_target_pairs={{2,4},{6,8},{10,12},{14,16},{18,20},{22,24},{26,28},{30,0},{4,2},{... | collective-permute-start | bytes 589832 | tf_op jit(solution)/shard_map/ppermute | solution.py:563
  47.8 3.7 %collective-permute-start.18 = (f32[32,128]{1,0:T(8,128)S(1)}, f32[32,128]{1,0:T(8,128)S(1)}, u32[]{:S(2)}, u32[]{:S(2)}) collective-permute-start(f32[32,128]{1,0:T(8,128)S(1)} %get-tuple-element.93.after_ref.refs_1_), channel_id=1, source_target_pairs={{0,6},{2,4},{4,2},{6,0},{8,14},{10,12},{12,10},{14,8},{16,22},{18,... | collective-permute-start | bytes 49160 | tf_op jit(solution)/shard_map/ppermute | solution.py:600
  48.2 3.7 %collective-permute-start.17 = (f32[32,128]{1,0:T(8,128)S(1)}, f32[32,128]{1,0:T(8,128)S(1)}, u32[]{:S(2)}, u32[]{:S(2)}) collective-permute-start(f32[32,128]{1,0:T(8,128)S(1)} %get-tuple-element.93.after_ref.refs_1_), channel_id=1, source_target_pairs={{0,4},{2,6},{4,0},{6,2},{8,12},{10,14},{12,8},{14,10},{16,20},{18,... | collective-permute-start | bytes 49160 | tf_op jit(solution)/shard_map/ppermute | solution.py:600
  48.6 3.3 %collective-permute-start.16 = (f32[32,128]{1,0:T(8,128)S(1)}, f32[32,128]{1,0:T(8,128)S(1)}, u32[]{:S(2)}, u32[]{:S(2)}) collective-permute-start(f32[32,128]{1,0:T(8,128)S(1)} %get-tuple-element.93.after_ref.refs_1_), channel_id=1, source_target_pairs={{0,2},{2,0},{4,6},{6,4},{8,10},{10,8},{12,14},{14,12},{16,18},{18,... | collective-permute-start | bytes 49160 | tf_op jit(solution)/shard_map/ppermute | solution.py:600
  51.9 8.9 %collective-permute-start.22 = (f32[4,64,256]{2,1,0:T(8,128)S(1)}, f32[4,64,256]{2,1,0:T(8,128)S(1)}, u32[]{:S(2)}, u32[]{:S(2)}) collective-permute-start(f32[4,64,256]{2,1,0:T(8,128)S(1)} %get-tuple-element.102.refs_0_), channel_id=1, source_target_pairs={{0,1},{1,0},{2,3},{3,2},{4,5},{5,4},{6,7},{7,6},{8,9},{9,8},{10,11... | collective-permute-start | bytes 786440 | tf_op jit(solution)/shard_map/ppermute | solution.py:557
  53.0 5.7 %collective-permute-start.21 = (f32[32,128]{1,0:T(8,128)S(1)}, f32[32,128]{1,0:T(8,128)S(1)}, u32[]{:S(2)}, u32[]{:S(2)}) collective-permute-start(f32[32,128]{1,0:T(8,128)S(1)} %add.4.refs_0_), channel_id=1, source_target_pairs={{0,24},{2,26},{4,28},{6,30},{8,16},{10,18},{12,20},{14,22},{16,8},... | collective-permute-start | bytes 49160 | tf_op jit(solution)/shard_map/ppermute | solution.py:600
  55.6 4.6 %collective-permute-start.20 = (f32[32,128]{1,0:T(8,128)S(1)}, f32[32,128]{1,0:T(8,128)S(1)}, u32[]{:S(2)}, u32[]{:S(2)}) collective-permute-start(f32[32,128]{1,0:T(8,128)S(1)} %add.4.refs_0_), channel_id=1, source_target_pairs={{0,16},{2,18},{4,20},{6,22},{8,24},{10,26},{12,28},{14,30},{16,0},... | collective-permute-start | bytes 49160 | tf_op jit(solution)/shard_map/ppermute | solution.py:600
  55.8 4.4 %collective-permute-start.19 = (f32[32,128]{1,0:T(8,128)S(1)}, f32[32,128]{1,0:T(8,128)S(1)}, u32[]{:S(2)}, u32[]{:S(2)}) collective-permute-start(f32[32,128]{1,0:T(8,128)S(1)} %add.4.refs_0_), channel_id=1, source_target_pairs={{0,8},{2,10},{4,12},{6,14},{8,0},{10,2},{12,4},{14,6},{16,24},{18,... | collective-permute-start | bytes 49160 | tf_op jit(solution)/shard_map/ppermute | solution.py:600
  64.7 3.2 %collective-permute-start.25 = (f32[32,128]{1,0:T(8,128)S(1)}, f32[32,128]{1,0:T(8,128)S(1)}, u32[]{:S(2)}, u32[]{:S(2)}) collective-permute-start(f32[32,128]{1,0:T(8,128)S(1)} %get-tuple-element.108.refs_0_), channel_id=1, source_target_pairs={{0,6},{2,4},{4,2},{6,0},{8,14},{10,12},{12,10},{14,8},{16,22},{18,... | collective-permute-start | bytes 49160 | tf_op jit(solution)/shard_map/ppermute | solution.py:600
  64.7 3.8 %collective-permute-start.24 = (f32[32,128]{1,0:T(8,128)S(1)}, f32[32,128]{1,0:T(8,128)S(1)}, u32[]{:S(2)}, u32[]{:S(2)}) collective-permute-start(f32[32,128]{1,0:T(8,128)S(1)} %get-tuple-element.108.refs_0_), channel_id=1, source_target_pairs={{0,4},{2,6},{4,0},{6,2},{8,12},{10,14},{12,8},{14,10},{16,20},{18,... | collective-permute-start | bytes 49160 | tf_op jit(solution)/shard_map/ppermute | solution.py:600
  65.2 3.4 %collective-permute-start.23 = (f32[32,128]{1,0:T(8,128)S(1)}, f32[32,128]{1,0:T(8,128)S(1)}, u32[]{:S(2)}, u32[]{:S(2)}) collective-permute-start(f32[32,128]{1,0:T(8,128)S(1)} %get-tuple-element.108.refs_0_), channel_id=1, source_target_pairs={{0,2},{2,0},{4,6},{6,4},{8,10},{10,8},{12,14},{14,12},{16,18},{18,... | collective-permute-start | bytes 49160 | tf_op jit(solution)/shard_map/ppermute | solution.py:600
  68.6 5.7 %collective-permute-start.28 = (f32[32,128]{1,0:T(8,128)S(1)}, f32[32,128]{1,0:T(8,128)S(1)}, u32[]{:S(2)}, u32[]{:S(2)}) collective-permute-start(f32[32,128]{1,0:T(8,128)S(1)} %add.5.refs_0_), channel_id=1, source_target_pairs={{0,24},{2,26},{4,28},{6,30},{8,16},{10,18},{12,20},{14,22},{16,8},... | collective-permute-start | bytes 49160 | tf_op jit(solution)/shard_map/ppermute | solution.py:600
  70.4 4.6 %collective-permute-start.27 = (f32[32,128]{1,0:T(8,128)S(1)}, f32[32,128]{1,0:T(8,128)S(1)}, u32[]{:S(2)}, u32[]{:S(2)}) collective-permute-start(f32[32,128]{1,0:T(8,128)S(1)} %add.5.refs_0_), channel_id=1, source_target_pairs={{0,16},{2,18},{4,20},{6,22},{8,24},{10,26},{12,28},{14,30},{16,0},... | collective-permute-start | bytes 49160 | tf_op jit(solution)/shard_map/ppermute | solution.py:600
  71.4 3.7 %collective-permute-start.26 = (f32[32,128]{1,0:T(8,128)S(1)}, f32[32,128]{1,0:T(8,128)S(1)}, u32[]{:S(2)}, u32[]{:S(2)}) collective-permute-start(f32[32,128]{1,0:T(8,128)S(1)} %add.5.refs_0_), channel_id=1, source_target_pairs={{0,8},{2,10},{4,12},{6,14},{8,0},{10,2},{12,4},{14,6},{16,24},{18,... | collective-permute-start | bytes 49160 | tf_op jit(solution)/shard_map/ppermute | solution.py:600
  (5 other events, 40.4 us)

commit v7 on v6

--- a/solution.py
+++ b/solution.py
@@ -577,9 +577,10 @@
 
 def in_stages(value, axis, beside=None):
     count = lax.axis_size(axis)
-    stride = 1
+    stride = count
     terms, firsts = [value], []
-    for size in stage_sizes(count):
+    for size in reversed(stage_sizes(count)):
+        stride //= size
         value = terms[0]
         if len(terms) > 1:
             unread = [] if beside is None else [beside]
@@ -598,7 +599,6 @@
                 other = digit ^ shift if size in (2, 4) else (digit + shift) % size
                 moves.append((i, i + (other - digit) * stride))
             terms.append(lax.ppermute(value, axis, moves))
-        stride *= size
         firsts = firsts or terms
     return terms, firsts
 

time: 76.6 us -> 77 us (level)
    ppermute x7, waiting for transfers between devices: 2.5 us -> 3.9 us  [rotated(): lax.ppermute(value, axis, [(i, (i + shift) % count) for i in range(count)])]
    ppermute x4, waiting for transfers between devices: 0.96 us -> 0.01 us  [swapped(): return lax.ppermute(value, axis, pairs + [(b, a) for a, b in pairs])]
where the time goes in v7:
time: 77 us; the launch traced here: 76.6 us
  starting transfers between devices  35 us (45%)
  Pallas kernels  27.8 us (36%)
  waiting for transfers between devices  12 us (16%)
  between operations  0.88 us (1%)
  local copies, waits for them, and re-layouts  0.86 us (1%)
    pallas_call x19, Pallas kernels, call(): pl.pallas_call(kernel, out_shape=shapes, in_specs=specs, out_specs=[pl.Bl...  27.8 us
    ppermute x18, starting transfers between devices, in_stages(): terms.append(lax.ppermute(value, axis, moves))  19 us
    ppermute x7, starting transfers between devices, rotated(): lax.ppermute(value, axis, [(i, (i + shift) % count) for i in range(count)])  10.3 us
    ppermute x18, waiting for transfers between devices, in_stages(): terms.append(lax.ppermute(value, axis, moves))  8.09 us
    ppermute x4, starting transfers between devices, swapped(): return lax.ppermute(value, axis, pairs + [(b, a) for a, b in pairs])  5.65 us
    ppermute x7, waiting for transfers between devices, rotated(): lax.ppermute(value, axis, [(i, (i + shift) % count) for i in range(count)])  3.9 us
  transfers between devices with their start and end apart: 29, of which 13 were waited for; matrix products, arithmetic and copies ran while one was open for 0% of the time, Pallas kernels for 25%

profile of v7, /device:TPU:0, one launch (start us, length us, event | category | flops | bytes accessed | tf_op | source)
XLA Modules:
  0.0 76.6 jit_solution(14675000569548137417)
XLA Ops:
  1.5 2.2 %project.2 = (f32[416,128]{1,0:T(8,128)S(1)}, f32[416,128]{1,0:T(8,128)S(1)}, bf16[64,512]{1,0:T(8,128)(2,1)S(1)}) custom-call(s32[1]{0:T(128)} %bitcast.2.me_ref, bf16[8,384,512]{2,1,0:T(8,128)(2,1)} %data_ref.3, bf16[64,512]{1,0:T(8,128)(2,1)S(1)} %bitcast.16), custom_call_target="tpu_custom_call" | custom-call | flops 330000000 | bytes 3702788 | tf_op jit(solution)/shard_map/project/pallas_call | solution.py:543
  3.7 3.0 %collective-permute-start.2 = (f32[416,128]{1,0:T(8,128)S(1)}, f32[416,128]{1,0:T(8,128)S(1)}, u32[]{:S(2)}, u32[]{:S(2)}) collective-permute-start(f32[416,128]{1,0:T(8,128)S(1)} %get-tuple-element.61), channel_id=1, source_target_pairs={{0,1},{1,0},{2,3},{3,2},{4,5},{5,4},{6,7},{7,6},{8,9},{9,8},{10,11... | collective-permute-start | bytes 638984 | tf_op jit(solution)/shard_map/ppermute | solution.py:557
  6.7 2.0 %project.3 = (f32[384,128]{1,0:T(8,128)S(1)}, f32[384,128]{1,0:T(8,128)S(1)}) custom-call(s32[1]{0:T(128)} %bitcast.2.me_ref, bf16[8,384,512]{2,1,0:T(8,128)(2,1)} %data_ref.3, bf16[64,512]{1,0:T(8,128)(2,1)S(1)} %get-tuple-element.57.factor_ref), custom_call_target="tpu_custom_call" | custom-call | flops 330000000 | bytes 3604484 | tf_op jit(solution)/shard_map/project/pallas_call | solution.py:543
  8.8 4.0 %collective-permute-start.1 = (f32[8,64]{1,0:T(8,128)S(1)}, f32[8,64]{1,0:T(8,128)S(1)}, u32[]{:S(2)}, u32[]{:S(2)}) collective-permute-start(f32[8,64]{1,0:T(8,128)S(1)} %copy-done.6), channel_id=1, source_target_pairs={{0,30},{2,0},{4,2},{6,4},{8,6},{10,8},{12,10},{14,12},{16,14},{18,... | collective-permute-start | bytes 6152 | tf_op jit(solution)/shard_map/ppermute | solution.py:557
  12.8 2.9 %setup.1 = (bf16[8,64,192]{2,1,0:T(8,128)(2,1)S(1)}, bf16[4,128,384]{2,1,0:T(8,128)(2,1)S(1)}, f32[8,128]{1,0:T(8,128)S(1)}, f32[8,64]{1,0:T(8,128)S(1)}, f32[64...) custom-call(s32[8]{0:T(128)S(1)} %copy-done.5, f32[416,128]{1,0:T(8,128)S(1)} %get-tuple-element.60.refs_0_, ...), custom_call_target="tpu_custom_call" | custom-call | flops 330000000 | bytes 2992160 | tf_op jit(solution)/shard_map/setup/pallas_call | solution.py:543
  16.0 2.5 %collective-permute-done.refs_0_.before_ref = f32[8,64]{1,0:T(8,128)S(1)} collective-permute-done((f32[8,64]{1,0:T(8,128)S(1)}, f32[8,64]{1,0:T(8,128)S(1)}, u32[]{:S(2)}, u32[]{:S(2)}) %collective-permute-start) | collective-permute-done | bytes 2080 | tf_op jit(solution)/shard_map/ppermute | solution.py:557
  18.5 1.2 %first.1 = (f32[8,64,192]{2,1,0:T(8,128)S(1)}, f32[8,64,192]{2,1,0:T(8,128)S(1)}, f32[4,64,128]{2,1,0:T(8,128)S(1)}) custom-call(s32[8]{0:T(128)S(1)} %copy-done.5, f32[8,64]{1,0:T(8,128)S(1)} %collective-permute-done.refs_0_.before_ref, f32[8,64]{1,0:T(8,128)S(1)} %collective-permute-done.1.refs_1_.after_ref, f32[8,64,192]{2,1,0:T(8,128)S(1)} %get-tuple-element.62.refs_2_, ...), custom_call_target="tpu_custom_call" | custom-call | flops 330000000 | bytes 3084320 | tf_op jit(solution)/shard_map/first/pallas_call | solution.py:543
  19.7 1.5 %collective-permute-start.4 = (f32[4,64,128]{2,1,0:T(8,128)S(1)}, f32[4,64,128]{2,1,0:T(8,128)S(1)}, u32[]{:S(2)}, u32[]{:S(2)}) collective-permute-start(f32[4,64,128]{2,1,0:T(8,128)S(1)} %get-tuple-element.72.refs_0_), channel_id=1, source_target_pairs={{0,1},{1,0},{2,3},{3,2},{4,5},{5,4},{6,7},{7,6},{8,9},{9,8},{10,11... | collective-permute-start | bytes 393224 | tf_op jit(solution)/shard_map/ppermute | solution.py:557
  21.3 1.2 %smooth.1 = (f32[8,64,192]{2,1,0:T(8,128)S(1)}, f32[8,128]{1,0:T(8,128)S(1)}, f32[8,128]{1,0:T(8,128)S(1)}, f32[8,64,192]{2,1,0:T(8,128)S(1)}, f32[4,64,192]{2,1,0:T(8,128)S(1)}, /*index=5*/f32[4,64,192]{2,1,0:T(8,128)S(1)}) custom-call(s32[1]{0:T(128)} %bitcast.odd_ref, s32[8]{0:T(128)S(1)} %copy-done.5, f32[8,64,192]{2,1,0:T(8,128)S(1)} %bitcast.10, ...), custom_call_target="tpu_custom_call" | custom-call | flops 330000000 | bytes 2576420 | tf_op jit(solution)/shard_map/smooth/pallas_call | solution.py:543
  22.5 2.8 %collective-permute-start.6 = (f32[4,64,192]{2,1,0:T(8,128)S(1)}, f32[4,64,192]{2,1,0:T(8,128)S(1)}, u32[]{:S(2)}, u32[]{:S(2)}) collective-permute-start(f32[4,64,192]{2,1,0:T(8,128)S(1)} %get-tuple-element.75), channel_id=1, source_target_pairs={{2,4},{6,8},{10,12},{14,16},{18,20},{22,24},{26,28},{30,0},{4,2},{... | collective-permute-start | bytes 589832 | tf_op jit(solution)/shard_map/ppermute | solution.py:563
  25.3 3.4 %polar.3 = (f32[4,64,128]{2,1,0:T(8,128)S(1)}, f32[32,128]{1,0:T(8,128)S(1)}, f32[4,64,128]{2,1,0:T(8,128)S(1)}) custom-call(f32[8,64,192]{2,1,0:T(8,128)S(1)} %get-tuple-element.71.after_ref.inside_ref, f32[64,64]{1,0:T(8,128)S(1)} %copy-done.7, f32[4,64,128]{2,1,0:T(8,128)S(1)} %get-tuple-element.72.refs_0_, f32[4,64,128]{2,1,0:T(8,128)S(1)} %collective-permute-done.4.refs_1_), custom_call_target="tpu_custom_call" | custom-call | flops 3300000000 | bytes 950272 | tf_op jit(solution)/shard_map/polar/pallas_call | solution.py:543
  28.7 1.2 %collective-permute-start.9 = (f32[32,128]{1,0:T(8,128)S(1)}, f32[32,128]{1,0:T(8,128)S(1)}, u32[]{:S(2)}, u32[]{:S(2)}) collective-permute-start(f32[32,128]{1,0:T(8,128)S(1)} %get-tuple-element.73.after_ref.refs_1_), channel_id=1, source_target_pairs={{0,24},{2,26},{4,28},{6,30},{8,16},{10,18},{12,20},{14,22},{16,8},... | collective-permute-start | bytes 49160 | tf_op jit(solution)/shard_map/ppermute | solution.py:601
  29.9 3.2 %collective-permute-start.7 = (f32[32,128]{1,0:T(8,128)S(1)}, f32[32,128]{1,0:T(8,128)S(1)}, u32[]{:S(2)}, u32[]{:S(2)}) collective-permute-start(f32[32,128]{1,0:T(8,128)S(1)} %get-tuple-element.73.after_ref.refs_1_), channel_id=1, source_target_pairs={{0,8},{2,10},{4,12},{6,14},{8,0},{10,2},{12,4},{14,6},{16,24},{18,... | collective-permute-start | bytes 49160 | tf_op jit(solution)/shard_map/ppermute | solution.py:601
  33.1 1.2 %ahead.2 = (f32[8,64,192]{2,1,0:T(8,128)S(1)}, f32[4,64,256]{2,1,0:T(8,128)S(1)}, f32[8,64,192]{2,1,0:T(8,128)S(1)}, f32[8,64,192]{2,1,0:T(8,128)S(1)}) custom-call(s32[1]{0:T(128)} %bitcast.odd_ref, f32[32,128]{1,0:T(8,128)S(1)} %get-tuple-element.73.after_ref.refs_1_, f32[8,64,192]{2,1,0:T(8,128)S(1)} %get-tuple-element.71.after_ref.inside_ref, ...), custom_call_target="tpu_custom_call" | custom-call | flops 330000000 | bytes 3624964 | tf_op jit(solution)/shard_map/ahead/pallas_call | solution.py:543
  34.8 1.2 %collective-permute-start.13 = (f32[4,64,256]{2,1,0:T(8,128)S(1)}, f32[4,64,256]{2,1,0:T(8,128)S(1)}, u32[]{:S(2)}, u32[]{:S(2)}) collective-permute-start(f32[4,64,256]{2,1,0:T(8,128)S(1)} %get-tuple-element.91.refs_0_), channel_id=1, source_target_pairs={{0,1},{1,0},{2,3},{3,2},{4,5},{5,4},{6,7},{7,6},{8,9},{9,8},{10,11... | collective-permute-start | bytes 786440 | tf_op jit(solution)/shard_map/ppermute | solution.py:557
  36.0 1.7 %collective-permute-start.11 = (f32[32,128]{1,0:T(8,128)S(1)}, f32[32,128]{1,0:T(8,128)S(1)}, u32[]{:S(2)}, u32[]{:S(2)}) collective-permute-start(f32[32,128]{1,0:T(8,128)S(1)} %add.3.refs_0_), channel_id=1, source_target_pairs={{0,4},{2,6},{4,0},{6,2},{8,12},{10,14},{12,8},{14,10},{16,20},{18,... | collective-permute-start | bytes 49160 | tf_op jit(solution)/shard_map/ppermute | solution.py:601
  37.9 1.3 %collective-permute-done.12.refs_3_ = f32[32,128]{1,0:T(8,128)S(1)} collective-permute-done((f32[32,128]{1,0:T(8,128)S(1)}, f32[32,128]{1,0:T(8,128)S(1)}, u32[]{:S(2)}, u32[]{:S(2)}) %collective-permute-start.12) | collective-permute-done | bytes 16416 | tf_op jit(solution)/shard_map/ppermute | solution.py:601
  42.0 1.9 %collective-permute-start.15 = (f32[4,64,192]{2,1,0:T(8,128)S(1)}, f32[4,64,192]{2,1,0:T(8,128)S(1)}, u32[]{:S(2)}, u32[]{:S(2)}) collective-permute-start(f32[4,64,192]{2,1,0:T(8,128)S(1)} %get-tuple-element.95), channel_id=1, source_target_pairs={{2,4},{6,8},{10,12},{14,16},{18,20},{22,24},{26,28},{30,0},{4,2},{... | collective-permute-start | bytes 589832 | tf_op jit(solution)/shard_map/ppermute | solution.py:563
  43.9 3.9 %polar.4 = (f32[4,64,128]{2,1,0:T(8,128)S(1)}, f32[32,128]{1,0:T(8,128)S(1)}, f32[4,64,128]{2,1,0:T(8,128)S(1)}) custom-call(f32[8,64,192]{2,1,0:T(8,128)S(1)} %get-tuple-element.88.after_ref.inside_ref, f32[64,64]{1,0:T(8,128)S(1)} %get-tuple-element.89.delta_ref, f32[4,64,128]{2,1,0:T(8,128)S(1)} %get-tuple-element.84.refs_0_.change_ref, ...), custom_call_target="tpu_custom_call" | custom-call | flops 330000000 | bytes 1474560 | tf_op jit(solution)/shard_map/polar/pallas_call | solution.py:543
  47.8 2.0 %collective-permute-start.18 = (f32[32,128]{1,0:T(8,128)S(1)}, f32[32,128]{1,0:T(8,128)S(1)}, u32[]{:S(2)}, u32[]{:S(2)}) collective-permute-start(f32[32,128]{1,0:T(8,128)S(1)} %get-tuple-element.93.after_ref.refs_1_), channel_id=1, source_target_pairs={{0,24},{2,26},{4,28},{6,30},{8,16},{10,18},{12,20},{14,22},{16,8},... | collective-permute-start | bytes 49160 | tf_op jit(solution)/shard_map/ppermute | solution.py:601
  49.8 2.4 %collective-permute-start.16 = (f32[32,128]{1,0:T(8,128)S(1)}, f32[32,128]{1,0:T(8,128)S(1)}, u32[]{:S(2)}, u32[]{:S(2)}) collective-permute-start(f32[32,128]{1,0:T(8,128)S(1)} %get-tuple-element.93.after_ref.refs_1_), channel_id=1, source_target_pairs={{0,8},{2,10},{4,12},{6,14},{8,0},{10,2},{12,4},{14,6},{16,24},{18,... | collective-permute-start | bytes 49160 | tf_op jit(solution)/shard_map/ppermute | solution.py:601
  52.3 1.4 %ahead.3 = (f32[8,64,192]{2,1,0:T(8,128)S(1)}, f32[4,64,256]{2,1,0:T(8,128)S(1)}) custom-call(s32[1]{0:T(128)} %bitcast.odd_ref, f32[32,128]{1,0:T(8,128)S(1)} %get-tuple-element.93.after_ref.refs_1_, f32[8,64,192]{2,1,0:T(8,128)S(1)} %get-tuple-element.88.after_ref.inside_ref, f32[4,64,192]{2,1,0:T(8,128)S(1)} %collective-permute-done.14.near_ref, ...), custom_call_target="tpu_custom_call" | custom-call | flops 330000000 | bytes 2838532 | tf_op jit(solution)/shard_map/ahead/pallas_call | solution.py:543
  55.6 1.3 %collective-permute-start.19 = (f32[32,128]{1,0:T(8,128)S(1)}, f32[32,128]{1,0:T(8,128)S(1)}, u32[]{:S(2)}, u32[]{:S(2)}) collective-permute-start(f32[32,128]{1,0:T(8,128)S(1)} %add.4.refs_0_), channel_id=1, source_target_pairs={{0,2},{2,0},{4,6},{6,4},{8,10},{10,8},{12,14},{14,12},{16,18},{18,... | collective-permute-start | bytes 49160 | tf_op jit(solution)/shard_map/ppermute | solution.py:601
  56.9 1.3 %collective-permute-done.21.refs_3_ = f32[32,128]{1,0:T(8,128)S(1)} collective-permute-done((f32[32,128]{1,0:T(8,128)S(1)}, f32[32,128]{1,0:T(8,128)S(1)}, u32[]{:S(2)}, u32[]{:S(2)}) %collective-permute-start.21) | collective-permute-done | bytes 16416 | tf_op jit(solution)/shard_map/ppermute | solution.py:601
  59.4 1.4 %collective-permute-done.22.refs_1_ = f32[4,64,256]{2,1,0:T(8,128)S(1)} collective-permute-done((f32[4,64,256]{2,1,0:T(8,128)S(1)}, f32[4,64,256]{2,1,0:T(8,128)S(1)}, u32[]{:S(2)}, u32[]{:S(2)}) %collective-permute-start.22) | collective-permute-done | bytes 262176 | tf_op jit(solution)/shard_map/ppermute | solution.py:557
  60.8 3.9 %polar.5 = (f32[4,64,128]{2,1,0:T(8,128)S(1)}, f32[32,128]{1,0:T(8,128)S(1)}) custom-call(f32[8,64,192]{2,1,0:T(8,128)S(1)} %get-tuple-element.88.after_ref.inside_ref, f32[64,64]{1,0:T(8,128)S(1)} %get-tuple-element.99.delta_ref, f32[4,64,128]{2,1,0:T(8,128)S(1)} %get-tuple-element.100.change_ref, f32[4,64,128]{2,1,0:T(8,128)S(1)} %get-tuple-element.101.old_ref, ...), custom_call_target="tpu_custom_call" | custom-call | flops 330000000 | bytes 1343488 | tf_op jit(solution)/shard_map/polar/pallas_call | solution.py:543
  64.7 1.9 %collective-permute-start.25 = (f32[32,128]{1,0:T(8,128)S(1)}, f32[32,128]{1,0:T(8,128)S(1)}, u32[]{:S(2)}, u32[]{:S(2)}) collective-permute-start(f32[32,128]{1,0:T(8,128)S(1)} %get-tuple-element.108.refs_0_), channel_id=1, source_target_pairs={{0,24},{2,26},{4,28},{6,30},{8,16},{10,18},{12,20},{14,22},{16,8},... | collective-permute-start | bytes 49160 | tf_op jit(solution)/shard_map/ppermute | solution.py:601
  67.8 1.4 %collective-permute-start.23 = (f32[32,128]{1,0:T(8,128)S(1)}, f32[32,128]{1,0:T(8,128)S(1)}, u32[]{:S(2)}, u32[]{:S(2)}) collective-permute-start(f32[32,128]{1,0:T(8,128)S(1)} %get-tuple-element.108.refs_0_), channel_id=1, source_target_pairs={{0,8},{2,10},{4,12},{6,14},{8,0},{10,2},{12,4},{14,6},{16,24},{18,... | collective-permute-start | bytes 49160 | tf_op jit(solution)/shard_map/ppermute | solution.py:601
  69.2 1.1 %collective-permute-done.25.refs_3_ = f32[32,128]{1,0:T(8,128)S(1)} collective-permute-done((f32[32,128]{1,0:T(8,128)S(1)}, f32[32,128]{1,0:T(8,128)S(1)}, u32[]{:S(2)}, u32[]{:S(2)}) %collective-permute-start.25) | collective-permute-done | bytes 16416 | tf_op jit(solution)/shard_map/ppermute | solution.py:601
  71.5 1.9 %collective-permute-start.27 = (f32[32,128]{1,0:T(8,128)S(1)}, f32[32,128]{1,0:T(8,128)S(1)}, u32[]{:S(2)}, u32[]{:S(2)}) collective-permute-start(f32[32,128]{1,0:T(8,128)S(1)} %add.5.refs_0_), channel_id=1, source_target_pairs={{0,4},{2,6},{4,0},{6,2},{8,12},{10,14},{12,8},{14,10},{16,20},{18,... | collective-permute-start | bytes 49160 | tf_op jit(solution)/shard_map/ppermute | solution.py:601
  73.5 1.2 %rows.3 = (bf16[8,192,192]{2,1,0:T(8,128)(2,1)S(1)}, f32[8,64,192]{2,1,0:T(8,128)}) custom-call(f32[4,64,128]{2,1,0:T(8,128)S(1)} %get-tuple-element.103.mixed_ref, f32[4,64,128]{2,1,0:T(8,128)S(1)} %get-tuple-element.100.change_ref, f32[4,64,128]{2,1,0:T(8,128)S(1)} %get-tuple-element.104.forward_ref, f32[8,64,192]{2,1,0:T(8,128)S(1)} %get-tuple-element.97.tall_ref, ...), custom_call_target="tpu_custom_call" | custom-call | flops 330000000 | bytes 2162688 | tf_op jit(solution)/shard_map/rows/pallas_call | solution.py:543
  75.3 1.2 %last.1 = (f32[8,64,192]{2,1,0:T(8,128)}, f32[64,64]{1,0:T(8,128)}) custom-call(bf16[8,192,192]{2,1,0:T(8,128)(2,1)S(1)} %get-tuple-element.107.mixed_tall_ref, f32[32,128]{1,0:T(8,128)S(1)} %add.5.refs_0_, f32[32,128]{1,0:T(8,128)S(1)} %collective-permute-done.26.refs_1_, f32[32,128]{1,0:T(8,128)S(1)} %collective-permute-done.27.refs_2_, ...), custom_call_target="tpu_custom_call" | custom-call | flops 330000000 | bytes 1064960 | tf_op jit(solution)/shard_map/last/pallas_call | solution.py:543
  (61 shorter events, 10.9 us)
Async XLA Ops:
  1.5 11.3 %copy-start.2 = (f32[8,192,64]{1,2,0:T(8,128)S(1)}, f32[8,192,64]{1,2,0:T(8,128)}, u32[]{:S(2)}) copy-start(f32[8,192,64]{1,2,0:T(8,128)} %param.16) | copy-start | bytes 1179652
  1.5 11.3 %copy-start.3 = (f32[8,192,64]{1,2,0:T(8,128)S(1)}, f32[8,192,64]{1,2,0:T(8,128)}, u32[]{:S(2)}) copy-start(f32[8,192,64]{1,2,0:T(8,128)} %param.14) | copy-start | bytes 1179652
  1.5 11.3 %copy-start.5 = (s32[8]{0:T(128)S(1)}, s32[8]{0:T(128)}, u32[]{:S(2)}) copy-start(s32[8]{0:T(128)} %order_ref.5) | copy-start | bytes 100
  3.7 9.1 %collective-permute-start.2 = (f32[416,128]{1,0:T(8,128)S(1)}, f32[416,128]{1,0:T(8,128)S(1)}, u32[]{:S(2)}, u32[]{:S(2)}) collective-permute-start(f32[416,128]{1,0:T(8,128)S(1)} %get-tuple-element.61), channel_id=1, source_target_pairs={{0,1},{1,0},{2,3},{3,2},{4,5},{5,4},{6,7},{7,6},{8,9},{9,8},{10,11... | collective-permute-start | bytes 638984 | tf_op jit(solution)/shard_map/ppermute | solution.py:557
  8.7 9.8 %collective-permute-start.3 = (f32[384,128]{1,0:T(8,128)S(1)}, f32[384,128]{1,0:T(8,128)S(1)}, u32[]{:S(2)}, u32[]{:S(2)}) collective-permute-start(f32[384,128]{1,0:T(8,128)S(1)} %get-tuple-element.65), channel_id=1, source_target_pairs={{0,1},{1,0},{2,3},{3,2},{4,5},{5,4},{6,7},{7,6},{8,9},{9,8},{10,11... | collective-permute-start | bytes 589832 | tf_op jit(solution)/shard_map/ppermute | solution.py:557
  8.8 7.2 %collective-permute-start.1 = (f32[8,64]{1,0:T(8,128)S(1)}, f32[8,64]{1,0:T(8,128)S(1)}, u32[]{:S(2)}, u32[]{:S(2)}) collective-permute-start(f32[8,64]{1,0:T(8,128)S(1)} %copy-done.6), channel_id=1, source_target_pairs={{0,30},{2,0},{4,2},{6,4},{8,6},{10,8},{12,10},{14,12},{16,14},{18,... | collective-permute-start | bytes 6152 | tf_op jit(solution)/shard_map/ppermute | solution.py:557
  12.8 5.7 %collective-permute-start = (f32[8,64]{1,0:T(8,128)S(1)}, f32[8,64]{1,0:T(8,128)S(1)}, u32[]{:S(2)}, u32[]{:S(2)}) collective-permute-start(f32[8,64]{1,0:T(8,128)S(1)} %copy-done.6), channel_id=1, source_target_pairs={{0,2},{2,4},{4,6},{6,8},{8,10},{10,12},{12,14},{14,16},{16,18},{18... | collective-permute-start | bytes 6152 | tf_op jit(solution)/shard_map/ppermute | solution.py:557
  19.7 5.6 %collective-permute-start.4 = (f32[4,64,128]{2,1,0:T(8,128)S(1)}, f32[4,64,128]{2,1,0:T(8,128)S(1)}, u32[]{:S(2)}, u32[]{:S(2)}) collective-permute-start(f32[4,64,128]{2,1,0:T(8,128)S(1)} %get-tuple-element.72.refs_0_), channel_id=1, source_target_pairs={{0,1},{1,0},{2,3},{3,2},{4,5},{5,4},{6,7},{7,6},{8,9},{9,8},{10,11... | collective-permute-start | bytes 393224 | tf_op jit(solution)/shard_map/ppermute | solution.py:557
  22.5 10.7 %collective-permute-start.5 = (f32[4,64,192]{2,1,0:T(8,128)S(1)}, f32[4,64,192]{2,1,0:T(8,128)S(1)}, u32[]{:S(2)}, u32[]{:S(2)}) collective-permute-start(f32[4,64,192]{2,1,0:T(8,128)S(1)} %get-tuple-element.74), channel_id=1, source_target_pairs={{0,2},{4,6},{8,10},{12,14},{16,18},{20,22},{24,26},{28,30},{2,0},{... | collective-permute-start | bytes 589832 | tf_op jit(solution)/shard_map/ppermute | solution.py:563
  22.5 10.6 %collective-permute-start.6 = (f32[4,64,192]{2,1,0:T(8,128)S(1)}, f32[4,64,192]{2,1,0:T(8,128)S(1)}, u32[]{:S(2)}, u32[]{:S(2)}) collective-permute-start(f32[4,64,192]{2,1,0:T(8,128)S(1)} %get-tuple-element.75), channel_id=1, source_target_pairs={{2,4},{6,8},{10,12},{14,16},{18,20},{22,24},{26,28},{30,0},{4,2},{... | collective-permute-start | bytes 589832 | tf_op jit(solution)/shard_map/ppermute | solution.py:563
  28.7 5.7 %collective-permute-start.9 = (f32[32,128]{1,0:T(8,128)S(1)}, f32[32,128]{1,0:T(8,128)S(1)}, u32[]{:S(2)}, u32[]{:S(2)}) collective-permute-start(f32[32,128]{1,0:T(8,128)S(1)} %get-tuple-element.73.after_ref.refs_1_), channel_id=1, source_target_pairs={{0,24},{2,26},{4,28},{6,30},{8,16},{10,18},{12,20},{14,22},{16,8},... | collective-permute-start | bytes 49160 | tf_op jit(solution)/shard_map/ppermute | solution.py:601
  29.9 4.7 %collective-permute-start.8 = (f32[32,128]{1,0:T(8,128)S(1)}, f32[32,128]{1,0:T(8,128)S(1)}, u32[]{:S(2)}, u32[]{:S(2)}) collective-permute-start(f32[32,128]{1,0:T(8,128)S(1)} %get-tuple-element.73.after_ref.refs_1_), channel_id=1, source_target_pairs={{0,16},{2,18},{4,20},{6,22},{8,24},{10,26},{12,28},{14,30},{16,0},... | collective-permute-start | bytes 49160 | tf_op jit(solution)/shard_map/ppermute | solution.py:601
  29.9 4.9 %collective-permute-start.7 = (f32[32,128]{1,0:T(8,128)S(1)}, f32[32,128]{1,0:T(8,128)S(1)}, u32[]{:S(2)}, u32[]{:S(2)}) collective-permute-start(f32[32,128]{1,0:T(8,128)S(1)} %get-tuple-element.73.after_ref.refs_1_), channel_id=1, source_target_pairs={{0,8},{2,10},{4,12},{6,14},{8,0},{10,2},{12,4},{14,6},{16,24},{18,... | collective-permute-start | bytes 49160 | tf_op jit(solution)/shard_map/ppermute | solution.py:601
  34.8 9.1 %collective-permute-start.13 = (f32[4,64,256]{2,1,0:T(8,128)S(1)}, f32[4,64,256]{2,1,0:T(8,128)S(1)}, u32[]{:S(2)}, u32[]{:S(2)}) collective-permute-start(f32[4,64,256]{2,1,0:T(8,128)S(1)} %get-tuple-element.91.refs_0_), channel_id=1, source_target_pairs={{0,1},{1,0},{2,3},{3,2},{4,5},{5,4},{6,7},{7,6},{8,9},{9,8},{10,11... | collective-permute-start | bytes 786440 | tf_op jit(solution)/shard_map/ppermute | solution.py:557
  36.0 3.2 %collective-permute-start.12 = (f32[32,128]{1,0:T(8,128)S(1)}, f32[32,128]{1,0:T(8,128)S(1)}, u32[]{:S(2)}, u32[]{:S(2)}) collective-permute-start(f32[32,128]{1,0:T(8,128)S(1)} %add.3.refs_0_), channel_id=1, source_target_pairs={{0,6},{2,4},{4,2},{6,0},{8,14},{10,12},{12,10},{14,8},{16,22},{18,... | collective-permute-start | bytes 49160 | tf_op jit(solution)/shard_map/ppermute | solution.py:601
  36.0 3.8 %collective-permute-start.11 = (f32[32,128]{1,0:T(8,128)S(1)}, f32[32,128]{1,0:T(8,128)S(1)}, u32[]{:S(2)}, u32[]{:S(2)}) collective-permute-start(f32[32,128]{1,0:T(8,128)S(1)} %add.3.refs_0_), channel_id=1, source_target_pairs={{0,4},{2,6},{4,0},{6,2},{8,12},{10,14},{12,8},{14,10},{16,20},{18,... | collective-permute-start | bytes 49160 | tf_op jit(solution)/shard_map/ppermute | solution.py:601
  37.7 2.1 %collective-permute-start.10 = (f32[32,128]{1,0:T(8,128)S(1)}, f32[32,128]{1,0:T(8,128)S(1)}, u32[]{:S(2)}, u32[]{:S(2)}) collective-permute-start(f32[32,128]{1,0:T(8,128)S(1)} %add.3.refs_0_), channel_id=1, source_target_pairs={{0,2},{2,0},{4,6},{6,4},{8,10},{10,8},{12,14},{14,12},{16,18},{18,... | collective-permute-start | bytes 49160 | tf_op jit(solution)/shard_map/ppermute | solution.py:601
  41.1 11.1 %collective-permute-start.14 = (f32[4,64,192]{2,1,0:T(8,128)S(1)}, f32[4,64,192]{2,1,0:T(8,128)S(1)}, u32[]{:S(2)}, u32[]{:S(2)}) collective-permute-start(f32[4,64,192]{2,1,0:T(8,128)S(1)} %get-tuple-element.94), channel_id=1, source_target_pairs={{0,2},{4,6},{8,10},{12,14},{16,18},{20,22},{24,26},{28,30},{2,0},{... | collective-permute-start | bytes 589832 | tf_op jit(solution)/shard_map/ppermute | solution.py:563
  42.0 10.2 %collective-permute-start.15 = (f32[4,64,192]{2,1,0:T(8,128)S(1)}, f32[4,64,192]{2,1,0:T(8,128)S(1)}, u32[]{:S(2)}, u32[]{:S(2)}) collective-permute-start(f32[4,64,192]{2,1,0:T(8,128)S(1)} %get-tuple-element.95), channel_id=1, source_target_pairs={{2,4},{6,8},{10,12},{14,16},{18,20},{22,24},{26,28},{30,0},{4,2},{... | collective-permute-start | bytes 589832 | tf_op jit(solution)/shard_map/ppermute | solution.py:563
  47.8 5.8 %collective-permute-start.18 = (f32[32,128]{1,0:T(8,128)S(1)}, f32[32,128]{1,0:T(8,128)S(1)}, u32[]{:S(2)}, u32[]{:S(2)}) collective-permute-start(f32[32,128]{1,0:T(8,128)S(1)} %get-tuple-element.93.after_ref.refs_1_), channel_id=1, source_target_pairs={{0,24},{2,26},{4,28},{6,30},{8,16},{10,18},{12,20},{14,22},{16,8},... | collective-permute-start | bytes 49160 | tf_op jit(solution)/shard_map/ppermute | solution.py:601
  49.8 4.6 %collective-permute-start.17 = (f32[32,128]{1,0:T(8,128)S(1)}, f32[32,128]{1,0:T(8,128)S(1)}, u32[]{:S(2)}, u32[]{:S(2)}) collective-permute-start(f32[32,128]{1,0:T(8,128)S(1)} %get-tuple-element.93.after_ref.refs_1_), channel_id=1, source_target_pairs={{0,16},{2,18},{4,20},{6,22},{8,24},{10,26},{12,28},{14,30},{16,0},... | collective-permute-start | bytes 49160 | tf_op jit(solution)/shard_map/ppermute | solution.py:601
  49.8 4.6 %collective-permute-start.16 = (f32[32,128]{1,0:T(8,128)S(1)}, f32[32,128]{1,0:T(8,128)S(1)}, u32[]{:S(2)}, u32[]{:S(2)}) collective-permute-start(f32[32,128]{1,0:T(8,128)S(1)} %get-tuple-element.93.after_ref.refs_1_), channel_id=1, source_target_pairs={{0,8},{2,10},{4,12},{6,14},{8,0},{10,2},{12,4},{14,6},{16,24},{18,... | collective-permute-start | bytes 49160 | tf_op jit(solution)/shard_map/ppermute | solution.py:601
  54.5 6.4 %collective-permute-start.22 = (f32[4,64,256]{2,1,0:T(8,128)S(1)}, f32[4,64,256]{2,1,0:T(8,128)S(1)}, u32[]{:S(2)}, u32[]{:S(2)}) collective-permute-start(f32[4,64,256]{2,1,0:T(8,128)S(1)} %get-tuple-element.102.refs_0_), channel_id=1, source_target_pairs={{0,1},{1,0},{2,3},{3,2},{4,5},{5,4},{6,7},{7,6},{8,9},{9,8},{10,11... | collective-permute-start | bytes 786440 | tf_op jit(solution)/shard_map/ppermute | solution.py:557
  55.1 3.2 %collective-permute-start.21 = (f32[32,128]{1,0:T(8,128)S(1)}, f32[32,128]{1,0:T(8,128)S(1)}, u32[]{:S(2)}, u32[]{:S(2)}) collective-permute-start(f32[32,128]{1,0:T(8,128)S(1)} %add.4.refs_0_), channel_id=1, source_target_pairs={{0,6},{2,4},{4,2},{6,0},{8,14},{10,12},{12,10},{14,8},{16,22},{18,... | collective-permute-start | bytes 49160 | tf_op jit(solution)/shard_map/ppermute | solution.py:601
  55.1 3.8 %collective-permute-start.20 = (f32[32,128]{1,0:T(8,128)S(1)}, f32[32,128]{1,0:T(8,128)S(1)}, u32[]{:S(2)}, u32[]{:S(2)}) collective-permute-start(f32[32,128]{1,0:T(8,128)S(1)} %add.4.refs_0_), channel_id=1, source_target_pairs={{0,4},{2,6},{4,0},{6,2},{8,12},{10,14},{12,8},{14,10},{16,20},{18,... | collective-permute-start | bytes 49160 | tf_op jit(solution)/shard_map/ppermute | solution.py:601
  55.6 3.3 %collective-permute-start.19 = (f32[32,128]{1,0:T(8,128)S(1)}, f32[32,128]{1,0:T(8,128)S(1)}, u32[]{:S(2)}, u32[]{:S(2)}) collective-permute-start(f32[32,128]{1,0:T(8,128)S(1)} %add.4.refs_0_), channel_id=1, source_target_pairs={{0,2},{2,0},{4,6},{6,4},{8,10},{10,8},{12,14},{14,12},{16,18},{18,... | collective-permute-start | bytes 49160 | tf_op jit(solution)/shard_map/ppermute | solution.py:601
  64.7 5.6 %collective-permute-start.25 = (f32[32,128]{1,0:T(8,128)S(1)}, f32[32,128]{1,0:T(8,128)S(1)}, u32[]{:S(2)}, u32[]{:S(2)}) collective-permute-start(f32[32,128]{1,0:T(8,128)S(1)} %get-tuple-element.108.refs_0_), channel_id=1, source_target_pairs={{0,24},{2,26},{4,28},{6,30},{8,16},{10,18},{12,20},{14,22},{16,8},... | collective-permute-start | bytes 49160 | tf_op jit(solution)/shard_map/ppermute | solution.py:601
  66.6 4.6 %collective-permute-start.24 = (f32[32,128]{1,0:T(8,128)S(1)}, f32[32,128]{1,0:T(8,128)S(1)}, u32[]{:S(2)}, u32[]{:S(2)}) collective-permute-start(f32[32,128]{1,0:T(8,128)S(1)} %get-tuple-element.108.refs_0_), channel_id=1, source_target_pairs={{0,16},{2,18},{4,20},{6,22},{8,24},{10,26},{12,28},{14,30},{16,0},... | collective-permute-start | bytes 49160 | tf_op jit(solution)/shard_map/ppermute | solution.py:601
  67.8 3.7 %collective-permute-start.23 = (f32[32,128]{1,0:T(8,128)S(1)}, f32[32,128]{1,0:T(8,128)S(1)}, u32[]{:S(2)}, u32[]{:S(2)}) collective-permute-start(f32[32,128]{1,0:T(8,128)S(1)} %get-tuple-element.108.refs_0_), channel_id=1, source_target_pairs={{0,8},{2,10},{4,12},{6,14},{8,0},{10,2},{12,4},{14,6},{16,24},{18,... | collective-permute-start | bytes 49160 | tf_op jit(solution)/shard_map/ppermute | solution.py:601
  71.5 3.2 %collective-permute-start.28 = (f32[32,128]{1,0:T(8,128)S(1)}, f32[32,128]{1,0:T(8,128)S(1)}, u32[]{:S(2)}, u32[]{:S(2)}) collective-permute-start(f32[32,128]{1,0:T(8,128)S(1)} %add.5.refs_0_), channel_id=1, source_target_pairs={{0,6},{2,4},{4,2},{6,0},{8,14},{10,12},{12,10},{14,8},{16,22},{18,... | collective-permute-start | bytes 49160 | tf_op jit(solution)/shard_map/ppermute | solution.py:601
  71.5 3.8 %collective-permute-start.27 = (f32[32,128]{1,0:T(8,128)S(1)}, f32[32,128]{1,0:T(8,128)S(1)}, u32[]{:S(2)}, u32[]{:S(2)}) collective-permute-start(f32[32,128]{1,0:T(8,128)S(1)} %add.5.refs_0_), channel_id=1, source_target_pairs={{0,4},{2,6},{4,0},{6,2},{8,12},{10,14},{12,8},{14,10},{16,20},{18,... | collective-permute-start | bytes 49160 | tf_op jit(solution)/shard_map/ppermute | solution.py:601
  73.4 1.9 %collective-permute-start.26 = (f32[32,128]{1,0:T(8,128)S(1)}, f32[32,128]{1,0:T(8,128)S(1)}, u32[]{:S(2)}, u32[]{:S(2)}) collective-permute-start(f32[32,128]{1,0:T(8,128)S(1)} %add.5.refs_0_), channel_id=1, source_target_pairs={{0,2},{2,0},{4,6},{6,4},{8,10},{10,8},{12,14},{14,12},{16,18},{18,... | collective-permute-start | bytes 49160 | tf_op jit(solution)/shard_map/ppermute | solution.py:601
  (5 other events, 40.4 us)

commit v8 on v6

--- a/solution.py
+++ b/solution.py
@@ -274,9 +274,11 @@
         now = later
     for j in range(count):
         inside_ref[j] = now[j]
+    rows = inside_ref.shape[2]
     for j in range(width):
-        near_ref[j] = jnp.where(odd == 1, now[j - width], now[count + j])
-        far_ref[j] = jnp.where(odd == 1, now[count + j], now[j - width])
+        lanes = slice((j % 2) * rows, (j % 2 + 1) * rows)
+        near_ref[j // 2, :, lanes] = jnp.where(odd == 1, now[j - width], now[count + j])
+        far_ref[j // 2, :, lanes] = jnp.where(odd == 1, now[count + j], now[j - width])
 
 
 def all_rho(before_ref, rho_ref, after_ref):
@@ -366,7 +368,7 @@
         left += [high, high, low]
         high, low = split(rights[at])
         right += [high, low, high]
-    partial = dot(jnp.concatenate(left, axis=1), jnp.concatenate(right, axis=1), NT)
+    partial = dot(jnp.concatenate(right, axis=1), jnp.concatenate(left, axis=1), NT)
     for at in range(len(roots)):
         (mixed,) = times_blocks([roots[at]], delta_blocks)
         mixed_ref[at] = mixed * scales[at]
@@ -410,16 +412,17 @@
     group, odd_ref, after_ref, inside_ref, near_ref, far_ref, target_ref, tall_ref, side_ref, rho_ref,
     inverse_ref, known_ref, cross_ref, *kept
 ):
-    count, rank, _ = inside_ref.shape
+    count, rank, rows = inside_ref.shape
     width = SWEEPS
     knowns, talls = [], []
     for k in range(count):
         aux = inside_ref[k]
-        if k < width:
-            aux = aux + jnp.where(odd_ref[0] == 1, near_ref[k], far_ref[k])
-        if k >= count - width:
-            at = k - count + width
-            aux = aux + jnp.where(odd_ref[0] == 1, far_ref[at], near_ref[at])
+        for at, mine, other in ((k, near_ref, far_ref), (k - count + width, far_ref, near_ref)):
+            if 0 <= at < width:
+                lanes = slice((at % 2) * rows, (at % 2 + 1) * rows)
+                aux = aux + jnp.where(
+                    odd_ref[0] == 1, mine[at // 2, :, lanes], other[at // 2, :, lanes]
+                )
         target, tall = target_ref[k], tall_ref[k]
         if kept:
             aux_ref, dual_ref = kept
@@ -459,9 +462,9 @@
     *sum_refs, delta_ref, change_ref, forward_ref = refs
     groups, rank, wide = mixed_ref.shape
     group = wide // rank
-    delta = new_delta(sum_refs, total, rank)
-    delta_ref[...] = delta
-    mixers = from_left(delta.T, [mixed_ref[at] for at in range(groups)])
+    turned = new_delta(sum_refs, total, rank)
+    delta_ref[...] = turned.T
+    mixers = from_left(turned, [mixed_ref[at] for at in range(groups)])
     place = lax.div(lax.broadcasted_iota(jnp.int32, (1, wide), 1), rank)
     for at in range(groups):
         mixer = mixers[at]
@@ -520,9 +523,9 @@
 
 def last_kernel(total, mixed_tall_ref, *refs):
     *sum_refs, coupled_ref, delta_ref = refs
-    delta = new_delta(sum_refs, total, delta_ref.shape[0])
-    delta_ref[...] = delta
-    delta_left = left_triple(delta.T)
+    turned = new_delta(sum_refs, total, delta_ref.shape[0])
+    delta_ref[...] = turned.T
+    delta_left = left_triple(turned)
     for k in range(coupled_ref.shape[0]):
         coupled_ref[k] = dot(delta_left, mixed_tall_ref[k])
 
@@ -620,13 +623,13 @@
     state = ((count, rank, rows), f32)
     quads = ((groups, rank, wide), f32)
     square = ((rank, rank), f32)
-    halo = ((SWEEPS, rank, rows), f32)
+    halo = (((SWEEPS + 1) // 2, rank, 2 * rows), f32)
     lanes = lambda height: ((height, 128), f32)
     scale = ((groups, 8, wide), f32)
 
     me = lax.axis_index("chan").astype(jnp.int32).reshape(1)
     odd = lax.rem(lax.axis_index("cuts"), 2).astype(jnp.int32).reshape(1)
-    early = count // 4
+    early = max(1, count // 8)
     own, received = [], []
     for first, pairs, lead in ((0, early, True), (2 * early, count // 2 - early, False)):
         height = pairs * rows + (rank // 2 if lead else 0)
@@ -635,7 +638,7 @@
             "project",
             [((height, 2 * rank), f32)] * parts + [(factor.shape, factor.dtype)] * lead,
             me, data, factor,
-            scalars=1, unread=1, limit=52,
+            scalars=1, unread=1, microseconds=2, limit=52,
             scratch=[
                 pltpu.VMEM((2 * pairs, all_rows, channels), data.dtype),
                 pltpu.SemaphoreType.DMA((4 * pairs,)),

time: 76.6 us -> 81.4 us (1.063)
  waiting for transfers between devices: 11.9 us -> 14.6 us
  starting transfers between devices: 35 us -> 37 us
    ppermute x7, waiting for transfers between devices: 2.5 us -> 5.51 us  [rotated(): lax.ppermute(value, axis, [(i, (i + shift) % count) for i in range(count)])]
    ppermute x4, starting transfers between devices: 5.43 us -> 7.3 us  [swapped(): return lax.ppermute(value, axis, pairs + [(b, a) for a, b in pairs])]
    ppermute x4, waiting for transfers between devices: 0.96 us -> 0.01 us  [swapped(): return lax.ppermute(value, axis, pairs + [(b, a) for a, b in pairs])]
  transfers between devices with their start and end apart: 29 -> 29, of which waited for: 13 -> 12; matrix products, arithmetic and copies ran while one was open for 0% -> 0% of each run, Pallas kernels for 25% -> 21%
where the time goes in v8:
time: 81.4 us; the launch traced here: 81.2 us
  starting transfers between devices  37 us (45%)
  Pallas kernels  27.8 us (34%)
  waiting for transfers between devices  14.6 us (18%)
  between operations  0.9 us (1%)
  local copies, waits for them, and re-layouts  0.88 us (1%)
    pallas_call x19, Pallas kernels, call(): pl.pallas_call(kernel, out_shape=shapes, in_specs=specs, out_specs=[pl.Bl...  27.8 us
    ppermute x18, starting transfers between devices, in_stages(): terms.append(lax.ppermute(value, axis, moves))  18.9 us
    ppermute x7, starting transfers between devices, rotated(): lax.ppermute(value, axis, [(i, (i + shift) % count) for i in range(count)])  10.7 us
    ppermute x18, waiting for transfers between devices, in_stages(): terms.append(lax.ppermute(value, axis, moves))  9.09 us
    ppermute x4, starting transfers between devices, swapped(): return lax.ppermute(value, axis, pairs + [(b, a) for a, b in pairs])  7.3 us
    ppermute x7, waiting for transfers between devices, rotated(): lax.ppermute(value, axis, [(i, (i + shift) % count) for i in range(count)])  5.51 us
  transfers between devices with their start and end apart: 29, of which 12 were waited for; matrix products, arithmetic and copies ran while one was open for 0% of the time, Pallas kernels for 21%

profile of v8, /device:TPU:0, one launch (start us, length us, event | category | flops | bytes accessed | tf_op | source)
XLA Modules:
  0.0 81.2 jit_solution(6799557324141254428)
XLA Ops:
  1.5 1.6 %project.2 = (f32[224,128]{1,0:T(8,128)S(1)}, f32[224,128]{1,0:T(8,128)S(1)}, bf16[64,512]{1,0:T(8,128)(2,1)S(1)}) custom-call(s32[1]{0:T(128)} %bitcast.2.me_ref, bf16[8,384,512]{2,1,0:T(8,128)(2,1)} %data_ref.3, bf16[64,512]{1,0:T(8,128)(2,1)S(1)} %bitcast.16), custom_call_target="tpu_custom_call" | custom-call | flops 2200000000 | bytes 3506180 | tf_op jit(solution)/shard_map/project/pallas_call | solution.py:546
  3.2 2.6 %project.3 = (f32[576,128]{1,0:T(8,128)S(1)}, f32[576,128]{1,0:T(8,128)S(1)}) custom-call(s32[1]{0:T(128)} %bitcast.2.me_ref, bf16[8,384,512]{2,1,0:T(8,128)(2,1)} %data_ref.3, bf16[64,512]{1,0:T(8,128)(2,1)S(1)} %get-tuple-element.57.factor_ref), custom_call_target="tpu_custom_call" | custom-call | flops 2200000000 | bytes 3801092 | tf_op jit(solution)/shard_map/project/pallas_call | solution.py:546
  5.8 3.0 %collective-permute-start.3 = (f32[576,128]{1,0:T(8,128)S(1)}, f32[576,128]{1,0:T(8,128)S(1)}, u32[]{:S(2)}, u32[]{:S(2)}) collective-permute-start(f32[576,128]{1,0:T(8,128)S(1)} %get-tuple-element.65), channel_id=1, source_target_pairs={{0,1},{1,0},{2,3},{3,2},{4,5},{5,4},{6,7},{7,6},{8,9},{9,8},{10,11... | collective-permute-start | bytes 884744 | tf_op jit(solution)/shard_map/ppermute | solution.py:560
  8.8 3.9 %collective-permute-start.1 = (f32[8,64]{1,0:T(8,128)S(1)}, f32[8,64]{1,0:T(8,128)S(1)}, u32[]{:S(2)}, u32[]{:S(2)}) collective-permute-start(f32[8,64]{1,0:T(8,128)S(1)} %copy-done.5), channel_id=1, source_target_pairs={{0,30},{2,0},{4,2},{6,4},{8,6},{10,8},{12,10},{14,12},{16,14},{18,... | collective-permute-start | bytes 6152 | tf_op jit(solution)/shard_map/ppermute | solution.py:560
  12.7 5.5 %collective-permute-done.2.refs_1_ = f32[224,128]{1,0:T(8,128)S(1)} collective-permute-done((f32[224,128]{1,0:T(8,128)S(1)}, f32[224,128]{1,0:T(8,128)S(1)}, u32[]{:S(2)}, u32[]{:S(2)}) %collective-permute-start.2) | collective-permute-done | bytes 114720 | tf_op jit(solution)/shard_map/ppermute | solution.py:560
  18.2 2.9 %setup.1 = (bf16[8,64,192]{2,1,0:T(8,128)(2,1)S(1)}, bf16[4,128,384]{2,1,0:T(8,128)(2,1)S(1)}, f32[8,128]{1,0:T(8,128)S(1)}, f32[8,64]{1,0:T(8,128)S(1)}, f32[64...) custom-call(s32[8]{0:T(128)S(1)} %copy-done.4, f32[224,128]{1,0:T(8,128)S(1)} %get-tuple-element.60.refs_0_, ...), custom_call_target="tpu_custom_call" | custom-call | flops 330000000 | bytes 2795552 | tf_op jit(solution)/shard_map/setup/pallas_call | solution.py:546
  21.4 1.4 %first.1 = (f32[8,64,192]{2,1,0:T(8,128)S(1)}, f32[8,64,192]{2,1,0:T(8,128)S(1)}, f32[4,64,128]{2,1,0:T(8,128)S(1)}) custom-call(s32[8]{0:T(128)S(1)} %copy-done.4, f32[8,64]{1,0:T(8,128)S(1)} %collective-permute-done.refs_0_.before_ref, f32[8,64]{1,0:T(8,128)S(1)} %collective-permute-done.1.refs_1_.after_ref, f32[8,64,192]{2,1,0:T(8,128)S(1)} %get-tuple-element.62.refs_2_, ...), custom_call_target="tpu_custom_call" | custom-call | flops 330000000 | bytes 3182624 | tf_op jit(solution)/shard_map/first/pallas_call | solution.py:546
  22.8 1.8 %collective-permute-start.4 = (f32[4,64,128]{2,1,0:T(8,128)S(1)}, f32[4,64,128]{2,1,0:T(8,128)S(1)}, u32[]{:S(2)}, u32[]{:S(2)}) collective-permute-start(f32[4,64,128]{2,1,0:T(8,128)S(1)} %get-tuple-element.72.refs_0_), channel_id=1, source_target_pairs={{0,1},{1,0},{2,3},{3,2},{4,5},{5,4},{6,7},{7,6},{8,9},{9,8},{10,11... | collective-permute-start | bytes 393224 | tf_op jit(solution)/shard_map/ppermute | solution.py:560
  24.6 1.1 %smooth.1 = (f32[8,64,192]{2,1,0:T(8,128)S(1)}, f32[8,128]{1,0:T(8,128)S(1)}, f32[8,128]{1,0:T(8,128)S(1)}, f32[8,64,192]{2,1,0:T(8,128)S(1)}, f32[2,64,384]{2,1,0:T(8,128)S(1)}, /*index=5*/f32[2,64,384]{2,1,0:T(8,128)S(1)}) custom-call(s32[1]{0:T(128)} %bitcast.odd_ref, s32[8]{0:T(128)S(1)} %copy-done.4, f32[8,64,192]{2,1,0:T(8,128)S(1)} %bitcast.10, ...), custom_call_target="tpu_custom_call" | custom-call | flops 330000000 | bytes 2674724 | tf_op jit(solution)/shard_map/smooth/pallas_call | solution.py:546
  25.8 4.7 %collective-permute-start.6 = (f32[2,64,384]{2,1,0:T(8,128)S(1)}, f32[2,64,384]{2,1,0:T(8,128)S(1)}, u32[]{:S(2)}, u32[]{:S(2)}) collective-permute-start(f32[2,64,384]{2,1,0:T(8,128)S(1)} %get-tuple-element.75), channel_id=1, source_target_pairs={{2,4},{6,8},{10,12},{14,16},{18,20},{22,24},{26,28},{30,0},{4,2},{... | collective-permute-start | bytes 589832 | tf_op jit(solution)/shard_map/ppermute | solution.py:566
  30.4 3.4 %polar.3 = (f32[4,64,128]{2,1,0:T(8,128)S(1)}, f32[32,128]{1,0:T(8,128)S(1)}, f32[4,64,128]{2,1,0:T(8,128)S(1)}) custom-call(f32[8,64,192]{2,1,0:T(8,128)S(1)} %get-tuple-element.71.after_ref.inside_ref, f32[64,64]{1,0:T(8,128)S(1)} %copy-done.7, f32[4,64,128]{2,1,0:T(8,128)S(1)} %get-tuple-element.72.refs_0_, f32[4,64,128]{2,1,0:T(8,128)S(1)} %collective-permute-done.4.refs_1_), custom_call_target="tpu_custom_call" | custom-call | flops 3300000000 | bytes 950272 | tf_op jit(solution)/shard_map/polar/pallas_call | solution.py:546
  34.0 1.8 %collective-permute-start.7 = (f32[32,128]{1,0:T(8,128)S(1)}, f32[32,128]{1,0:T(8,128)S(1)}, u32[]{:S(2)}, u32[]{:S(2)}) collective-permute-start(f32[32,128]{1,0:T(8,128)S(1)} %get-tuple-element.73.after_ref.refs_1_), channel_id=1, source_target_pairs={{0,2},{2,0},{4,6},{6,4},{8,10},{10,8},{12,14},{14,12},{16,18},{18,... | collective-permute-start | bytes 49160 | tf_op jit(solution)/shard_map/ppermute | solution.py:603
  35.8 1.2 %ahead.2 = (f32[8,64,192]{2,1,0:T(8,128)S(1)}, f32[4,64,256]{2,1,0:T(8,128)S(1)}, f32[8,64,192]{2,1,0:T(8,128)S(1)}, f32[8,64,192]{2,1,0:T(8,128)S(1)}) custom-call(s32[1]{0:T(128)} %bitcast.odd_ref, f32[32,128]{1,0:T(8,128)S(1)} %get-tuple-element.73.after_ref.refs_1_, f32[8,64,192]{2,1,0:T(8,128)S(1)} %get-tuple-element.71.after_ref.inside_ref, ...), custom_call_target="tpu_custom_call" | custom-call | flops 330000000 | bytes 3624964 | tf_op jit(solution)/shard_map/ahead/pallas_call | solution.py:546
  38.3 2.2 %collective-permute-start.12 = (f32[32,128]{1,0:T(8,128)S(1)}, f32[32,128]{1,0:T(8,128)S(1)}, u32[]{:S(2)}, u32[]{:S(2)}) collective-permute-start(f32[32,128]{1,0:T(8,128)S(1)} %add.3.refs_0_), channel_id=1, source_target_pairs={{0,24},{2,26},{4,28},{6,30},{8,16},{10,18},{12,20},{14,22},{16,8},... | collective-permute-start | bytes 49160 | tf_op jit(solution)/shard_map/ppermute | solution.py:603
  40.5 2.2 %collective-permute-start.10 = (f32[32,128]{1,0:T(8,128)S(1)}, f32[32,128]{1,0:T(8,128)S(1)}, u32[]{:S(2)}, u32[]{:S(2)}) collective-permute-start(f32[32,128]{1,0:T(8,128)S(1)} %add.3.refs_0_), channel_id=1, source_target_pairs={{0,8},{2,10},{4,12},{6,14},{8,0},{10,2},{12,4},{14,6},{16,24},{18,... | collective-permute-start | bytes 49160 | tf_op jit(solution)/shard_map/ppermute | solution.py:603
  42.6 1.1 %collective-permute-done.12.refs_3_ = f32[32,128]{1,0:T(8,128)S(1)} collective-permute-done((f32[32,128]{1,0:T(8,128)S(1)}, f32[32,128]{1,0:T(8,128)S(1)}, u32[]{:S(2)}, u32[]{:S(2)}) %collective-permute-start.12) | collective-permute-done | bytes 16416 | tf_op jit(solution)/shard_map/ppermute | solution.py:603
  43.8 1.3 %collective-permute-done.11.refs_2_ = f32[32,128]{1,0:T(8,128)S(1)} collective-permute-done((f32[32,128]{1,0:T(8,128)S(1)}, f32[32,128]{1,0:T(8,128)S(1)}, u32[]{:S(2)}, u32[]{:S(2)}) %collective-permute-start.11) | collective-permute-done | bytes 16416 | tf_op jit(solution)/shard_map/ppermute | solution.py:603
  46.4 2.5 %collective-permute-start.15 = (f32[2,64,384]{2,1,0:T(8,128)S(1)}, f32[2,64,384]{2,1,0:T(8,128)S(1)}, u32[]{:S(2)}, u32[]{:S(2)}) collective-permute-start(f32[2,64,384]{2,1,0:T(8,128)S(1)} %get-tuple-element.95), channel_id=1, source_target_pairs={{2,4},{6,8},{10,12},{14,16},{18,20},{22,24},{26,28},{30,0},{4,2},{... | collective-permute-start | bytes 589832 | tf_op jit(solution)/shard_map/ppermute | solution.py:566
  49.0 3.9 %polar.4 = (f32[4,64,128]{2,1,0:T(8,128)S(1)}, f32[32,128]{1,0:T(8,128)S(1)}, f32[4,64,128]{2,1,0:T(8,128)S(1)}) custom-call(f32[8,64,192]{2,1,0:T(8,128)S(1)} %get-tuple-element.88.after_ref.inside_ref, f32[64,64]{1,0:T(8,128)S(1)} %get-tuple-element.89.delta_ref, f32[4,64,128]{2,1,0:T(8,128)S(1)} %get-tuple-element.84.refs_0_.change_ref, ...), custom_call_target="tpu_custom_call" | custom-call | flops 330000000 | bytes 1474560 | tf_op jit(solution)/shard_map/polar/pallas_call | solution.py:546
  54.8 1.4 %ahead.3 = (f32[8,64,192]{2,1,0:T(8,128)S(1)}, f32[4,64,256]{2,1,0:T(8,128)S(1)}) custom-call(s32[1]{0:T(128)} %bitcast.odd_ref, f32[32,128]{1,0:T(8,128)S(1)} %get-tuple-element.93.after_ref.refs_1_, f32[8,64,192]{2,1,0:T(8,128)S(1)} %get-tuple-element.88.after_ref.inside_ref, f32[2,64,384]{2,1,0:T(8,128)S(1)} %collective-permute-done.14.near_ref, ...), custom_call_target="tpu_custom_call" | custom-call | flops 330000000 | bytes 2838532 | tf_op jit(solution)/shard_map/ahead/pallas_call | solution.py:546
  56.8 1.4 %collective-permute-start.22 = (f32[4,64,256]{2,1,0:T(8,128)S(1)}, f32[4,64,256]{2,1,0:T(8,128)S(1)}, u32[]{:S(2)}, u32[]{:S(2)}) collective-permute-start(f32[4,64,256]{2,1,0:T(8,128)S(1)} %get-tuple-element.102.refs_0_), channel_id=1, source_target_pairs={{0,1},{1,0},{2,3},{3,2},{4,5},{5,4},{6,7},{7,6},{8,9},{9,8},{10,11... | collective-permute-start | bytes 786440 | tf_op jit(solution)/shard_map/ppermute | solution.py:560
  58.2 1.8 %collective-permute-start.21 = (f32[32,128]{1,0:T(8,128)S(1)}, f32[32,128]{1,0:T(8,128)S(1)}, u32[]{:S(2)}, u32[]{:S(2)}) collective-permute-start(f32[32,128]{1,0:T(8,128)S(1)} %add.4.refs_0_), channel_id=1, source_target_pairs={{0,24},{2,26},{4,28},{6,30},{8,16},{10,18},{12,20},{14,22},{16,8},... | collective-permute-start | bytes 49160 | tf_op jit(solution)/shard_map/ppermute | solution.py:603
  60.0 2.6 %collective-permute-start.19 = (f32[32,128]{1,0:T(8,128)S(1)}, f32[32,128]{1,0:T(8,128)S(1)}, u32[]{:S(2)}, u32[]{:S(2)}) collective-permute-start(f32[32,128]{1,0:T(8,128)S(1)} %add.4.refs_0_), channel_id=1, source_target_pairs={{0,8},{2,10},{4,12},{6,14},{8,0},{10,2},{12,4},{14,6},{16,24},{18,... | collective-permute-start | bytes 49160 | tf_op jit(solution)/shard_map/ppermute | solution.py:603
  62.6 1.1 %collective-permute-done.21.refs_3_ = f32[32,128]{1,0:T(8,128)S(1)} collective-permute-done((f32[32,128]{1,0:T(8,128)S(1)}, f32[32,128]{1,0:T(8,128)S(1)}, u32[]{:S(2)}, u32[]{:S(2)}) %collective-permute-start.21) | collective-permute-done | bytes 16416 | tf_op jit(solution)/shard_map/ppermute | solution.py:603
  65.1 3.9 %polar.5 = (f32[4,64,128]{2,1,0:T(8,128)S(1)}, f32[32,128]{1,0:T(8,128)S(1)}) custom-call(f32[8,64,192]{2,1,0:T(8,128)S(1)} %get-tuple-element.88.after_ref.inside_ref, f32[64,64]{1,0:T(8,128)S(1)} %get-tuple-element.99.delta_ref, f32[4,64,128]{2,1,0:T(8,128)S(1)} %get-tuple-element.100.change_ref, f32[4,64,128]{2,1,0:T(8,128)S(1)} %get-tuple-element.101.old_ref, ...), custom_call_target="tpu_custom_call" | custom-call | flops 330000000 | bytes 1343488 | tf_op jit(solution)/shard_map/polar/pallas_call | solution.py:546
  71.0 1.3 %collective-permute-done.25.refs_3_ = f32[32,128]{1,0:T(8,128)S(1)} collective-permute-done((f32[32,128]{1,0:T(8,128)S(1)}, f32[32,128]{1,0:T(8,128)S(1)}, u32[]{:S(2)}, u32[]{:S(2)}) %collective-permute-start.25) | collective-permute-done | bytes 16416 | tf_op jit(solution)/shard_map/ppermute | solution.py:603
  72.9 2.1 %collective-permute-start.28 = (f32[32,128]{1,0:T(8,128)S(1)}, f32[32,128]{1,0:T(8,128)S(1)}, u32[]{:S(2)}, u32[]{:S(2)}) collective-permute-start(f32[32,128]{1,0:T(8,128)S(1)} %add.5.refs_0_), channel_id=1, source_target_pairs={{0,24},{2,26},{4,28},{6,30},{8,16},{10,18},{12,20},{14,22},{16,8},... | collective-permute-start | bytes 49160 | tf_op jit(solution)/shard_map/ppermute | solution.py:603
  75.0 1.1 %collective-permute-start.27 = (f32[32,128]{1,0:T(8,128)S(1)}, f32[32,128]{1,0:T(8,128)S(1)}, u32[]{:S(2)}, u32[]{:S(2)}) collective-permute-start(f32[32,128]{1,0:T(8,128)S(1)} %add.5.refs_0_), channel_id=1, source_target_pairs={{0,16},{2,18},{4,20},{6,22},{8,24},{10,26},{12,28},{14,30},{16,0},... | collective-permute-start | bytes 49160 | tf_op jit(solution)/shard_map/ppermute | solution.py:603
  76.2 1.2 %collective-permute-start.26 = (f32[32,128]{1,0:T(8,128)S(1)}, f32[32,128]{1,0:T(8,128)S(1)}, u32[]{:S(2)}, u32[]{:S(2)}) collective-permute-start(f32[32,128]{1,0:T(8,128)S(1)} %add.5.refs_0_), channel_id=1, source_target_pairs={{0,8},{2,10},{4,12},{6,14},{8,0},{10,2},{12,4},{14,6},{16,24},{18,... | collective-permute-start | bytes 49160 | tf_op jit(solution)/shard_map/ppermute | solution.py:603
  77.4 1.2 %rows.3 = (bf16[8,192,192]{2,1,0:T(8,128)(2,1)S(1)}, f32[8,64,192]{2,1,0:T(8,128)}) custom-call(f32[4,64,128]{2,1,0:T(8,128)S(1)} %get-tuple-element.103.mixed_ref, f32[4,64,128]{2,1,0:T(8,128)S(1)} %get-tuple-element.100.change_ref, f32[4,64,128]{2,1,0:T(8,128)S(1)} %get-tuple-element.104.forward_ref, f32[8,64,192]{2,1,0:T(8,128)S(1)} %get-tuple-element.97.tall_ref, ...), custom_call_target="tpu_custom_call" | custom-call | flops 330000000 | bytes 2162688 | tf_op jit(solution)/shard_map/rows/pallas_call | solution.py:546
  78.6 1.2 %collective-permute-done.27.refs_2_ = f32[32,128]{1,0:T(8,128)S(1)} collective-permute-done((f32[32,128]{1,0:T(8,128)S(1)}, f32[32,128]{1,0:T(8,128)S(1)}, u32[]{:S(2)}, u32[]{:S(2)}) %collective-permute-start.27) | collective-permute-done | bytes 16416 | tf_op jit(solution)/shard_map/ppermute | solution.py:603
  80.0 1.1 %last.1 = (f32[8,64,192]{2,1,0:T(8,128)}, f32[64,64]{1,0:T(8,128)}) custom-call(bf16[8,192,192]{2,1,0:T(8,128)(2,1)S(1)} %get-tuple-element.107.mixed_tall_ref, f32[32,128]{1,0:T(8,128)S(1)} %add.5.refs_0_, f32[32,128]{1,0:T(8,128)S(1)} %collective-permute-done.26.refs_1_, f32[32,128]{1,0:T(8,128)S(1)} %collective-permute-done.27.refs_2_, ...), custom_call_target="tpu_custom_call" | custom-call | flops 330000000 | bytes 1064960 | tf_op jit(solution)/shard_map/last/pallas_call | solution.py:546
  (61 shorter events, 10.6 us)
Async XLA Ops:
  3.1 15.1 %copy-start = (f32[8,192,64]{1,2,0:T(8,128)S(1)}, f32[8,192,64]{1,2,0:T(8,128)}, u32[]{:S(2)}) copy-start(f32[8,192,64]{1,2,0:T(8,128)} %param.13) | copy-start | bytes 1179652
  3.1 15.1 %copy-start.1 = (f32[8,192,64]{1,2,0:T(8,128)S(1)}, f32[8,192,64]{1,2,0:T(8,128)}, u32[]{:S(2)}) copy-start(f32[8,192,64]{1,2,0:T(8,128)} %param.15) | copy-start | bytes 1179652
  3.1 15.1 %copy-start.2 = (f32[8,192,64]{1,2,0:T(8,128)S(1)}, f32[8,192,64]{1,2,0:T(8,128)}, u32[]{:S(2)}) copy-start(f32[8,192,64]{1,2,0:T(8,128)} %param.16) | copy-start | bytes 1179652
  5.8 15.6 %collective-permute-start.3 = (f32[576,128]{1,0:T(8,128)S(1)}, f32[576,128]{1,0:T(8,128)S(1)}, u32[]{:S(2)}, u32[]{:S(2)}) collective-permute-start(f32[576,128]{1,0:T(8,128)S(1)} %get-tuple-element.65), channel_id=1, source_target_pairs={{0,1},{1,0},{2,3},{3,2},{4,5},{5,4},{6,7},{7,6},{8,9},{9,8},{10,11... | collective-permute-start | bytes 884744 | tf_op jit(solution)/shard_map/ppermute | solution.py:560
  8.8 9.5 %collective-permute-start.2 = (f32[224,128]{1,0:T(8,128)S(1)}, f32[224,128]{1,0:T(8,128)S(1)}, u32[]{:S(2)}, u32[]{:S(2)}) collective-permute-start(f32[224,128]{1,0:T(8,128)S(1)} %get-tuple-element.61), channel_id=1, source_target_pairs={{0,1},{1,0},{2,3},{3,2},{4,5},{5,4},{6,7},{7,6},{8,9},{9,8},{10,11... | collective-permute-start | bytes 344072 | tf_op jit(solution)/shard_map/ppermute | solution.py:560
  8.8 12.5 %collective-permute-start.1 = (f32[8,64]{1,0:T(8,128)S(1)}, f32[8,64]{1,0:T(8,128)S(1)}, u32[]{:S(2)}, u32[]{:S(2)}) collective-permute-start(f32[8,64]{1,0:T(8,128)S(1)} %copy-done.5), channel_id=1, source_target_pairs={{0,30},{2,0},{4,2},{6,4},{8,6},{10,8},{12,10},{14,12},{16,14},{18,... | collective-permute-start | bytes 6152 | tf_op jit(solution)/shard_map/ppermute | solution.py:560
  12.7 8.7 %collective-permute-start = (f32[8,64]{1,0:T(8,128)S(1)}, f32[8,64]{1,0:T(8,128)S(1)}, u32[]{:S(2)}, u32[]{:S(2)}) collective-permute-start(f32[8,64]{1,0:T(8,128)S(1)} %copy-done.5), channel_id=1, source_target_pairs={{0,2},{2,4},{4,6},{6,8},{8,10},{10,12},{12,14},{14,16},{16,18},{18... | collective-permute-start | bytes 6152 | tf_op jit(solution)/shard_map/ppermute | solution.py:560
  22.8 7.6 %collective-permute-start.4 = (f32[4,64,128]{2,1,0:T(8,128)S(1)}, f32[4,64,128]{2,1,0:T(8,128)S(1)}, u32[]{:S(2)}, u32[]{:S(2)}) collective-permute-start(f32[4,64,128]{2,1,0:T(8,128)S(1)} %get-tuple-element.72.refs_0_), channel_id=1, source_target_pairs={{0,1},{1,0},{2,3},{3,2},{4,5},{5,4},{6,7},{7,6},{8,9},{9,8},{10,11... | collective-permute-start | bytes 393224 | tf_op jit(solution)/shard_map/ppermute | solution.py:560
  25.7 10.1 %collective-permute-start.5 = (f32[2,64,384]{2,1,0:T(8,128)S(1)}, f32[2,64,384]{2,1,0:T(8,128)S(1)}, u32[]{:S(2)}, u32[]{:S(2)}) collective-permute-start(f32[2,64,384]{2,1,0:T(8,128)S(1)} %get-tuple-element.74), channel_id=1, source_target_pairs={{0,2},{4,6},{8,10},{12,14},{16,18},{20,22},{24,26},{28,30},{2,0},{... | collective-permute-start | bytes 589832 | tf_op jit(solution)/shard_map/ppermute | solution.py:566
  25.8 10.0 %collective-permute-start.6 = (f32[2,64,384]{2,1,0:T(8,128)S(1)}, f32[2,64,384]{2,1,0:T(8,128)S(1)}, u32[]{:S(2)}, u32[]{:S(2)}) collective-permute-start(f32[2,64,384]{2,1,0:T(8,128)S(1)} %get-tuple-element.75), channel_id=1, source_target_pairs={{2,4},{6,8},{10,12},{14,16},{18,20},{22,24},{26,28},{30,0},{4,2},{... | collective-permute-start | bytes 589832 | tf_op jit(solution)/shard_map/ppermute | solution.py:566
  33.8 3.2 %collective-permute-start.9 = (f32[32,128]{1,0:T(8,128)S(1)}, f32[32,128]{1,0:T(8,128)S(1)}, u32[]{:S(2)}, u32[]{:S(2)}) collective-permute-start(f32[32,128]{1,0:T(8,128)S(1)} %get-tuple-element.73.after_ref.refs_1_), channel_id=1, source_target_pairs={{0,6},{2,4},{4,2},{6,0},{8,14},{10,12},{12,10},{14,8},{16,22},{18,... | collective-permute-start | bytes 49160 | tf_op jit(solution)/shard_map/ppermute | solution.py:603
  33.9 3.8 %collective-permute-start.8 = (f32[32,128]{1,0:T(8,128)S(1)}, f32[32,128]{1,0:T(8,128)S(1)}, u32[]{:S(2)}, u32[]{:S(2)}) collective-permute-start(f32[32,128]{1,0:T(8,128)S(1)} %get-tuple-element.73.after_ref.refs_1_), channel_id=1, source_target_pairs={{0,4},{2,6},{4,0},{6,2},{8,12},{10,14},{12,8},{14,10},{16,20},{18,... | collective-permute-start | bytes 49160 | tf_op jit(solution)/shard_map/ppermute | solution.py:603
  34.0 3.7 %collective-permute-start.7 = (f32[32,128]{1,0:T(8,128)S(1)}, f32[32,128]{1,0:T(8,128)S(1)}, u32[]{:S(2)}, u32[]{:S(2)}) collective-permute-start(f32[32,128]{1,0:T(8,128)S(1)} %get-tuple-element.73.after_ref.refs_1_), channel_id=1, source_target_pairs={{0,2},{2,0},{4,6},{6,4},{8,10},{10,8},{12,14},{14,12},{16,18},{18,... | collective-permute-start | bytes 49160 | tf_op jit(solution)/shard_map/ppermute | solution.py:603
  37.7 11.3 %collective-permute-start.13 = (f32[4,64,256]{2,1,0:T(8,128)S(1)}, f32[4,64,256]{2,1,0:T(8,128)S(1)}, u32[]{:S(2)}, u32[]{:S(2)}) collective-permute-start(f32[4,64,256]{2,1,0:T(8,128)S(1)} %get-tuple-element.91.refs_0_), channel_id=1, source_target_pairs={{0,1},{1,0},{2,3},{3,2},{4,5},{5,4},{6,7},{7,6},{8,9},{9,8},{10,11... | collective-permute-start | bytes 786440 | tf_op jit(solution)/shard_map/ppermute | solution.py:560
  38.3 5.5 %collective-permute-start.12 = (f32[32,128]{1,0:T(8,128)S(1)}, f32[32,128]{1,0:T(8,128)S(1)}, u32[]{:S(2)}, u32[]{:S(2)}) collective-permute-start(f32[32,128]{1,0:T(8,128)S(1)} %add.3.refs_0_), channel_id=1, source_target_pairs={{0,24},{2,26},{4,28},{6,30},{8,16},{10,18},{12,20},{14,22},{16,8},... | collective-permute-start | bytes 49160 | tf_op jit(solution)/shard_map/ppermute | solution.py:603
  40.5 4.6 %collective-permute-start.11 = (f32[32,128]{1,0:T(8,128)S(1)}, f32[32,128]{1,0:T(8,128)S(1)}, u32[]{:S(2)}, u32[]{:S(2)}) collective-permute-start(f32[32,128]{1,0:T(8,128)S(1)} %add.3.refs_0_), channel_id=1, source_target_pairs={{0,16},{2,18},{4,20},{6,22},{8,24},{10,26},{12,28},{14,30},{16,0},... | collective-permute-start | bytes 49160 | tf_op jit(solution)/shard_map/ppermute | solution.py:603
  40.5 4.6 %collective-permute-start.10 = (f32[32,128]{1,0:T(8,128)S(1)}, f32[32,128]{1,0:T(8,128)S(1)}, u32[]{:S(2)}, u32[]{:S(2)}) collective-permute-start(f32[32,128]{1,0:T(8,128)S(1)} %add.3.refs_0_), channel_id=1, source_target_pairs={{0,8},{2,10},{4,12},{6,14},{8,0},{10,2},{12,4},{14,6},{16,24},{18,... | collective-permute-start | bytes 49160 | tf_op jit(solution)/shard_map/ppermute | solution.py:603
  46.4 8.4 %collective-permute-start.14 = (f32[2,64,384]{2,1,0:T(8,128)S(1)}, f32[2,64,384]{2,1,0:T(8,128)S(1)}, u32[]{:S(2)}, u32[]{:S(2)}) collective-permute-start(f32[2,64,384]{2,1,0:T(8,128)S(1)} %get-tuple-element.94), channel_id=1, source_target_pairs={{0,2},{4,6},{8,10},{12,14},{16,18},{20,22},{24,26},{28,30},{2,0},{... | collective-permute-start | bytes 589832 | tf_op jit(solution)/shard_map/ppermute | solution.py:566
  46.4 8.4 %collective-permute-start.15 = (f32[2,64,384]{2,1,0:T(8,128)S(1)}, f32[2,64,384]{2,1,0:T(8,128)S(1)}, u32[]{:S(2)}, u32[]{:S(2)}) collective-permute-start(f32[2,64,384]{2,1,0:T(8,128)S(1)} %get-tuple-element.95), channel_id=1, source_target_pairs={{2,4},{6,8},{10,12},{14,16},{18,20},{22,24},{26,28},{30,0},{4,2},{... | collective-permute-start | bytes 589832 | tf_op jit(solution)/shard_map/ppermute | solution.py:566
  52.9 3.3 %collective-permute-start.18 = (f32[32,128]{1,0:T(8,128)S(1)}, f32[32,128]{1,0:T(8,128)S(1)}, u32[]{:S(2)}, u32[]{:S(2)}) collective-permute-start(f32[32,128]{1,0:T(8,128)S(1)} %get-tuple-element.93.after_ref.refs_1_), channel_id=1, source_target_pairs={{0,6},{2,4},{4,2},{6,0},{8,14},{10,12},{12,10},{14,8},{16,22},{18,... | collective-permute-start | bytes 49160 | tf_op jit(solution)/shard_map/ppermute | solution.py:603
  53.0 3.8 %collective-permute-start.17 = (f32[32,128]{1,0:T(8,128)S(1)}, f32[32,128]{1,0:T(8,128)S(1)}, u32[]{:S(2)}, u32[]{:S(2)}) collective-permute-start(f32[32,128]{1,0:T(8,128)S(1)} %get-tuple-element.93.after_ref.refs_1_), channel_id=1, source_target_pairs={{0,4},{2,6},{4,0},{6,2},{8,12},{10,14},{12,8},{14,10},{16,20},{18,... | collective-permute-start | bytes 49160 | tf_op jit(solution)/shard_map/ppermute | solution.py:603
  53.8 3.0 %collective-permute-start.16 = (f32[32,128]{1,0:T(8,128)S(1)}, f32[32,128]{1,0:T(8,128)S(1)}, u32[]{:S(2)}, u32[]{:S(2)}) collective-permute-start(f32[32,128]{1,0:T(8,128)S(1)} %get-tuple-element.93.after_ref.refs_1_), channel_id=1, source_target_pairs={{0,2},{2,0},{4,6},{6,4},{8,10},{10,8},{12,14},{14,12},{16,18},{18,... | collective-permute-start | bytes 49160 | tf_op jit(solution)/shard_map/ppermute | solution.py:603
  56.8 8.4 %collective-permute-start.22 = (f32[4,64,256]{2,1,0:T(8,128)S(1)}, f32[4,64,256]{2,1,0:T(8,128)S(1)}, u32[]{:S(2)}, u32[]{:S(2)}) collective-permute-start(f32[4,64,256]{2,1,0:T(8,128)S(1)} %get-tuple-element.102.refs_0_), channel_id=1, source_target_pairs={{0,1},{1,0},{2,3},{3,2},{4,5},{5,4},{6,7},{7,6},{8,9},{9,8},{10,11... | collective-permute-start | bytes 786440 | tf_op jit(solution)/shard_map/ppermute | solution.py:560
  58.2 5.5 %collective-permute-start.21 = (f32[32,128]{1,0:T(8,128)S(1)}, f32[32,128]{1,0:T(8,128)S(1)}, u32[]{:S(2)}, u32[]{:S(2)}) collective-permute-start(f32[32,128]{1,0:T(8,128)S(1)} %add.4.refs_0_), channel_id=1, source_target_pairs={{0,24},{2,26},{4,28},{6,30},{8,16},{10,18},{12,20},{14,22},{16,8},... | collective-permute-start | bytes 49160 | tf_op jit(solution)/shard_map/ppermute | solution.py:603
  60.0 4.6 %collective-permute-start.20 = (f32[32,128]{1,0:T(8,128)S(1)}, f32[32,128]{1,0:T(8,128)S(1)}, u32[]{:S(2)}, u32[]{:S(2)}) collective-permute-start(f32[32,128]{1,0:T(8,128)S(1)} %add.4.refs_0_), channel_id=1, source_target_pairs={{0,16},{2,18},{4,20},{6,22},{8,24},{10,26},{12,28},{14,30},{16,0},... | collective-permute-start | bytes 49160 | tf_op jit(solution)/shard_map/ppermute | solution.py:603
  60.0 4.6 %collective-permute-start.19 = (f32[32,128]{1,0:T(8,128)S(1)}, f32[32,128]{1,0:T(8,128)S(1)}, u32[]{:S(2)}, u32[]{:S(2)}) collective-permute-start(f32[32,128]{1,0:T(8,128)S(1)} %add.4.refs_0_), channel_id=1, source_target_pairs={{0,8},{2,10},{4,12},{6,14},{8,0},{10,2},{12,4},{14,6},{16,24},{18,... | collective-permute-start | bytes 49160 | tf_op jit(solution)/shard_map/ppermute | solution.py:603
  69.1 3.2 %collective-permute-start.25 = (f32[32,128]{1,0:T(8,128)S(1)}, f32[32,128]{1,0:T(8,128)S(1)}, u32[]{:S(2)}, u32[]{:S(2)}) collective-permute-start(f32[32,128]{1,0:T(8,128)S(1)} %get-tuple-element.108.refs_0_), channel_id=1, source_target_pairs={{0,6},{2,4},{4,2},{6,0},{8,14},{10,12},{12,10},{14,8},{16,22},{18,... | collective-permute-start | bytes 49160 | tf_op jit(solution)/shard_map/ppermute | solution.py:603
  69.1 3.8 %collective-permute-start.24 = (f32[32,128]{1,0:T(8,128)S(1)}, f32[32,128]{1,0:T(8,128)S(1)}, u32[]{:S(2)}, u32[]{:S(2)}) collective-permute-start(f32[32,128]{1,0:T(8,128)S(1)} %get-tuple-element.108.refs_0_), channel_id=1, source_target_pairs={{0,4},{2,6},{4,0},{6,2},{8,12},{10,14},{12,8},{14,10},{16,20},{18,... | collective-permute-start | bytes 49160 | tf_op jit(solution)/shard_map/ppermute | solution.py:603
  69.9 3.0 %collective-permute-start.23 = (f32[32,128]{1,0:T(8,128)S(1)}, f32[32,128]{1,0:T(8,128)S(1)}, u32[]{:S(2)}, u32[]{:S(2)}) collective-permute-start(f32[32,128]{1,0:T(8,128)S(1)} %get-tuple-element.108.refs_0_), channel_id=1, source_target_pairs={{0,2},{2,0},{4,6},{6,4},{8,10},{10,8},{12,14},{14,12},{16,18},{18,... | collective-permute-start | bytes 49160 | tf_op jit(solution)/shard_map/ppermute | solution.py:603
  72.9 5.7 %collective-permute-start.28 = (f32[32,128]{1,0:T(8,128)S(1)}, f32[32,128]{1,0:T(8,128)S(1)}, u32[]{:S(2)}, u32[]{:S(2)}) collective-permute-start(f32[32,128]{1,0:T(8,128)S(1)} %add.5.refs_0_), channel_id=1, source_target_pairs={{0,24},{2,26},{4,28},{6,30},{8,16},{10,18},{12,20},{14,22},{16,8},... | collective-permute-start | bytes 49160 | tf_op jit(solution)/shard_map/ppermute | solution.py:603
  75.0 4.8 %collective-permute-start.27 = (f32[32,128]{1,0:T(8,128)S(1)}, f32[32,128]{1,0:T(8,128)S(1)}, u32[]{:S(2)}, u32[]{:S(2)}) collective-permute-start(f32[32,128]{1,0:T(8,128)S(1)} %add.5.refs_0_), channel_id=1, source_target_pairs={{0,16},{2,18},{4,20},{6,22},{8,24},{10,26},{12,28},{14,30},{16,0},... | collective-permute-start | bytes 49160 | tf_op jit(solution)/shard_map/ppermute | solution.py:603
  76.2 3.9 %collective-permute-start.26 = (f32[32,128]{1,0:T(8,128)S(1)}, f32[32,128]{1,0:T(8,128)S(1)}, u32[]{:S(2)}, u32[]{:S(2)}) collective-permute-start(f32[32,128]{1,0:T(8,128)S(1)} %add.5.refs_0_), channel_id=1, source_target_pairs={{0,8},{2,10},{4,12},{6,14},{8,0},{10,2},{12,4},{14,6},{16,24},{18,... | collective-permute-start | bytes 49160 | tf_op jit(solution)/shard_map/ppermute | solution.py:603
  (5 other events, 46.0 us)

commit v9 on v8

--- a/solution.py
+++ b/solution.py
@@ -629,7 +629,7 @@
 
     me = lax.axis_index("chan").astype(jnp.int32).reshape(1)
     odd = lax.rem(lax.axis_index("cuts"), 2).astype(jnp.int32).reshape(1)
-    early = max(1, count // 8)
+    early = count // 4
     own, received = [], []
     for first, pairs, lead in ((0, early, True), (2 * early, count // 2 - early, False)):
         height = pairs * rows + (rank // 2 if lead else 0)
@@ -638,7 +638,7 @@
             "project",
             [((height, 2 * rank), f32)] * parts + [(factor.shape, factor.dtype)] * lead,
             me, data, factor,
-            scalars=1, unread=1, microseconds=2, limit=52,
+            scalars=1, unread=1, limit=52,
             scratch=[
                 pltpu.VMEM((2 * pairs, all_rows, channels), data.dtype),
                 pltpu.SemaphoreType.DMA((4 * pairs,)),

time: 81.4 us -> 76.3 us (0.937)
  waiting for transfers between devices: 14.6 us -> 11.6 us
  starting transfers between devices: 37 us -> 35 us
    ppermute x7, waiting for transfers between devices: 5.51 us -> 2.5 us  [rotated(): lax.ppermute(value, axis, [(i, (i + shift) % count) for i in range(count)])]
    ppermute x4, starting transfers between devices: 7.3 us -> 5.44 us  [swapped(): return lax.ppermute(value, axis, pairs + [(b, a) for a, b in pairs])]
  transfers between devices with their start and end apart: 29 -> 29, of which waited for: 12 -> 12; matrix products, arithmetic and copies ran while one was open for 0% -> 0% of each run, Pallas kernels for 21% -> 25%
where the time goes in v9:
time: 76.3 us; the launch traced here: 76.1 us
  starting transfers between devices  35 us (46%)
  Pallas kernels  27.8 us (36%)
  waiting for transfers between devices  11.6 us (15%)
  between operations  0.89 us (1%)
  local copies, waits for them, and re-layouts  0.86 us (1%)
    pallas_call x19, Pallas kernels, call(): pl.pallas_call(kernel, out_shape=shapes, in_specs=specs, out_specs=[pl.Bl...  27.8 us
    ppermute x18, starting transfers between devices, in_stages(): terms.append(lax.ppermute(value, axis, moves))  18.9 us
    ppermute x7, starting transfers between devices, rotated(): lax.ppermute(value, axis, [(i, (i + shift) % count) for i in range(count)])  10.6 us
    ppermute x18, waiting for transfers between devices, in_stages(): terms.append(lax.ppermute(value, axis, moves))  9.05 us
    ppermute x4, starting transfers between devices, swapped(): return lax.ppermute(value, axis, pairs + [(b, a) for a, b in pairs])  5.44 us
    ppermute x7, waiting for transfers between devices, rotated(): lax.ppermute(value, axis, [(i, (i + shift) % count) for i in range(count)])  2.5 us
  transfers between devices with their start and end apart: 29, of which 12 were waited for; matrix products, arithmetic and copies ran while one was open for 0% of the time, Pallas kernels for 25%

profile of v9, /device:TPU:0, one launch (start us, length us, event | category | flops | bytes accessed | tf_op | source)
XLA Modules:
  0.0 76.1 jit_solution(2888395774873078189)
XLA Ops:
  1.5 2.2 %project.2 = (f32[416,128]{1,0:T(8,128)S(1)}, f32[416,128]{1,0:T(8,128)S(1)}, bf16[64,512]{1,0:T(8,128)(2,1)S(1)}) custom-call(s32[1]{0:T(128)} %bitcast.2.me_ref, bf16[8,384,512]{2,1,0:T(8,128)(2,1)} %data_ref.3, bf16[64,512]{1,0:T(8,128)(2,1)S(1)} %bitcast.16), custom_call_target="tpu_custom_call" | custom-call | flops 330000000 | bytes 3702788 | tf_op jit(solution)/shard_map/project/pallas_call | solution.py:546
  3.7 3.0 %collective-permute-start.2 = (f32[416,128]{1,0:T(8,128)S(1)}, f32[416,128]{1,0:T(8,128)S(1)}, u32[]{:S(2)}, u32[]{:S(2)}) collective-permute-start(f32[416,128]{1,0:T(8,128)S(1)} %get-tuple-element.61), channel_id=1, source_target_pairs={{0,1},{1,0},{2,3},{3,2},{4,5},{5,4},{6,7},{7,6},{8,9},{9,8},{10,11... | collective-permute-start | bytes 638984 | tf_op jit(solution)/shard_map/ppermute | solution.py:560
  6.7 2.0 %project.3 = (f32[384,128]{1,0:T(8,128)S(1)}, f32[384,128]{1,0:T(8,128)S(1)}) custom-call(s32[1]{0:T(128)} %bitcast.2.me_ref, bf16[8,384,512]{2,1,0:T(8,128)(2,1)} %data_ref.3, bf16[64,512]{1,0:T(8,128)(2,1)S(1)} %get-tuple-element.57.factor_ref), custom_call_target="tpu_custom_call" | custom-call | flops 330000000 | bytes 3604484 | tf_op jit(solution)/shard_map/project/pallas_call | solution.py:546
  8.8 4.0 %collective-permute-start.1 = (f32[8,64]{1,0:T(8,128)S(1)}, f32[8,64]{1,0:T(8,128)S(1)}, u32[]{:S(2)}, u32[]{:S(2)}) collective-permute-start(f32[8,64]{1,0:T(8,128)S(1)} %copy-done.6), channel_id=1, source_target_pairs={{0,30},{2,0},{4,2},{6,4},{8,6},{10,8},{12,10},{14,12},{16,14},{18,... | collective-permute-start | bytes 6152 | tf_op jit(solution)/shard_map/ppermute | solution.py:560
  12.8 2.9 %setup.1 = (bf16[8,64,192]{2,1,0:T(8,128)(2,1)S(1)}, bf16[4,128,384]{2,1,0:T(8,128)(2,1)S(1)}, f32[8,128]{1,0:T(8,128)S(1)}, f32[8,64]{1,0:T(8,128)S(1)}, f32[64...) custom-call(s32[8]{0:T(128)S(1)} %copy-done.5, f32[416,128]{1,0:T(8,128)S(1)} %get-tuple-element.60.refs_0_, ...), custom_call_target="tpu_custom_call" | custom-call | flops 330000000 | bytes 2992160 | tf_op jit(solution)/shard_map/setup/pallas_call | solution.py:546
  16.0 2.5 %collective-permute-done.refs_0_.before_ref = f32[8,64]{1,0:T(8,128)S(1)} collective-permute-done((f32[8,64]{1,0:T(8,128)S(1)}, f32[8,64]{1,0:T(8,128)S(1)}, u32[]{:S(2)}, u32[]{:S(2)}) %collective-permute-start) | collective-permute-done | bytes 2080 | tf_op jit(solution)/shard_map/ppermute | solution.py:560
  18.5 1.2 %first.1 = (f32[8,64,192]{2,1,0:T(8,128)S(1)}, f32[8,64,192]{2,1,0:T(8,128)S(1)}, f32[4,64,128]{2,1,0:T(8,128)S(1)}) custom-call(s32[8]{0:T(128)S(1)} %copy-done.5, f32[8,64]{1,0:T(8,128)S(1)} %collective-permute-done.refs_0_.before_ref, f32[8,64]{1,0:T(8,128)S(1)} %collective-permute-done.1.refs_1_.after_ref, f32[8,64,192]{2,1,0:T(8,128)S(1)} %get-tuple-element.62.refs_2_, ...), custom_call_target="tpu_custom_call" | custom-call | flops 330000000 | bytes 3084320 | tf_op jit(solution)/shard_map/first/pallas_call | solution.py:546
  19.7 1.5 %collective-permute-start.4 = (f32[4,64,128]{2,1,0:T(8,128)S(1)}, f32[4,64,128]{2,1,0:T(8,128)S(1)}, u32[]{:S(2)}, u32[]{:S(2)}) collective-permute-start(f32[4,64,128]{2,1,0:T(8,128)S(1)} %get-tuple-element.72.refs_0_), channel_id=1, source_target_pairs={{0,1},{1,0},{2,3},{3,2},{4,5},{5,4},{6,7},{7,6},{8,9},{9,8},{10,11... | collective-permute-start | bytes 393224 | tf_op jit(solution)/shard_map/ppermute | solution.py:560
  21.3 1.2 %smooth.1 = (f32[8,64,192]{2,1,0:T(8,128)S(1)}, f32[8,128]{1,0:T(8,128)S(1)}, f32[8,128]{1,0:T(8,128)S(1)}, f32[8,64,192]{2,1,0:T(8,128)S(1)}, f32[2,64,384]{2,1,0:T(8,128)S(1)}, /*index=5*/f32[2,64,384]{2,1,0:T(8,128)S(1)}) custom-call(s32[1]{0:T(128)} %bitcast.odd_ref, s32[8]{0:T(128)S(1)} %copy-done.5, f32[8,64,192]{2,1,0:T(8,128)S(1)} %bitcast.10, ...), custom_call_target="tpu_custom_call" | custom-call | flops 330000000 | bytes 2576420 | tf_op jit(solution)/shard_map/smooth/pallas_call | solution.py:546
  22.5 2.8 %collective-permute-start.6 = (f32[2,64,384]{2,1,0:T(8,128)S(1)}, f32[2,64,384]{2,1,0:T(8,128)S(1)}, u32[]{:S(2)}, u32[]{:S(2)}) collective-permute-start(f32[2,64,384]{2,1,0:T(8,128)S(1)} %get-tuple-element.75), channel_id=1, source_target_pairs={{2,4},{6,8},{10,12},{14,16},{18,20},{22,24},{26,28},{30,0},{4,2},{... | collective-permute-start | bytes 589832 | tf_op jit(solution)/shard_map/ppermute | solution.py:566
  25.3 3.4 %polar.3 = (f32[4,64,128]{2,1,0:T(8,128)S(1)}, f32[32,128]{1,0:T(8,128)S(1)}, f32[4,64,128]{2,1,0:T(8,128)S(1)}) custom-call(f32[8,64,192]{2,1,0:T(8,128)S(1)} %get-tuple-element.71.after_ref.inside_ref, f32[64,64]{1,0:T(8,128)S(1)} %copy-done.7, f32[4,64,128]{2,1,0:T(8,128)S(1)} %get-tuple-element.72.refs_0_, f32[4,64,128]{2,1,0:T(8,128)S(1)} %collective-permute-done.4.refs_1_), custom_call_target="tpu_custom_call" | custom-call | flops 3300000000 | bytes 950272 | tf_op jit(solution)/shard_map/polar/pallas_call | solution.py:546
  28.8 1.8 %collective-permute-start.7 = (f32[32,128]{1,0:T(8,128)S(1)}, f32[32,128]{1,0:T(8,128)S(1)}, u32[]{:S(2)}, u32[]{:S(2)}) collective-permute-start(f32[32,128]{1,0:T(8,128)S(1)} %get-tuple-element.73.after_ref.refs_1_), channel_id=1, source_target_pairs={{0,2},{2,0},{4,6},{6,4},{8,10},{10,8},{12,14},{14,12},{16,18},{18,... | collective-permute-start | bytes 49160 | tf_op jit(solution)/shard_map/ppermute | solution.py:603
  30.6 1.2 %ahead.2 = (f32[8,64,192]{2,1,0:T(8,128)S(1)}, f32[4,64,256]{2,1,0:T(8,128)S(1)}, f32[8,64,192]{2,1,0:T(8,128)S(1)}, f32[8,64,192]{2,1,0:T(8,128)S(1)}) custom-call(s32[1]{0:T(128)} %bitcast.odd_ref, f32[32,128]{1,0:T(8,128)S(1)} %get-tuple-element.73.after_ref.refs_1_, f32[8,64,192]{2,1,0:T(8,128)S(1)} %get-tuple-element.71.after_ref.inside_ref, ...), custom_call_target="tpu_custom_call" | custom-call | flops 330000000 | bytes 3624964 | tf_op jit(solution)/shard_map/ahead/pallas_call | solution.py:546
  33.5 1.8 %collective-permute-start.12 = (f32[32,128]{1,0:T(8,128)S(1)}, f32[32,128]{1,0:T(8,128)S(1)}, u32[]{:S(2)}, u32[]{:S(2)}) collective-permute-start(f32[32,128]{1,0:T(8,128)S(1)} %add.3.refs_0_), channel_id=1, source_target_pairs={{0,24},{2,26},{4,28},{6,30},{8,16},{10,18},{12,20},{14,22},{16,8},... | collective-permute-start | bytes 49160 | tf_op jit(solution)/shard_map/ppermute | solution.py:603
  35.4 2.6 %collective-permute-start.10 = (f32[32,128]{1,0:T(8,128)S(1)}, f32[32,128]{1,0:T(8,128)S(1)}, u32[]{:S(2)}, u32[]{:S(2)}) collective-permute-start(f32[32,128]{1,0:T(8,128)S(1)} %add.3.refs_0_), channel_id=1, source_target_pairs={{0,8},{2,10},{4,12},{6,14},{8,0},{10,2},{12,4},{14,6},{16,24},{18,... | collective-permute-start | bytes 49160 | tf_op jit(solution)/shard_map/ppermute | solution.py:603
  37.9 1.2 %collective-permute-done.12.refs_3_ = f32[32,128]{1,0:T(8,128)S(1)} collective-permute-done((f32[32,128]{1,0:T(8,128)S(1)}, f32[32,128]{1,0:T(8,128)S(1)}, u32[]{:S(2)}, u32[]{:S(2)}) %collective-permute-start.12) | collective-permute-done | bytes 16416 | tf_op jit(solution)/shard_map/ppermute | solution.py:603
  41.4 2.5 %collective-permute-start.15 = (f32[2,64,384]{2,1,0:T(8,128)S(1)}, f32[2,64,384]{2,1,0:T(8,128)S(1)}, u32[]{:S(2)}, u32[]{:S(2)}) collective-permute-start(f32[2,64,384]{2,1,0:T(8,128)S(1)} %get-tuple-element.95), channel_id=1, source_target_pairs={{2,4},{6,8},{10,12},{14,16},{18,20},{22,24},{26,28},{30,0},{4,2},{... | collective-permute-start | bytes 589832 | tf_op jit(solution)/shard_map/ppermute | solution.py:566
  43.9 3.9 %polar.4 = (f32[4,64,128]{2,1,0:T(8,128)S(1)}, f32[32,128]{1,0:T(8,128)S(1)}, f32[4,64,128]{2,1,0:T(8,128)S(1)}) custom-call(f32[8,64,192]{2,1,0:T(8,128)S(1)} %get-tuple-element.88.after_ref.inside_ref, f32[64,64]{1,0:T(8,128)S(1)} %get-tuple-element.89.delta_ref, f32[4,64,128]{2,1,0:T(8,128)S(1)} %get-tuple-element.84.refs_0_.change_ref, ...), custom_call_target="tpu_custom_call" | custom-call | flops 330000000 | bytes 1474560 | tf_op jit(solution)/shard_map/polar/pallas_call | solution.py:546
  48.7 1.1 %collective-permute-start.16 = (f32[32,128]{1,0:T(8,128)S(1)}, f32[32,128]{1,0:T(8,128)S(1)}, u32[]{:S(2)}, u32[]{:S(2)}) collective-permute-start(f32[32,128]{1,0:T(8,128)S(1)} %get-tuple-element.93.after_ref.refs_1_), channel_id=1, source_target_pairs={{0,2},{2,0},{4,6},{6,4},{8,10},{10,8},{12,14},{14,12},{16,18},{18,... | collective-permute-start | bytes 49160 | tf_op jit(solution)/shard_map/ppermute | solution.py:603
  49.7 1.4 %ahead.3 = (f32[8,64,192]{2,1,0:T(8,128)S(1)}, f32[4,64,256]{2,1,0:T(8,128)S(1)}) custom-call(s32[1]{0:T(128)} %bitcast.odd_ref, f32[32,128]{1,0:T(8,128)S(1)} %get-tuple-element.93.after_ref.refs_1_, f32[8,64,192]{2,1,0:T(8,128)S(1)} %get-tuple-element.88.after_ref.inside_ref, f32[2,64,384]{2,1,0:T(8,128)S(1)} %collective-permute-done.14.near_ref, ...), custom_call_target="tpu_custom_call" | custom-call | flops 330000000 | bytes 2838532 | tf_op jit(solution)/shard_map/ahead/pallas_call | solution.py:546
  52.0 1.1 %collective-permute-start.22 = (f32[4,64,256]{2,1,0:T(8,128)S(1)}, f32[4,64,256]{2,1,0:T(8,128)S(1)}, u32[]{:S(2)}, u32[]{:S(2)}) collective-permute-start(f32[4,64,256]{2,1,0:T(8,128)S(1)} %get-tuple-element.102.refs_0_), channel_id=1, source_target_pairs={{0,1},{1,0},{2,3},{3,2},{4,5},{5,4},{6,7},{7,6},{8,9},{9,8},{10,11... | collective-permute-start | bytes 786440 | tf_op jit(solution)/shard_map/ppermute | solution.py:560
  53.1 2.6 %collective-permute-start.21 = (f32[32,128]{1,0:T(8,128)S(1)}, f32[32,128]{1,0:T(8,128)S(1)}, u32[]{:S(2)}, u32[]{:S(2)}) collective-permute-start(f32[32,128]{1,0:T(8,128)S(1)} %add.4.refs_0_), channel_id=1, source_target_pairs={{0,24},{2,26},{4,28},{6,30},{8,16},{10,18},{12,20},{14,22},{16,8},... | collective-permute-start | bytes 49160 | tf_op jit(solution)/shard_map/ppermute | solution.py:603
  55.9 1.6 %collective-permute-start.19 = (f32[32,128]{1,0:T(8,128)S(1)}, f32[32,128]{1,0:T(8,128)S(1)}, u32[]{:S(2)}, u32[]{:S(2)}) collective-permute-start(f32[32,128]{1,0:T(8,128)S(1)} %add.4.refs_0_), channel_id=1, source_target_pairs={{0,8},{2,10},{4,12},{6,14},{8,0},{10,2},{12,4},{14,6},{16,24},{18,... | collective-permute-start | bytes 49160 | tf_op jit(solution)/shard_map/ppermute | solution.py:603
  57.5 1.1 %collective-permute-done.21.refs_3_ = f32[32,128]{1,0:T(8,128)S(1)} collective-permute-done((f32[32,128]{1,0:T(8,128)S(1)}, f32[32,128]{1,0:T(8,128)S(1)}, u32[]{:S(2)}, u32[]{:S(2)}) %collective-permute-start.21) | collective-permute-done | bytes 16416 | tf_op jit(solution)/shard_map/ppermute | solution.py:603
  58.6 1.7 %collective-permute-done.20.refs_2_ = f32[32,128]{1,0:T(8,128)S(1)} collective-permute-done((f32[32,128]{1,0:T(8,128)S(1)}, f32[32,128]{1,0:T(8,128)S(1)}, u32[]{:S(2)}, u32[]{:S(2)}) %collective-permute-start.20) | collective-permute-done | bytes 16416 | tf_op jit(solution)/shard_map/ppermute | solution.py:603
  60.8 3.9 %polar.5 = (f32[4,64,128]{2,1,0:T(8,128)S(1)}, f32[32,128]{1,0:T(8,128)S(1)}) custom-call(f32[8,64,192]{2,1,0:T(8,128)S(1)} %get-tuple-element.88.after_ref.inside_ref, f32[64,64]{1,0:T(8,128)S(1)} %get-tuple-element.99.delta_ref, f32[4,64,128]{2,1,0:T(8,128)S(1)} %get-tuple-element.100.change_ref, f32[4,64,128]{2,1,0:T(8,128)S(1)} %get-tuple-element.101.old_ref, ...), custom_call_target="tpu_custom_call" | custom-call | flops 330000000 | bytes 1343488 | tf_op jit(solution)/shard_map/polar/pallas_call | solution.py:546
  65.0 1.6 %collective-permute-start.23 = (f32[32,128]{1,0:T(8,128)S(1)}, f32[32,128]{1,0:T(8,128)S(1)}, u32[]{:S(2)}, u32[]{:S(2)}) collective-permute-start(f32[32,128]{1,0:T(8,128)S(1)} %get-tuple-element.108.refs_0_), channel_id=1, source_target_pairs={{0,2},{2,0},{4,6},{6,4},{8,10},{10,8},{12,14},{14,12},{16,18},{18,... | collective-permute-start | bytes 49160 | tf_op jit(solution)/shard_map/ppermute | solution.py:603
  66.6 1.3 %collective-permute-done.25.refs_3_ = f32[32,128]{1,0:T(8,128)S(1)} collective-permute-done((f32[32,128]{1,0:T(8,128)S(1)}, f32[32,128]{1,0:T(8,128)S(1)}, u32[]{:S(2)}, u32[]{:S(2)}) %collective-permute-start.25) | collective-permute-done | bytes 16416 | tf_op jit(solution)/shard_map/ppermute | solution.py:603
  68.6 1.5 %collective-permute-start.28 = (f32[32,128]{1,0:T(8,128)S(1)}, f32[32,128]{1,0:T(8,128)S(1)}, u32[]{:S(2)}, u32[]{:S(2)}) collective-permute-start(f32[32,128]{1,0:T(8,128)S(1)} %add.5.refs_0_), channel_id=1, source_target_pairs={{0,24},{2,26},{4,28},{6,30},{8,16},{10,18},{12,20},{14,22},{16,8},... | collective-permute-start | bytes 49160 | tf_op jit(solution)/shard_map/ppermute | solution.py:603
  71.0 2.0 %collective-permute-start.26 = (f32[32,128]{1,0:T(8,128)S(1)}, f32[32,128]{1,0:T(8,128)S(1)}, u32[]{:S(2)}, u32[]{:S(2)}) collective-permute-start(f32[32,128]{1,0:T(8,128)S(1)} %add.5.refs_0_), channel_id=1, source_target_pairs={{0,8},{2,10},{4,12},{6,14},{8,0},{10,2},{12,4},{14,6},{16,24},{18,... | collective-permute-start | bytes 49160 | tf_op jit(solution)/shard_map/ppermute | solution.py:603
  73.0 1.2 %rows.3 = (bf16[8,192,192]{2,1,0:T(8,128)(2,1)S(1)}, f32[8,64,192]{2,1,0:T(8,128)}) custom-call(f32[4,64,128]{2,1,0:T(8,128)S(1)} %get-tuple-element.103.mixed_ref, f32[4,64,128]{2,1,0:T(8,128)S(1)} %get-tuple-element.100.change_ref, f32[4,64,128]{2,1,0:T(8,128)S(1)} %get-tuple-element.104.forward_ref, f32[8,64,192]{2,1,0:T(8,128)S(1)} %get-tuple-element.97.tall_ref, ...), custom_call_target="tpu_custom_call" | custom-call | flops 330000000 | bytes 2162688 | tf_op jit(solution)/shard_map/rows/pallas_call | solution.py:546
  74.9 1.1 %last.1 = (f32[8,64,192]{2,1,0:T(8,128)}, f32[64,64]{1,0:T(8,128)}) custom-call(bf16[8,192,192]{2,1,0:T(8,128)(2,1)S(1)} %get-tuple-element.107.mixed_tall_ref, f32[32,128]{1,0:T(8,128)S(1)} %add.5.refs_0_, f32[32,128]{1,0:T(8,128)S(1)} %collective-permute-done.26.refs_1_, f32[32,128]{1,0:T(8,128)S(1)} %collective-permute-done.27.refs_2_, ...), custom_call_target="tpu_custom_call" | custom-call | flops 330000000 | bytes 1064960 | tf_op jit(solution)/shard_map/last/pallas_call | solution.py:546
  (61 shorter events, 10.3 us)
Async XLA Ops:
  1.5 11.3 %copy-start.2 = (f32[8,192,64]{1,2,0:T(8,128)S(1)}, f32[8,192,64]{1,2,0:T(8,128)}, u32[]{:S(2)}) copy-start(f32[8,192,64]{1,2,0:T(8,128)} %param.16) | copy-start | bytes 1179652
  1.5 11.3 %copy-start.3 = (f32[8,192,64]{1,2,0:T(8,128)S(1)}, f32[8,192,64]{1,2,0:T(8,128)}, u32[]{:S(2)}) copy-start(f32[8,192,64]{1,2,0:T(8,128)} %param.14) | copy-start | bytes 1179652
  1.5 11.3 %copy-start.5 = (s32[8]{0:T(128)S(1)}, s32[8]{0:T(128)}, u32[]{:S(2)}) copy-start(s32[8]{0:T(128)} %order_ref.5) | copy-start | bytes 100
  3.7 9.1 %collective-permute-start.2 = (f32[416,128]{1,0:T(8,128)S(1)}, f32[416,128]{1,0:T(8,128)S(1)}, u32[]{:S(2)}, u32[]{:S(2)}) collective-permute-start(f32[416,128]{1,0:T(8,128)S(1)} %get-tuple-element.61), channel_id=1, source_target_pairs={{0,1},{1,0},{2,3},{3,2},{4,5},{5,4},{6,7},{7,6},{8,9},{9,8},{10,11... | collective-permute-start | bytes 638984 | tf_op jit(solution)/shard_map/ppermute | solution.py:560
  8.7 9.8 %collective-permute-start.3 = (f32[384,128]{1,0:T(8,128)S(1)}, f32[384,128]{1,0:T(8,128)S(1)}, u32[]{:S(2)}, u32[]{:S(2)}) collective-permute-start(f32[384,128]{1,0:T(8,128)S(1)} %get-tuple-element.65), channel_id=1, source_target_pairs={{0,1},{1,0},{2,3},{3,2},{4,5},{5,4},{6,7},{7,6},{8,9},{9,8},{10,11... | collective-permute-start | bytes 589832 | tf_op jit(solution)/shard_map/ppermute | solution.py:560
  8.8 7.2 %collective-permute-start.1 = (f32[8,64]{1,0:T(8,128)S(1)}, f32[8,64]{1,0:T(8,128)S(1)}, u32[]{:S(2)}, u32[]{:S(2)}) collective-permute-start(f32[8,64]{1,0:T(8,128)S(1)} %copy-done.6), channel_id=1, source_target_pairs={{0,30},{2,0},{4,2},{6,4},{8,6},{10,8},{12,10},{14,12},{16,14},{18,... | collective-permute-start | bytes 6152 | tf_op jit(solution)/shard_map/ppermute | solution.py:560
  12.8 5.7 %collective-permute-start = (f32[8,64]{1,0:T(8,128)S(1)}, f32[8,64]{1,0:T(8,128)S(1)}, u32[]{:S(2)}, u32[]{:S(2)}) collective-permute-start(f32[8,64]{1,0:T(8,128)S(1)} %copy-done.6), channel_id=1, source_target_pairs={{0,2},{2,4},{4,6},{6,8},{8,10},{10,12},{12,14},{14,16},{16,18},{18... | collective-permute-start | bytes 6152 | tf_op jit(solution)/shard_map/ppermute | solution.py:560
  19.7 5.5 %collective-permute-start.4 = (f32[4,64,128]{2,1,0:T(8,128)S(1)}, f32[4,64,128]{2,1,0:T(8,128)S(1)}, u32[]{:S(2)}, u32[]{:S(2)}) collective-permute-start(f32[4,64,128]{2,1,0:T(8,128)S(1)} %get-tuple-element.72.refs_0_), channel_id=1, source_target_pairs={{0,1},{1,0},{2,3},{3,2},{4,5},{5,4},{6,7},{7,6},{8,9},{9,8},{10,11... | collective-permute-start | bytes 393224 | tf_op jit(solution)/shard_map/ppermute | solution.py:560
  22.4 8.2 %collective-permute-start.5 = (f32[2,64,384]{2,1,0:T(8,128)S(1)}, f32[2,64,384]{2,1,0:T(8,128)S(1)}, u32[]{:S(2)}, u32[]{:S(2)}) collective-permute-start(f32[2,64,384]{2,1,0:T(8,128)S(1)} %get-tuple-element.74), channel_id=1, source_target_pairs={{0,2},{4,6},{8,10},{12,14},{16,18},{20,22},{24,26},{28,30},{2,0},{... | collective-permute-start | bytes 589832 | tf_op jit(solution)/shard_map/ppermute | solution.py:566
  22.5 8.1 %collective-permute-start.6 = (f32[2,64,384]{2,1,0:T(8,128)S(1)}, f32[2,64,384]{2,1,0:T(8,128)S(1)}, u32[]{:S(2)}, u32[]{:S(2)}) collective-permute-start(f32[2,64,384]{2,1,0:T(8,128)S(1)} %get-tuple-element.75), channel_id=1, source_target_pairs={{2,4},{6,8},{10,12},{14,16},{18,20},{22,24},{26,28},{30,0},{4,2},{... | collective-permute-start | bytes 589832 | tf_op jit(solution)/shard_map/ppermute | solution.py:566
  28.7 3.2 %collective-permute-start.9 = (f32[32,128]{1,0:T(8,128)S(1)}, f32[32,128]{1,0:T(8,128)S(1)}, u32[]{:S(2)}, u32[]{:S(2)}) collective-permute-start(f32[32,128]{1,0:T(8,128)S(1)} %get-tuple-element.73.after_ref.refs_1_), channel_id=1, source_target_pairs={{0,6},{2,4},{4,2},{6,0},{8,14},{10,12},{12,10},{14,8},{16,22},{18,... | collective-permute-start | bytes 49160 | tf_op jit(solution)/shard_map/ppermute | solution.py:603
  28.8 3.8 %collective-permute-start.8 = (f32[32,128]{1,0:T(8,128)S(1)}, f32[32,128]{1,0:T(8,128)S(1)}, u32[]{:S(2)}, u32[]{:S(2)}) collective-permute-start(f32[32,128]{1,0:T(8,128)S(1)} %get-tuple-element.73.after_ref.refs_1_), channel_id=1, source_target_pairs={{0,4},{2,6},{4,0},{6,2},{8,12},{10,14},{12,8},{14,10},{16,20},{18,... | collective-permute-start | bytes 49160 | tf_op jit(solution)/shard_map/ppermute | solution.py:603
  28.8 3.7 %collective-permute-start.7 = (f32[32,128]{1,0:T(8,128)S(1)}, f32[32,128]{1,0:T(8,128)S(1)}, u32[]{:S(2)}, u32[]{:S(2)}) collective-permute-start(f32[32,128]{1,0:T(8,128)S(1)} %get-tuple-element.73.after_ref.refs_1_), channel_id=1, source_target_pairs={{0,2},{2,0},{4,6},{6,4},{8,10},{10,8},{12,14},{14,12},{16,18},{18,... | collective-permute-start | bytes 49160 | tf_op jit(solution)/shard_map/ppermute | solution.py:603
  32.6 11.3 %collective-permute-start.13 = (f32[4,64,256]{2,1,0:T(8,128)S(1)}, f32[4,64,256]{2,1,0:T(8,128)S(1)}, u32[]{:S(2)}, u32[]{:S(2)}) collective-permute-start(f32[4,64,256]{2,1,0:T(8,128)S(1)} %get-tuple-element.91.refs_0_), channel_id=1, source_target_pairs={{0,1},{1,0},{2,3},{3,2},{4,5},{5,4},{6,7},{7,6},{8,9},{9,8},{10,11... | collective-permute-start | bytes 786440 | tf_op jit(solution)/shard_map/ppermute | solution.py:560
  33.5 5.5 %collective-permute-start.12 = (f32[32,128]{1,0:T(8,128)S(1)}, f32[32,128]{1,0:T(8,128)S(1)}, u32[]{:S(2)}, u32[]{:S(2)}) collective-permute-start(f32[32,128]{1,0:T(8,128)S(1)} %add.3.refs_0_), channel_id=1, source_target_pairs={{0,24},{2,26},{4,28},{6,30},{8,16},{10,18},{12,20},{14,22},{16,8},... | collective-permute-start | bytes 49160 | tf_op jit(solution)/shard_map/ppermute | solution.py:603
  35.4 4.6 %collective-permute-start.11 = (f32[32,128]{1,0:T(8,128)S(1)}, f32[32,128]{1,0:T(8,128)S(1)}, u32[]{:S(2)}, u32[]{:S(2)}) collective-permute-start(f32[32,128]{1,0:T(8,128)S(1)} %add.3.refs_0_), channel_id=1, source_target_pairs={{0,16},{2,18},{4,20},{6,22},{8,24},{10,26},{12,28},{14,30},{16,0},... | collective-permute-start | bytes 49160 | tf_op jit(solution)/shard_map/ppermute | solution.py:603
  35.4 4.6 %collective-permute-start.10 = (f32[32,128]{1,0:T(8,128)S(1)}, f32[32,128]{1,0:T(8,128)S(1)}, u32[]{:S(2)}, u32[]{:S(2)}) collective-permute-start(f32[32,128]{1,0:T(8,128)S(1)} %add.3.refs_0_), channel_id=1, source_target_pairs={{0,8},{2,10},{4,12},{6,14},{8,0},{10,2},{12,4},{14,6},{16,24},{18,... | collective-permute-start | bytes 49160 | tf_op jit(solution)/shard_map/ppermute | solution.py:603
  41.3 8.5 %collective-permute-start.14 = (f32[2,64,384]{2,1,0:T(8,128)S(1)}, f32[2,64,384]{2,1,0:T(8,128)S(1)}, u32[]{:S(2)}, u32[]{:S(2)}) collective-permute-start(f32[2,64,384]{2,1,0:T(8,128)S(1)} %get-tuple-element.94), channel_id=1, source_target_pairs={{0,2},{4,6},{8,10},{12,14},{16,18},{20,22},{24,26},{28,30},{2,0},{... | collective-permute-start | bytes 589832 | tf_op jit(solution)/shard_map/ppermute | solution.py:566
  41.4 8.4 %collective-permute-start.15 = (f32[2,64,384]{2,1,0:T(8,128)S(1)}, f32[2,64,384]{2,1,0:T(8,128)S(1)}, u32[]{:S(2)}, u32[]{:S(2)}) collective-permute-start(f32[2,64,384]{2,1,0:T(8,128)S(1)} %get-tuple-element.95), channel_id=1, source_target_pairs={{2,4},{6,8},{10,12},{14,16},{18,20},{22,24},{26,28},{30,0},{4,2},{... | collective-permute-start | bytes 589832 | tf_op jit(solution)/shard_map/ppermute | solution.py:566
  47.8 3.3 %collective-permute-start.18 = (f32[32,128]{1,0:T(8,128)S(1)}, f32[32,128]{1,0:T(8,128)S(1)}, u32[]{:S(2)}, u32[]{:S(2)}) collective-permute-start(f32[32,128]{1,0:T(8,128)S(1)} %get-tuple-element.93.after_ref.refs_1_), channel_id=1, source_target_pairs={{0,6},{2,4},{4,2},{6,0},{8,14},{10,12},{12,10},{14,8},{16,22},{18,... | collective-permute-start | bytes 49160 | tf_op jit(solution)/shard_map/ppermute | solution.py:603
  48.2 3.7 %collective-permute-start.17 = (f32[32,128]{1,0:T(8,128)S(1)}, f32[32,128]{1,0:T(8,128)S(1)}, u32[]{:S(2)}, u32[]{:S(2)}) collective-permute-start(f32[32,128]{1,0:T(8,128)S(1)} %get-tuple-element.93.after_ref.refs_1_), channel_id=1, source_target_pairs={{0,4},{2,6},{4,0},{6,2},{8,12},{10,14},{12,8},{14,10},{16,20},{18,... | collective-permute-start | bytes 49160 | tf_op jit(solution)/shard_map/ppermute | solution.py:603
  48.7 3.3 %collective-permute-start.16 = (f32[32,128]{1,0:T(8,128)S(1)}, f32[32,128]{1,0:T(8,128)S(1)}, u32[]{:S(2)}, u32[]{:S(2)}) collective-permute-start(f32[32,128]{1,0:T(8,128)S(1)} %get-tuple-element.93.after_ref.refs_1_), channel_id=1, source_target_pairs={{0,2},{2,0},{4,6},{6,4},{8,10},{10,8},{12,14},{14,12},{16,18},{18,... | collective-permute-start | bytes 49160 | tf_op jit(solution)/shard_map/ppermute | solution.py:603
  52.0 8.8 %collective-permute-start.22 = (f32[4,64,256]{2,1,0:T(8,128)S(1)}, f32[4,64,256]{2,1,0:T(8,128)S(1)}, u32[]{:S(2)}, u32[]{:S(2)}) collective-permute-start(f32[4,64,256]{2,1,0:T(8,128)S(1)} %get-tuple-element.102.refs_0_), channel_id=1, source_target_pairs={{0,1},{1,0},{2,3},{3,2},{4,5},{5,4},{6,7},{7,6},{8,9},{9,8},{10,11... | collective-permute-start | bytes 786440 | tf_op jit(solution)/shard_map/ppermute | solution.py:560
  53.1 5.5 %collective-permute-start.21 = (f32[32,128]{1,0:T(8,128)S(1)}, f32[32,128]{1,0:T(8,128)S(1)}, u32[]{:S(2)}, u32[]{:S(2)}) collective-permute-start(f32[32,128]{1,0:T(8,128)S(1)} %add.4.refs_0_), channel_id=1, source_target_pairs={{0,24},{2,26},{4,28},{6,30},{8,16},{10,18},{12,20},{14,22},{16,8},... | collective-permute-start | bytes 49160 | tf_op jit(solution)/shard_map/ppermute | solution.py:603
  55.6 4.6 %collective-permute-start.20 = (f32[32,128]{1,0:T(8,128)S(1)}, f32[32,128]{1,0:T(8,128)S(1)}, u32[]{:S(2)}, u32[]{:S(2)}) collective-permute-start(f32[32,128]{1,0:T(8,128)S(1)} %add.4.refs_0_), channel_id=1, source_target_pairs={{0,16},{2,18},{4,20},{6,22},{8,24},{10,26},{12,28},{14,30},{16,0},... | collective-permute-start | bytes 49160 | tf_op jit(solution)/shard_map/ppermute | solution.py:603
  55.9 4.4 %collective-permute-start.19 = (f32[32,128]{1,0:T(8,128)S(1)}, f32[32,128]{1,0:T(8,128)S(1)}, u32[]{:S(2)}, u32[]{:S(2)}) collective-permute-start(f32[32,128]{1,0:T(8,128)S(1)} %add.4.refs_0_), channel_id=1, source_target_pairs={{0,8},{2,10},{4,12},{6,14},{8,0},{10,2},{12,4},{14,6},{16,24},{18,... | collective-permute-start | bytes 49160 | tf_op jit(solution)/shard_map/ppermute | solution.py:603
  64.7 3.2 %collective-permute-start.25 = (f32[32,128]{1,0:T(8,128)S(1)}, f32[32,128]{1,0:T(8,128)S(1)}, u32[]{:S(2)}, u32[]{:S(2)}) collective-permute-start(f32[32,128]{1,0:T(8,128)S(1)} %get-tuple-element.108.refs_0_), channel_id=1, source_target_pairs={{0,6},{2,4},{4,2},{6,0},{8,14},{10,12},{12,10},{14,8},{16,22},{18,... | collective-permute-start | bytes 49160 | tf_op jit(solution)/shard_map/ppermute | solution.py:603
  64.8 3.8 %collective-permute-start.24 = (f32[32,128]{1,0:T(8,128)S(1)}, f32[32,128]{1,0:T(8,128)S(1)}, u32[]{:S(2)}, u32[]{:S(2)}) collective-permute-start(f32[32,128]{1,0:T(8,128)S(1)} %get-tuple-element.108.refs_0_), channel_id=1, source_target_pairs={{0,4},{2,6},{4,0},{6,2},{8,12},{10,14},{12,8},{14,10},{16,20},{18,... | collective-permute-start | bytes 49160 | tf_op jit(solution)/shard_map/ppermute | solution.py:603
  65.0 3.6 %collective-permute-start.23 = (f32[32,128]{1,0:T(8,128)S(1)}, f32[32,128]{1,0:T(8,128)S(1)}, u32[]{:S(2)}, u32[]{:S(2)}) collective-permute-start(f32[32,128]{1,0:T(8,128)S(1)} %get-tuple-element.108.refs_0_), channel_id=1, source_target_pairs={{0,2},{2,0},{4,6},{6,4},{8,10},{10,8},{12,14},{14,12},{16,18},{18,... | collective-permute-start | bytes 49160 | tf_op jit(solution)/shard_map/ppermute | solution.py:603
  68.6 5.8 %collective-permute-start.28 = (f32[32,128]{1,0:T(8,128)S(1)}, f32[32,128]{1,0:T(8,128)S(1)}, u32[]{:S(2)}, u32[]{:S(2)}) collective-permute-start(f32[32,128]{1,0:T(8,128)S(1)} %add.5.refs_0_), channel_id=1, source_target_pairs={{0,24},{2,26},{4,28},{6,30},{8,16},{10,18},{12,20},{14,22},{16,8},... | collective-permute-start | bytes 49160 | tf_op jit(solution)/shard_map/ppermute | solution.py:603
  70.1 4.7 %collective-permute-start.27 = (f32[32,128]{1,0:T(8,128)S(1)}, f32[32,128]{1,0:T(8,128)S(1)}, u32[]{:S(2)}, u32[]{:S(2)}) collective-permute-start(f32[32,128]{1,0:T(8,128)S(1)} %add.5.refs_0_), channel_id=1, source_target_pairs={{0,16},{2,18},{4,20},{6,22},{8,24},{10,26},{12,28},{14,30},{16,0},... | collective-permute-start | bytes 49160 | tf_op jit(solution)/shard_map/ppermute | solution.py:603
  71.0 3.9 %collective-permute-start.26 = (f32[32,128]{1,0:T(8,128)S(1)}, f32[32,128]{1,0:T(8,128)S(1)}, u32[]{:S(2)}, u32[]{:S(2)}) collective-permute-start(f32[32,128]{1,0:T(8,128)S(1)} %add.5.refs_0_), channel_id=1, source_target_pairs={{0,8},{2,10},{4,12},{6,14},{8,0},{10,2},{12,4},{14,6},{16,24},{18,... | collective-permute-start | bytes 49160 | tf_op jit(solution)/shard_map/ppermute | solution.py:603
  (5 other events, 40.4 us)

commit v10 on v9

--- a/solution.py
+++ b/solution.py
@@ -93,19 +93,25 @@
 
 
 def project_kernel(first, pairs, rows, lead, me_ref, data_ref, factor_ref, *refs):
-    *outs, held, arrived = refs
-    half = data_ref.shape[1] // 2
+    *outs, held, factor_held, arrived, factor_arrived = refs
+    pieces = arrived.shape[0] // (2 * pairs)
+    height = data_ref.shape[1] // pieces
+    factor_copy = pltpu.make_async_copy(factor_ref, factor_held, factor_arrived)
+    factor_copy.start()
     copies = []
     for k in range(2 * pairs):
-        for at in range(2):
-            place = pl.ds(at * half, half)
+        for at in range(pieces):
+            place = pl.ds(at * height, height)
             copies.append(
                 pltpu.make_async_copy(
-                    data_ref.at[first + k, place, :], held.at[k, place, :], arrived.at[2 * k + at]
+                    data_ref.at[first + k, place, :],
+                    held.at[k, place, :],
+                    arrived.at[pieces * k + at],
                 )
             )
             copies[-1].start()
-    factor = factor_ref[...]
+    factor_copy.wait()
+    factor = factor_held[...]
     rank = factor.shape[0]
     if lead:
         *outs, again_ref = outs
@@ -120,7 +126,7 @@
         jnp.concatenate([empty, factor], axis=0),
     ]
     for pair in range(pairs):
-        for copy in copies[4 * pair : 4 * pair + 4]:
+        for copy in copies[2 * pieces * pair : 2 * pieces * (pair + 1)]:
             copy.wait()
         for part in reversed(range(parts)):
             start = pl.multiple_of(lax.rem(me_ref[0] + part, parts) * rows, 16)
@@ -146,8 +152,10 @@
     rho = jnp.sum(weights * weights * diagonal, axis=1, keepdims=True) / rank
     rho_ref[...] = jnp.broadcast_to(rho, rho_ref.shape)
 
-    edge = 34.0 / 32.0
-    lead = 4.0 * edge**3 / (4.0 * edge**3 - 3.0 * edge)
+    centre = rank / 2.0 + 2.0
+    edge = centre / (rank / 2.0)
+    size = 8.0 * edge**4 - 8.0 * edge**2 + 1.0
+    fourth, second, unit_part = 8.0 * edge**4 / size, -8.0 * edge**2 / size, 1.0 / size
     mask = block_mask(rank, group)
     wide = wide_eye(rank, group)
     starts = range(0, count, group)
@@ -155,9 +163,9 @@
     for first in starts:
         scaled = []
         for k in range(first, first + group):
-            unit = 1.0 / (34.0 * rho[k : k + 1, :])
+            unit = 1.0 / (centre * rho[k : k + 1, :])
             column = columns[:, k : k + 1]
-            scaled.append(column * gram * weights[k : k + 1, :] * unit + (2.0 / 34.0) * eye)
+            scaled.append(column * gram * weights[k : k + 1, :] * unit + (2.0 / centre) * eye)
         systems.append(jnp.concatenate(scaled, axis=1))
     inverses, rests = [], []
     for system in systems:
@@ -165,22 +173,23 @@
         blocks = block_diagonal(rest, mask, group)
         (square,) = times_blocks([rest], blocks)
         (cube,) = times_blocks([square], blocks)
-        inverses.append(wide + lead * (rest + square))
-        rests.append(lead * cube - (lead - 1.0) * rest)
+        (quartic,) = times_blocks([square], block_diagonal(square, mask, group))
+        inverses.append(fourth * (wide + rest + square + cube) + second * (wide + rest))
+        rests.append(fourth * quartic + second * square + unit_part * wide)
     for step in range(4):
         for at in range(len(systems)):
             blocks = block_diagonal(rests[at], mask, group)
-            more, rests[at] = times_blocks([inverses[at], rests[at]], blocks)
+            more, *rest = times_blocks([inverses[at], rests[at]][: 2 if step < 3 else 1], blocks)
             inverses[at] = inverses[at] + more
-    for step in range(2):
-        for at in range(len(systems)):
-            (product,) = times_blocks([inverses[at]], block_diagonal(systems[at], mask, group))
-            blocks = block_diagonal(wide - product, mask, group)
-            (more,) = times_blocks([inverses[at]], blocks)
-            inverses[at] = inverses[at] + more
+            rests[at] = rest[0] if rest else None
+    for at in range(len(systems)):
+        (product,) = times_blocks([inverses[at]], block_diagonal(systems[at], mask, group))
+        blocks = block_diagonal(wide - product, mask, group)
+        (more,) = times_blocks([inverses[at]], blocks)
+        inverses[at] = inverses[at] + more
     for k in range(count):
         place = (k % group) * rank
-        unit = 1.0 / (34.0 * rho[k : k + 1, :])
+        unit = 1.0 / (centre * rho[k : k + 1, :])
         inverse = inverses[k // group][:, place : place + rank] * unit
         inverse_ref[k] = left_triple(inverse)
         base_ref[k] = dot(
@@ -630,6 +639,7 @@
     me = lax.axis_index("chan").astype(jnp.int32).reshape(1)
     odd = lax.rem(lax.axis_index("cuts"), 2).astype(jnp.int32).reshape(1)
     early = count // 4
+    pieces = next(pieces for pieces in (4, 2, 1) if all_rows % (16 * pieces) == 0)
     own, received = [], []
     for first, pairs, lead in ((0, early, True), (2 * early, count // 2 - early, False)):
         height = pairs * rows + (rank // 2 if lead else 0)
@@ -638,10 +648,12 @@
             "project",
             [((height, 2 * rank), f32)] * parts + [(factor.shape, factor.dtype)] * lead,
             me, data, factor,
-            scalars=1, unread=1, limit=52,
+            scalars=1, unread=2, limit=52,
             scratch=[
                 pltpu.VMEM((2 * pairs, all_rows, channels), data.dtype),
-                pltpu.SemaphoreType.DMA((4 * pairs,)),
+                pltpu.VMEM(factor.shape, factor.dtype),
+                pltpu.SemaphoreType.DMA((2 * pairs * pieces,)),
+                pltpu.SemaphoreType.DMA,
             ],
         )
         if lead:

time: 76.3 us -> 76.6 us (level)
  transfers between devices with their start and end apart: 29 -> 29, of which waited for: 12 -> 11; matrix products, arithmetic and copies ran while one was open for 0% -> 0% of each run, Pallas kernels for 25% -> 26%
where the time goes in v10:
time: 76.6 us; the launch traced here: 76.4 us
  starting transfers between devices  35 us (46%)
  Pallas kernels  28.2 us (37%)
  waiting for transfers between devices  11.4 us (15%)
  between operations  0.88 us (1%)
  local copies, waits for them, and re-layouts  0.86 us (1%)
    pallas_call x19, Pallas kernels, call(): pl.pallas_call(kernel, out_shape=shapes, in_specs=specs, out_specs=[pl.Bl...  28.2 us
    ppermute x18, starting transfers between devices, in_stages(): terms.append(lax.ppermute(value, axis, moves))  18.9 us
    ppermute x7, starting transfers between devices, rotated(): lax.ppermute(value, axis, [(i, (i + shift) % count) for i in range(count)])  10.6 us
    ppermute x18, waiting for transfers between devices, in_stages(): terms.append(lax.ppermute(value, axis, moves))  9.08 us
    ppermute x4, starting transfers between devices, swapped(): return lax.ppermute(value, axis, pairs + [(b, a) for a, b in pairs])  5.43 us
    ppermute x7, waiting for transfers between devices, rotated(): lax.ppermute(value, axis, [(i, (i + shift) % count) for i in range(count)])  2.35 us
  transfers between devices with their start and end apart: 29, of which 11 were waited for; matrix products, arithmetic and copies ran while one was open for 0% of the time, Pallas kernels for 26%

profile of v10, /device:TPU:0, one launch (start us, length us, event | category | flops | bytes accessed | tf_op | source)
XLA Modules:
  0.0 76.4 jit_solution(7567088299251938768)
XLA Ops:
  1.5 2.3 %project.2 = (f32[416,128]{1,0:T(8,128)S(1)}, f32[416,128]{1,0:T(8,128)S(1)}, bf16[64,512]{1,0:T(8,128)(2,1)S(1)}) custom-call(s32[1]{0:T(128)} %bitcast.2.me_ref, bf16[8,384,512]{2,1,0:T(8,128)(2,1)} %data_ref.3, bf16[64,512]{1,0:T(8,128)(2,1)S(1)} %bitcast.16), custom_call_target="tpu_custom_call" | custom-call | flops 330000000 | bytes 3702788 | tf_op jit(solution)/shard_map/project/pallas_call | solution.py:555
  3.8 3.0 %collective-permute-start.2 = (f32[416,128]{1,0:T(8,128)S(1)}, f32[416,128]{1,0:T(8,128)S(1)}, u32[]{:S(2)}, u32[]{:S(2)}) collective-permute-start(f32[416,128]{1,0:T(8,128)S(1)} %get-tuple-element.61), channel_id=1, source_target_pairs={{0,1},{1,0},{2,3},{3,2},{4,5},{5,4},{6,7},{7,6},{8,9},{9,8},{10,11... | collective-permute-start | bytes 638984 | tf_op jit(solution)/shard_map/ppermute | solution.py:569
  6.8 2.1 %project.3 = (f32[384,128]{1,0:T(8,128)S(1)}, f32[384,128]{1,0:T(8,128)S(1)}) custom-call(s32[1]{0:T(128)} %bitcast.2.me_ref, bf16[8,384,512]{2,1,0:T(8,128)(2,1)} %data_ref.3, bf16[64,512]{1,0:T(8,128)(2,1)S(1)} %get-tuple-element.57.factor_ref), custom_call_target="tpu_custom_call" | custom-call | flops 330000000 | bytes 3604484 | tf_op jit(solution)/shard_map/project/pallas_call | solution.py:555
  9.1 3.9 %collective-permute-start.1 = (f32[8,64]{1,0:T(8,128)S(1)}, f32[8,64]{1,0:T(8,128)S(1)}, u32[]{:S(2)}, u32[]{:S(2)}) collective-permute-start(f32[8,64]{1,0:T(8,128)S(1)} %copy-done.6), channel_id=1, source_target_pairs={{0,30},{2,0},{4,2},{6,4},{8,6},{10,8},{12,10},{14,12},{16,14},{18,... | collective-permute-start | bytes 6152 | tf_op jit(solution)/shard_map/ppermute | solution.py:569
  13.1 3.0 %setup.1 = (bf16[8,64,192]{2,1,0:T(8,128)(2,1)S(1)}, bf16[4,128,384]{2,1,0:T(8,128)(2,1)S(1)}, f32[8,128]{1,0:T(8,128)S(1)}, f32[8,64]{1,0:T(8,128)S(1)}, f32[64...) custom-call(s32[8]{0:T(128)S(1)} %copy-done.5, f32[416,128]{1,0:T(8,128)S(1)} %get-tuple-element.60.refs_0_, ...), custom_call_target="tpu_custom_call" | custom-call | flops 330000000 | bytes 2992160 | tf_op jit(solution)/shard_map/setup/pallas_call | solution.py:555
  16.4 2.3 %collective-permute-done.refs_0_.before_ref = f32[8,64]{1,0:T(8,128)S(1)} collective-permute-done((f32[8,64]{1,0:T(8,128)S(1)}, f32[8,64]{1,0:T(8,128)S(1)}, u32[]{:S(2)}, u32[]{:S(2)}) %collective-permute-start) | collective-permute-done | bytes 2080 | tf_op jit(solution)/shard_map/ppermute | solution.py:569
  18.8 1.2 %first.1 = (f32[8,64,192]{2,1,0:T(8,128)S(1)}, f32[8,64,192]{2,1,0:T(8,128)S(1)}, f32[4,64,128]{2,1,0:T(8,128)S(1)}) custom-call(s32[8]{0:T(128)S(1)} %copy-done.5, f32[8,64]{1,0:T(8,128)S(1)} %collective-permute-done.refs_0_.before_ref, f32[8,64]{1,0:T(8,128)S(1)} %collective-permute-done.1.refs_1_.after_ref, f32[8,64,192]{2,1,0:T(8,128)S(1)} %get-tuple-element.62.refs_2_, ...), custom_call_target="tpu_custom_call" | custom-call | flops 330000000 | bytes 3084320 | tf_op jit(solution)/shard_map/first/pallas_call | solution.py:555
  20.0 1.5 %collective-permute-start.4 = (f32[4,64,128]{2,1,0:T(8,128)S(1)}, f32[4,64,128]{2,1,0:T(8,128)S(1)}, u32[]{:S(2)}, u32[]{:S(2)}) collective-permute-start(f32[4,64,128]{2,1,0:T(8,128)S(1)} %get-tuple-element.72.refs_0_), channel_id=1, source_target_pairs={{0,1},{1,0},{2,3},{3,2},{4,5},{5,4},{6,7},{7,6},{8,9},{9,8},{10,11... | collective-permute-start | bytes 393224 | tf_op jit(solution)/shard_map/ppermute | solution.py:569
  21.6 1.2 %smooth.1 = (f32[8,64,192]{2,1,0:T(8,128)S(1)}, f32[8,128]{1,0:T(8,128)S(1)}, f32[8,128]{1,0:T(8,128)S(1)}, f32[8,64,192]{2,1,0:T(8,128)S(1)}, f32[2,64,384]{2,1,0:T(8,128)S(1)}, /*index=5*/f32[2,64,384]{2,1,0:T(8,128)S(1)}) custom-call(s32[1]{0:T(128)} %bitcast.odd_ref, s32[8]{0:T(128)S(1)} %copy-done.5, f32[8,64,192]{2,1,0:T(8,128)S(1)} %bitcast.10, ...), custom_call_target="tpu_custom_call" | custom-call | flops 330000000 | bytes 2576420 | tf_op jit(solution)/shard_map/smooth/pallas_call | solution.py:555
  22.8 2.8 %collective-permute-start.6 = (f32[2,64,384]{2,1,0:T(8,128)S(1)}, f32[2,64,384]{2,1,0:T(8,128)S(1)}, u32[]{:S(2)}, u32[]{:S(2)}) collective-permute-start(f32[2,64,384]{2,1,0:T(8,128)S(1)} %get-tuple-element.75), channel_id=1, source_target_pairs={{2,4},{6,8},{10,12},{14,16},{18,20},{22,24},{26,28},{30,0},{4,2},{... | collective-permute-start | bytes 589832 | tf_op jit(solution)/shard_map/ppermute | solution.py:575
  25.6 3.4 %polar.3 = (f32[4,64,128]{2,1,0:T(8,128)S(1)}, f32[32,128]{1,0:T(8,128)S(1)}, f32[4,64,128]{2,1,0:T(8,128)S(1)}) custom-call(f32[8,64,192]{2,1,0:T(8,128)S(1)} %get-tuple-element.71.after_ref.inside_ref, f32[64,64]{1,0:T(8,128)S(1)} %copy-done.7, f32[4,64,128]{2,1,0:T(8,128)S(1)} %get-tuple-element.72.refs_0_, f32[4,64,128]{2,1,0:T(8,128)S(1)} %collective-permute-done.4.refs_1_), custom_call_target="tpu_custom_call" | custom-call | flops 3300000000 | bytes 950272 | tf_op jit(solution)/shard_map/polar/pallas_call | solution.py:555
  29.1 1.8 %collective-permute-start.7 = (f32[32,128]{1,0:T(8,128)S(1)}, f32[32,128]{1,0:T(8,128)S(1)}, u32[]{:S(2)}, u32[]{:S(2)}) collective-permute-start(f32[32,128]{1,0:T(8,128)S(1)} %get-tuple-element.73.after_ref.refs_1_), channel_id=1, source_target_pairs={{0,2},{2,0},{4,6},{6,4},{8,10},{10,8},{12,14},{14,12},{16,18},{18,... | collective-permute-start | bytes 49160 | tf_op jit(solution)/shard_map/ppermute | solution.py:612
  30.9 1.2 %ahead.2 = (f32[8,64,192]{2,1,0:T(8,128)S(1)}, f32[4,64,256]{2,1,0:T(8,128)S(1)}, f32[8,64,192]{2,1,0:T(8,128)S(1)}, f32[8,64,192]{2,1,0:T(8,128)S(1)}) custom-call(s32[1]{0:T(128)} %bitcast.odd_ref, f32[32,128]{1,0:T(8,128)S(1)} %get-tuple-element.73.after_ref.refs_1_, f32[8,64,192]{2,1,0:T(8,128)S(1)} %get-tuple-element.71.after_ref.inside_ref, ...), custom_call_target="tpu_custom_call" | custom-call | flops 330000000 | bytes 3624964 | tf_op jit(solution)/shard_map/ahead/pallas_call | solution.py:555
  33.8 2.0 %collective-permute-start.12 = (f32[32,128]{1,0:T(8,128)S(1)}, f32[32,128]{1,0:T(8,128)S(1)}, u32[]{:S(2)}, u32[]{:S(2)}) collective-permute-start(f32[32,128]{1,0:T(8,128)S(1)} %add.3.refs_0_), channel_id=1, source_target_pairs={{0,24},{2,26},{4,28},{6,30},{8,16},{10,18},{12,20},{14,22},{16,8},... | collective-permute-start | bytes 49160 | tf_op jit(solution)/shard_map/ppermute | solution.py:612
  35.8 2.4 %collective-permute-start.10 = (f32[32,128]{1,0:T(8,128)S(1)}, f32[32,128]{1,0:T(8,128)S(1)}, u32[]{:S(2)}, u32[]{:S(2)}) collective-permute-start(f32[32,128]{1,0:T(8,128)S(1)} %add.3.refs_0_), channel_id=1, source_target_pairs={{0,8},{2,10},{4,12},{6,14},{8,0},{10,2},{12,4},{14,6},{16,24},{18,... | collective-permute-start | bytes 49160 | tf_op jit(solution)/shard_map/ppermute | solution.py:612
  38.2 1.2 %collective-permute-done.12.refs_3_ = f32[32,128]{1,0:T(8,128)S(1)} collective-permute-done((f32[32,128]{1,0:T(8,128)S(1)}, f32[32,128]{1,0:T(8,128)S(1)}, u32[]{:S(2)}, u32[]{:S(2)}) %collective-permute-start.12) | collective-permute-done | bytes 16416 | tf_op jit(solution)/shard_map/ppermute | solution.py:612
  41.8 2.5 %collective-permute-start.15 = (f32[2,64,384]{2,1,0:T(8,128)S(1)}, f32[2,64,384]{2,1,0:T(8,128)S(1)}, u32[]{:S(2)}, u32[]{:S(2)}) collective-permute-start(f32[2,64,384]{2,1,0:T(8,128)S(1)} %get-tuple-element.95), channel_id=1, source_target_pairs={{2,4},{6,8},{10,12},{14,16},{18,20},{22,24},{26,28},{30,0},{4,2},{... | collective-permute-start | bytes 589832 | tf_op jit(solution)/shard_map/ppermute | solution.py:575
  44.3 3.9 %polar.4 = (f32[4,64,128]{2,1,0:T(8,128)S(1)}, f32[32,128]{1,0:T(8,128)S(1)}, f32[4,64,128]{2,1,0:T(8,128)S(1)}) custom-call(f32[8,64,192]{2,1,0:T(8,128)S(1)} %get-tuple-element.88.after_ref.inside_ref, f32[64,64]{1,0:T(8,128)S(1)} %get-tuple-element.89.delta_ref, f32[4,64,128]{2,1,0:T(8,128)S(1)} %get-tuple-element.84.refs_0_.change_ref, ...), custom_call_target="tpu_custom_call" | custom-call | flops 330000000 | bytes 1474560 | tf_op jit(solution)/shard_map/polar/pallas_call | solution.py:555
  49.1 1.1 %collective-permute-start.16 = (f32[32,128]{1,0:T(8,128)S(1)}, f32[32,128]{1,0:T(8,128)S(1)}, u32[]{:S(2)}, u32[]{:S(2)}) collective-permute-start(f32[32,128]{1,0:T(8,128)S(1)} %get-tuple-element.93.after_ref.refs_1_), channel_id=1, source_target_pairs={{0,2},{2,0},{4,6},{6,4},{8,10},{10,8},{12,14},{14,12},{16,18},{18,... | collective-permute-start | bytes 49160 | tf_op jit(solution)/shard_map/ppermute | solution.py:612
  50.2 1.4 %ahead.3 = (f32[8,64,192]{2,1,0:T(8,128)S(1)}, f32[4,64,256]{2,1,0:T(8,128)S(1)}) custom-call(s32[1]{0:T(128)} %bitcast.odd_ref, f32[32,128]{1,0:T(8,128)S(1)} %get-tuple-element.93.after_ref.refs_1_, f32[8,64,192]{2,1,0:T(8,128)S(1)} %get-tuple-element.88.after_ref.inside_ref, f32[2,64,384]{2,1,0:T(8,128)S(1)} %collective-permute-done.14.near_ref, ...), custom_call_target="tpu_custom_call" | custom-call | flops 330000000 | bytes 2838532 | tf_op jit(solution)/shard_map/ahead/pallas_call | solution.py:555
  52.3 1.1 %collective-permute-start.22 = (f32[4,64,256]{2,1,0:T(8,128)S(1)}, f32[4,64,256]{2,1,0:T(8,128)S(1)}, u32[]{:S(2)}, u32[]{:S(2)}) collective-permute-start(f32[4,64,256]{2,1,0:T(8,128)S(1)} %get-tuple-element.102.refs_0_), channel_id=1, source_target_pairs={{0,1},{1,0},{2,3},{3,2},{4,5},{5,4},{6,7},{7,6},{8,9},{9,8},{10,11... | collective-permute-start | bytes 786440 | tf_op jit(solution)/shard_map/ppermute | solution.py:569
  53.4 2.6 %collective-permute-start.21 = (f32[32,128]{1,0:T(8,128)S(1)}, f32[32,128]{1,0:T(8,128)S(1)}, u32[]{:S(2)}, u32[]{:S(2)}) collective-permute-start(f32[32,128]{1,0:T(8,128)S(1)} %add.4.refs_0_), channel_id=1, source_target_pairs={{0,24},{2,26},{4,28},{6,30},{8,16},{10,18},{12,20},{14,22},{16,8},... | collective-permute-start | bytes 49160 | tf_op jit(solution)/shard_map/ppermute | solution.py:612
  56.1 1.6 %collective-permute-start.19 = (f32[32,128]{1,0:T(8,128)S(1)}, f32[32,128]{1,0:T(8,128)S(1)}, u32[]{:S(2)}, u32[]{:S(2)}) collective-permute-start(f32[32,128]{1,0:T(8,128)S(1)} %add.4.refs_0_), channel_id=1, source_target_pairs={{0,8},{2,10},{4,12},{6,14},{8,0},{10,2},{12,4},{14,6},{16,24},{18,... | collective-permute-start | bytes 49160 | tf_op jit(solution)/shard_map/ppermute | solution.py:612
  57.7 1.1 %collective-permute-done.21.refs_3_ = f32[32,128]{1,0:T(8,128)S(1)} collective-permute-done((f32[32,128]{1,0:T(8,128)S(1)}, f32[32,128]{1,0:T(8,128)S(1)}, u32[]{:S(2)}, u32[]{:S(2)}) %collective-permute-start.21) | collective-permute-done | bytes 16416 | tf_op jit(solution)/shard_map/ppermute | solution.py:612
  58.9 1.7 %collective-permute-done.20.refs_2_ = f32[32,128]{1,0:T(8,128)S(1)} collective-permute-done((f32[32,128]{1,0:T(8,128)S(1)}, f32[32,128]{1,0:T(8,128)S(1)}, u32[]{:S(2)}, u32[]{:S(2)}) %collective-permute-start.20) | collective-permute-done | bytes 16416 | tf_op jit(solution)/shard_map/ppermute | solution.py:612
  61.1 3.9 %polar.5 = (f32[4,64,128]{2,1,0:T(8,128)S(1)}, f32[32,128]{1,0:T(8,128)S(1)}) custom-call(f32[8,64,192]{2,1,0:T(8,128)S(1)} %get-tuple-element.88.after_ref.inside_ref, f32[64,64]{1,0:T(8,128)S(1)} %get-tuple-element.99.delta_ref, f32[4,64,128]{2,1,0:T(8,128)S(1)} %get-tuple-element.100.change_ref, f32[4,64,128]{2,1,0:T(8,128)S(1)} %get-tuple-element.101.old_ref, ...), custom_call_target="tpu_custom_call" | custom-call | flops 330000000 | bytes 1343488 | tf_op jit(solution)/shard_map/polar/pallas_call | solution.py:555
  65.3 1.6 %collective-permute-start.23 = (f32[32,128]{1,0:T(8,128)S(1)}, f32[32,128]{1,0:T(8,128)S(1)}, u32[]{:S(2)}, u32[]{:S(2)}) collective-permute-start(f32[32,128]{1,0:T(8,128)S(1)} %get-tuple-element.108.refs_0_), channel_id=1, source_target_pairs={{0,2},{2,0},{4,6},{6,4},{8,10},{10,8},{12,14},{14,12},{16,18},{18,... | collective-permute-start | bytes 49160 | tf_op jit(solution)/shard_map/ppermute | solution.py:612
  66.9 1.3 %collective-permute-done.25.refs_3_ = f32[32,128]{1,0:T(8,128)S(1)} collective-permute-done((f32[32,128]{1,0:T(8,128)S(1)}, f32[32,128]{1,0:T(8,128)S(1)}, u32[]{:S(2)}, u32[]{:S(2)}) %collective-permute-start.25) | collective-permute-done | bytes 16416 | tf_op jit(solution)/shard_map/ppermute | solution.py:612
  68.9 1.5 %collective-permute-start.28 = (f32[32,128]{1,0:T(8,128)S(1)}, f32[32,128]{1,0:T(8,128)S(1)}, u32[]{:S(2)}, u32[]{:S(2)}) collective-permute-start(f32[32,128]{1,0:T(8,128)S(1)} %add.5.refs_0_), channel_id=1, source_target_pairs={{0,24},{2,26},{4,28},{6,30},{8,16},{10,18},{12,20},{14,22},{16,8},... | collective-permute-start | bytes 49160 | tf_op jit(solution)/shard_map/ppermute | solution.py:612
  71.3 2.0 %collective-permute-start.26 = (f32[32,128]{1,0:T(8,128)S(1)}, f32[32,128]{1,0:T(8,128)S(1)}, u32[]{:S(2)}, u32[]{:S(2)}) collective-permute-start(f32[32,128]{1,0:T(8,128)S(1)} %add.5.refs_0_), channel_id=1, source_target_pairs={{0,8},{2,10},{4,12},{6,14},{8,0},{10,2},{12,4},{14,6},{16,24},{18,... | collective-permute-start | bytes 49160 | tf_op jit(solution)/shard_map/ppermute | solution.py:612
  73.3 1.2 %rows.3 = (bf16[8,192,192]{2,1,0:T(8,128)(2,1)S(1)}, f32[8,64,192]{2,1,0:T(8,128)}) custom-call(f32[4,64,128]{2,1,0:T(8,128)S(1)} %get-tuple-element.103.mixed_ref, f32[4,64,128]{2,1,0:T(8,128)S(1)} %get-tuple-element.100.change_ref, f32[4,64,128]{2,1,0:T(8,128)S(1)} %get-tuple-element.104.forward_ref, f32[8,64,192]{2,1,0:T(8,128)S(1)} %get-tuple-element.97.tall_ref, ...), custom_call_target="tpu_custom_call" | custom-call | flops 330000000 | bytes 2162688 | tf_op jit(solution)/shard_map/rows/pallas_call | solution.py:555
  75.2 1.1 %last.1 = (f32[8,64,192]{2,1,0:T(8,128)}, f32[64,64]{1,0:T(8,128)}) custom-call(bf16[8,192,192]{2,1,0:T(8,128)(2,1)S(1)} %get-tuple-element.107.mixed_tall_ref, f32[32,128]{1,0:T(8,128)S(1)} %add.5.refs_0_, f32[32,128]{1,0:T(8,128)S(1)} %collective-permute-done.26.refs_1_, f32[32,128]{1,0:T(8,128)S(1)} %collective-permute-done.27.refs_2_, ...), custom_call_target="tpu_custom_call" | custom-call | flops 330000000 | bytes 1064960 | tf_op jit(solution)/shard_map/last/pallas_call | solution.py:555
  (61 shorter events, 10.4 us)
Async XLA Ops:
  1.5 11.6 %copy-start.2 = (f32[8,192,64]{1,2,0:T(8,128)S(1)}, f32[8,192,64]{1,2,0:T(8,128)}, u32[]{:S(2)}) copy-start(f32[8,192,64]{1,2,0:T(8,128)} %param.16) | copy-start | bytes 1179652
  1.5 11.6 %copy-start.3 = (f32[8,192,64]{1,2,0:T(8,128)S(1)}, f32[8,192,64]{1,2,0:T(8,128)}, u32[]{:S(2)}) copy-start(f32[8,192,64]{1,2,0:T(8,128)} %param.14) | copy-start | bytes 1179652
  1.5 11.6 %copy-start.5 = (s32[8]{0:T(128)S(1)}, s32[8]{0:T(128)}, u32[]{:S(2)}) copy-start(s32[8]{0:T(128)} %order_ref.5) | copy-start | bytes 100
  3.8 9.2 %collective-permute-start.2 = (f32[416,128]{1,0:T(8,128)S(1)}, f32[416,128]{1,0:T(8,128)S(1)}, u32[]{:S(2)}, u32[]{:S(2)}) collective-permute-start(f32[416,128]{1,0:T(8,128)S(1)} %get-tuple-element.61), channel_id=1, source_target_pairs={{0,1},{1,0},{2,3},{3,2},{4,5},{5,4},{6,7},{7,6},{8,9},{9,8},{10,11... | collective-permute-start | bytes 638984 | tf_op jit(solution)/shard_map/ppermute | solution.py:569
  9.0 9.8 %collective-permute-start.3 = (f32[384,128]{1,0:T(8,128)S(1)}, f32[384,128]{1,0:T(8,128)S(1)}, u32[]{:S(2)}, u32[]{:S(2)}) collective-permute-start(f32[384,128]{1,0:T(8,128)S(1)} %get-tuple-element.65), channel_id=1, source_target_pairs={{0,1},{1,0},{2,3},{3,2},{4,5},{5,4},{6,7},{7,6},{8,9},{9,8},{10,11... | collective-permute-start | bytes 589832 | tf_op jit(solution)/shard_map/ppermute | solution.py:569
  9.1 7.3 %collective-permute-start.1 = (f32[8,64]{1,0:T(8,128)S(1)}, f32[8,64]{1,0:T(8,128)S(1)}, u32[]{:S(2)}, u32[]{:S(2)}) collective-permute-start(f32[8,64]{1,0:T(8,128)S(1)} %copy-done.6), channel_id=1, source_target_pairs={{0,30},{2,0},{4,2},{6,4},{8,6},{10,8},{12,10},{14,12},{16,14},{18,... | collective-permute-start | bytes 6152 | tf_op jit(solution)/shard_map/ppermute | solution.py:569
  13.0 5.7 %collective-permute-start = (f32[8,64]{1,0:T(8,128)S(1)}, f32[8,64]{1,0:T(8,128)S(1)}, u32[]{:S(2)}, u32[]{:S(2)}) collective-permute-start(f32[8,64]{1,0:T(8,128)S(1)} %copy-done.6), channel_id=1, source_target_pairs={{0,2},{2,4},{4,6},{6,8},{8,10},{10,12},{12,14},{14,16},{16,18},{18... | collective-permute-start | bytes 6152 | tf_op jit(solution)/shard_map/ppermute | solution.py:569
  20.0 5.6 %collective-permute-start.4 = (f32[4,64,128]{2,1,0:T(8,128)S(1)}, f32[4,64,128]{2,1,0:T(8,128)S(1)}, u32[]{:S(2)}, u32[]{:S(2)}) collective-permute-start(f32[4,64,128]{2,1,0:T(8,128)S(1)} %get-tuple-element.72.refs_0_), channel_id=1, source_target_pairs={{0,1},{1,0},{2,3},{3,2},{4,5},{5,4},{6,7},{7,6},{8,9},{9,8},{10,11... | collective-permute-start | bytes 393224 | tf_op jit(solution)/shard_map/ppermute | solution.py:569
  22.7 8.2 %collective-permute-start.5 = (f32[2,64,384]{2,1,0:T(8,128)S(1)}, f32[2,64,384]{2,1,0:T(8,128)S(1)}, u32[]{:S(2)}, u32[]{:S(2)}) collective-permute-start(f32[2,64,384]{2,1,0:T(8,128)S(1)} %get-tuple-element.74), channel_id=1, source_target_pairs={{0,2},{4,6},{8,10},{12,14},{16,18},{20,22},{24,26},{28,30},{2,0},{... | collective-permute-start | bytes 589832 | tf_op jit(solution)/shard_map/ppermute | solution.py:575
  22.8 8.1 %collective-permute-start.6 = (f32[2,64,384]{2,1,0:T(8,128)S(1)}, f32[2,64,384]{2,1,0:T(8,128)S(1)}, u32[]{:S(2)}, u32[]{:S(2)}) collective-permute-start(f32[2,64,384]{2,1,0:T(8,128)S(1)} %get-tuple-element.75), channel_id=1, source_target_pairs={{2,4},{6,8},{10,12},{14,16},{18,20},{22,24},{26,28},{30,0},{4,2},{... | collective-permute-start | bytes 589832 | tf_op jit(solution)/shard_map/ppermute | solution.py:575
  29.0 3.2 %collective-permute-start.9 = (f32[32,128]{1,0:T(8,128)S(1)}, f32[32,128]{1,0:T(8,128)S(1)}, u32[]{:S(2)}, u32[]{:S(2)}) collective-permute-start(f32[32,128]{1,0:T(8,128)S(1)} %get-tuple-element.73.after_ref.refs_1_), channel_id=1, source_target_pairs={{0,6},{2,4},{4,2},{6,0},{8,14},{10,12},{12,10},{14,8},{16,22},{18,... | collective-permute-start | bytes 49160 | tf_op jit(solution)/shard_map/ppermute | solution.py:612
  29.1 3.8 %collective-permute-start.8 = (f32[32,128]{1,0:T(8,128)S(1)}, f32[32,128]{1,0:T(8,128)S(1)}, u32[]{:S(2)}, u32[]{:S(2)}) collective-permute-start(f32[32,128]{1,0:T(8,128)S(1)} %get-tuple-element.73.after_ref.refs_1_), channel_id=1, source_target_pairs={{0,4},{2,6},{4,0},{6,2},{8,12},{10,14},{12,8},{14,10},{16,20},{18,... | collective-permute-start | bytes 49160 | tf_op jit(solution)/shard_map/ppermute | solution.py:612
  29.1 3.7 %collective-permute-start.7 = (f32[32,128]{1,0:T(8,128)S(1)}, f32[32,128]{1,0:T(8,128)S(1)}, u32[]{:S(2)}, u32[]{:S(2)}) collective-permute-start(f32[32,128]{1,0:T(8,128)S(1)} %get-tuple-element.73.after_ref.refs_1_), channel_id=1, source_target_pairs={{0,2},{2,0},{4,6},{6,4},{8,10},{10,8},{12,14},{14,12},{16,18},{18,... | collective-permute-start | bytes 49160 | tf_op jit(solution)/shard_map/ppermute | solution.py:612
  32.9 11.5 %collective-permute-start.13 = (f32[4,64,256]{2,1,0:T(8,128)S(1)}, f32[4,64,256]{2,1,0:T(8,128)S(1)}, u32[]{:S(2)}, u32[]{:S(2)}) collective-permute-start(f32[4,64,256]{2,1,0:T(8,128)S(1)} %get-tuple-element.91.refs_0_), channel_id=1, source_target_pairs={{0,1},{1,0},{2,3},{3,2},{4,5},{5,4},{6,7},{7,6},{8,9},{9,8},{10,11... | collective-permute-start | bytes 786440 | tf_op jit(solution)/shard_map/ppermute | solution.py:569
  33.8 5.6 %collective-permute-start.12 = (f32[32,128]{1,0:T(8,128)S(1)}, f32[32,128]{1,0:T(8,128)S(1)}, u32[]{:S(2)}, u32[]{:S(2)}) collective-permute-start(f32[32,128]{1,0:T(8,128)S(1)} %add.3.refs_0_), channel_id=1, source_target_pairs={{0,24},{2,26},{4,28},{6,30},{8,16},{10,18},{12,20},{14,22},{16,8},... | collective-permute-start | bytes 49160 | tf_op jit(solution)/shard_map/ppermute | solution.py:612
  35.8 4.6 %collective-permute-start.11 = (f32[32,128]{1,0:T(8,128)S(1)}, f32[32,128]{1,0:T(8,128)S(1)}, u32[]{:S(2)}, u32[]{:S(2)}) collective-permute-start(f32[32,128]{1,0:T(8,128)S(1)} %add.3.refs_0_), channel_id=1, source_target_pairs={{0,16},{2,18},{4,20},{6,22},{8,24},{10,26},{12,28},{14,30},{16,0},... | collective-permute-start | bytes 49160 | tf_op jit(solution)/shard_map/ppermute | solution.py:612
  35.8 4.6 %collective-permute-start.10 = (f32[32,128]{1,0:T(8,128)S(1)}, f32[32,128]{1,0:T(8,128)S(1)}, u32[]{:S(2)}, u32[]{:S(2)}) collective-permute-start(f32[32,128]{1,0:T(8,128)S(1)} %add.3.refs_0_), channel_id=1, source_target_pairs={{0,8},{2,10},{4,12},{6,14},{8,0},{10,2},{12,4},{14,6},{16,24},{18,... | collective-permute-start | bytes 49160 | tf_op jit(solution)/shard_map/ppermute | solution.py:612
  41.7 8.4 %collective-permute-start.14 = (f32[2,64,384]{2,1,0:T(8,128)S(1)}, f32[2,64,384]{2,1,0:T(8,128)S(1)}, u32[]{:S(2)}, u32[]{:S(2)}) collective-permute-start(f32[2,64,384]{2,1,0:T(8,128)S(1)} %get-tuple-element.94), channel_id=1, source_target_pairs={{0,2},{4,6},{8,10},{12,14},{16,18},{20,22},{24,26},{28,30},{2,0},{... | collective-permute-start | bytes 589832 | tf_op jit(solution)/shard_map/ppermute | solution.py:575
  41.8 8.4 %collective-permute-start.15 = (f32[2,64,384]{2,1,0:T(8,128)S(1)}, f32[2,64,384]{2,1,0:T(8,128)S(1)}, u32[]{:S(2)}, u32[]{:S(2)}) collective-permute-start(f32[2,64,384]{2,1,0:T(8,128)S(1)} %get-tuple-element.95), channel_id=1, source_target_pairs={{2,4},{6,8},{10,12},{14,16},{18,20},{22,24},{26,28},{30,0},{4,2},{... | collective-permute-start | bytes 589832 | tf_op jit(solution)/shard_map/ppermute | solution.py:575
  48.2 3.3 %collective-permute-start.18 = (f32[32,128]{1,0:T(8,128)S(1)}, f32[32,128]{1,0:T(8,128)S(1)}, u32[]{:S(2)}, u32[]{:S(2)}) collective-permute-start(f32[32,128]{1,0:T(8,128)S(1)} %get-tuple-element.93.after_ref.refs_1_), channel_id=1, source_target_pairs={{0,6},{2,4},{4,2},{6,0},{8,14},{10,12},{12,10},{14,8},{16,22},{18,... | collective-permute-start | bytes 49160 | tf_op jit(solution)/shard_map/ppermute | solution.py:612
  48.5 3.7 %collective-permute-start.17 = (f32[32,128]{1,0:T(8,128)S(1)}, f32[32,128]{1,0:T(8,128)S(1)}, u32[]{:S(2)}, u32[]{:S(2)}) collective-permute-start(f32[32,128]{1,0:T(8,128)S(1)} %get-tuple-element.93.after_ref.refs_1_), channel_id=1, source_target_pairs={{0,4},{2,6},{4,0},{6,2},{8,12},{10,14},{12,8},{14,10},{16,20},{18,... | collective-permute-start | bytes 49160 | tf_op jit(solution)/shard_map/ppermute | solution.py:612
  49.1 3.2 %collective-permute-start.16 = (f32[32,128]{1,0:T(8,128)S(1)}, f32[32,128]{1,0:T(8,128)S(1)}, u32[]{:S(2)}, u32[]{:S(2)}) collective-permute-start(f32[32,128]{1,0:T(8,128)S(1)} %get-tuple-element.93.after_ref.refs_1_), channel_id=1, source_target_pairs={{0,2},{2,0},{4,6},{6,4},{8,10},{10,8},{12,14},{14,12},{16,18},{18,... | collective-permute-start | bytes 49160 | tf_op jit(solution)/shard_map/ppermute | solution.py:612
  52.3 8.8 %collective-permute-start.22 = (f32[4,64,256]{2,1,0:T(8,128)S(1)}, f32[4,64,256]{2,1,0:T(8,128)S(1)}, u32[]{:S(2)}, u32[]{:S(2)}) collective-permute-start(f32[4,64,256]{2,1,0:T(8,128)S(1)} %get-tuple-element.102.refs_0_), channel_id=1, source_target_pairs={{0,1},{1,0},{2,3},{3,2},{4,5},{5,4},{6,7},{7,6},{8,9},{9,8},{10,11... | collective-permute-start | bytes 786440 | tf_op jit(solution)/shard_map/ppermute | solution.py:569
  53.4 5.5 %collective-permute-start.21 = (f32[32,128]{1,0:T(8,128)S(1)}, f32[32,128]{1,0:T(8,128)S(1)}, u32[]{:S(2)}, u32[]{:S(2)}) collective-permute-start(f32[32,128]{1,0:T(8,128)S(1)} %add.4.refs_0_), channel_id=1, source_target_pairs={{0,24},{2,26},{4,28},{6,30},{8,16},{10,18},{12,20},{14,22},{16,8},... | collective-permute-start | bytes 49160 | tf_op jit(solution)/shard_map/ppermute | solution.py:612
  55.9 4.6 %collective-permute-start.20 = (f32[32,128]{1,0:T(8,128)S(1)}, f32[32,128]{1,0:T(8,128)S(1)}, u32[]{:S(2)}, u32[]{:S(2)}) collective-permute-start(f32[32,128]{1,0:T(8,128)S(1)} %add.4.refs_0_), channel_id=1, source_target_pairs={{0,16},{2,18},{4,20},{6,22},{8,24},{10,26},{12,28},{14,30},{16,0},... | collective-permute-start | bytes 49160 | tf_op jit(solution)/shard_map/ppermute | solution.py:612
  56.1 4.4 %collective-permute-start.19 = (f32[32,128]{1,0:T(8,128)S(1)}, f32[32,128]{1,0:T(8,128)S(1)}, u32[]{:S(2)}, u32[]{:S(2)}) collective-permute-start(f32[32,128]{1,0:T(8,128)S(1)} %add.4.refs_0_), channel_id=1, source_target_pairs={{0,8},{2,10},{4,12},{6,14},{8,0},{10,2},{12,4},{14,6},{16,24},{18,... | collective-permute-start | bytes 49160 | tf_op jit(solution)/shard_map/ppermute | solution.py:612
  65.0 3.2 %collective-permute-start.25 = (f32[32,128]{1,0:T(8,128)S(1)}, f32[32,128]{1,0:T(8,128)S(1)}, u32[]{:S(2)}, u32[]{:S(2)}) collective-permute-start(f32[32,128]{1,0:T(8,128)S(1)} %get-tuple-element.108.refs_0_), channel_id=1, source_target_pairs={{0,6},{2,4},{4,2},{6,0},{8,14},{10,12},{12,10},{14,8},{16,22},{18,... | collective-permute-start | bytes 49160 | tf_op jit(solution)/shard_map/ppermute | solution.py:612
  65.0 3.8 %collective-permute-start.24 = (f32[32,128]{1,0:T(8,128)S(1)}, f32[32,128]{1,0:T(8,128)S(1)}, u32[]{:S(2)}, u32[]{:S(2)}) collective-permute-start(f32[32,128]{1,0:T(8,128)S(1)} %get-tuple-element.108.refs_0_), channel_id=1, source_target_pairs={{0,4},{2,6},{4,0},{6,2},{8,12},{10,14},{12,8},{14,10},{16,20},{18,... | collective-permute-start | bytes 49160 | tf_op jit(solution)/shard_map/ppermute | solution.py:612
  65.3 3.5 %collective-permute-start.23 = (f32[32,128]{1,0:T(8,128)S(1)}, f32[32,128]{1,0:T(8,128)S(1)}, u32[]{:S(2)}, u32[]{:S(2)}) collective-permute-start(f32[32,128]{1,0:T(8,128)S(1)} %get-tuple-element.108.refs_0_), channel_id=1, source_target_pairs={{0,2},{2,0},{4,6},{6,4},{8,10},{10,8},{12,14},{14,12},{16,18},{18,... | collective-permute-start | bytes 49160 | tf_op jit(solution)/shard_map/ppermute | solution.py:612
  68.9 5.7 %collective-permute-start.28 = (f32[32,128]{1,0:T(8,128)S(1)}, f32[32,128]{1,0:T(8,128)S(1)}, u32[]{:S(2)}, u32[]{:S(2)}) collective-permute-start(f32[32,128]{1,0:T(8,128)S(1)} %add.5.refs_0_), channel_id=1, source_target_pairs={{0,24},{2,26},{4,28},{6,30},{8,16},{10,18},{12,20},{14,22},{16,8},... | collective-permute-start | bytes 49160 | tf_op jit(solution)/shard_map/ppermute | solution.py:612
  70.4 4.6 %collective-permute-start.27 = (f32[32,128]{1,0:T(8,128)S(1)}, f32[32,128]{1,0:T(8,128)S(1)}, u32[]{:S(2)}, u32[]{:S(2)}) collective-permute-start(f32[32,128]{1,0:T(8,128)S(1)} %add.5.refs_0_), channel_id=1, source_target_pairs={{0,16},{2,18},{4,20},{6,22},{8,24},{10,26},{12,28},{14,30},{16,0},... | collective-permute-start | bytes 49160 | tf_op jit(solution)/shard_map/ppermute | solution.py:612
  71.3 3.9 %collective-permute-start.26 = (f32[32,128]{1,0:T(8,128)S(1)}, f32[32,128]{1,0:T(8,128)S(1)}, u32[]{:S(2)}, u32[]{:S(2)}) collective-permute-start(f32[32,128]{1,0:T(8,128)S(1)} %add.5.refs_0_), channel_id=1, source_target_pairs={{0,8},{2,10},{4,12},{6,14},{8,0},{10,2},{12,4},{14,6},{16,24},{18,... | collective-permute-start | bytes 49160 | tf_op jit(solution)/shard_map/ppermute | solution.py:612
  (5 other events, 41.1 us)
